TPU v7x, 256 devices: a whole 4x4x8 slice. The times are simulated.
256 devices in a mesh: gx: 32 (over x, z_lo, core), ka: 8 (over y, z_hi).
Axes of the slice: x: 4, y: 4, z: 8 (z_hi: 2, z_lo: 4; z = z_hi * 4 + z_lo), core: 2. Of those that a mesh axis runs over, the one named last changes fastest.
Arguments:
- density: float32 [128, 64, 128, 128], P('gx', None, 'ka'), may hold values from -6 to 6
- potential_x: float32 [128, 128], P('gx'), may hold values from -6 to 6
- potential_y: float32 [64, 128], replicated, may hold values from -6 to 6
- speeds_x: float32 [128], P('ka'), may hold values from 0.2 to 1.5
- speeds_y: float32 [128], replicated, may hold values from 0.2 to 1.5
- upwind_x: int32 [128], P('ka'), may hold values from 0 to 1
- upwind_y: int32 [128], replicated, may hold values from 0 to 1
Outputs:
- advanced: float32 [128, 64, 128, 128], P('gx', None, 'ka')
Inputs may be any that keep to these rules, and one draw needn't show every extreme that they name: `upwind_x`: 1 means drift toward higher positions, 0 toward lower. `upwind_y`: 1 means drift toward higher positions, 0 toward lower.
All inputs are finite; a program needn't handle non-finite values.
Results may differ from a plain program's by a relative error of at most 0.0003.
Values sent between devices are 32-bit elements; how exact they have to be, the bound alone decides.
No kernel may reach another device: no remote copies, remote signals or barrier semaphores. Data moves between devices by JAX's collectives and lax.ppermute only.
A program may use at most 64 MiB of HBM per device.

v0:
```python
import math

import jax
import jax.numpy as jnp
from jax import lax
from jax.sharding import PartitionSpec as P

KX = 128
KY = 128


step_size = 0.25


def extended(cells, sides, width):
    for axis, dim in sides:
        count = lax.axis_size(axis)
        ends = count - 1
        head = lax.slice_in_dim(cells, 0, width, axis=dim)
        tail = lax.slice_in_dim(cells, cells.shape[dim] - width, cells.shape[dim], axis=dim)
        cells = jnp.concatenate(
            [
                lax.ppermute(tail, axis, [(i, (i + 1) % count) for i in range(ends)]),
                cells,
                lax.ppermute(head, axis, [((i + 1) % count, i) for i in range(ends)]),
            ],
            axis=dim,
        )
    return cells


def tables(count):
    index = jnp.arange(count, dtype=jnp.int32)
    product = index[:, None] * index[None, :] % count
    angle = product.astype(jnp.float32) * (2.0 * math.pi / count)
    cosine = jnp.cos(angle)
    sine = jnp.sin(angle)
    forward = jnp.concatenate([cosine, sine], 0)
    backward = jnp.concatenate([sine, -cosine], 0) / count
    return (forward, backward)


def wigner_first(field, potential, forward, backward):
    hatted = jnp.einsum("ak,xykq->xyaq", forward, field, precision=lax.Precision.HIGHEST)
    weight = jnp.concatenate([potential, potential], 1)
    hatted = hatted * weight[:, None, :, None]
    return jnp.einsum("ak,xyaq->xykq", backward, hatted, precision=lax.Precision.HIGHEST)


def wigner_second(field, potential, forward, backward):
    hatted = jnp.einsum("aq,xykq->xyka", forward, field, precision=lax.Precision.HIGHEST)
    weight = jnp.concatenate([potential, potential], 1)
    hatted = hatted * weight[None, :, None, :]
    return jnp.einsum("aq,xyka->xykq", backward, hatted, precision=lax.Precision.HIGHEST)


def upwind(center, lower_two, lower_one, upper_one, upper_two, velocity):
    toward = velocity > 0
    first = jnp.where(toward, lower_one, upper_one)
    second = jnp.where(toward, lower_two, upper_two)
    return -jnp.abs(velocity) * (3.0 * center - 4.0 * first + second) * 0.5


def drift_terms(padded, vel_x, vel_y):
    center = padded[2:-2, 2:-2]
    along_x = upwind(
        center,
        padded[0:-4, 2:-2],
        padded[1:-3, 2:-2],
        padded[3:-1, 2:-2],
        padded[4:, 2:-2],
        vel_x[None, None, :, None],
    )
    along_y = upwind(
        center,
        padded[2:-2, 0:-4],
        padded[2:-2, 1:-3],
        padded[2:-2, 3:-1],
        padded[2:-2, 4:],
        vel_y[None, None, None, :],
    )
    return along_x + along_y


def per_device(density, potential_x, potential_y, speeds_x, speeds_y, upwind_x, upwind_y):
    vel_local = (2 * upwind_x - 1).astype(jnp.float32) * speeds_x
    vel_y = (2 * upwind_y - 1).astype(jnp.float32) * speeds_y
    tabs_x = tables(KX)
    tabs_y = tables(KY)

    def operator_slab(field):
        padded = extended(field, (("gx", 0),), 2)
        padded = jnp.pad(padded, ((0, 0), (2, 2), (0, 0), (0, 0)))
        drift = drift_terms(padded, vel_local, vel_y)
        result = wigner_first(
            lax.all_to_all(field, "ka", split_axis=1, concat_axis=2, tiled=True),
            potential_x,
            tabs_x[0],
            tabs_x[1],
        )
        first = lax.all_to_all(result, "ka", split_axis=2, concat_axis=1, tiled=True)
        second = wigner_second(field, potential_y, tabs_y[0], tabs_y[1])
        return drift + first + second

    section = density + step_size * operator_slab(density)
    later = operator_slab(section)
    return 0.5 * (density + section + step_size * later)


def solution(mesh):
    in_specs = (P("gx", None, "ka", None), P("gx", None), P(), P("ka"), P(), P("ka"), P())
    out_specs = P("gx", None, "ka", None)
    return jax.shard_map(
        per_device, mesh=mesh, in_specs=in_specs, out_specs=out_specs, check_vma=False
    )
```

profile of v0, /device:TPU:39, one launch (start us, length us, event | category | flops | bytes accessed | tf_op | source)
XLA Modules:
  0.0 319.0 jit_solution(7187165788555484893)
XLA Ops:
  0.0 3.2 %copy.35 = f32[4,64,16,128]{3,2,0,1:T(8,128)} copy(f32[4,64,16,128]{3,2,1,0:T(8,128)} %param.7) | data formatting | bytes 4194304 | tf_op args[0]
  3.2 10.0 %all-to-all-start = ((f32[4,64,16,128]{3,2,0,1:T(8,128)}), f32[4,64,16,128]{3,2,0,1:T(8,128)S(1)}, u32[]{:S(2)}, u32[]{:S(2)}) async-start(f32[4,64,16,128]{3,2,0,1:T(8,128)} %copy.35), calls=%async_computation | async-start | bytes 4194304 | tf_op jit(solution)/shard_map/all_to_all | solution.py:96
  13.3 0.3 fusion.68
  13.6 0.3 fusion.66
  13.8 52.2 %all-to-all-done = f32[4,64,16,128]{3,2,0,1:T(8,128)S(1)} async-done(((f32[4,64,16,128]{3,2,0,1:T(8,128)}), f32[4,64,16,128]{3,2,0,1:T(8,128)S(1)}, u32[]{:S(2)}, u32[]{:S(2)}) %all-to-all-start) | async-done | bytes 2097184 | tf_op jit(solution)/shard_map/all_to_all | solution.py:96
  66.1 1.3 copy-done.5
  67.4 1.9 copy.37
  69.3 3.6 %fusion.65 = f32[256,4,8,128]{3,0,2,1:T(8,128)S(1)} fusion(f32[4,8,128,128]{3,2,1,0:T(8,128)S(1)} %bitcast.55, f32[128,128]{1,0:T(8,128)S(1)} %get-tuple-element.11, f32[128,128]{1,0:T(8,128)S(1)} %get-tuple-element.12), kind=kOutput, calls=%fused_computation.83 | convolution fusion | flops 1610645504 | bytes 6422528 | tf_op jit(solution)/shard_map/ak,xykq->xyaq/dot_general | solution.py:44
  72.9 6.9 %fusion.45 = f32[4,8,128,128]{2,3,1,0:T(8,128)S(1)} fusion(f32[256,4,8,128]{3,0,2,1:T(8,128)S(1)} %fusion.65, f32[4,256]{1,0:T(4,128)S(1)} %constant_dynamic-update-slice_fusion.4, f32[128,128]{1,0:T(8,128)S(1)} %fusion.68, f32[128,128]{1,0:T(8,128)S(1)} %get-tuple-element.11), kind=kOutput, calls=%fused_computation.65 | convolution fusion | flops 1611726848 | bytes 6426624 | tf_op jit(solution)/shard_map/ak,xyaq->xykq/dot_general | solution.py:47
  79.7 2.0 copy.39
  81.7 4.7 %all-to-all-start.1 = ((f32[4,8,128,128]{3,1,0,2:T(8,128)}), f32[4,8,128,128]{3,1,0,2:T(8,128)}, u32[]{:S(2)}, u32[]{:S(2)}) async-start(f32[4,8,128,128]{3,1,0,2:T(8,128)} %copy.39), calls=%async_computation.1 | async-start | bytes 4194304 | tf_op jit(solution)/shard_map/all_to_all | solution.py:101
  86.4 0.0 copy-start.11
  86.4 0.0 copy-start.12
  86.4 0.0 copy-start.13
  86.4 0.0 copy-start.14
  86.4 0.0 copy-start.9
  86.5 0.1 fusion.82
  86.6 4.0 %collective-permute-start = (f32[2,64,16,128]{3,2,1,0:T(8,128)S(1)}, f32[2,64,16,128]{3,2,1,0:T(8,128)S(1)}, u32[]{:S(2)}, u32[]{:S(2)}) collective-permute-start(f32[2,64,16,128]{3,2,1,0:T(8,128)S(1)} %get-tuple-element.9), channel_id=1, source_target_pairs={{0,8},{8,16},{16,24},{24,32},{32,40},{40,48},{48,56},{56,64},{64,7... | collective-permute-start | bytes 3145736 | tf_op jit(solution)/shard_map/ppermute | solution.py:23
  90.6 1.9 collective-permute-start.1
  92.7 5.1 %fusion.64 = f32[256,4,64,16]{0,3,2,1:T(8,128)} fusion(f32[4,64,16,128]{3,2,1,0:T(8,128)S(1)} %copy-done, f32[128,128]{1,0:T(8,128)S(1)} %get-tuple-element.11, f32[128,128]{1,0:T(8,128)S(1)} %get-tuple-element.12), kind=kOutput, calls=%fused_computation.82 | convolution fusion | flops 1610645504 | bytes 6422528 | tf_op jit(solution)/shard_map/aq,xykq->xyka/dot_general | solution.py:51
  97.8 37.8 %collective-permute-done = f32[2,64,16,128]{3,2,1,0:T(8,128)S(1)} collective-permute-done((f32[2,64,16,128]{3,2,1,0:T(8,128)S(1)}, f32[2,64,16,128]{3,2,1,0:T(8,128)S(1)}, u32[]{:S(2)}, u32[]{:S(2)}) %collective-permute-start) | collective-permute-done | bytes 1048608 | tf_op jit(solution)/shard_map/ppermute | solution.py:23
  135.6 0.1 constant_dynamic-update-slice_fusion.1
  135.7 1.6 constant_dynamic-update-slice_fusion
  137.3 0.0 collective-permute-done.1
  137.3 1.6 copy-done.8
  138.9 1.0 constant_dynamic-update-slice_fusion.2
  140.0 2.2 select_maximum_fusion.2
  142.2 0.0 all-to-all-done.1
  142.2 3.0 copy.41
  145.2 8.5 %fusion.34 = f32[4,64,16,128]{3,2,1,0:T(8,128)S(1)} fusion(f32[4,64,16,128]{3,2,1,0:T(8,128)S(1)} %copy-done, f32[4,64,16,128]{3,2,1,0:T(8,128)S(1)} %bitcast.60, f32[8,68,16,128]{3,2,1,0:T(8,128)} %select_maximum_fusion.2, f32[6,64,16,128]{3,2,1,0:T(8,128)} %constant_dynamic-update-slice_fusion.2, f32[6,64,16,128]{3,2,1,0:T(8,128)} %copy-done.8, ...), kind=kOutput, calls=%fused_computation.51 | convolution fusion | flops 1621688320 | bytes 27460304 | tf_op jit(solution)/shard_map/aq,xyka->xykq/dot_general | solution.py:54
  153.7 0.3 copy.42
  154.0 1.0 copy-done.1
  155.0 61.8 %all_to_all.72 = f32[4,64,16,128]{3,2,0,1:T(8,128)S(1)} all-to-all(f32[4,64,16,128]{3,2,0,1:T(8,128)S(1)} %copy.42), channel_id=1, replica_groups=mesh['gx'=32,'ka'=8] {'ka'}, dimensions={1} | all-to-all | bytes 4194304 | tf_op jit(solution)/shard_map/all_to_all | solution.py:96
  216.8 0.3 copy.44
  217.0 3.6 %fusion.63 = f32[4,8,128,256]{3,2,1,0:T(8,128)S(1)} fusion(f32[4,8,128,128]{3,2,1,0:T(8,128)S(1)} %bitcast.56, f32[128,128]{1,0:T(8,128)S(1)} %get-tuple-element.11, f32[128,128]{1,0:T(8,128)S(1)} %get-tuple-element.12), kind=kOutput, calls=%fused_computation.81 | convolution fusion | flops 1610645504 | bytes 6422528 | tf_op jit(solution)/shard_map/ak,xykq->xyaq/dot_general | solution.py:44
  220.7 4.7 %fusion.46 = f32[4,8,128,128]{2,3,1,0:T(8,128)} fusion(f32[4,8,128,256]{3,2,1,0:T(8,128)S(1)} %fusion.63, f32[4,256]{1,0:T(4,128)S(1)} %constant_dynamic-update-slice_fusion.4, f32[128,128]{1,0:T(8,128)S(1)} %fusion.68, f32[128,128]{1,0:T(8,128)S(1)} %get-tuple-element.11), kind=kOutput, calls=%fused_computation.66 | convolution fusion | flops 1611726848 | bytes 6426624 | tf_op jit(solution)/shard_map/ak,xyaq->xykq/dot_general | solution.py:47
  225.4 3.1 copy.46
  228.5 4.3 %all-to-all-start.3 = ((f32[4,8,128,128]{3,1,0,2:T(8,128)}), f32[4,8,128,128]{3,1,0,2:T(8,128)}, u32[]{:S(2)}, u32[]{:S(2)}) async-start(f32[4,8,128,128]{3,1,0,2:T(8,128)} %copy.46), calls=%async_computation.3 | async-start | bytes 4194304 | tf_op jit(solution)/shard_map/all_to_all | solution.py:101
  232.9 1.8 fusion.81
  234.7 5.3 %collective-permute-start.2 = (f32[2,64,16,128]{3,2,1,0:T(8,128)S(1)}, f32[2,64,16,128]{3,2,1,0:T(8,128)S(1)}, u32[]{:S(2)}, u32[]{:S(2)}) collective-permute-start(f32[2,64,16,128]{3,2,1,0:T(8,128)S(1)} %get-tuple-element.5), channel_id=1, source_target_pairs={{0,8},{8,16},{16,24},{24,32},{32,40},{40,48},{48,56},{56,64},{64,7... | collective-permute-start | bytes 3145736 | tf_op jit(solution)/shard_map/ppermute | solution.py:23
  240.0 2.2 collective-permute-start.3
  242.2 5.1 %fusion.62 = f32[4,64,16,256]{3,2,1,0:T(8,128)} fusion(f32[4,64,16,128]{3,2,1,0:T(8,128)S(1)} %copy-done.2, f32[128,128]{1,0:T(8,128)S(1)} %get-tuple-element.11, f32[128,128]{1,0:T(8,128)S(1)} %get-tuple-element.12), kind=kOutput, calls=%fused_computation.80 | convolution fusion | flops 1610645504 | bytes 6422528 | tf_op jit(solution)/shard_map/aq,xykq->xyka/dot_general | solution.py:51
  247.3 56.9 %collective-permute-done.2 = f32[2,64,16,128]{3,2,1,0:T(8,128)S(1)} collective-permute-done((f32[2,64,16,128]{3,2,1,0:T(8,128)S(1)}, f32[2,64,16,128]{3,2,1,0:T(8,128)S(1)}, u32[]{:S(2)}, u32[]{:S(2)}) %collective-permute-start.2) | collective-permute-done | bytes 1048608 | tf_op jit(solution)/shard_map/ppermute | solution.py:23
  304.2 0.0 collective-permute-done.3
  304.2 1.0 copy-done.6
  305.2 2.3 select_maximum_fusion
  307.4 3.0 copy.48
  310.4 8.6 %fusion.20 = f32[4,64,16,128]{3,2,1,0:T(8,128)} fusion(f32[4,64,16,128]{3,2,1,0:T(8,128)S(1)} %bitcast.59, f32[4,64,16,128]{3,2,1,0:T(8,128)S(1)} %copy-done.3, f32[2,64,16,128]{3,2,1,0:T(8,128)S(1)} %copy-done.7, f32[2,64,16,128]{3,2,1,0:T(8,128)S(1)} %collective-permute-done.2, f32[8,68,16,128]{3,2,1,0:T(8,128)} %select_maximum_fusion, ...), kind=kOutput, calls=%fused_computation.32 | convolution fusion | flops 1624834048 | bytes 23266000 | tf_op jit(solution)/shard_map/aq,xyka->xykq/dot_general | solution.py:54
  (29 shorter events, 0.1 us)
Async XLA Ops:
  3.2 10.1 %copy-start.10 = (f32[4,128]{1,0:T(4,128)S(1)}, f32[4,128]{1,0:T(4,128)}, u32[]{:S(2)}) copy-start(f32[4,128]{1,0:T(4,128)} %param.8) | copy-start | bytes 6148
  3.2 62.9 %all-to-all-start = ((f32[4,64,16,128]{3,2,0,1:T(8,128)}), f32[4,64,16,128]{3,2,0,1:T(8,128)S(1)}, u32[]{:S(2)}, u32[]{:S(2)}) async-start(f32[4,64,16,128]{3,2,0,1:T(8,128)} %copy.35), calls=%async_computation | async-start | bytes 4194304 | tf_op jit(solution)/shard_map/all_to_all | solution.py:96
  66.1 1.3 copy-start.5
  81.7 4.7 %copy-start = (f32[4,64,16,128]{3,2,1,0:T(8,128)S(1)}, f32[4,64,16,128]{3,2,1,0:T(8,128)}, u32[]{:S(2)}) copy-start(f32[4,64,16,128]{3,2,1,0:T(8,128)} %param.7) | copy-start | bytes 6291460
  81.7 60.5 %all-to-all-start.1 = ((f32[4,8,128,128]{3,1,0,2:T(8,128)}), f32[4,8,128,128]{3,1,0,2:T(8,128)}, u32[]{:S(2)}, u32[]{:S(2)}) async-start(f32[4,8,128,128]{3,1,0,2:T(8,128)} %copy.39), calls=%async_computation.1 | async-start | bytes 4194304 | tf_op jit(solution)/shard_map/all_to_all | solution.py:101
  86.4 6.1 %copy-start.11 = (f32[16]{0:T(128)S(1)}, f32[16]{0:T(128)}, u32[]{:S(2)}) copy-start(f32[16]{0:T(128)} %param.10) | copy-start | bytes 196
  86.4 6.1 %copy-start.12 = (s32[16]{0:T(128)S(1)}, s32[16]{0:T(128)}, u32[]{:S(2)}) copy-start(s32[16]{0:T(128)} %param.12) | copy-start | bytes 196
  86.4 6.2 %copy-start.13 = (f32[128]{0:T(128)S(1)}, f32[128]{0:T(128)}, u32[]{:S(2)}) copy-start(f32[128]{0:T(128)} %param.11) | copy-start | bytes 1540
  86.4 6.2 %copy-start.14 = (s32[128]{0:T(128)S(1)}, s32[128]{0:T(128)}, u32[]{:S(2)}) copy-start(s32[128]{0:T(128)} %param.13) | copy-start | bytes 1540
  86.4 6.2 %copy-start.9 = (f32[64,128]{1,0:T(8,128)S(1)}, f32[64,128]{1,0:T(8,128)}, u32[]{:S(2)}) copy-start(f32[64,128]{1,0:T(8,128)} %param.9) | copy-start | bytes 98308
  86.6 49.0 %collective-permute-start = (f32[2,64,16,128]{3,2,1,0:T(8,128)S(1)}, f32[2,64,16,128]{3,2,1,0:T(8,128)S(1)}, u32[]{:S(2)}, u32[]{:S(2)}) collective-permute-start(f32[2,64,16,128]{3,2,1,0:T(8,128)S(1)} %get-tuple-element.9), channel_id=1, source_target_pairs={{0,8},{8,16},{16,24},{24,32},{32,40},{40,48},{48,56},{56,64},{64,7... | collective-permute-start | bytes 3145736 | tf_op jit(solution)/shard_map/ppermute | solution.py:23
  90.6 46.7 %collective-permute-start.1 = (f32[2,64,16,128]{3,2,1,0:T(8,128)S(1)}, f32[2,64,16,128]{3,2,1,0:T(8,128)S(1)}, u32[]{:S(2)}, u32[]{:S(2)}) collective-permute-start(f32[2,64,16,128]{3,2,1,0:T(8,128)S(1)} %get-tuple-element.10), channel_id=1, source_target_pairs={{8,0},{16,8},{24,16},{32,24},{40,32},{48,40},{56,48},{64,56},{72,6... | collective-permute-start | bytes 3145736 | tf_op jit(solution)/shard_map/ppermute | solution.py:25
  137.3 1.6 copy-start.8
  142.2 3.0 copy-start.4
  153.7 1.3 copy-start.1
  228.5 78.9 %all-to-all-start.3 = ((f32[4,8,128,128]{3,1,0,2:T(8,128)}), f32[4,8,128,128]{3,1,0,2:T(8,128)}, u32[]{:S(2)}, u32[]{:S(2)}) async-start(f32[4,8,128,128]{3,1,0,2:T(8,128)} %copy.46), calls=%async_computation.3 | async-start | bytes 4194304 | tf_op jit(solution)/shard_map/all_to_all | solution.py:101
  232.9 9.3 %copy-start.2 = (f32[4,64,16,128]{3,2,1,0:T(8,128)S(1)}, f32[4,64,16,128]{3,2,1,0:T(8,128)}, u32[]{:S(2)}) copy-start(f32[4,64,16,128]{3,2,1,0:T(8,128)} %copy-done.1) | copy-start | bytes 6291460
  234.7 69.5 %collective-permute-start.2 = (f32[2,64,16,128]{3,2,1,0:T(8,128)S(1)}, f32[2,64,16,128]{3,2,1,0:T(8,128)S(1)}, u32[]{:S(2)}, u32[]{:S(2)}) collective-permute-start(f32[2,64,16,128]{3,2,1,0:T(8,128)S(1)} %get-tuple-element.5), channel_id=1, source_target_pairs={{0,8},{8,16},{16,24},{24,32},{32,40},{40,48},{48,56},{56,64},{64,7... | collective-permute-start | bytes 3145736 | tf_op jit(solution)/shard_map/ppermute | solution.py:23
  240.0 64.2 %collective-permute-start.3 = (f32[2,64,16,128]{3,2,1,0:T(8,128)S(1)}, f32[2,64,16,128]{3,2,1,0:T(8,128)S(1)}, u32[]{:S(2)}, u32[]{:S(2)}) collective-permute-start(f32[2,64,16,128]{3,2,1,0:T(8,128)S(1)} %get-tuple-element.6), channel_id=1, source_target_pairs={{8,0},{16,8},{24,16},{32,24},{40,32},{48,40},{56,48},{64,56},{72,6... | collective-permute-start | bytes 3145736 | tf_op jit(solution)/shard_map/ppermute | solution.py:25
  304.2 1.0 copy-start.6
  307.4 3.0 copy-start.3
  307.4 3.0 copy-start.7
where the time goes:
time: 321 us; the launch traced here: 319 us
  waiting for transfers between devices  147 us (46%)
  blocking collectives  61.8 us (19%)
  matrix products  46.2 us (14%)
  starting transfers between devices  32.4 us (10%)
  local copies, waits for them, and re-layouts  26.3 us (8%)
  other arithmetic  5.08 us (2%)
    ppermute x2, waiting for transfers between devices, extended(): lax.ppermute(tail, axis, [(i, (i + 1) % count) for i in range(ends)])  94.7 us
    all_to_all x1, blocking collectives, operator_slab(): lax.all_to_all(field, 'ka', split_axis=1, concat_axis=2, tiled=True)  61.8 us
    all_to_all x1, waiting for transfers between devices, operator_slab(): lax.all_to_all(field, 'ka', split_axis=1, concat_axis=2, tiled=True)  52.2 us
    dot_general x2, matrix products, wigner_second(): jnp.einsum('aq,xyka->xykq', backward, hatted, precision=lax.Precision.HIG...  17.1 us
    dot_general x2, matrix products, wigner_first(): jnp.einsum('ak,xyaq->xykq', backward, hatted, precision=lax.Precision.HIG...  11.6 us
    dot_general x2, matrix products, wigner_second(): jnp.einsum('aq,xykq->xyka', forward, field, precision=lax.Precision.HIGHEST)  10.2 us
    all_to_all x1, starting transfers between devices, operator_slab(): lax.all_to_all(field, 'ka', split_axis=1, concat_axis=2, tiled=True)  10 us
    ppermute x2, starting transfers between devices, extended(): lax.ppermute(tail, axis, [(i, (i + 1) % count) for i in range(ends)])  9.27 us
  transfers between devices with their start and end apart: 7, of which 3 were waited for; matrix products, arithmetic and copies ran while one was open for 6% of the time, Pallas kernels for 0%

commit v1 on v0

v1 whole, which is shorter than its diff:
```python
import functools
import math

import jax
import jax.numpy as jnp
import numpy as np
from jax import lax
from jax.experimental import pallas as pl
from jax.experimental.pallas import tpu as pltpu
from jax.sharding import PartitionSpec as P


F32 = jnp.float32
BF16 = jnp.bfloat16
K = 128
AXES = ("gx", "ka")
SLOTS = [(dy, ds) for dy in (0, 2, 1, 3) for ds in (0, 1)]
VMEM = pl.BlockSpec(memory_space=pltpu.VMEM)
SMEM = pl.BlockSpec(memory_space=pltpu.SMEM)


def flat(x, y, z, core):
    return ((x * 4 + z % 4) * 2 + core) * 8 + y * 2 + z // 4


def place(block, part):
    x, low, core = block // 8, block // 2 % 4, block % 2
    half = part // 4
    y = part if half == 0 else 7 - part
    z = (low + 2 if x % 2 == 0 else 5 - low) + 4 * half
    return flat(x, y, z % 8, core)


def part_of(y, half):
    return y if half == 0 else 7 - y


def slot_part(ka, slot):
    dy, ds = SLOTS[slot]
    return part_of((ka // 2 + dy) % 4, (ka % 2) ^ ds)


def host_tables():
    table = np.zeros((256, 24), np.int32)
    for block in range(32):
        for ka in range(8):
            me = block * 8 + ka
            for slot in range(8):
                part = slot_part(ka, slot)
                table[me, slot] = part
                table[place(block, part), 8 + slot] = ka
            host = place(block, ka)
            table[host, 16] = block
            table[host, 17] = ka
    return table


def exchange_pairs(slot):
    return [
        (block * 8 + ka, place(block, slot_part(ka, slot)))
        for block in range(32)
        for ka in range(8)
    ]


def x_pairs(step):
    return [
        (place(block, part), place(block + step, part))
        for block in range(32)
        for part in range(8)
        if 0 <= block + step < 32
    ]


def y_pairs(step):
    return [
        (place(block, part), place(block, part + step))
        for block in range(32)
        for part in range(8)
        if 0 <= part + step < 8 and part // 4 == (part + step) // 4
    ]


def edge_pairs(y):
    return [
        (place(block, part_of(3, half)), place(block, part_of(y, half)))
        for block in range(32)
        for half in range(2)
    ]


def send(value, pairs):
    return lax.ppermute(value, AXES, pairs)


def halves(value):
    high = value.astype(BF16)
    return high, (value - high.astype(F32)).astype(BF16)


def circulant(row):
    return pltpu.roll(jnp.broadcast_to(row, (K, K)), 0, 1, stride=1, stride_axis=0)


def right_table(row):
    high, low = halves(circulant(row))
    return jnp.concatenate(
        [
            jnp.concatenate([high, low], 1),
            jnp.concatenate([high, jnp.zeros_like(low)], 1),
        ],
        0,
    )


def left_table(row):
    high, low = halves(circulant(row))
    return jnp.concatenate(
        [
            jnp.concatenate([high, high], 1),
            jnp.concatenate([low, jnp.zeros_like(low)], 1),
        ],
        0,
    )


def times_right(rows, table):
    both = jnp.dot(jnp.concatenate(halves(rows), 1), table, preferred_element_type=F32)
    return both[:, :K] + both[:, K:]


def times_left(table, first, second):
    high_0, low_0 = halves(first)
    high_1, low_1 = halves(second)
    stacked = jnp.concatenate(
        [jnp.concatenate([high_0, high_1], 1), jnp.concatenate([low_0, low_1], 1)], 0
    )
    both = jnp.dot(table, stacked, preferred_element_type=F32)
    both = both[:K] + both[K:]
    return both[:, :K], both[:, K:]


def slope(center, one, two):
    return 3.0 * center - 4.0 * one + two


def local_kernel(g_ref, ty_ref, vy_ref, out_ref, pad):
    vy = vy_ref[...].reshape(1, 1, K)
    toward = jnp.broadcast_to(vy > 0, (4, 16, K))
    rate = jnp.abs(vy) * 0.125

    def rows(ref, y):
        return ref[:, y]

    def step(value, one_low, two_low, one_high, two_high, table):
        one = jnp.where(toward, one_low, one_high)
        two = jnp.where(toward, two_low, two_high)
        wigner = times_right(value.reshape(64, K), table).reshape(4, 16, K)
        return wigner - rate * slope(value, one, two)

    edge = jnp.zeros((4, 2, 16, K), F32)
    pad[0, :, 0:2] = edge
    pad[0, :, 66:68] = edge
    pad[1, :, 0:2] = edge
    pad[1, :, 66:68] = edge
    for y in range(64):
        pad[0, :, y + 2] = g_ref[:, y]

    def turn(source, into):
        @pl.loop(0, 8)
        def _(group):
            block = ty_ref[pl.ds(pl.multiple_of(group * 8, 8), 8), :]
            for inner in range(8):
                y = group * 8 + inner
                value = pad[source, :, y + 2]
                moved = step(
                    value,
                    pad[source, :, y + 1],
                    pad[source, :, y],
                    pad[source, :, y + 3],
                    pad[source, :, y + 4],
                    right_table(block[inner : inner + 1]),
                )
                into(y, value, moved)

    def first(y, value, moved):
        pad[1, :, y + 2] = value + moved

    def second(y, value, moved):
        out_ref[:, y] = 0.5 * (pad[0, :, y + 2] + value + moved)

    turn(0, first)
    turn(1, second)


def gather_kernel(info_ref, *refs):
    pieces, (head_ref, tail_ref) = refs[:8], refs[8:]
    for slot in range(8):
        at = pl.ds(pl.multiple_of(info_ref[0, 8 + slot] * 16, 16), 16)
        head_ref[:, :, at, :] = pieces[slot][0:2]
        tail_ref[:, :, at, :] = pieces[slot][2:4]


def first_kernel(
    info_ref, head_ref, tail_ref, low_ref, high_ref, tx_ref, vx_ref, vy_ref,
    u_head_ref, u_tail_ref, y_low_ref, y_high_ref, e0_ref, e1_ref, e2_ref, e3_ref, tables,
):
    layers = [low_ref.at[0], low_ref.at[1], head_ref.at[0], head_ref.at[1], tail_ref.at[0], tail_ref.at[1], high_ref.at[0], high_ref.at[1]]
    outs = [u_head_ref.at[0], u_head_ref.at[1], u_tail_ref.at[0], u_tail_ref.at[1]]
    for x in range(4):
        tables[x] = left_table(tx_ref[x : x + 1, :])

    @pl.loop(0, 4)
    def _(pair):
        vx = vx_ref[...]
        toward = vx > 0
        rate = jnp.abs(vx) * 0.125
        for x in range(4):
            mine = [layers[x + 2][pair * 2 + i] for i in range(2)]
            wigner = times_left(tables[x], mine[0], mine[1])
            for i in range(2):
                y = pair * 2 + i
                one = jnp.where(toward, layers[x + 1][y], layers[x + 3][y])
                two = jnp.where(toward, layers[x][y], layers[x + 4][y])
                outs[x][y] = wigner[i] - rate * slope(mine[i], one, two)

    vy = vy_ref[...]
    upper = info_ref[0, 17] == 3
    keep = jnp.logical_or(
        jnp.logical_and(vy > 0, upper), jnp.logical_and(vy <= 0, jnp.logical_not(upper))
    )
    weight = jnp.where(keep, jnp.abs(vy) * -0.125, 0.0)
    for x in range(4):
        y_low_ref[x] = outs[x][0:2]
        y_high_ref[x] = outs[x][6:8]
        for part, ref in enumerate((e0_ref, e1_ref, e2_ref, e3_ref)):
            at = slice(32 * part, 32 * part + 32)
            near = jnp.where(upper, outs[x][7, at], outs[x][0, at])
            far = jnp.where(upper, outs[x][6, at], outs[x][1, at])
            one = weight * (far - 4.0 * near)
            two = weight * near
            ref[x, 0] = jnp.where(upper, one, two)
            ref[x, 1] = jnp.where(upper, two, one)


def second_kernel(
    info_ref, u_head_ref, u_tail_ref, low_ref, high_ref, y_low_ref, y_high_ref,
    e0_ref, e1_ref, e2_ref, e3_ref, tx_ref, ty_ref, vx_ref, vy_ref, *refs,
):
    pieces, (result, tables) = refs[:8], refs[8:]
    layers = [low_ref.at[0], low_ref.at[1], u_head_ref.at[0], u_head_ref.at[1], u_tail_ref.at[0], u_tail_ref.at[1], high_ref.at[0], high_ref.at[1]]
    for x in range(4):
        tables[x] = left_table(0.5 * tx_ref[x : x + 1, :])

    def row(x, y):
        if y < 0:
            return y_low_ref[x, y + 2]
        if y > 7:
            return y_high_ref[x, y - 8]
        return layers[x + 2][y]

    vx = vx_ref[...]
    toward = vx > 0
    rate = jnp.abs(vx) * 0.0625
    vy = jnp.broadcast_to(vy_ref[...], (K, K))
    toward_y = vy > 0
    rate_y = jnp.abs(vy) * 0.125
    for pair in range(4):
        right = [right_table(ty_ref[pair * 2 + i : pair * 2 + i + 1, :]) for i in range(2)]
        for x in range(4):
            mine = [layers[x + 2][pair * 2 + i] for i in range(2)]
            wigner = times_left(tables[x], mine[0], mine[1])
            for i in range(2):
                y = pair * 2 + i
                one = jnp.where(toward, layers[x + 1][y], layers[x + 3][y])
                two = jnp.where(toward, layers[x][y], layers[x + 4][y])
                total = mine[i] + wigner[i] - rate * slope(mine[i], one, two)
                total += times_right(mine[i], right[i])
                one = jnp.where(toward_y, row(x, y - 1), row(x, y + 1))
                two = jnp.where(toward_y, row(x, y - 2), row(x, y + 2))
                result[x, y] = total - rate_y * slope(mine[i], one, two)

    last = info_ref[0, 18] == 3
    half = info_ref[0, 19]
    for slot, (dy, ds) in enumerate(SLOTS):
        at = pl.ds(pl.multiple_of(info_ref[0, 8 + slot] * 16, 16), 16)
        pieces[slot][:, 0:8] = result[:, :, at, :]
        if dy == 0:
            at = pl.ds(pl.multiple_of((half ^ ds) * 16, 16), 16)
            own = jnp.where(last, e3_ref[:, :, at, :], 0.0)
            others = e0_ref[:, :, at, :] + e1_ref[:, :, at, :] + e2_ref[:, :, at, :]
            pieces[slot][:, 8:10] = own + others


def final_kernel(info_ref, local_ref, *refs):
    pieces, out_ref = refs[:8], refs[8]
    for slot, (dy, ds) in enumerate(SLOTS):
        at = pl.ds(pl.multiple_of(info_ref[0, slot] * 8, 8), 8)
        out_ref[:, at] = local_ref[:, at] + pieces[slot][:, 0:8]
    for slot, (dy, ds) in enumerate(SLOTS):
        if dy == 0:
            half = info_ref[0, 20] ^ ds
            at = pl.ds(jnp.where(half == 0, 32, 30), 2)
            out_ref[:, at] = out_ref[:, at] + pieces[slot][:, 8:10]


def cost(flops, size):
    return pl.CostEstimate(flops=flops, bytes_accessed=size, transcendentals=0)


PARAMS = pltpu.CompilerParams(vmem_limit_bytes=40 * 1024 * 1024)
MIB = 1 << 20


def array(*shape):
    return jax.ShapeDtypeStruct(shape, F32)


def sine_table(sign):
    index = np.arange(K)
    angle = (sign * index[:, None] * index[None, :] % K) * (2.0 * math.pi / K)
    return (np.sin(angle) / K).astype(np.float32)


def per_device(table, density, potential_x, potential_y, speeds_x, speeds_y, upwind_x, upwind_y):
    me = lax.axis_index("gx") * 8 + lax.axis_index("ka")
    info = lax.dynamic_slice(jnp.asarray(table), (me, 0), (1, table.shape[1]))

    pieces = []
    for slot in range(8):
        start = info[0, slot] * 8
        piece = lax.dynamic_slice(density, (0, start, 0, 0), (4, 8, 16, K))
        pieces.append(send(piece, exchange_pairs(slot)))
    moved_x = send(potential_x, exchange_pairs(0))
    vel_x = lax.all_gather((2 * upwind_x - 1).astype(F32) * speeds_x, "ka", tiled=True)
    vx = jnp.broadcast_to(vel_x[:, None], (K, K))
    vy = ((2 * upwind_y - 1).astype(F32) * speeds_y).reshape(1, K)

    highest = lax.Precision.HIGHEST
    ty = 0.25 * jnp.dot(potential_y, jnp.asarray(sine_table(1)), precision=highest)
    tx = 0.25 * jnp.dot(moved_x, jnp.asarray(sine_table(-1)), precision=highest)
    ty_own = lax.dynamic_slice(ty, (info[0, 17] * 8, 0), (8, K))

    local = pl.pallas_call(
        local_kernel,
        out_shape=array(4, 64, 16, K),
        in_specs=[VMEM] * 3,
        out_specs=VMEM,
        scratch_shapes=[pltpu.VMEM((2, 4, 68, 16, K), F32)],
        compiler_params=PARAMS,
        cost_estimate=cost(4 * 10**9, 4 * MIB),
        name="local_part",
    )(density, ty, vy)

    head, tail = pl.pallas_call(
        gather_kernel,
        out_shape=[array(2, 8, K, K)] * 2,
        in_specs=[SMEM] + [VMEM] * 8,
        out_specs=[VMEM] * 2,
        compiler_params=PARAMS,
        cost_estimate=cost(0, 4 * MIB),
        name="gather_kx",
    )(info, *pieces)
    low = send(tail, x_pairs(1))
    high = send(head, x_pairs(-1))

    u_head, u_tail, y_low, y_high, *edges = pl.pallas_call(
        first_kernel,
        out_shape=[array(2, 8, K, K)] * 2 + [array(4, 2, K, K)] * 2 + [array(4, 2, 32, K)] * 4,
        in_specs=[SMEM] + [VMEM] * 7,
        out_specs=[VMEM] * 8,
        scratch_shapes=[pltpu.VMEM((4, 2 * K, 2 * K), BF16)],
        compiler_params=PARAMS,
        cost_estimate=cost(10**9, 8 * MIB),
        name="first_turn",
    )(info, head, tail, low, high, tx, vx, vy)
    low = send(u_tail, x_pairs(1))
    high = send(u_head, x_pairs(-1))
    y_under = send(y_high, y_pairs(1))
    y_over = send(y_low, y_pairs(-1))
    edges = [send(edges[y], edge_pairs(y)) for y in range(3)] + [edges[3]]

    back = pl.pallas_call(
        second_kernel,
        out_shape=[array(4, 10 if dy == 0 else 8, 16, K) for dy, ds in SLOTS],
        in_specs=[SMEM] + [VMEM] * 14,
        out_specs=[VMEM] * 8,
        scratch_shapes=[pltpu.VMEM((4, 8, K, K), F32), pltpu.VMEM((4, 2 * K, 2 * K), BF16)],
        compiler_params=PARAMS,
        cost_estimate=cost(2 * 10**9, 10 * MIB),
        name="second_turn",
    )(info, u_head, u_tail, low, high, y_under, y_over, *edges, tx, ty_own, vx, vy)
    pieces = [
        send(back[slot], [(there, here) for here, there in exchange_pairs(slot)])
        for slot in range(8)
    ]

    return pl.pallas_call(
        final_kernel,
        grid=(4,),
        out_shape=array(4, 64, 16, K),
        in_specs=[SMEM, pl.BlockSpec((1, 64, 16, K), lambda x: (x, 0, 0, 0))]
        + [
            pl.BlockSpec((1, 10 if dy == 0 else 8, 16, K), lambda x: (x, 0, 0, 0))
            for dy, ds in SLOTS
        ],
        out_specs=pl.BlockSpec((1, 64, 16, K), lambda x: (x, 0, 0, 0)),
        compiler_params=PARAMS,
        cost_estimate=cost(0, 6 * MIB),
        name="add_back",
    )(info, local, *pieces)


def solution(mesh):
    table = host_tables()
    for block in range(32):
        for part in range(8):
            host = place(block, part)
            table[host, 18] = part if part < 4 else 7 - part
            table[host, 19] = part // 4
            table[block * 8 + part, 20] = part % 2
    in_specs = (P("gx", None, "ka", None), P("gx", None), P(), P("ka"), P(), P("ka"), P())
    out_specs = P("gx", None, "ka", None)
    return jax.shard_map(
        functools.partial(per_device, table),
        mesh=mesh,
        in_specs=in_specs,
        out_specs=out_specs,
        check_vma=False,
    )
```

time: 321 us -> 210 us (0.65)
  waiting for transfers between devices: 147 us -> 78.2 us
  matrix products: 46.2 us -> 0.34 us
  starting transfers between devices: 32.4 us -> 72.4 us
  blocking collectives: 61.8 us -> 25.6 us
  local copies, waits for them, and re-layouts: 26.3 us -> 6.24 us
  Pallas kernels: 0 us -> 18 us
  between operations: 0.32 us -> 6.48 us
  other arithmetic: 5.08 us -> 0.11 us
    all_to_all x1 -> x0, blocking collectives: 61.8 us -> none  [operator_slab(): lax.all_to_all(field, 'ka', split_axis=1, concat_axis=2, tiled=True)]
    ppermute x4 -> x26, starting transfers between devices: 13.4 us -> 72.4 us  [send(): return lax.ppermute(value, AXES, pairs)]
    all_to_all x3 -> x0, waiting for transfers between devices: 52.2 us -> none  [the longest x1 52.2 us: operator_slab(): lax.all_to_all(field, 'ka', split_axis=1, concat_axis=2, tiled=True)]
    dot_general x8 -> x2, matrix products: 46.2 us -> 0.34 us  [the longest x1 0.18 us: per_device(): jnp.dot(potential_y, jnp.asarray(sine_table(1)), precision=highest)]
    unnamed x0 -> x1, blocking collectives: none -> 25.6 us
    all_to_all x3 -> x0, starting transfers between devices: 19.1 us -> none  [the longest x1 10 us: operator_slab(): lax.all_to_all(field, 'ka', split_axis=1, concat_axis=2, tiled=True)]
    pallas_call x0 -> x5, Pallas kernels: none -> 18 us  [the longest x1 6.41 us: per_device(): pl.pallas_call(local_kernel, out_shape=array(4, 64, 16, K), in_specs=[VME...]
    ppermute x4 -> x26, waiting for transfers between devices: 94.7 us -> 78.2 us  [send(): return lax.ppermute(value, AXES, pairs)]
  transfers between devices with their start and end apart: 7 -> 26, of which waited for: 3 -> 13; matrix products, arithmetic and copies ran while one was open for 6% -> 1% of each run, Pallas kernels for 0% -> 3%
where the time goes in v1:
time: 210 us; the launch traced here: 207 us
  waiting for transfers between devices  78.2 us (37%)
  starting transfers between devices  72.4 us (34%)
  blocking collectives  25.6 us (12%)
  Pallas kernels  18 us (9%)
  between operations  6.48 us (3%)
  local copies, waits for them, and re-layouts  6.24 us (3%)
    ppermute x26, waiting for transfers between devices, send(): return lax.ppermute(value, AXES, pairs)  78.2 us
    ppermute x26, starting transfers between devices, send(): return lax.ppermute(value, AXES, pairs)  72.4 us
    unnamed x1, blocking collectives  25.6 us
    pallas_call x1, Pallas kernels, per_device(): pl.pallas_call(local_kernel, out_shape=array(4, 64, 16, K), in_specs=[VME...  6.41 us
    pallas_call x1, Pallas kernels, per_device(): pl.pallas_call(first_kernel, out_shape=[array(2, 8, K, K)] * 2 + [array(4...  4.31 us
  transfers between devices with their start and end apart: 26, of which 13 were waited for; matrix products, arithmetic and copies ran while one was open for 1% of the time, Pallas kernels for 3%

profile of v1, /device:TPU:39, one launch (start us, length us, event | category | flops | bytes accessed | tf_op | source)
XLA Modules:
  0.0 207.4 jit_solution(8365934920449322073)
XLA Ops:
  0.0 0.7 constant_dynamic-slice_fusion.8.info_ref
  0.7 0.7 fusion.1
  6.3 1.7 constant_dynamic-slice_fusion
  8.1 2.4 %collective-permute-start.7 = (f32[4,8,16,128]{3,2,1,0:T(8,128)S(1)}, f32[4,8,16,128]{3,2,1,0:T(8,128)S(1)}, u32[]{:S(2)}, u32[]{:S(2)}) collective-permute-start(f32[4,8,16,128]{3,2,1,0:T(8,128)S(1)} %get-tuple-element.41), channel_id=1, source_target_pairs={{0,39},{1,38},{2,33},{3,32},{4,35},{5,34},{6,37},{7,36},{8,47},{9,... | collective-permute-start | bytes 786440 | tf_op jit(solution)/shard_map/ppermute | solution.py:93
  10.5 6.6 %collective-permute-start.4 = (f32[4,8,16,128]{3,2,1,0:T(8,128)S(1)}, f32[4,8,16,128]{3,2,1,0:T(8,128)S(1)}, u32[]{:S(2)}, u32[]{:S(2)}) collective-permute-start(f32[4,8,16,128]{3,2,1,0:T(8,128)S(1)} %get-tuple-element.43), channel_id=1, source_target_pairs={{0,34},{1,35},{2,36},{3,37},{4,38},{5,39},{6,32},{7,33},{8,42},{9,... | collective-permute-start | bytes 786440 | tf_op jit(solution)/shard_map/ppermute | solution.py:93
  17.1 4.3 %collective-permute-start.3 = (f32[4,8,16,128]{3,2,1,0:T(8,128)S(1)}, f32[4,8,16,128]{3,2,1,0:T(8,128)S(1)}, u32[]{:S(2)}, u32[]{:S(2)}) collective-permute-start(f32[4,8,16,128]{3,2,1,0:T(8,128)S(1)} %get-tuple-element.44), channel_id=1, source_target_pairs={{0,37},{1,36},{2,39},{3,38},{4,33},{5,32},{6,35},{7,34},{8,45},{9,... | collective-permute-start | bytes 786440 | tf_op jit(solution)/shard_map/ppermute | solution.py:93
  21.4 0.7 collective-permute-start.1
  22.1 23.8 %collective-permute-done.5.refs_5_ = f32[4,8,16,128]{3,2,1,0:T(8,128)S(1)} collective-permute-done((f32[4,8,16,128]{3,2,1,0:T(8,128)S(1)}, f32[4,8,16,128]{3,2,1,0:T(8,128)S(1)}, u32[]{:S(2)}, u32[]{:S(2)}) %collective-permute-start.5) | collective-permute-done | bytes 262176 | tf_op jit(solution)/shard_map/ppermute | solution.py:93
  45.9 6.5 %collective-permute-start = (f32[4,8,16,128]{3,2,1,0:T(8,128)S(1)}, f32[4,8,16,128]{3,2,1,0:T(8,128)S(1)}, u32[]{:S(2)}, u32[]{:S(2)}) collective-permute-start(f32[4,8,16,128]{3,2,1,0:T(8,128)S(1)} %get-tuple-element.47), channel_id=1, source_target_pairs={{0,32},{1,33},{2,34},{3,35},{4,36},{5,37},{6,38},{7,39},{8,40},{9,... | collective-permute-start | bytes 786440 | tf_op jit(solution)/shard_map/ppermute | solution.py:93
  52.4 4.9 %collective-permute-done.3.refs_3_ = f32[4,8,16,128]{3,2,1,0:T(8,128)S(1)} collective-permute-done((f32[4,8,16,128]{3,2,1,0:T(8,128)S(1)}, f32[4,8,16,128]{3,2,1,0:T(8,128)S(1)}, u32[]{:S(2)}, u32[]{:S(2)}) %collective-permute-start.3) | collective-permute-done | bytes 262176 | tf_op jit(solution)/shard_map/ppermute | solution.py:93
  57.3 1.5 collective-permute-done.1.refs_1_
  58.8 4.2 %collective-permute-done.6.refs_6_ = f32[4,8,16,128]{3,2,1,0:T(8,128)S(1)} collective-permute-done((f32[4,8,16,128]{3,2,1,0:T(8,128)S(1)}, f32[4,8,16,128]{3,2,1,0:T(8,128)S(1)}, u32[]{:S(2)}, u32[]{:S(2)}) %collective-permute-start.6) | collective-permute-done | bytes 262176 | tf_op jit(solution)/shard_map/ppermute | solution.py:93
  63.1 0.7 gather_kx.1
  63.8 4.7 %collective-permute-start.9 = (f32[2,8,128,128]{3,2,1,0:T(8,128)S(1)}, f32[2,8,128,128]{3,2,1,0:T(8,128)S(1)}, u32[]{:S(2)}, u32[]{:S(2)}) collective-permute-start(f32[2,8,128,128]{3,2,1,0:T(8,128)S(1)} %get-tuple-element.23.head_ref), channel_id=1, source_target_pairs={{40,32},{42,34},{44,36},{46,38},{47,39},{45,37},{43,35},{41,33},{4... | collective-permute-start | bytes 3145736 | tf_op jit(solution)/shard_map/ppermute | solution.py:93
  68.5 3.6 %collective-permute-start.8 = (f32[2,8,128,128]{3,2,1,0:T(8,128)S(1)}, f32[2,8,128,128]{3,2,1,0:T(8,128)}, u32[]{:S(2)}, u32[]{:S(2)}) collective-permute-start(f32[2,8,128,128]{3,2,1,0:T(8,128)S(1)} %get-tuple-element.24.tail_ref), channel_id=1, source_target_pairs={{32,40},{34,42},{36,44},{38,46},{39,47},{37,45},{35,43},{33,41},{4... | collective-permute-start | bytes 3145736 | tf_op jit(solution)/shard_map/ppermute | solution.py:93
  72.2 5.1 %collective-permute-start.10 = (f32[4,128]{1,0:T(4,128)S(1)}, f32[4,128]{1,0:T(4,128)S(1)}, u32[]{:S(2)}, u32[]{:S(2)}) collective-permute-start(f32[4,128]{1,0:T(4,128)S(1)} %copy-done.10), channel_id=1, source_target_pairs={{0,32},{1,33},{2,34},{3,35},{4,36},{5,37},{6,38},{7,39},{8,40},{9,... | collective-permute-start | bytes 6152 | tf_op jit(solution)/shard_map/ppermute | solution.py:93
  77.3 0.6 dynamic-slice.1
  78.6 0.1 multiply_dynamic-update-slice_fusion
  78.7 25.6 %all-reduce = f32[128]{0:T(128)S(1)} all-reduce(f32[128]{0:T(128)S(1)} %multiply_dynamic-update-slice_fusion), channel_id=1, replica_groups=mesh['gx'=32,'ka'=8] {'ka'}, use_global_device_ids=true, to_apply=%add | all-reduce | flops 128 | bytes 1024
  104.3 0.2 fusion.tx_ref
  104.5 4.3 %first_turn.1 = (f32[2,8,128,128]{3,2,1,0:T(8,128)}, f32[2,8,128,128]{3,2,1,0:T(8,128)}, f32[4,2,128,128]{3,2,1,0:T(8,128)}, f32[4,2,128,128]{3,2,1,0:T(8,128)},...) custom-call(s32[1,24]{1,0:T(1,128)S(1)} %constant_dynamic-slice_fusi, ...), custom_call_target="tpu_custom_call" | custom-call | flops 1000000000 | bytes 8388608 | tf_op jit(solution)/shard_map/first_turn/pallas_call | solution.py:367
  108.8 4.4 %collective-permute-start.12 = (f32[2,8,128,128]{3,2,1,0:T(8,128)}, f32[2,8,128,128]{3,2,1,0:T(8,128)S(1)}, u32[]{:S(2)}, u32[]{:S(2)}) collective-permute-start(f32[2,8,128,128]{3,2,1,0:T(8,128)} %get-tuple-element.25.u_head_ref), channel_id=1, source_target_pairs={{40,32},{42,34},{44,36},{46,38},{47,39},{45,37},{43,35},{41,33},{4... | collective-permute-start | bytes 3145736 | tf_op jit(solution)/shard_map/ppermute | solution.py:93
  113.3 1.9 collective-permute-start.11
  115.2 1.3 collective-permute-start.15
  116.5 1.3 collective-permute-start.13
  117.8 4.8 %collective-permute-start.14 = (f32[4,2,128,128]{3,2,1,0:T(8,128)}, f32[4,2,128,128]{3,2,1,0:T(8,128)}, u32[]{:S(2)}, u32[]{:S(2)}) collective-permute-start(f32[4,2,128,128]{3,2,1,0:T(8,128)} %get-tuple-element.28), channel_id=1, source_target_pairs={{34,32},{36,34},{38,36},{37,39},{35,37},{33,35},{42,40},{44,42},{4... | collective-permute-start | bytes 1572872 | tf_op jit(solution)/shard_map/ppermute | solution.py:93
  122.6 0.3 collective-permute-done.15.e0_ref
  122.9 0.7 collective-permute-start.16
  123.5 0.7 collective-permute-start.17
  124.2 0.2 convolution_multiply_fusion
  125.0 0.6 copy-done.4
  125.7 5.9 %collective-permute-done.13.y_low_ref = f32[4,2,128,128]{3,2,1,0:T(8,128)S(1)} collective-permute-done((f32[4,2,128,128]{3,2,1,0:T(8,128)}, f32[4,2,128,128]{3,2,1,0:T(8,128)S(1)}, u32[]{:S(2)}, u32[]{:S(2)}) %collective-permute-start.13) | collective-permute-done | bytes 524320 | tf_op jit(solution)/shard_map/ppermute | solution.py:93
  131.6 1.0 collective-permute-done.14.y_high_ref
  132.6 0.9 copy-done.3
  133.5 0.9 copy-done.5
  134.4 4.1 %second_turn.1 = (f32[4,10,16,128]{3,2,1,0:T(8,128)S(1)}, f32[4,10,16,128]{3,2,1,0:T(8,128)S(1)}, f32[4,8,16,128]{3,2,1,0:T(8,128)S(1)}, f32[4,8,16,128]{3,2,1,0...) custom-call(s32[1,24]{1,0:T(1,128)S(1)} %constant_dynamic-slice_fusi, ...), custom_call_target="tpu_custom_call" | custom-call | flops 2000000000 | bytes 10485760 | tf_op jit(solution)/shard_map/second_turn/pallas_call | solution.py:383
  138.5 15.2 %collective-permute-start.20 = (f32[4,8,16,128]{3,2,1,0:T(8,128)S(1)}, f32[4,8,16,128]{3,2,1,0:T(8,128)S(1)}, u32[]{:S(2)}, u32[]{:S(2)}) collective-permute-start(f32[4,8,16,128]{3,2,1,0:T(8,128)S(1)} %get-tuple-element.35), channel_id=1, source_target_pairs={{36,0},{37,1},{38,2},{39,3},{32,4},{33,5},{34,6},{35,7},{44,8},{45... | collective-permute-start | bytes 786440 | tf_op jit(solution)/shard_map/ppermute | solution.py:93
  153.7 2.3 %collective-permute-start.23 = (f32[4,8,16,128]{3,2,1,0:T(8,128)S(1)}, f32[4,8,16,128]{3,2,1,0:T(8,128)S(1)}, u32[]{:S(2)}, u32[]{:S(2)}) collective-permute-start(f32[4,8,16,128]{3,2,1,0:T(8,128)S(1)} %get-tuple-element.38), channel_id=1, source_target_pairs={{35,0},{34,1},{37,2},{36,3},{39,4},{38,5},{33,6},{32,7},{43,8},{42... | collective-permute-start | bytes 786440 | tf_op jit(solution)/shard_map/ppermute | solution.py:93
  156.0 5.4 %collective-permute-start.24 = (f32[4,8,16,128]{3,2,1,0:T(8,128)S(1)}, f32[4,8,16,128]{3,2,1,0:T(8,128)S(1)}, u32[]{:S(2)}, u32[]{:S(2)}) collective-permute-start(f32[4,8,16,128]{3,2,1,0:T(8,128)S(1)} %get-tuple-element.39), channel_id=1, source_target_pairs={{38,0},{39,1},{32,2},{33,3},{34,4},{35,5},{36,6},{37,7},{46,8},{47... | collective-permute-start | bytes 786440 | tf_op jit(solution)/shard_map/ppermute | solution.py:93
  161.3 0.6 collective-permute-done.20.refs_2_
  162.0 5.0 %collective-permute-done.21.refs_3_ = f32[4,8,16,128]{3,2,1,0:T(8,128)S(1)} collective-permute-done((f32[4,8,16,128]{3,2,1,0:T(8,128)S(1)}, f32[4,8,16,128]{3,2,1,0:T(8,128)S(1)}, u32[]{:S(2)}, u32[]{:S(2)}) %collective-permute-start.21) | collective-permute-done | bytes 262176 | tf_op jit(solution)/shard_map/ppermute | solution.py:93
  167.0 3.7 %collective-permute-done.22.refs_4_ = f32[4,8,16,128]{3,2,1,0:T(8,128)S(1)} collective-permute-done((f32[4,8,16,128]{3,2,1,0:T(8,128)S(1)}, f32[4,8,16,128]{3,2,1,0:T(8,128)S(1)}, u32[]{:S(2)}, u32[]{:S(2)}) %collective-permute-start.22) | collective-permute-done | bytes 262176 | tf_op jit(solution)/shard_map/ppermute | solution.py:93
  170.7 0.6 collective-permute-start.19
  171.3 6.4 %local_part.1.local_ref = f32[4,64,16,128]{3,2,1,0:T(8,128)S(1)} custom-call(f32[4,64,16,128]{3,2,1,0:T(8,128)S(1)} %copy-done.1, f32[64,128]{1,0:T(8,128)S(1)} %bitcast.21, f32[1,128]{1,0:T(1,128)S(1)} %multiply_bitcast_fusion.vy_ref), custom_call_target="tpu_custom_call" | custom-call | flops 4000000000 | bytes 4194304 | tf_op jit(solution)/shard_map/local_part/pallas_call | solution.py:344
  177.7 1.7 collective-permute-done.23.refs_5_
  179.4 11.6 %collective-permute-done.25.refs_7_ = f32[4,8,16,128]{3,2,1,0:T(8,128)S(1)} collective-permute-done((f32[4,8,16,128]{3,2,1,0:T(8,128)S(1)}, f32[4,8,16,128]{3,2,1,0:T(8,128)S(1)}, u32[]{:S(2)}, u32[]{:S(2)}) %collective-permute-start.25) | collective-permute-done | bytes 262176 | tf_op jit(solution)/shard_map/ppermute | solution.py:93
  191.0 13.9 %collective-permute-done.19.refs_1_ = f32[4,10,16,128]{3,2,1,0:T(8,128)S(1)} collective-permute-done((f32[4,10,16,128]{3,2,1,0:T(8,128)S(1)}, f32[4,10,16,128]{3,2,1,0:T(8,128)S(1)}, u32[]{:S(2)}, u32[]{:S(2)}) %collective-permute-start.19) | collective-permute-done | bytes 327712 | tf_op jit(solution)/shard_map/ppermute | solution.py:93
  204.9 2.4 %add_back.1 = f32[4,64,16,128]{3,2,1,0:T(8,128)} custom-call(s32[1,24]{1,0:T(1,128)S(1)} %constant_dynamic-slice_fusion.8.info_ref, f32[4,64,16,128]{3,2,1,0:T(8,128)S(1)} %local_part.1.local_ref, f32[4,10,16,128]{3,2,1,0:T(8,128)S(1)} %collective-permute-done.18.refs_0_, f32[4,10,16,128]{3,2,1,0:T(8,128)S(1)} %collective-permute-done.19.refs_1_, ...), custom_call_target="tpu_custom_call" | custom-call | bytes 6291456 | tf_op jit(solution)/shard_map/add_back/pallas_call | solution.py:398
  (49 shorter events, 0.3 us)
Async XLA Ops:
  0.0 124.2 %copy-start = (f32[64,128]{1,0:T(8,128)S(1)}, f32[64,128]{1,0:T(8,128)}, u32[]{:S(2)}) copy-start(f32[64,128]{1,0:T(8,128)} %param.12) | copy-start | bytes 98308
  8.0 64.2 %copy-start.10 = (f32[4,128]{1,0:T(4,128)S(1)}, f32[4,128]{1,0:T(4,128)}, u32[]{:S(2)}) copy-start(f32[4,128]{1,0:T(4,128)} %param.11) | copy-start | bytes 6148
  8.0 69.3 %copy-start.13 = (u32[256]{0:T(256)S(1)}, u32[256]{0:T(256)}, u32[]{:S(2)}) copy-start(u32[256]{0:T(256)} %constant.51) | copy-start | bytes 3076
  8.0 70.5 %copy-start.11 = (f32[128]{0:T(128)S(1)}, f32[128]{0:T(128)}, u32[]{:S(2)}) copy-start(f32[128]{0:T(128)} %param.14) | copy-start | bytes 1540
  8.0 70.5 %copy-start.12 = (s32[128]{0:T(128)S(1)}, s32[128]{0:T(128)}, u32[]{:S(2)}) copy-start(s32[128]{0:T(128)} %param.16) | copy-start | bytes 1540
  8.1 70.5 %copy-start.8 = (f32[16]{0:T(128)S(1)}, f32[16]{0:T(128)}, u32[]{:S(2)}) copy-start(f32[16]{0:T(128)} %param.13) | copy-start | bytes 196
  8.1 70.5 %copy-start.9 = (s32[16]{0:T(128)S(1)}, s32[16]{0:T(128)}, u32[]{:S(2)}) copy-start(s32[16]{0:T(128)} %param.15) | copy-start | bytes 196
  8.1 96.2 %copy-start.7 = (f32[128,128]{1,0:T(8,128)S(1)}, f32[128,128]{1,0:T(8,128)}, u32[]{:S(2)}) copy-start(f32[128,128]{1,0:T(8,128)} %constant.46.clone) | copy-start | bytes 196612
  8.1 13.3 %collective-permute-start.7 = (f32[4,8,16,128]{3,2,1,0:T(8,128)S(1)}, f32[4,8,16,128]{3,2,1,0:T(8,128)S(1)}, u32[]{:S(2)}, u32[]{:S(2)}) collective-permute-start(f32[4,8,16,128]{3,2,1,0:T(8,128)S(1)} %get-tuple-element.41), channel_id=1, source_target_pairs={{0,39},{1,38},{2,33},{3,32},{4,35},{5,34},{6,37},{7,36},{8,47},{9,... | collective-permute-start | bytes 786440 | tf_op jit(solution)/shard_map/ppermute | solution.py:93
  10.4 35.5 %collective-permute-start.5 = (f32[4,8,16,128]{3,2,1,0:T(8,128)S(1)}, f32[4,8,16,128]{3,2,1,0:T(8,128)S(1)}, u32[]{:S(2)}, u32[]{:S(2)}) collective-permute-start(f32[4,8,16,128]{3,2,1,0:T(8,128)S(1)} %get-tuple-element.42), channel_id=1, source_target_pairs={{0,35},{1,34},{2,37},{3,36},{4,39},{5,38},{6,33},{7,32},{8,43},{9,... | collective-permute-start | bytes 786440 | tf_op jit(solution)/shard_map/ppermute | solution.py:93
  10.5 41.9 %collective-permute-start.4 = (f32[4,8,16,128]{3,2,1,0:T(8,128)S(1)}, f32[4,8,16,128]{3,2,1,0:T(8,128)S(1)}, u32[]{:S(2)}, u32[]{:S(2)}) collective-permute-start(f32[4,8,16,128]{3,2,1,0:T(8,128)S(1)} %get-tuple-element.43), channel_id=1, source_target_pairs={{0,34},{1,35},{2,36},{3,37},{4,38},{5,39},{6,32},{7,33},{8,42},{9,... | collective-permute-start | bytes 786440 | tf_op jit(solution)/shard_map/ppermute | solution.py:93
  17.1 40.2 %collective-permute-start.3 = (f32[4,8,16,128]{3,2,1,0:T(8,128)S(1)}, f32[4,8,16,128]{3,2,1,0:T(8,128)S(1)}, u32[]{:S(2)}, u32[]{:S(2)}) collective-permute-start(f32[4,8,16,128]{3,2,1,0:T(8,128)S(1)} %get-tuple-element.44), channel_id=1, source_target_pairs={{0,37},{1,36},{2,39},{3,38},{4,33},{5,32},{6,35},{7,34},{8,45},{9,... | collective-permute-start | bytes 786440 | tf_op jit(solution)/shard_map/ppermute | solution.py:93
  21.4 35.9 %collective-permute-start.2 = (f32[4,8,16,128]{3,2,1,0:T(8,128)S(1)}, f32[4,8,16,128]{3,2,1,0:T(8,128)S(1)}, u32[]{:S(2)}, u32[]{:S(2)}) collective-permute-start(f32[4,8,16,128]{3,2,1,0:T(8,128)S(1)} %get-tuple-element.45), channel_id=1, source_target_pairs={{0,36},{1,37},{2,38},{3,39},{4,32},{5,33},{6,34},{7,35},{8,44},{9,... | collective-permute-start | bytes 786440 | tf_op jit(solution)/shard_map/ppermute | solution.py:93
  21.4 37.5 %collective-permute-start.1 = (f32[4,8,16,128]{3,2,1,0:T(8,128)S(1)}, f32[4,8,16,128]{3,2,1,0:T(8,128)S(1)}, u32[]{:S(2)}, u32[]{:S(2)}) collective-permute-start(f32[4,8,16,128]{3,2,1,0:T(8,128)S(1)} %get-tuple-element.46), channel_id=1, source_target_pairs={{0,33},{1,32},{2,35},{3,34},{4,37},{5,36},{6,39},{7,38},{8,41},{9,... | collective-permute-start | bytes 786440 | tf_op jit(solution)/shard_map/ppermute | solution.py:93
  45.9 12.9 %collective-permute-start = (f32[4,8,16,128]{3,2,1,0:T(8,128)S(1)}, f32[4,8,16,128]{3,2,1,0:T(8,128)S(1)}, u32[]{:S(2)}, u32[]{:S(2)}) collective-permute-start(f32[4,8,16,128]{3,2,1,0:T(8,128)S(1)} %get-tuple-element.47), channel_id=1, source_target_pairs={{0,32},{1,33},{2,34},{3,35},{4,36},{5,37},{6,38},{7,39},{8,40},{9,... | collective-permute-start | bytes 786440 | tf_op jit(solution)/shard_map/ppermute | solution.py:93
  52.4 10.7 %collective-permute-start.6 = (f32[4,8,16,128]{3,2,1,0:T(8,128)S(1)}, f32[4,8,16,128]{3,2,1,0:T(8,128)S(1)}, u32[]{:S(2)}, u32[]{:S(2)}) collective-permute-start(f32[4,8,16,128]{3,2,1,0:T(8,128)S(1)} %get-tuple-element.48), channel_id=1, source_target_pairs={{0,38},{1,39},{2,32},{3,33},{4,34},{5,35},{6,36},{7,37},{8,46},{9,... | collective-permute-start | bytes 786440 | tf_op jit(solution)/shard_map/ppermute | solution.py:93
  63.8 40.6 %collective-permute-start.9 = (f32[2,8,128,128]{3,2,1,0:T(8,128)S(1)}, f32[2,8,128,128]{3,2,1,0:T(8,128)S(1)}, u32[]{:S(2)}, u32[]{:S(2)}) collective-permute-start(f32[2,8,128,128]{3,2,1,0:T(8,128)S(1)} %get-tuple-element.23.head_ref), channel_id=1, source_target_pairs={{40,32},{42,34},{44,36},{46,38},{47,39},{45,37},{43,35},{41,33},{4... | collective-permute-start | bytes 3145736 | tf_op jit(solution)/shard_map/ppermute | solution.py:93
  68.5 35.9 %collective-permute-start.8 = (f32[2,8,128,128]{3,2,1,0:T(8,128)S(1)}, f32[2,8,128,128]{3,2,1,0:T(8,128)}, u32[]{:S(2)}, u32[]{:S(2)}) collective-permute-start(f32[2,8,128,128]{3,2,1,0:T(8,128)S(1)} %get-tuple-element.24.tail_ref), channel_id=1, source_target_pairs={{32,40},{34,42},{36,44},{38,46},{39,47},{37,45},{35,43},{33,41},{4... | collective-permute-start | bytes 3145736 | tf_op jit(solution)/shard_map/ppermute | solution.py:93
  72.2 32.1 %collective-permute-start.10 = (f32[4,128]{1,0:T(4,128)S(1)}, f32[4,128]{1,0:T(4,128)S(1)}, u32[]{:S(2)}, u32[]{:S(2)}) collective-permute-start(f32[4,128]{1,0:T(4,128)S(1)} %copy-done.10), channel_id=1, source_target_pairs={{0,32},{1,33},{2,34},{3,35},{4,36},{5,37},{6,38},{7,39},{8,40},{9,... | collective-permute-start | bytes 6152 | tf_op jit(solution)/shard_map/ppermute | solution.py:93
  104.5 19.7 %copy-start.6 = (f32[128,128]{1,0:T(8,128)S(1)}, f32[128,128]{1,0:T(8,128)}, u32[]{:S(2)}) copy-start(f32[128,128]{1,0:T(8,128)} %constant.45.clone) | copy-start | bytes 196612
  108.8 23.7 %collective-permute-start.12 = (f32[2,8,128,128]{3,2,1,0:T(8,128)}, f32[2,8,128,128]{3,2,1,0:T(8,128)S(1)}, u32[]{:S(2)}, u32[]{:S(2)}) collective-permute-start(f32[2,8,128,128]{3,2,1,0:T(8,128)} %get-tuple-element.25.u_head_ref), channel_id=1, source_target_pairs={{40,32},{42,34},{44,36},{46,38},{47,39},{45,37},{43,35},{41,33},{4... | collective-permute-start | bytes 3145736 | tf_op jit(solution)/shard_map/ppermute | solution.py:93
  113.3 19.3 %collective-permute-start.11 = (f32[2,8,128,128]{3,2,1,0:T(8,128)}, f32[2,8,128,128]{3,2,1,0:T(8,128)S(1)}, u32[]{:S(2)}, u32[]{:S(2)}) collective-permute-start(f32[2,8,128,128]{3,2,1,0:T(8,128)} %get-tuple-element.26.u_tail_ref), channel_id=1, source_target_pairs={{32,40},{34,42},{36,44},{38,46},{39,47},{37,45},{35,43},{33,41},{4... | collective-permute-start | bytes 3145736 | tf_op jit(solution)/shard_map/ppermute | solution.py:93
  115.2 7.7 %collective-permute-start.15 = (f32[4,2,32,128]{3,2,1,0:T(8,128)S(1)}, f32[4,2,32,128]{3,2,1,0:T(8,128)S(1)}, u32[]{:S(2)}, u32[]{:S(2)}) collective-permute-start(f32[4,2,32,128]{3,2,1,0:T(8,128)S(1)} %get-tuple-element.29), channel_id=1, source_target_pairs={{38,32},{39,33},{46,40},{47,41},{54,48},{55,49},{62,56},{63,57},{7... | collective-permute-start | bytes 393224 | tf_op jit(solution)/shard_map/ppermute | solution.py:93
  116.5 15.1 %collective-permute-start.13 = (f32[4,2,128,128]{3,2,1,0:T(8,128)}, f32[4,2,128,128]{3,2,1,0:T(8,128)S(1)}, u32[]{:S(2)}, u32[]{:S(2)}) collective-permute-start(f32[4,2,128,128]{3,2,1,0:T(8,128)} %get-tuple-element.27), channel_id=1, source_target_pairs={{32,34},{34,36},{36,38},{39,37},{37,35},{35,33},{40,42},{42,44},{4... | collective-permute-start | bytes 1572872 | tf_op jit(solution)/shard_map/ppermute | solution.py:93
  117.8 14.8 %collective-permute-start.14 = (f32[4,2,128,128]{3,2,1,0:T(8,128)}, f32[4,2,128,128]{3,2,1,0:T(8,128)}, u32[]{:S(2)}, u32[]{:S(2)}) collective-permute-start(f32[4,2,128,128]{3,2,1,0:T(8,128)} %get-tuple-element.28), channel_id=1, source_target_pairs={{34,32},{36,34},{38,36},{37,39},{35,37},{33,35},{42,40},{44,42},{4... | collective-permute-start | bytes 1572872 | tf_op jit(solution)/shard_map/ppermute | solution.py:93
  122.9 0.7 collective-permute-start.16
  123.5 9.0 %copy-start.2 = (f32[4,2,32,128]{3,2,1,0:T(8,128)}, f32[4,2,32,128]{3,2,1,0:T(8,128)S(1)}, u32[]{:S(2)}) copy-start(f32[4,2,32,128]{3,2,1,0:T(8,128)S(1)} %collective-permute-done.16.e1_ref) | copy-start | bytes 393220
  123.5 1.5 collective-permute-start.17
  125.0 0.7 copy-start.4
  132.6 0.9 copy-start.3
  133.5 0.9 copy-start.5
  134.4 36.9 %copy-start.1 = (f32[4,64,16,128]{3,2,1,0:T(8,128)S(1)}, f32[4,64,16,128]{3,2,1,0:T(8,128)}, u32[]{:S(2)}) copy-start(f32[4,64,16,128]{3,2,1,0:T(8,128)} %g_ref.1) | copy-start | bytes 6291460
  138.5 23.5 %collective-permute-start.20 = (f32[4,8,16,128]{3,2,1,0:T(8,128)S(1)}, f32[4,8,16,128]{3,2,1,0:T(8,128)S(1)}, u32[]{:S(2)}, u32[]{:S(2)}) collective-permute-start(f32[4,8,16,128]{3,2,1,0:T(8,128)S(1)} %get-tuple-element.35), channel_id=1, source_target_pairs={{36,0},{37,1},{38,2},{39,3},{32,4},{33,5},{34,6},{35,7},{44,8},{45... | collective-permute-start | bytes 786440 | tf_op jit(solution)/shard_map/ppermute | solution.py:93
  153.7 13.3 %collective-permute-start.21 = (f32[4,8,16,128]{3,2,1,0:T(8,128)S(1)}, f32[4,8,16,128]{3,2,1,0:T(8,128)S(1)}, u32[]{:S(2)}, u32[]{:S(2)}) collective-permute-start(f32[4,8,16,128]{3,2,1,0:T(8,128)S(1)} %get-tuple-element.36), channel_id=1, source_target_pairs={{37,0},{36,1},{39,2},{38,3},{33,4},{32,5},{35,6},{34,7},{45,8},{44... | collective-permute-start | bytes 786440 | tf_op jit(solution)/shard_map/ppermute | solution.py:93
  153.7 17.0 %collective-permute-start.22 = (f32[4,8,16,128]{3,2,1,0:T(8,128)S(1)}, f32[4,8,16,128]{3,2,1,0:T(8,128)S(1)}, u32[]{:S(2)}, u32[]{:S(2)}) collective-permute-start(f32[4,8,16,128]{3,2,1,0:T(8,128)S(1)} %get-tuple-element.37), channel_id=1, source_target_pairs={{34,0},{35,1},{36,2},{37,3},{38,4},{39,5},{32,6},{33,7},{42,8},{43... | collective-permute-start | bytes 786440 | tf_op jit(solution)/shard_map/ppermute | solution.py:93
  153.7 25.7 %collective-permute-start.23 = (f32[4,8,16,128]{3,2,1,0:T(8,128)S(1)}, f32[4,8,16,128]{3,2,1,0:T(8,128)S(1)}, u32[]{:S(2)}, u32[]{:S(2)}) collective-permute-start(f32[4,8,16,128]{3,2,1,0:T(8,128)S(1)} %get-tuple-element.38), channel_id=1, source_target_pairs={{35,0},{34,1},{37,2},{36,3},{39,4},{38,5},{33,6},{32,7},{43,8},{42... | collective-permute-start | bytes 786440 | tf_op jit(solution)/shard_map/ppermute | solution.py:93
  156.0 23.5 %collective-permute-start.24 = (f32[4,8,16,128]{3,2,1,0:T(8,128)S(1)}, f32[4,8,16,128]{3,2,1,0:T(8,128)S(1)}, u32[]{:S(2)}, u32[]{:S(2)}) collective-permute-start(f32[4,8,16,128]{3,2,1,0:T(8,128)S(1)} %get-tuple-element.39), channel_id=1, source_target_pairs={{38,0},{39,1},{32,2},{33,3},{34,4},{35,5},{36,6},{37,7},{46,8},{47... | collective-permute-start | bytes 786440 | tf_op jit(solution)/shard_map/ppermute | solution.py:93
  162.0 29.1 %collective-permute-start.25 = (f32[4,8,16,128]{3,2,1,0:T(8,128)S(1)}, f32[4,8,16,128]{3,2,1,0:T(8,128)S(1)}, u32[]{:S(2)}, u32[]{:S(2)}) collective-permute-start(f32[4,8,16,128]{3,2,1,0:T(8,128)S(1)} %get-tuple-element.40), channel_id=1, source_target_pairs={{39,0},{38,1},{33,2},{32,3},{35,4},{34,5},{37,6},{36,7},{47,8},{46... | collective-permute-start | bytes 786440 | tf_op jit(solution)/shard_map/ppermute | solution.py:93
  167.0 24.1 %collective-permute-start.18 = (f32[4,10,16,128]{3,2,1,0:T(8,128)S(1)}, f32[4,10,16,128]{3,2,1,0:T(8,128)S(1)}, u32[]{:S(2)}, u32[]{:S(2)}) collective-permute-start(f32[4,10,16,128]{3,2,1,0:T(8,128)S(1)} %get-tuple-element.33), channel_id=1, source_target_pairs={{32,0},{33,1},{34,2},{35,3},{36,4},{37,5},{38,6},{39,7},{40,8},{41... | collective-permute-start | bytes 983048 | tf_op jit(solution)/shard_map/ppermute | solution.py:93
  170.7 34.2 %collective-permute-start.19 = (f32[4,10,16,128]{3,2,1,0:T(8,128)S(1)}, f32[4,10,16,128]{3,2,1,0:T(8,128)S(1)}, u32[]{:S(2)}, u32[]{:S(2)}) collective-permute-start(f32[4,10,16,128]{3,2,1,0:T(8,128)S(1)} %get-tuple-element.34), channel_id=1, source_target_pairs={{33,0},{32,1},{35,2},{34,3},{37,4},{36,5},{39,6},{38,7},{41,8},{40... | collective-permute-start | bytes 983048 | tf_op jit(solution)/shard_map/ppermute | solution.py:93

commit v2 on v1

v2 whole, which is shorter than its diff:
```python
import math

import jax
import jax.numpy as jnp
import numpy as np
from jax import lax
from jax.experimental import pallas as pl
from jax.experimental.pallas import tpu as pltpu
from jax.sharding import PartitionSpec as P


F32 = jnp.float32
BF16 = jnp.bfloat16
K = 128
AXES = ("gx", "ka")
SLOTS = [(dy, ds) for dy in (0, 2, 1, 3) for ds in (0, 1)]
VMEM = pl.BlockSpec(memory_space=pltpu.VMEM)


def flat(x, y, z, core):
    return ((x * 4 + z % 4) * 2 + core) * 8 + y * 2 + z // 4


def place(block, part):
    x, low, core = block // 8, block // 2 % 4, block % 2
    half = part // 4
    y = part if half == 0 else 7 - part
    z = (low + 2 if x % 2 == 0 else 5 - low) + 4 * half
    return flat(x, y, z % 8, core)


def part_of(y, half):
    return y if half == 0 else 7 - y


def slot_part(ka, slot):
    dy, ds = SLOTS[slot]
    return part_of((ka // 2 + dy) % 4, (ka % 2) ^ ds)


def exchange_pairs(slot):
    return [
        (block * 8 + ka, place(block, slot_part(ka, slot)))
        for block in range(32)
        for ka in range(8)
    ]


def x_pairs(step):
    return [
        (place(block, part), place(block + step, part))
        for block in range(32)
        for part in range(8)
        if 0 <= block + step < 32
    ]


def y_pairs(step):
    return [
        (place(block, part), place(block, part + step))
        for block in range(32)
        for part in range(8)
        if 0 <= part + step < 8 and part // 4 == (part + step) // 4
    ] + [
        (place(block, part), place(block, part_of(0, part // 4)))
        for block in range(32)
        for part in [3 if step == 1 else 4]
    ]


def edge_pairs():
    return [
        (place(block, part_of(3, half)), place(block, part_of(1, half)))
        for block in range(32)
        for half in range(2)
    ]


def send(value, pairs):
    return lax.ppermute(value, AXES, pairs)


def as_source():
    ka = lax.axis_index("ka")
    return ka >> 1, ka & 1


def as_host():
    gx, ka = lax.axis_index("gx"), lax.axis_index("ka")
    z = (ka & 1) * 4 + ((gx >> 1) & 3)
    turn = jnp.where(((gx >> 3) & 1) == 0, z - 2, 5 - z) & 7
    return ka >> 1, turn >> 2


def part_index(y, half):
    return y + half * (7 - 2 * y)


def rows_to(slot):
    y, half = as_source()
    dy, ds = SLOTS[slot]
    return pl.ds(pl.multiple_of(part_index((y + dy) & 3, half ^ ds) * 8, 8), 8)


def kx_of(slot):
    y, half = as_host()
    dy, ds = SLOTS[slot]
    return pl.ds(pl.multiple_of((((y - dy) & 3) * 2 + (half ^ ds)) * 16, 16), 16)


def halves(value):
    high = value.astype(BF16)
    return high, (value - high.astype(F32)).astype(BF16)


def circulant(row):
    return pltpu.roll(jnp.broadcast_to(row, (K, K)), 0, 1, stride=1, stride_axis=0)


def right_table(row):
    high, low = halves(circulant(row))
    return jnp.concatenate(
        [
            jnp.concatenate([high, low], 1),
            jnp.concatenate([high, jnp.zeros_like(low)], 1),
        ],
        0,
    )


def left_table(row):
    high, low = halves(circulant(row))
    return jnp.concatenate(
        [
            jnp.concatenate([high, high], 1),
            jnp.concatenate([low, jnp.zeros_like(low)], 1),
        ],
        0,
    )


def times_right(rows, table):
    both = jnp.dot(jnp.concatenate(halves(rows), 1), table, preferred_element_type=F32)
    return both[:, :K] + both[:, K:]


def times_left(table, first, second):
    high_0, low_0 = halves(first)
    high_1, low_1 = halves(second)
    stacked = jnp.concatenate(
        [jnp.concatenate([high_0, high_1], 1), jnp.concatenate([low_0, low_1], 1)], 0
    )
    both = jnp.dot(table, stacked, preferred_element_type=F32)
    both = both[:K] + both[K:]
    return both[:, :K], both[:, K:]


def slope(center, one, two):
    return 3.0 * center - 4.0 * one + two


def local_kernel(g_ref, ty_ref, vy_ref, out_ref, pad):
    vy = vy_ref[...].reshape(1, 1, K)
    toward = jnp.broadcast_to(vy > 0, (4, 16, K))
    rate = jnp.abs(vy) * 0.125

    def step(value, one_low, two_low, one_high, two_high, table):
        one = jnp.where(toward, one_low, one_high)
        two = jnp.where(toward, two_low, two_high)
        wigner = times_right(value.reshape(64, K), table).reshape(4, 16, K)
        return wigner - rate * slope(value, one, two)

    edge = jnp.zeros((4, 2, 16, K), F32)
    pad[0, :, 0:2] = edge
    pad[0, :, 66:68] = edge
    pad[1, :, 0:2] = edge
    pad[1, :, 66:68] = edge
    for y in range(64):
        pad[0, :, y + 2] = g_ref[:, y]

    def turn(source, into):
        @pl.loop(0, 8)
        def _(group):
            block = ty_ref[pl.ds(pl.multiple_of(group * 8, 8), 8), :]
            for inner in range(8):
                y = group * 8 + inner
                value = pad[source, :, y + 2]
                moved = step(
                    value,
                    pad[source, :, y + 1],
                    pad[source, :, y],
                    pad[source, :, y + 3],
                    pad[source, :, y + 4],
                    right_table(block[inner : inner + 1]),
                )
                into(y, value, moved)

    def first(y, value, moved):
        pad[1, :, y + 2] = value + moved

    def second(y, value, moved):
        out_ref[:, y] = 0.5 * (pad[0, :, y + 2] + value + moved)

    turn(0, first)
    turn(1, second)


def pack_kernel(g_ref, vel_ref, potential_ref, *pieces):
    for slot in range(8):
        at = rows_to(slot)
        for x in range(4):
            pieces[slot][8 * x : 8 * x + 8] = g_ref[x, at]
        pieces[slot][32] = vel_ref[...]
    pieces[0][33, 0:4] = potential_ref[...]
    pieces[0][33, 4:16] = jnp.zeros((12, K), F32)


def cut_kernel(*refs):
    pieces, (head_ref, tail_ref) = refs[:4], refs[4:]
    for i in range(4):
        head_ref[i] = pieces[i][0:16]
        tail_ref[i] = pieces[i][16:32]


def inner_drift(center, x, layer, toward, rate):
    total = 3.0 * center
    for step, factor in ((1, -4.0), (2, 1.0)):
        low = layer(x - step) if x - step >= 0 else None
        high = layer(x + step) if x + step <= 3 else None
        if low is None:
            if high is not None:
                total += factor * jnp.where(toward, 0.0, high)
        elif high is None:
            total += factor * jnp.where(toward, low, 0.0)
        else:
            total += factor * jnp.where(toward, low, high)
    return -rate * total


def first_kernel(*refs):
    pieces, sine_ref, (u_ref, vx_ref, tx_ref), (field, tables) = refs[:8], refs[8], refs[9:12], refs[12:]
    for slot in range(8):
        at = kx_of(slot)
        for x in range(4):
            field[x, :, at, :] = pieces[slot][8 * x : 8 * x + 8]
        vx_ref[at, :] = pieces[slot][32]
    tx_ref[...] = 0.25 * jnp.dot(
        pieces[0][33, 0:8], sine_ref[...], precision=lax.Precision.HIGHEST, preferred_element_type=F32
    )
    for x in range(4):
        tables[x] = left_table(tx_ref[x : x + 1, :])

    @pl.loop(0, 4)
    def _(pair):
        vx = vx_ref[...]
        toward = vx > 0
        rate = jnp.abs(vx) * 0.125
        for x in range(4):
            mine = [field[x, pair * 2 + i] for i in range(2)]
            wigner = times_left(tables[x], mine[0], mine[1])
            for i in range(2):
                y = pair * 2 + i
                u_ref[x, y] = wigner[i] + inner_drift(mine[i], x, lambda at: field[at, y], toward, rate)


def first_edge_kernel(
    inner_ref, low_a_ref, low_b_ref, high_a_ref, high_b_ref, vx_ref, vy_ref,
    u_head_ref, u_tail_ref, y_low_ref, y_high_ref, edge_ref, own_edge_ref,
):
    for slot in range(8):
        at = kx_of(slot)
        low = (low_a_ref if slot < 4 else low_b_ref).at[slot % 4]
        high = (high_a_ref if slot < 4 else high_b_ref).at[slot % 4]
        vx = vx_ref[at, :]
        up = (jnp.maximum(vx, 0.0) * 0.125)[None]
        down = (jnp.maximum(-vx, 0.0) * 0.125)[None]
        near = low[8:16]
        u_head_ref[0, :, at, :] = inner_ref[0, :, at, :] + up * (4.0 * near - low[0:8])
        u_head_ref[1, :, at, :] = inner_ref[1, :, at, :] - up * near
        near = high[0:8]
        u_tail_ref[0, :, at, :] = inner_ref[2, :, at, :] - down * near
        u_tail_ref[1, :, at, :] = inner_ref[3, :, at, :] + down * (4.0 * near - high[8:16])

    vy = vy_ref[...]
    y_place, half = as_host()
    upper = half == 0
    last = y_place == 3
    keep = jnp.logical_or(
        jnp.logical_and(vy > 0, upper), jnp.logical_and(vy <= 0, jnp.logical_not(upper))
    )
    weight = jnp.where(keep, jnp.abs(vy) * -0.125, 0.0)
    for x in range(4):
        u = u_head_ref.at[x] if x < 2 else u_tail_ref.at[x - 2]
        y_low_ref[x, :, 0:K] = jnp.where(jnp.logical_and(last, jnp.logical_not(upper)), 0.0, u[0:2])
        y_high_ref[x, :, 0:K] = jnp.where(jnp.logical_and(last, upper), 0.0, u[6:8])
        parts = []
        for part in range(4):
            at = slice(32 * part, 32 * part + 32)
            near = jnp.where(upper, u[7, at], u[0, at])
            far = jnp.where(upper, u[6, at], u[1, at])
            one = weight * (far - 4.0 * near)
            two = weight * near
            parts.append((jnp.where(upper, one, two), jnp.where(upper, two, one)))
        for row in range(2):
            y_low_ref[x, row, K : K + 32] = jnp.where(upper, parts[2][row], parts[0][row])
            y_high_ref[x, row, K : K + 32] = jnp.where(upper, parts[0][row], parts[2][row])
            edge_ref[x, row] = parts[1][row]
            own_edge_ref[x, row] = parts[3][row]


def second_kernel(u_head_ref, u_tail_ref, tx_ref, ty_ref, vx_ref, vy_ref, out_ref, tables):
    layers = [u_head_ref.at[0], u_head_ref.at[1], u_tail_ref.at[0], u_tail_ref.at[1]]
    for x in range(4):
        tables[x] = left_table(0.5 * tx_ref[x : x + 1, :])
    y_place, half = as_host()
    ty = ty_ref[pl.ds(pl.multiple_of(part_index(y_place, half) * 8, 8), 8), :]

    vx = vx_ref[...]
    toward = vx > 0
    rate = jnp.abs(vx) * 0.0625
    vy = jnp.broadcast_to(vy_ref[...], (K, K))
    toward_y = vy > 0
    rate_y = jnp.abs(vy) * 0.125
    zero = jnp.zeros((K, K), F32)
    for pair in range(4):
        right = [right_table(ty[pair * 2 + i : pair * 2 + i + 1, :]) for i in range(2)]
        for x in range(4):
            mine = [layers[x][pair * 2 + i] for i in range(2)]
            wigner = times_left(tables[x], mine[0], mine[1])
            for i in range(2):
                y = pair * 2 + i
                total = mine[i] + wigner[i]
                total += inner_drift(mine[i], x, lambda at: layers[at][y], toward, rate)
                total += times_right(mine[i], right[i])
                near = [layers[x][at] if 0 <= at < 8 else zero for at in (y - 2, y - 1, y + 1, y + 2)]
                one = jnp.where(toward_y, near[1], near[2])
                two = jnp.where(toward_y, near[0], near[3])
                out_ref[x, y] = total - rate_y * slope(mine[i], one, two)


def second_edge_kernel(
    inner_ref, low_ref, high_ref, y_low_ref, y_high_ref, edge_ref, own_edge_ref, vx_ref, vy_ref, *pieces
):
    vy = vy_ref[...].reshape(1, 1, K)
    up_y = jnp.maximum(vy, 0.0) * 0.125
    down_y = jnp.maximum(-vy, 0.0) * 0.125

    def total(at, x):
        vx = vx_ref[at, :]
        up = (jnp.maximum(vx, 0.0) * 0.0625)[None]
        down = (jnp.maximum(-vx, 0.0) * 0.0625)[None]
        value = inner_ref[x, :, at, :]
        if x == 0:
            value += up * (4.0 * low_ref[1, :, at, :] - low_ref[0, :, at, :])
        if x == 1:
            value -= up * low_ref[1, :, at, :]
        if x == 2:
            value -= down * high_ref[0, :, at, :]
        if x == 3:
            value += down * (4.0 * high_ref[0, :, at, :] - high_ref[1, :, at, :])
        near, far = y_low_ref[x, 1:2, at, :], y_low_ref[x, 0:1, at, :]
        rows = [up_y * (4.0 * near - far), -up_y * near]
        near, far = y_high_ref[x, 0:1, at, :], y_high_ref[x, 1:2, at, :]
        rows += [-down_y * near, down_y * (4.0 * near - far)]
        return value, rows

    for slot in range(8):
        at = kx_of(slot)
        for x in range(4):
            value, rows = total(at, x)
            pieces[slot][x, 0:2] = value[0:2] + jnp.concatenate(rows[:2], 0)
            pieces[slot][x, 2:6] = value[2:6]
            pieces[slot][x, 6:8] = value[6:8] + jnp.concatenate(rows[2:], 0)

    y_place, half = as_host()
    ends = jnp.logical_or(y_place == 0, y_place == 2)
    under = jnp.logical_and(ends, (y_place == 0) == (half == 0))
    for slot in range(2):
        at = pl.multiple_of((half ^ SLOTS[slot][1]) * 16, 16)
        with_rows = pl.ds(pl.multiple_of(K + at, 16), 16)
        at = pl.ds(at, 16)
        for x in range(4):
            alone = jnp.where(y_place == 3, own_edge_ref[x, :, at, :], edge_ref[x, :, at, :])
            paired = jnp.where(under, y_low_ref[x, :, with_rows, :], y_high_ref[x, :, with_rows, :])
            pieces[slot][x, 8:10] = jnp.where(ends, paired, alone)


def final_kernel(local_ref, *refs):
    pieces, out_ref = refs[:8], refs[8]
    for slot in range(8):
        at = rows_to(slot)
        out_ref[:, at] = local_ref[:, at] + pieces[slot][:, 0:8]
    for slot in range(2):
        half = as_source()[1] ^ SLOTS[slot][1]
        at = pl.ds(32 - 2 * half, 2)
        out_ref[:, at] = out_ref[:, at] + pieces[slot][:, 8:10]


MIB = 1 << 20


def array(*shape):
    return jax.ShapeDtypeStruct(shape, F32)


def params():
    return pltpu.CompilerParams(vmem_limit_bytes=40 * MIB)


def cost(flops, mib):
    return pl.CostEstimate(flops=flops, bytes_accessed=mib * MIB, transcendentals=0)


def call(kernel, outs, scratch=(), flops=0, mib=4):
    def run(*operands):
        return pl.pallas_call(
            kernel,
            out_shape=outs,
            in_specs=[VMEM] * len(operands),
            out_specs=[VMEM] * len(outs) if isinstance(outs, list) else VMEM,
            scratch_shapes=list(scratch),
            compiler_params=params(),
            cost_estimate=cost(flops, mib),
            name=kernel.__name__,
        )(*operands)

    return run


def sine_table(sign):
    index = np.arange(K)
    angle = (sign * index[:, None] * index[None, :] % K) * (2.0 * math.pi / K)
    return (np.sin(angle) / K).astype(np.float32)


def back(pairs):
    return [(there, here) for here, there in pairs]


def per_device(density, potential_x, potential_y, speeds_x, speeds_y, upwind_x, upwind_y):
    vel_x = (2 * upwind_x - 1).astype(F32) * speeds_x
    vel_x = jnp.broadcast_to(vel_x[:, None], (16, K))
    vy = ((2 * upwind_y - 1).astype(F32) * speeds_y).reshape(1, K)

    pieces = call(pack_kernel, [array(34, 16, K)] + [array(33, 16, K)] * 7)(density, vel_x, potential_x)
    pieces = [send(piece, exchange_pairs(slot)) for slot, piece in enumerate(pieces)]

    highest = lax.Precision.HIGHEST
    ty = 0.25 * jnp.dot(potential_y, jnp.asarray(sine_table(1)), precision=highest)
    local = call(
        local_kernel, array(4, 64, 16, K), [pltpu.VMEM((2, 4, 68, 16, K), F32)], 4 * 10**9
    )(density, ty, vy)

    low, high = [], []
    for group in range(2):
        head, tail = call(cut_kernel, [array(4, 16, 16, K)] * 2, mib=2)(*pieces[4 * group : 4 * group + 4])
        low.append(send(tail, x_pairs(1)))
        high.append(send(head, x_pairs(-1)))
    left_tables = pltpu.VMEM((4, 2 * K, 2 * K), BF16)
    inner, vx, tx = call(
        first_kernel,
        [array(4, 8, K, K), array(K, K), array(8, K)],
        [pltpu.VMEM((4, 8, K, K), F32), left_tables],
        2 * 10**9,
    )(*pieces, jnp.asarray(sine_table(-1)))
    u_head, u_tail, y_low, y_high, edge, own_edge = call(
        first_edge_kernel,
        [array(2, 8, K, K)] * 2 + [array(4, 2, K + 32, K)] * 2 + [array(4, 2, 32, K)] * 2,
    )(inner, *low, *high, vx, vy)

    low = send(u_tail, x_pairs(1))
    high = send(u_head, x_pairs(-1))
    y_under = send(y_high, y_pairs(1))
    y_over = send(y_low, y_pairs(-1))
    edge = send(edge, edge_pairs())
    inner = call(second_kernel, array(4, 8, K, K), [left_tables], 3 * 10**9)(u_head, u_tail, tx, ty, vx, vy)
    pieces = call(second_edge_kernel, [array(4, 10, 16, K)] * 2 + [array(4, 8, 16, K)] * 6)(
        inner, low, high, y_under, y_over, edge, own_edge, vx, vy
    )
    pieces = [send(piece, back(exchange_pairs(slot))) for slot, piece in enumerate(pieces)]

    def by_x(*shape):
        return pl.BlockSpec((1, *shape), lambda x: (x, 0, 0, 0))

    return pl.pallas_call(
        final_kernel,
        grid=(4,),
        out_shape=array(4, 64, 16, K),
        in_specs=[by_x(64, 16, K)] + [by_x(10, 16, K)] * 2 + [by_x(8, 16, K)] * 6,
        out_specs=by_x(64, 16, K),
        compiler_params=params(),
        cost_estimate=cost(0, 6),
        name="final_kernel",
    )(local, *pieces)


def solution(mesh):
    in_specs = (P("gx", None, "ka", None), P("gx", None), P(), P("ka"), P(), P("ka"), P())
    out_specs = P("gx", None, "ka", None)
    return jax.shard_map(
        per_device, mesh=mesh, in_specs=in_specs, out_specs=out_specs, check_vma=False
    )
```

time: 210 us -> 167 us (0.80)
  the two profiles are of different devices: /device:TPU:39 before, /device:TPU:31 now
where the time goes in v2:
time: 167 us
  starting transfers between devices  94.6 us (57%)
  waiting for transfers between devices  55.3 us (33%)
  Pallas kernels  13.6 us (8%)
  local copies, waits for them, and re-layouts  2.37 us (1%)
    ppermute x25, starting transfers between devices, send(): return lax.ppermute(value, AXES, pairs)  94.6 us
    ppermute x25, waiting for transfers between devices, send(): return lax.ppermute(value, AXES, pairs)  55.3 us
    pallas_call x8, Pallas kernels, run(): pl.pallas_call(kernel, out_shape=outs, in_specs=[VMEM] * len(operands), o...  11.7 us
  transfers between devices with their start and end apart: 25, of which 13 were waited for; matrix products, arithmetic and copies ran while one was open for 0% of the time, Pallas kernels for 6%

profile of v2, /device:TPU:31, one launch (start us, length us, event | category | flops | bytes accessed | tf_op | source)
XLA Modules:
  0.0 167.0 jit_solution(6781548185227792650)
XLA Ops:
  0.0 0.7 convert_multiply_fusion
  0.7 0.1 broadcast_in_dim.2.vel_ref
  0.8 1.6 copy-done.1
  2.4 0.7 copy-done.3
  3.0 0.1 pack_kernel.1
  3.2 6.2 %collective-permute-start.4 = (f32[33,16,128]{2,1,0:T(8,128)S(1)}, f32[33,16,128]{2,1,0:T(8,128)S(1)}, u32[]{:S(2)}, u32[]{:S(2)}) collective-permute-start(f32[33,16,128]{2,1,0:T(8,128)S(1)} %get-tuple-element.38), channel_id=1, source_target_pairs={{0,34},{1,35},{2,36},{3,37},{4,38},{5,39},{6,32},{7,33},{8,42},{9,... | collective-permute-start | bytes 811016 | tf_op jit(solution)/shard_map/ppermute | solution.py:80
  9.4 1.7 %collective-permute-start.5 = (f32[33,16,128]{2,1,0:T(8,128)S(1)}, f32[33,16,128]{2,1,0:T(8,128)S(1)}, u32[]{:S(2)}, u32[]{:S(2)}) collective-permute-start(f32[33,16,128]{2,1,0:T(8,128)S(1)} %get-tuple-element.39), channel_id=1, source_target_pairs={{0,35},{1,34},{2,37},{3,36},{4,39},{5,38},{6,33},{7,32},{8,43},{9,... | collective-permute-start | bytes 811016 | tf_op jit(solution)/shard_map/ppermute | solution.py:80
  11.1 0.3 collective-permute-start.6
  11.5 4.0 %collective-permute-start = (f32[34,16,128]{2,1,0:T(8,128)S(1)}, f32[34,16,128]{2,1,0:T(8,128)S(1)}, u32[]{:S(2)}, u32[]{:S(2)}) collective-permute-start(f32[34,16,128]{2,1,0:T(8,128)S(1)} %get-tuple-element.34), channel_id=1, source_target_pairs={{0,32},{1,33},{2,34},{3,35},{4,36},{5,37},{6,38},{7,39},{8,40},{9,... | collective-permute-start | bytes 835592 | tf_op jit(solution)/shard_map/ppermute | solution.py:80
  15.5 2.0 %collective-permute-start.7 = (f32[33,16,128]{2,1,0:T(8,128)S(1)}, f32[33,16,128]{2,1,0:T(8,128)S(1)}, u32[]{:S(2)}, u32[]{:S(2)}) collective-permute-start(f32[33,16,128]{2,1,0:T(8,128)S(1)} %get-tuple-element.41), channel_id=1, source_target_pairs={{0,39},{1,38},{2,33},{3,32},{4,35},{5,34},{6,37},{7,36},{8,47},{9,... | collective-permute-start | bytes 811016 | tf_op jit(solution)/shard_map/ppermute | solution.py:80
  17.5 5.3 %collective-permute-start.1 = (f32[33,16,128]{2,1,0:T(8,128)S(1)}, f32[33,16,128]{2,1,0:T(8,128)S(1)}, u32[]{:S(2)}, u32[]{:S(2)}) collective-permute-start(f32[33,16,128]{2,1,0:T(8,128)S(1)} %get-tuple-element.35), channel_id=1, source_target_pairs={{0,33},{1,32},{2,35},{3,34},{4,37},{5,36},{6,39},{7,38},{8,41},{9,... | collective-permute-start | bytes 811016 | tf_op jit(solution)/shard_map/ppermute | solution.py:80
  22.8 1.2 collective-permute-done.5.refs_5_.refs_1_
  24.0 0.7 collective-permute-start.2
  24.7 2.8 %collective-permute-done.6.refs_6_.refs_2_ = f32[33,16,128]{2,1,0:T(8,128)S(1)} collective-permute-done((f32[33,16,128]{2,1,0:T(8,128)S(1)}, f32[33,16,128]{2,1,0:T(8,128)S(1)}, u32[]{:S(2)}, u32[]{:S(2)}) %collective-permute-start.6) | collective-permute-done | bytes 270368 | tf_op jit(solution)/shard_map/ppermute | solution.py:80
  27.5 8.3 %collective-permute-start.3 = (f32[33,16,128]{2,1,0:T(8,128)S(1)}, f32[33,16,128]{2,1,0:T(8,128)S(1)}, u32[]{:S(2)}, u32[]{:S(2)}) collective-permute-start(f32[33,16,128]{2,1,0:T(8,128)S(1)} %get-tuple-element.37), channel_id=1, source_target_pairs={{0,37},{1,36},{2,39},{3,38},{4,33},{5,32},{6,35},{7,34},{8,45},{9,... | collective-permute-start | bytes 811016 | tf_op jit(solution)/shard_map/ppermute | solution.py:80
  35.9 4.3 %collective-permute-start.11 = (f32[4,16,16,128]{3,2,1,0:T(8,128)S(1)}, f32[4,16,16,128]{3,2,1,0:T(8,128)S(1)}, u32[]{:S(2)}, u32[]{:S(2)}) collective-permute-start(f32[4,16,16,128]{3,2,1,0:T(8,128)S(1)} %get-tuple-element.46), channel_id=1, source_target_pairs={{40,32},{42,34},{44,36},{46,38},{47,39},{45,37},{43,35},{41,33},{4... | collective-permute-start | bytes 1572872 | tf_op jit(solution)/shard_map/ppermute | solution.py:80
  40.2 1.5 collective-permute-done.1.refs_1_
  41.7 15.2 %collective-permute-start.9 = (f32[4,16,16,128]{3,2,1,0:T(8,128)S(1)}, f32[4,16,16,128]{3,2,1,0:T(8,128)S(1)}, u32[]{:S(2)}, u32[]{:S(2)}) collective-permute-start(f32[4,16,16,128]{3,2,1,0:T(8,128)S(1)} %get-tuple-element.44), channel_id=1, source_target_pairs={{32,40},{34,42},{36,44},{38,46},{39,47},{37,45},{35,43},{33,41},{4... | collective-permute-start | bytes 1572872 | tf_op jit(solution)/shard_map/ppermute | solution.py:80
  56.9 3.7 %collective-permute-done.3.refs_3_ = f32[33,16,128]{2,1,0:T(8,128)S(1)} collective-permute-done((f32[33,16,128]{2,1,0:T(8,128)S(1)}, f32[33,16,128]{2,1,0:T(8,128)S(1)}, u32[]{:S(2)}, u32[]{:S(2)}) %collective-permute-start.3) | collective-permute-done | bytes 270368 | tf_op jit(solution)/shard_map/ppermute | solution.py:80
  60.6 0.1 cut_kernel.2
  60.6 3.8 %collective-permute-start.10 = (f32[4,16,16,128]{3,2,1,0:T(8,128)S(1)}, f32[4,16,16,128]{3,2,1,0:T(8,128)S(1)}, u32[]{:S(2)}, u32[]{:S(2)}) collective-permute-start(f32[4,16,16,128]{3,2,1,0:T(8,128)S(1)} %get-tuple-element.45), channel_id=1, source_target_pairs={{40,32},{42,34},{44,36},{46,38},{47,39},{45,37},{43,35},{41,33},{4... | collective-permute-start | bytes 1572872 | tf_op jit(solution)/shard_map/ppermute | solution.py:80
  64.4 4.4 %collective-permute-start.8 = (f32[4,16,16,128]{3,2,1,0:T(8,128)S(1)}, f32[4,16,16,128]{3,2,1,0:T(8,128)S(1)}, u32[]{:S(2)}, u32[]{:S(2)}) collective-permute-start(f32[4,16,16,128]{3,2,1,0:T(8,128)S(1)} %get-tuple-element.43), channel_id=1, source_target_pairs={{32,40},{34,42},{36,44},{38,46},{39,47},{37,45},{35,43},{33,41},{4... | collective-permute-start | bytes 1572872 | tf_op jit(solution)/shard_map/ppermute | solution.py:80
  68.9 1.7 %first_kernel.1 = (f32[4,8,128,128]{3,2,1,0:T(8,128)S(1)}, f32[128,128]{1,0:T(8,128)S(1)}, f32[8,128]{1,0:T(8,128)S(1)}) custom-call(f32[34,16,128]{2,1,0:T(8,128)S(1)} %collective-permute-done.refs_0_, f32[33,16,128]{2,1,0:T(8,128)S(1)} %collective-permute-done.1.refs_1_, f32[33,16,128]{2,1,0:T(8,128)S(1)} %collective-permute-done.2.refs_2_, ...), custom_call_target="tpu_custom_call" | custom-call | flops 2000000000 | bytes 4194304 | tf_op jit(solution)/shard_map/first_kernel/pallas_call | solution.py:416
  70.6 3.2 %collective-permute-done.10.high_a_ref = f32[4,16,16,128]{3,2,1,0:T(8,128)S(1)} collective-permute-done((f32[4,16,16,128]{3,2,1,0:T(8,128)S(1)}, f32[4,16,16,128]{3,2,1,0:T(8,128)S(1)}, u32[]{:S(2)}, u32[]{:S(2)}) %collective-permute-start.10) | collective-permute-done | bytes 524320 | tf_op jit(solution)/shard_map/ppermute | solution.py:80
  73.7 1.2 collective-permute-done.8.low_a_ref
  74.9 0.5 first_edge_kernel.1
  75.4 5.6 %collective-permute-start.12 = (f32[2,8,128,128]{3,2,1,0:T(8,128)S(1)}, f32[2,8,128,128]{3,2,1,0:T(8,128)S(1)}, u32[]{:S(2)}, u32[]{:S(2)}) collective-permute-start(f32[2,8,128,128]{3,2,1,0:T(8,128)S(1)} %get-tuple-element.49.u_tail_ref), channel_id=1, source_target_pairs={{32,40},{34,42},{36,44},{38,46},{39,47},{37,45},{35,43},{33,41},{4... | collective-permute-start | bytes 3145736 | tf_op jit(solution)/shard_map/ppermute | solution.py:80
  81.0 1.9 %collective-permute-start.13 = (f32[2,8,128,128]{3,2,1,0:T(8,128)S(1)}, f32[2,8,128,128]{3,2,1,0:T(8,128)S(1)}, u32[]{:S(2)}, u32[]{:S(2)}) collective-permute-start(f32[2,8,128,128]{3,2,1,0:T(8,128)S(1)} %get-tuple-element.48.u_head_ref), channel_id=1, source_target_pairs={{40,32},{42,34},{44,36},{46,38},{47,39},{45,37},{43,35},{41,33},{4... | collective-permute-start | bytes 3145736 | tf_op jit(solution)/shard_map/ppermute | solution.py:80
  82.9 1.9 %collective-permute-start.14 = (f32[4,2,160,128]{3,2,1,0:T(8,128)S(1)}, f32[4,2,160,128]{3,2,1,0:T(8,128)S(1)}, u32[]{:S(2)}, u32[]{:S(2)}) collective-permute-start(f32[4,2,160,128]{3,2,1,0:T(8,128)S(1)} %get-tuple-element.51), channel_id=1, source_target_pairs={{32,34},{34,36},{36,38},{39,37},{37,35},{35,33},{40,42},{42,44},{4... | collective-permute-start | bytes 1966088 | tf_op jit(solution)/shard_map/ppermute | solution.py:80
  84.9 3.0 %collective-permute-start.15 = (f32[4,2,160,128]{3,2,1,0:T(8,128)S(1)}, f32[4,2,160,128]{3,2,1,0:T(8,128)S(1)}, u32[]{:S(2)}, u32[]{:S(2)}) collective-permute-start(f32[4,2,160,128]{3,2,1,0:T(8,128)S(1)} %get-tuple-element.52), channel_id=1, source_target_pairs={{34,32},{36,34},{38,36},{37,39},{35,37},{33,35},{42,40},{44,42},{4... | collective-permute-start | bytes 1966088 | tf_op jit(solution)/shard_map/ppermute | solution.py:80
  87.9 0.2 fusion.ty_ref
  88.1 4.1 %collective-permute-start.16 = (f32[4,2,32,128]{3,2,1,0:T(8,128)S(1)}, f32[4,2,32,128]{3,2,1,0:T(8,128)S(1)}, u32[]{:S(2)}, u32[]{:S(2)}) collective-permute-start(f32[4,2,32,128]{3,2,1,0:T(8,128)S(1)} %get-tuple-element.53), channel_id=1, source_target_pairs={{38,34},{39,35},{46,42},{47,43},{54,50},{55,51},{62,58},{63,59},{7... | collective-permute-start | bytes 393224 | tf_op jit(solution)/shard_map/ppermute | solution.py:80
  92.2 2.4 %second_kernel.1.inner_ref = f32[4,8,128,128]{3,2,1,0:T(8,128)S(1)} custom-call(f32[2,8,128,128]{3,2,1,0:T(8,128)S(1)} %get-tuple-element.48.u_head_ref, f32[2,8,128,128]{3,2,1,0:T(8,128)S(1)} %get-tuple-element.49.u_tail_ref, f32[8,128]{1,0:T(8,128)S(1)} %get-tuple-element.50.tx_ref, f32[64,128]{1,0:T(8,128)S(1)} %fusion.ty_ref, ...), custom_call_target="tpu_custom_call" | custom-call | flops 3000000000 | bytes 4194304 | tf_op jit(solution)/shard_map/second_kernel/pallas_call | solution.py:416
  94.6 7.3 %collective-permute-done.16.edge_ref = f32[4,2,32,128]{3,2,1,0:T(8,128)S(1)} collective-permute-done((f32[4,2,32,128]{3,2,1,0:T(8,128)S(1)}, f32[4,2,32,128]{3,2,1,0:T(8,128)S(1)}, u32[]{:S(2)}, u32[]{:S(2)}) %collective-permute-start.16) | collective-permute-done | bytes 131104 | tf_op jit(solution)/shard_map/ppermute | solution.py:80
  101.9 1.6 collective-permute-done.15.y_high_ref
  103.6 0.4 second_edge_kernel.1
  104.0 4.3 %collective-permute-start.19 = (f32[4,8,16,128]{3,2,1,0:T(8,128)S(1)}, f32[4,8,16,128]{3,2,1,0:T(8,128)S(1)}, u32[]{:S(2)}, u32[]{:S(2)}) collective-permute-start(f32[4,8,16,128]{3,2,1,0:T(8,128)S(1)} %get-tuple-element.57), channel_id=1, source_target_pairs={{36,0},{37,1},{38,2},{39,3},{32,4},{33,5},{34,6},{35,7},{44,8},{45... | collective-permute-start | bytes 786440 | tf_op jit(solution)/shard_map/ppermute | solution.py:80
  108.3 2.2 %collective-permute-start.20 = (f32[4,8,16,128]{3,2,1,0:T(8,128)S(1)}, f32[4,8,16,128]{3,2,1,0:T(8,128)S(1)}, u32[]{:S(2)}, u32[]{:S(2)}) collective-permute-start(f32[4,8,16,128]{3,2,1,0:T(8,128)S(1)} %get-tuple-element.58), channel_id=1, source_target_pairs={{37,0},{36,1},{39,2},{38,3},{33,4},{32,5},{35,6},{34,7},{45,8},{44... | collective-permute-start | bytes 786440 | tf_op jit(solution)/shard_map/ppermute | solution.py:80
  110.4 3.5 %collective-permute-start.17 = (f32[4,10,16,128]{3,2,1,0:T(8,128)S(1)}, f32[4,10,16,128]{3,2,1,0:T(8,128)S(1)}, u32[]{:S(2)}, u32[]{:S(2)}) collective-permute-start(f32[4,10,16,128]{3,2,1,0:T(8,128)S(1)} %get-tuple-element.55), channel_id=1, source_target_pairs={{32,0},{33,1},{34,2},{35,3},{36,4},{37,5},{38,6},{39,7},{40,8},{41... | collective-permute-start | bytes 983048 | tf_op jit(solution)/shard_map/ppermute | solution.py:80
  113.9 12.9 %collective-permute-done.19.refs_2_ = f32[4,8,16,128]{3,2,1,0:T(8,128)S(1)} collective-permute-done((f32[4,8,16,128]{3,2,1,0:T(8,128)S(1)}, f32[4,8,16,128]{3,2,1,0:T(8,128)S(1)}, u32[]{:S(2)}, u32[]{:S(2)}) %collective-permute-start.19) | collective-permute-done | bytes 262176 | tf_op jit(solution)/shard_map/ppermute | solution.py:80
  126.8 4.4 %collective-permute-done.20.refs_3_ = f32[4,8,16,128]{3,2,1,0:T(8,128)S(1)} collective-permute-done((f32[4,8,16,128]{3,2,1,0:T(8,128)S(1)}, f32[4,8,16,128]{3,2,1,0:T(8,128)S(1)}, u32[]{:S(2)}, u32[]{:S(2)}) %collective-permute-start.20) | collective-permute-done | bytes 262176 | tf_op jit(solution)/shard_map/ppermute | solution.py:80
  131.2 0.9 collective-permute-start.23
  132.1 0.7 collective-permute-done.21.refs_4_
  132.8 11.0 %collective-permute-start.24 = (f32[4,8,16,128]{3,2,1,0:T(8,128)S(1)}, f32[4,8,16,128]{3,2,1,0:T(8,128)S(1)}, u32[]{:S(2)}, u32[]{:S(2)}) collective-permute-start(f32[4,8,16,128]{3,2,1,0:T(8,128)S(1)} %get-tuple-element.62), channel_id=1, source_target_pairs={{39,0},{38,1},{33,2},{32,3},{35,4},{34,5},{37,6},{36,7},{47,8},{46... | collective-permute-start | bytes 786440 | tf_op jit(solution)/shard_map/ppermute | solution.py:80
  143.8 6.4 %local_kernel.1.local_ref = f32[4,64,16,128]{3,2,1,0:T(8,128)S(1)} custom-call(f32[4,64,16,128]{3,2,1,0:T(8,128)S(1)} %copy-done.2, f32[64,128]{1,0:T(8,128)S(1)} %fusion.ty_ref, f32[1,128]{1,0:T(1,128)S(1)} %multiply_bitcast_fusion.vy_ref), custom_call_target="tpu_custom_call" | custom-call | flops 4000000000 | bytes 4194304 | tf_op jit(solution)/shard_map/local_kernel/pallas_call | solution.py:416
  150.3 11.2 %collective-permute-done.23.refs_6_ = f32[4,8,16,128]{3,2,1,0:T(8,128)S(1)} collective-permute-done((f32[4,8,16,128]{3,2,1,0:T(8,128)S(1)}, f32[4,8,16,128]{3,2,1,0:T(8,128)S(1)}, u32[]{:S(2)}, u32[]{:S(2)}) %collective-permute-start.23) | collective-permute-done | bytes 262176 | tf_op jit(solution)/shard_map/ppermute | solution.py:80
  161.5 3.6 %collective-permute-done.24.refs_7_ = f32[4,8,16,128]{3,2,1,0:T(8,128)S(1)} collective-permute-done((f32[4,8,16,128]{3,2,1,0:T(8,128)S(1)}, f32[4,8,16,128]{3,2,1,0:T(8,128)S(1)}, u32[]{:S(2)}, u32[]{:S(2)}) %collective-permute-start.24) | collective-permute-done | bytes 262176 | tf_op jit(solution)/shard_map/ppermute | solution.py:80
  165.0 1.9 %final_kernel.1 = f32[4,64,16,128]{3,2,1,0:T(8,128)} custom-call(f32[4,64,16,128]{3,2,1,0:T(8,128)S(1)} %local_kernel.1.local_ref, f32[4,10,16,128]{3,2,1,0:T(8,128)S(1)} %collective-permute-done.17.refs_0_, f32[4,10,16,128]{3,2,1,0:T(8,128)S(1)} %collective-permute-done.18.refs_1_, f32[4,8,16,128]{3,2,1,0:T(8,128)S(1)} %collective-permute-done.19.refs_2_, ...), custom_call_target="tpu_custom_call" | custom-call | bytes 6291456 | tf_op jit(solution)/shard_map/final_kernel/pallas_call | solution.py:485
  (31 shorter events, 0.1 us)
Async XLA Ops:
  0.0 87.9 %copy-start = (f32[64,128]{1,0:T(8,128)S(1)}, f32[64,128]{1,0:T(8,128)}, u32[]{:S(2)}) copy-start(f32[64,128]{1,0:T(8,128)} %param.11) | copy-start | bytes 98308
  0.8 1.6 copy-start.1
  2.4 0.7 copy-start.3
  3.0 65.8 %copy-start.6 = (f32[128]{0:T(128)S(1)}, f32[128]{0:T(128)}, u32[]{:S(2)}) copy-start(f32[128]{0:T(128)} %param.13) | copy-start | bytes 1540
  3.0 65.8 %copy-start.7 = (s32[128]{0:T(128)S(1)}, s32[128]{0:T(128)}, u32[]{:S(2)}) copy-start(s32[128]{0:T(128)} %param.15) | copy-start | bytes 1540
  3.0 65.8 %copy-start.4 = (f32[128,128]{1,0:T(8,128)S(1)}, f32[128,128]{1,0:T(8,128)}, u32[]{:S(2)}) copy-start(f32[128,128]{1,0:T(8,128)} %constant.15.clone.refs_8_) | copy-start | bytes 196612
  3.2 14.3 %collective-permute-start.4 = (f32[33,16,128]{2,1,0:T(8,128)S(1)}, f32[33,16,128]{2,1,0:T(8,128)S(1)}, u32[]{:S(2)}, u32[]{:S(2)}) collective-permute-start(f32[33,16,128]{2,1,0:T(8,128)S(1)} %get-tuple-element.38), channel_id=1, source_target_pairs={{0,34},{1,35},{2,36},{3,37},{4,38},{5,39},{6,32},{7,33},{8,42},{9,... | collective-permute-start | bytes 811016 | tf_op jit(solution)/shard_map/ppermute | solution.py:80
  9.4 14.6 %collective-permute-start.5 = (f32[33,16,128]{2,1,0:T(8,128)S(1)}, f32[33,16,128]{2,1,0:T(8,128)S(1)}, u32[]{:S(2)}, u32[]{:S(2)}) collective-permute-start(f32[33,16,128]{2,1,0:T(8,128)S(1)} %get-tuple-element.39), channel_id=1, source_target_pairs={{0,35},{1,34},{2,37},{3,36},{4,39},{5,38},{6,33},{7,32},{8,43},{9,... | collective-permute-start | bytes 811016 | tf_op jit(solution)/shard_map/ppermute | solution.py:80
  11.1 16.3 %collective-permute-start.6 = (f32[33,16,128]{2,1,0:T(8,128)S(1)}, f32[33,16,128]{2,1,0:T(8,128)S(1)}, u32[]{:S(2)}, u32[]{:S(2)}) collective-permute-start(f32[33,16,128]{2,1,0:T(8,128)S(1)} %get-tuple-element.40), channel_id=1, source_target_pairs={{0,38},{1,39},{2,32},{3,33},{4,34},{5,35},{6,36},{7,37},{8,46},{9,... | collective-permute-start | bytes 811016 | tf_op jit(solution)/shard_map/ppermute | solution.py:80
  11.5 49.1 %collective-permute-start = (f32[34,16,128]{2,1,0:T(8,128)S(1)}, f32[34,16,128]{2,1,0:T(8,128)S(1)}, u32[]{:S(2)}, u32[]{:S(2)}) collective-permute-start(f32[34,16,128]{2,1,0:T(8,128)S(1)} %get-tuple-element.34), channel_id=1, source_target_pairs={{0,32},{1,33},{2,34},{3,35},{4,36},{5,37},{6,38},{7,39},{8,40},{9,... | collective-permute-start | bytes 835592 | tf_op jit(solution)/shard_map/ppermute | solution.py:80
  15.5 20.3 %collective-permute-start.7 = (f32[33,16,128]{2,1,0:T(8,128)S(1)}, f32[33,16,128]{2,1,0:T(8,128)S(1)}, u32[]{:S(2)}, u32[]{:S(2)}) collective-permute-start(f32[33,16,128]{2,1,0:T(8,128)S(1)} %get-tuple-element.41), channel_id=1, source_target_pairs={{0,39},{1,38},{2,33},{3,32},{4,35},{5,34},{6,37},{7,36},{8,47},{9,... | collective-permute-start | bytes 811016 | tf_op jit(solution)/shard_map/ppermute | solution.py:80
  17.5 24.2 %collective-permute-start.1 = (f32[33,16,128]{2,1,0:T(8,128)S(1)}, f32[33,16,128]{2,1,0:T(8,128)S(1)}, u32[]{:S(2)}, u32[]{:S(2)}) collective-permute-start(f32[33,16,128]{2,1,0:T(8,128)S(1)} %get-tuple-element.35), channel_id=1, source_target_pairs={{0,33},{1,32},{2,35},{3,34},{4,37},{5,36},{6,39},{7,38},{8,41},{9,... | collective-permute-start | bytes 811016 | tf_op jit(solution)/shard_map/ppermute | solution.py:80
  24.0 32.9 %collective-permute-start.2 = (f32[33,16,128]{2,1,0:T(8,128)S(1)}, f32[33,16,128]{2,1,0:T(8,128)S(1)}, u32[]{:S(2)}, u32[]{:S(2)}) collective-permute-start(f32[33,16,128]{2,1,0:T(8,128)S(1)} %get-tuple-element.36), channel_id=1, source_target_pairs={{0,36},{1,37},{2,38},{3,39},{4,32},{5,33},{6,34},{7,35},{8,44},{9,... | collective-permute-start | bytes 811016 | tf_op jit(solution)/shard_map/ppermute | solution.py:80
  27.5 33.1 %collective-permute-start.3 = (f32[33,16,128]{2,1,0:T(8,128)S(1)}, f32[33,16,128]{2,1,0:T(8,128)S(1)}, u32[]{:S(2)}, u32[]{:S(2)}) collective-permute-start(f32[33,16,128]{2,1,0:T(8,128)S(1)} %get-tuple-element.37), channel_id=1, source_target_pairs={{0,37},{1,36},{2,39},{3,38},{4,33},{5,32},{6,35},{7,34},{8,45},{9,... | collective-permute-start | bytes 811016 | tf_op jit(solution)/shard_map/ppermute | solution.py:80
  35.9 34.7 %collective-permute-start.11 = (f32[4,16,16,128]{3,2,1,0:T(8,128)S(1)}, f32[4,16,16,128]{3,2,1,0:T(8,128)S(1)}, u32[]{:S(2)}, u32[]{:S(2)}) collective-permute-start(f32[4,16,16,128]{3,2,1,0:T(8,128)S(1)} %get-tuple-element.46), channel_id=1, source_target_pairs={{40,32},{42,34},{44,36},{46,38},{47,39},{45,37},{43,35},{41,33},{4... | collective-permute-start | bytes 1572872 | tf_op jit(solution)/shard_map/ppermute | solution.py:80
  41.7 28.9 %collective-permute-start.9 = (f32[4,16,16,128]{3,2,1,0:T(8,128)S(1)}, f32[4,16,16,128]{3,2,1,0:T(8,128)S(1)}, u32[]{:S(2)}, u32[]{:S(2)}) collective-permute-start(f32[4,16,16,128]{3,2,1,0:T(8,128)S(1)} %get-tuple-element.44), channel_id=1, source_target_pairs={{32,40},{34,42},{36,44},{38,46},{39,47},{37,45},{35,43},{33,41},{4... | collective-permute-start | bytes 1572872 | tf_op jit(solution)/shard_map/ppermute | solution.py:80
  60.6 13.1 %collective-permute-start.10 = (f32[4,16,16,128]{3,2,1,0:T(8,128)S(1)}, f32[4,16,16,128]{3,2,1,0:T(8,128)S(1)}, u32[]{:S(2)}, u32[]{:S(2)}) collective-permute-start(f32[4,16,16,128]{3,2,1,0:T(8,128)S(1)} %get-tuple-element.45), channel_id=1, source_target_pairs={{40,32},{42,34},{44,36},{46,38},{47,39},{45,37},{43,35},{41,33},{4... | collective-permute-start | bytes 1572872 | tf_op jit(solution)/shard_map/ppermute | solution.py:80
  64.4 10.5 %collective-permute-start.8 = (f32[4,16,16,128]{3,2,1,0:T(8,128)S(1)}, f32[4,16,16,128]{3,2,1,0:T(8,128)S(1)}, u32[]{:S(2)}, u32[]{:S(2)}) collective-permute-start(f32[4,16,16,128]{3,2,1,0:T(8,128)S(1)} %get-tuple-element.43), channel_id=1, source_target_pairs={{32,40},{34,42},{36,44},{38,46},{39,47},{37,45},{35,43},{33,41},{4... | collective-permute-start | bytes 1572872 | tf_op jit(solution)/shard_map/ppermute | solution.py:80
  74.9 13.0 %copy-start.5 = (f32[128,128]{1,0:T(8,128)S(1)}, f32[128,128]{1,0:T(8,128)}, u32[]{:S(2)}) copy-start(f32[128,128]{1,0:T(8,128)} %constant.14.clone) | copy-start | bytes 196612
  75.4 28.1 %collective-permute-start.12 = (f32[2,8,128,128]{3,2,1,0:T(8,128)S(1)}, f32[2,8,128,128]{3,2,1,0:T(8,128)S(1)}, u32[]{:S(2)}, u32[]{:S(2)}) collective-permute-start(f32[2,8,128,128]{3,2,1,0:T(8,128)S(1)} %get-tuple-element.49.u_tail_ref), channel_id=1, source_target_pairs={{32,40},{34,42},{36,44},{38,46},{39,47},{37,45},{35,43},{33,41},{4... | collective-permute-start | bytes 3145736 | tf_op jit(solution)/shard_map/ppermute | solution.py:80
  81.0 22.5 %collective-permute-start.13 = (f32[2,8,128,128]{3,2,1,0:T(8,128)S(1)}, f32[2,8,128,128]{3,2,1,0:T(8,128)S(1)}, u32[]{:S(2)}, u32[]{:S(2)}) collective-permute-start(f32[2,8,128,128]{3,2,1,0:T(8,128)S(1)} %get-tuple-element.48.u_head_ref), channel_id=1, source_target_pairs={{40,32},{42,34},{44,36},{46,38},{47,39},{45,37},{43,35},{41,33},{4... | collective-permute-start | bytes 3145736 | tf_op jit(solution)/shard_map/ppermute | solution.py:80
  82.9 19.0 %collective-permute-start.14 = (f32[4,2,160,128]{3,2,1,0:T(8,128)S(1)}, f32[4,2,160,128]{3,2,1,0:T(8,128)S(1)}, u32[]{:S(2)}, u32[]{:S(2)}) collective-permute-start(f32[4,2,160,128]{3,2,1,0:T(8,128)S(1)} %get-tuple-element.51), channel_id=1, source_target_pairs={{32,34},{34,36},{36,38},{39,37},{37,35},{35,33},{40,42},{42,44},{4... | collective-permute-start | bytes 1966088 | tf_op jit(solution)/shard_map/ppermute | solution.py:80
  84.9 18.7 %collective-permute-start.15 = (f32[4,2,160,128]{3,2,1,0:T(8,128)S(1)}, f32[4,2,160,128]{3,2,1,0:T(8,128)S(1)}, u32[]{:S(2)}, u32[]{:S(2)}) collective-permute-start(f32[4,2,160,128]{3,2,1,0:T(8,128)S(1)} %get-tuple-element.52), channel_id=1, source_target_pairs={{34,32},{36,34},{38,36},{37,39},{35,37},{33,35},{42,40},{44,42},{4... | collective-permute-start | bytes 1966088 | tf_op jit(solution)/shard_map/ppermute | solution.py:80
  88.1 13.8 %collective-permute-start.16 = (f32[4,2,32,128]{3,2,1,0:T(8,128)S(1)}, f32[4,2,32,128]{3,2,1,0:T(8,128)S(1)}, u32[]{:S(2)}, u32[]{:S(2)}) collective-permute-start(f32[4,2,32,128]{3,2,1,0:T(8,128)S(1)} %get-tuple-element.53), channel_id=1, source_target_pairs={{38,34},{39,35},{46,42},{47,43},{54,50},{55,51},{62,58},{63,59},{7... | collective-permute-start | bytes 393224 | tf_op jit(solution)/shard_map/ppermute | solution.py:80
  103.5 40.3 %copy-start.2 = (f32[4,64,16,128]{3,2,1,0:T(8,128)S(1)}, f32[4,64,16,128]{3,2,1,0:T(8,128)}, u32[]{:S(2)}) copy-start(f32[4,64,16,128]{3,2,1,0:T(8,128)} %g_ref.3) | copy-start | bytes 6291460
  104.0 22.8 %collective-permute-start.19 = (f32[4,8,16,128]{3,2,1,0:T(8,128)S(1)}, f32[4,8,16,128]{3,2,1,0:T(8,128)S(1)}, u32[]{:S(2)}, u32[]{:S(2)}) collective-permute-start(f32[4,8,16,128]{3,2,1,0:T(8,128)S(1)} %get-tuple-element.57), channel_id=1, source_target_pairs={{36,0},{37,1},{38,2},{39,3},{32,4},{33,5},{34,6},{35,7},{44,8},{45... | collective-permute-start | bytes 786440 | tf_op jit(solution)/shard_map/ppermute | solution.py:80
  108.3 22.9 %collective-permute-start.20 = (f32[4,8,16,128]{3,2,1,0:T(8,128)S(1)}, f32[4,8,16,128]{3,2,1,0:T(8,128)S(1)}, u32[]{:S(2)}, u32[]{:S(2)}) collective-permute-start(f32[4,8,16,128]{3,2,1,0:T(8,128)S(1)} %get-tuple-element.58), channel_id=1, source_target_pairs={{37,0},{36,1},{39,2},{38,3},{33,4},{32,5},{35,6},{34,7},{45,8},{44... | collective-permute-start | bytes 786440 | tf_op jit(solution)/shard_map/ppermute | solution.py:80
  110.4 22.4 %collective-permute-start.21 = (f32[4,8,16,128]{3,2,1,0:T(8,128)S(1)}, f32[4,8,16,128]{3,2,1,0:T(8,128)S(1)}, u32[]{:S(2)}, u32[]{:S(2)}) collective-permute-start(f32[4,8,16,128]{3,2,1,0:T(8,128)S(1)} %get-tuple-element.59), channel_id=1, source_target_pairs={{34,0},{35,1},{36,2},{37,3},{38,4},{39,5},{32,6},{33,7},{42,8},{43... | collective-permute-start | bytes 786440 | tf_op jit(solution)/shard_map/ppermute | solution.py:80
  110.4 54.6 %collective-permute-start.17 = (f32[4,10,16,128]{3,2,1,0:T(8,128)S(1)}, f32[4,10,16,128]{3,2,1,0:T(8,128)S(1)}, u32[]{:S(2)}, u32[]{:S(2)}) collective-permute-start(f32[4,10,16,128]{3,2,1,0:T(8,128)S(1)} %get-tuple-element.55), channel_id=1, source_target_pairs={{32,0},{33,1},{34,2},{35,3},{36,4},{37,5},{38,6},{39,7},{40,8},{41... | collective-permute-start | bytes 983048 | tf_op jit(solution)/shard_map/ppermute | solution.py:80
  113.9 51.2 %collective-permute-start.18 = (f32[4,10,16,128]{3,2,1,0:T(8,128)S(1)}, f32[4,10,16,128]{3,2,1,0:T(8,128)S(1)}, u32[]{:S(2)}, u32[]{:S(2)}) collective-permute-start(f32[4,10,16,128]{3,2,1,0:T(8,128)S(1)} %get-tuple-element.56), channel_id=1, source_target_pairs={{33,0},{32,1},{35,2},{34,3},{37,4},{36,5},{39,6},{38,7},{41,8},{40... | collective-permute-start | bytes 983048 | tf_op jit(solution)/shard_map/ppermute | solution.py:80
  126.8 23.5 %collective-permute-start.22 = (f32[4,8,16,128]{3,2,1,0:T(8,128)S(1)}, f32[4,8,16,128]{3,2,1,0:T(8,128)S(1)}, u32[]{:S(2)}, u32[]{:S(2)}) collective-permute-start(f32[4,8,16,128]{3,2,1,0:T(8,128)S(1)} %get-tuple-element.60), channel_id=1, source_target_pairs={{35,0},{34,1},{37,2},{36,3},{39,4},{38,5},{33,6},{32,7},{43,8},{42... | collective-permute-start | bytes 786440 | tf_op jit(solution)/shard_map/ppermute | solution.py:80
  131.2 30.3 %collective-permute-start.23 = (f32[4,8,16,128]{3,2,1,0:T(8,128)S(1)}, f32[4,8,16,128]{3,2,1,0:T(8,128)S(1)}, u32[]{:S(2)}, u32[]{:S(2)}) collective-permute-start(f32[4,8,16,128]{3,2,1,0:T(8,128)S(1)} %get-tuple-element.61), channel_id=1, source_target_pairs={{38,0},{39,1},{32,2},{33,3},{34,4},{35,5},{36,6},{37,7},{46,8},{47... | collective-permute-start | bytes 786440 | tf_op jit(solution)/shard_map/ppermute | solution.py:80
  132.8 32.2 %collective-permute-start.24 = (f32[4,8,16,128]{3,2,1,0:T(8,128)S(1)}, f32[4,8,16,128]{3,2,1,0:T(8,128)S(1)}, u32[]{:S(2)}, u32[]{:S(2)}) collective-permute-start(f32[4,8,16,128]{3,2,1,0:T(8,128)S(1)} %get-tuple-element.62), channel_id=1, source_target_pairs={{39,0},{38,1},{33,2},{32,3},{35,4},{34,5},{37,6},{36,7},{47,8},{46... | collective-permute-start | bytes 786440 | tf_op jit(solution)/shard_map/ppermute | solution.py:80

commit v3 on v2

v3 whole, which is shorter than its diff:
```python
import functools
import math

import jax
import jax.numpy as jnp
import numpy as np
from jax import lax
from jax.experimental import pallas as pl
from jax.experimental.pallas import tpu as pltpu
from jax.sharding import PartitionSpec as P


F32 = jnp.float32
BF16 = jnp.bfloat16
K = 128
AXES = ("gx", "ka")
SLOTS = [(dy, ds) for dy in (3, 0, 1, 2) for ds in (0, 1)]
GROUPS = (range(0, 2), range(2, 8))
FIRST = SLOTS.index((0, 0))
VMEM = pl.BlockSpec(memory_space=pltpu.VMEM)


def flat(x, y, z, core):
    return ((x * 4 + z % 4) * 2 + core) * 8 + y * 2 + z // 4


def place(block, part):
    x, low, core = block // 8, block // 2 % 4, block % 2
    half = part // 4
    y = part if half == 0 else 7 - part
    z = (low + 2 if x % 2 == 0 else 5 - low) + 4 * half
    return flat(x, y, z % 8, core)


def part_of(y, half):
    return y if half == 0 else 7 - y


def slot_part(ka, slot):
    dy, ds = SLOTS[slot]
    return part_of((ka // 2 + dy) % 4, (ka % 2) ^ ds)


def exchange_pairs(slot):
    return [
        (block * 8 + ka, place(block, slot_part(ka, slot)))
        for block in range(32)
        for ka in range(8)
    ]


def x_pairs(step):
    return [
        (place(block, part), place((block + step) % 32, part))
        for block in range(32)
        for part in range(8)
    ]


def y_pairs(step):
    return [
        (place(block, 4 * half + part), place(block, 4 * half + (part + step) % 4))
        for block in range(32)
        for half in range(2)
        for part in range(4)
    ]


def send(value, pairs):
    return lax.ppermute(value, AXES, pairs)


def as_source():
    ka = lax.axis_index("ka")
    return ka >> 1, ka & 1


def as_host():
    gx, ka = lax.axis_index("gx"), lax.axis_index("ka")
    z = (ka & 1) * 4 + ((gx >> 1) & 3)
    turn = jnp.where(((gx >> 3) & 1) == 0, z - 2, 5 - z) & 7
    return ka >> 1, turn >> 2, (gx & 25) + (turn & 3) * 2


def part_index(y, half):
    return y + half * (7 - 2 * y)


def rows_to(slot):
    y, half = as_source()
    dy, ds = SLOTS[slot]
    return pl.ds(pl.multiple_of(part_index((y + dy) & 3, half ^ ds) * 8, 8), 8)


def kx_of(slot):
    y, half, block = as_host()
    dy, ds = SLOTS[slot]
    return pl.ds(pl.multiple_of((((y - dy) & 3) * 2 + (half ^ ds)) * 16, 16), 16)


def halves(value):
    high = value.astype(BF16)
    return high, (value - high.astype(F32)).astype(BF16)


def circulant(row):
    return pltpu.roll(jnp.broadcast_to(row, (K, K)), 0, 1, stride=1, stride_axis=0)


def right_table(row):
    high, low = halves(circulant(row))
    return jnp.concatenate(
        [
            jnp.concatenate([high, low], 1),
            jnp.concatenate([high, jnp.zeros_like(low)], 1),
        ],
        0,
    )


def left_table(row):
    high, low = halves(circulant(row))
    return jnp.concatenate(
        [
            jnp.concatenate([high, high], 1),
            jnp.concatenate([low, jnp.zeros_like(low)], 1),
        ],
        0,
    )


def times_right(rows, table):
    both = jnp.dot(jnp.concatenate(halves(rows), 1), table, preferred_element_type=F32)
    return both[:, :K] + both[:, K:]


def times_left(table, first, second):
    high_0, low_0 = halves(first)
    high_1, low_1 = halves(second)
    stacked = jnp.concatenate(
        [jnp.concatenate([high_0, high_1], 1), jnp.concatenate([low_0, low_1], 1)], 0
    )
    both = jnp.dot(table, stacked, preferred_element_type=F32)
    both = both[:K] + both[K:]
    return both[:, :K], both[:, K:]


def slope(center, one, two):
    return 3.0 * center - 4.0 * one + two


def local_kernel(g_ref, ty_ref, vy_ref, out_ref, pad):
    vy = vy_ref[...].reshape(1, 1, K)
    toward = jnp.broadcast_to(vy > 0, (4, 16, K))
    rate = jnp.abs(vy) * 0.125

    def step(value, one_low, two_low, one_high, two_high, table):
        one = jnp.where(toward, one_low, one_high)
        two = jnp.where(toward, two_low, two_high)
        wigner = times_right(value.reshape(64, K), table).reshape(4, 16, K)
        return wigner - rate * slope(value, one, two)

    edge = jnp.zeros((4, 2, 16, K), F32)
    pad[0, :, 0:2] = edge
    pad[0, :, 66:68] = edge
    pad[1, :, 0:2] = edge
    pad[1, :, 66:68] = edge
    for y in range(64):
        pad[0, :, y + 2] = g_ref[:, y]

    def turn(source, into):
        @pl.loop(0, 8)
        def _(group):
            block = ty_ref[pl.ds(pl.multiple_of(group * 8, 8), 8), :]
            for inner in range(8):
                y = group * 8 + inner
                value = pad[source, :, y + 2]
                moved = step(
                    value,
                    pad[source, :, y + 1],
                    pad[source, :, y],
                    pad[source, :, y + 3],
                    pad[source, :, y + 4],
                    right_table(block[inner : inner + 1]),
                )
                into(y, value, moved)

    def first(y, value, moved):
        pad[1, :, y + 2] = value + moved

    def second(y, value, moved):
        out_ref[:, y] = 0.5 * (pad[0, :, y + 2] + value + moved)

    turn(0, first)
    turn(1, second)


def pack_kernel(g_ref, vel_ref, potential_ref, *pieces):
    y, half = as_source()
    for slot in range(8):
        at = rows_to(slot)
        for x in range(4):
            pieces[slot][8 * x : 8 * x + 8] = g_ref[x, at]
        pieces[slot][32] = vel_ref[...]
        dy, ds = SLOTS[slot]
        if dy == 0:
            at = pl.ds(32 - 2 * (half ^ ds), 2)
            for x in range(4):
                pieces[slot][33 + 2 * x : 35 + 2 * x] = g_ref[x, at]
    pieces[FIRST][41, 0:4] = potential_ref[...]
    pieces[FIRST][41, 4:16] = jnp.zeros((12, K), F32)


def cut_kernel(slots, *refs):
    pieces, outs = refs[: len(slots)], refs[len(slots) :]
    head_ref, tail_ref, y_low_ref, y_high_ref = outs[:4]
    for i, slot in enumerate(slots):
        head_ref[i] = pieces[i][0:16]
        tail_ref[i] = pieces[i][16:32]
        for x in range(4):
            y_low_ref[i, 2 * x : 2 * x + 2] = pieces[i][8 * x : 8 * x + 2]
            y_high_ref[i, 2 * x : 2 * x + 2] = pieces[i][8 * x + 6 : 8 * x + 8]
        dy, ds = SLOTS[slot]
        if dy == 0:
            rows = pieces[i][33:41]
            y_low_ref[len(slots) + ds] = rows
            y_high_ref[len(slots) + ds] = rows
            outs[4][ds] = rows


def inner_drift(center, x, layer, toward, rate):
    total = 3.0 * center
    for step, factor in ((1, -4.0), (2, 1.0)):
        low = layer(x - step) if x - step >= 0 else None
        high = layer(x + step) if x + step <= 3 else None
        if low is None:
            if high is not None:
                total += factor * jnp.where(toward, 0.0, high)
        elif high is None:
            total += factor * jnp.where(toward, low, 0.0)
        else:
            total += factor * jnp.where(toward, low, high)
    return -rate * total


def outer_drift(x, low, high, up, down):
    if x == 0:
        return up * (4.0 * low(0) - low(1))
    if x == 1:
        return -up * low(0)
    if x == 2:
        return -down * high(0)
    return down * (4.0 * high(0) - high(1))


def rates(vx_ref, at, factor):
    vx = vx_ref[at, :]
    block = as_host()[2]
    up = jnp.where(block == 0, 0.0, jnp.maximum(vx, 0.0) * factor)
    down = jnp.where(block == 31, 0.0, jnp.maximum(-vx, 0.0) * factor)
    return up[None], down[None]


def first_kernel(*refs):
    pieces, (sine_ref, ty_ref, vy_ref), (v_ref, vx_ref, tx_ref), (field, tables) = refs[:8], refs[8:11], refs[11:14], refs[14:]
    for slot in range(8):
        at = kx_of(slot)
        for x in range(4):
            field[x, :, at, :] = pieces[slot][8 * x : 8 * x + 8]
        vx_ref[at, :] = pieces[slot][32]
    tx_ref[...] = 0.25 * jnp.dot(
        pieces[FIRST][41, 0:8], sine_ref[...], precision=lax.Precision.HIGHEST, preferred_element_type=F32
    )
    for x in range(4):
        tables[x] = left_table(0.5 * tx_ref[x : x + 1, :])
    y_place, half, block = as_host()
    ty = ty_ref[pl.ds(pl.multiple_of(part_index(y_place, half) * 8, 8), 8), :]

    vx = vx_ref[...]
    toward = vx > 0
    rate = jnp.abs(vx) * 0.0625
    vy = jnp.broadcast_to(vy_ref[...], (K, K))
    toward_y = vy > 0
    rate_y = jnp.abs(vy) * 0.125
    zero = jnp.zeros((K, K), F32)
    for pair in range(4):
        right = [right_table(ty[pair * 2 + i : pair * 2 + i + 1, :]) for i in range(2)]
        for x in range(4):
            mine = [field[x, pair * 2 + i] for i in range(2)]
            wigner = times_left(tables[x], mine[0], mine[1])
            for i in range(2):
                y = pair * 2 + i
                total = mine[i] + wigner[i]
                total += inner_drift(mine[i], x, lambda at: field[at, y], toward, rate)
                total += times_right(mine[i], right[i])
                near = [field[x, at] if 0 <= at < 8 else zero for at in (y - 2, y - 1, y + 1, y + 2)]
                one = jnp.where(toward_y, near[1], near[2])
                two = jnp.where(toward_y, near[0], near[3])
                v_ref[x, y] = total - rate_y * slope(mine[i], one, two)


def first_edge_kernel(
    inner_ref, low_a_ref, low_b_ref, high_a_ref, high_b_ref, under_a_ref, under_b_ref, over_a_ref, over_b_ref,
    ring_ref, own_0_ref, own_1_ref, vx_ref, vy_ref, v_ref, *outs,
):
    y_place, half, block = as_host()
    middle = jnp.where(y_place == 3, 1.0, 0.0)
    under_middle, over_middle = y_place == 3 * half, y_place == 3 - 3 * half
    vy = vy_ref[...].reshape(1, 1, K)
    up_y = jnp.maximum(vy, 0.0) * 0.125
    down_y = jnp.maximum(-vy, 0.0) * 0.125
    by_group = ((low_a_ref, high_a_ref, under_a_ref, over_a_ref), (low_b_ref, high_b_ref, under_b_ref, over_b_ref))

    def beside(side, pair, rows):
        slot = SLOTS.index(pair)
        group = int(slot in GROUPS[1])
        return by_group[group][side][slot - GROUPS[group].start, rows]

    for slot in range(8):
        dy, ds = SLOTS[slot]
        at = kx_of(slot)
        group = int(slot in GROUPS[1])
        low_ref, high_ref = by_group[group][:2]
        up, down = rates(vx_ref, at, 0.0625)
        i = slot - GROUPS[group].start
        for x in range(4):
            rows = slice(2 * x, 2 * x + 2)
            if dy == 0:
                across = (own_0_ref, own_1_ref)[ds][33 + 2 * x : 35 + 2 * x]
            elif dy == 2:
                across = ring_ref[ds, rows]
            else:
                across = jnp.where(half == dy // 3, under_b_ref[6 + ds, rows], over_b_ref[6 + ds, rows])
            before, after = ((dy + 3) % 4, ds), ((dy + 1) % 4, ds)
            under = jnp.where(half == 0, beside(2, before, rows), beside(2, after, rows))
            over = jnp.where(half == 0, beside(3, after, rows), beside(3, before, rows))
            under = jnp.where(under_middle, across * middle, under)
            over = jnp.where(over_middle, across * middle, over)
            value = inner_ref[x, :, at, :] + outer_drift(
                x,
                lambda n: low_ref[i, 8 - 8 * n : 16 - 8 * n],
                lambda n: high_ref[i, 8 * n : 8 * n + 8],
                up,
                down,
            )
            bottom = jnp.concatenate([up_y * (4.0 * under[1:2] - under[0:1]), -up_y * under[1:2]], 0)
            top = jnp.concatenate([-down_y * over[0:1], down_y * (4.0 * over[0:1] - over[1:2])], 0)
            value = jnp.concatenate([value[0:2] + bottom, value[2:6], value[6:8] + top], 0)
            v_ref[x, :, at, :] = value
            side = outs[2 * (slot // 4) + x // 2]
            side[slot % 4, 8 * (x % 2) : 8 * (x % 2) + 8] = value


def second_kernel(v_ref, tx_ref, vx_ref, out_ref, tables):
    for x in range(4):
        tables[x] = left_table(tx_ref[x : x + 1, :])

    @pl.loop(0, 4)
    def _(pair):
        vx = vx_ref[...]
        toward = vx > 0
        rate = jnp.abs(vx) * 0.125
        for x in range(4):
            mine = [v_ref[x, pair * 2 + i] for i in range(2)]
            wigner = times_left(tables[x], mine[0], mine[1])
            for i in range(2):
                y = pair * 2 + i
                out_ref[x, y] = wigner[i] + inner_drift(mine[i], x, lambda at: v_ref[at, y], toward, rate)


def second_edge_kernel(slots, inner_ref, low_ref, high_ref, vx_ref, *pieces):
    for i, slot in enumerate(slots):
        at = kx_of(slot)
        up, down = rates(vx_ref, at, 0.125)
        for x in range(4):
            pieces[i][x] = inner_ref[x, :, at, :] + outer_drift(
                x,
                lambda n: low_ref[i, 8 - 8 * n : 16 - 8 * n],
                lambda n: high_ref[i, 8 * n : 8 * n + 8],
                up,
                down,
            )


def final_kernel(local_ref, *refs):
    pieces, out_ref = refs[:8], refs[8]
    for slot in range(8):
        at = rows_to(slot)
        out_ref[:, at] = local_ref[:, at] + pieces[slot][...]


MIB = 1 << 20


def array(*shape):
    return jax.ShapeDtypeStruct(shape, F32)


def params():
    return pltpu.CompilerParams(vmem_limit_bytes=40 * MIB)


def cost(flops, mib):
    return pl.CostEstimate(flops=flops, bytes_accessed=mib * MIB, transcendentals=0)


def call(kernel, outs, scratch=(), flops=0, mib=4):
    def run(*operands):
        return pl.pallas_call(
            kernel,
            out_shape=outs,
            in_specs=[VMEM] * len(operands),
            out_specs=[VMEM] * len(outs) if isinstance(outs, list) else VMEM,
            scratch_shapes=list(scratch),
            compiler_params=params(),
            cost_estimate=cost(flops, mib),
            name=(kernel.func if isinstance(kernel, functools.partial) else kernel).__name__,
        )(*operands)

    return run


def sine_table(sign):
    index = np.arange(K)
    angle = (sign * index[:, None] * index[None, :] % K) * (2.0 * math.pi / K)
    return (np.sin(angle) / K).astype(np.float32)


def back(pairs):
    return [(there, here) for here, there in pairs]


def per_device(density, potential_x, potential_y, speeds_x, speeds_y, upwind_x, upwind_y):
    vel_x = (2 * upwind_x - 1).astype(F32) * speeds_x
    vel_x = jnp.broadcast_to(vel_x[:, None], (16, K))
    vy = ((2 * upwind_y - 1).astype(F32) * speeds_y).reshape(1, K)

    sizes = [33 + 8 * (dy == 0) + (slot == FIRST) for slot, (dy, ds) in enumerate(SLOTS)]
    pieces = call(pack_kernel, [array(size, 16, K) for size in sizes])(density, vel_x, potential_x)
    pieces = [send(piece, exchange_pairs(slot)) for slot, piece in enumerate(pieces)]

    highest = lax.Precision.HIGHEST
    ty = 0.25 * jnp.dot(potential_y, jnp.asarray(sine_table(1)), precision=highest)
    local = call(
        local_kernel, array(4, 64, 16, K), [pltpu.VMEM((2, 4, 68, 16, K), F32)], 4 * 10**9
    )(density, ty, vy)

    low, high, under, over = [None] * 2, [None] * 2, [None] * 2, [None] * 2
    for group in (1, 0):
        slots = GROUPS[group]
        middle = FIRST in slots
        rows = array(len(slots) + 2 * middle, 8, 16, K)
        head, tail, y_low, y_high, *ring = call(
            functools.partial(cut_kernel, slots),
            [array(len(slots), 16, 16, K)] * 2 + [rows] * 2 + [array(2, 8, 16, K)] * middle,
            mib=2,
        )(*pieces[slots.start : slots.stop])
        low[group] = send(tail, x_pairs(1))
        high[group] = send(head, x_pairs(-1))
        under[group] = send(y_high, y_pairs(1))
        over[group] = send(y_low, y_pairs(-1))
        if middle:
            across = send(ring[0], y_pairs(2))
            pieces[0], low[1], high[1], under[1], over[1], across = lax.optimization_barrier(
                (pieces[0], low[1], high[1], under[1], over[1], across)
            )
    left_tables = pltpu.VMEM((4, 2 * K, 2 * K), BF16)
    inner, vx, tx = call(
        first_kernel,
        [array(4, 8, K, K), array(K, K), array(8, K)],
        [pltpu.VMEM((4, 8, K, K), F32), left_tables],
        3 * 10**9,
    )(*pieces, jnp.asarray(sine_table(-1)), ty, vy)
    v, *sides = call(first_edge_kernel, [array(4, 8, K, K)] + [array(4, 16, 16, K)] * 4)(
        inner, *low, *high, *under, *over, across, pieces[FIRST], pieces[FIRST + 1], vx, vy
    )
    low = [send(sides[2 * group + 1], x_pairs(1)) for group in range(2)]
    high = [send(sides[2 * group], x_pairs(-1)) for group in range(2)]
    inner = call(second_kernel, array(4, 8, K, K), [left_tables], 2 * 10**9)(v, tx, vx)
    pieces = []
    for group, slots in enumerate((range(0, 4), range(4, 8))):
        cut = call(functools.partial(second_edge_kernel, slots), [array(4, 8, 16, K)] * 4, mib=2)(
            inner, low[group], high[group], vx
        )
        pieces += [send(piece, back(exchange_pairs(slot))) for slot, piece in zip(slots, cut)]

    def by_x(*shape):
        return pl.BlockSpec((1, *shape), lambda x: (x, 0, 0, 0))

    return pl.pallas_call(
        final_kernel,
        grid=(4,),
        out_shape=array(4, 64, 16, K),
        in_specs=[by_x(64, 16, K)] + [by_x(8, 16, K)] * 8,
        out_specs=by_x(64, 16, K),
        compiler_params=params(),
        cost_estimate=cost(0, 6),
        name="final_kernel",
    )(local, *pieces)


def solution(mesh):
    in_specs = (P("gx", None, "ka", None), P("gx", None), P(), P("ka"), P(), P("ka"), P())
    out_specs = P("gx", None, "ka", None)
    return jax.shard_map(
        per_device, mesh=mesh, in_specs=in_specs, out_specs=out_specs, check_vma=False
    )
```

time: 167 us -> 166 us (level)
  the two profiles are of different devices: /device:TPU:31 before, /device:TPU:39 now
where the time goes in v3:
time: 166 us
  starting transfers between devices  97.2 us (59%)
  waiting for transfers between devices  51.5 us (31%)
  Pallas kernels  13.3 us (8%)
  local copies, waits for them, and re-layouts  2.37 us (1%)
    ppermute x29, starting transfers between devices, send(): return lax.ppermute(value, AXES, pairs)  97.2 us
    ppermute x29, waiting for transfers between devices, send(): return lax.ppermute(value, AXES, pairs)  51.5 us
    pallas_call x9, Pallas kernels, run(): pl.pallas_call(kernel, out_shape=outs, in_specs=[VMEM] * len(operands), o...  11.4 us
  transfers between devices with their start and end apart: 29, of which 12 were waited for; matrix products, arithmetic and copies ran while one was open for 0% of the time, Pallas kernels for 6%

profile of v3, /device:TPU:39, one launch (start us, length us, event | category | flops | bytes accessed | tf_op | source)
XLA Modules:
  0.0 165.5 jit_solution(17407497355985323273)
XLA Ops:
  0.0 0.7 convert_multiply_fusion
  0.8 1.6 copy-done.1
  2.4 0.7 copy-done.3
  3.1 0.2 pack_kernel.1
  3.2 6.6 %collective-permute-start.3 = (f32[33,16,128]{2,1,0:T(8,128)S(1)}, f32[33,16,128]{2,1,0:T(8,128)S(1)}, u32[]{:S(2)}, u32[]{:S(2)}) collective-permute-start(f32[33,16,128]{2,1,0:T(8,128)S(1)} %get-tuple-element.47), channel_id=1, source_target_pairs={{0,34},{1,35},{2,36},{3,37},{4,38},{5,39},{6,32},{7,33},{8,42},{9,... | collective-permute-start | bytes 811016 | tf_op jit(solution)/shard_map/ppermute | solution.py:70
  9.9 0.7 collective-permute-start.2
  10.6 1.7 %collective-permute-start.4 = (f32[33,16,128]{2,1,0:T(8,128)S(1)}, f32[33,16,128]{2,1,0:T(8,128)S(1)}, u32[]{:S(2)}, u32[]{:S(2)}) collective-permute-start(f32[33,16,128]{2,1,0:T(8,128)S(1)} %get-tuple-element.48), channel_id=1, source_target_pairs={{0,35},{1,34},{2,37},{3,36},{4,39},{5,38},{6,33},{7,32},{8,43},{9,... | collective-permute-start | bytes 811016 | tf_op jit(solution)/shard_map/ppermute | solution.py:70
  12.4 5.5 %collective-permute-start.5 = (f32[33,16,128]{2,1,0:T(8,128)S(1)}, f32[33,16,128]{2,1,0:T(8,128)S(1)}, u32[]{:S(2)}, u32[]{:S(2)}) collective-permute-start(f32[33,16,128]{2,1,0:T(8,128)S(1)} %get-tuple-element.49), channel_id=1, source_target_pairs={{0,36},{1,37},{2,38},{3,39},{4,32},{5,33},{6,34},{7,35},{8,44},{9,... | collective-permute-start | bytes 811016 | tf_op jit(solution)/shard_map/ppermute | solution.py:70
  17.8 1.4 collective-permute-done.3.refs_2_.refs_4_
  19.2 0.8 collective-permute-start.6
  20.0 10.8 %collective-permute-done.4.refs_3_.refs_5_ = f32[33,16,128]{2,1,0:T(8,128)S(1)} collective-permute-done((f32[33,16,128]{2,1,0:T(8,128)S(1)}, f32[33,16,128]{2,1,0:T(8,128)S(1)}, u32[]{:S(2)}, u32[]{:S(2)}) %collective-permute-start.4) | collective-permute-done | bytes 270368 | tf_op jit(solution)/shard_map/ppermute | solution.py:70
  30.8 6.7 %collective-permute-start = (f32[33,16,128]{2,1,0:T(8,128)S(1)}, f32[33,16,128]{2,1,0:T(8,128)S(1)}, u32[]{:S(2)}, u32[]{:S(2)}) collective-permute-start(f32[33,16,128]{2,1,0:T(8,128)S(1)} %get-tuple-element.44), channel_id=1, source_target_pairs={{0,38},{1,39},{2,32},{3,33},{4,34},{5,35},{6,36},{7,37},{8,46},{9,... | collective-permute-start | bytes 811016 | tf_op jit(solution)/shard_map/ppermute | solution.py:70
  37.5 2.2 %collective-permute-done.5.refs_4_.refs_6_ = f32[33,16,128]{2,1,0:T(8,128)S(1)} collective-permute-done((f32[33,16,128]{2,1,0:T(8,128)S(1)}, f32[33,16,128]{2,1,0:T(8,128)S(1)}, u32[]{:S(2)}, u32[]{:S(2)}) %collective-permute-start.5) | collective-permute-done | bytes 270368 | tf_op jit(solution)/shard_map/ppermute | solution.py:70
  39.8 4.8 %collective-permute-done.6.refs_5_.refs_7_ = f32[33,16,128]{2,1,0:T(8,128)S(1)} collective-permute-done((f32[33,16,128]{2,1,0:T(8,128)S(1)}, f32[33,16,128]{2,1,0:T(8,128)S(1)}, u32[]{:S(2)}, u32[]{:S(2)}) %collective-permute-start.6) | collective-permute-done | bytes 270368 | tf_op jit(solution)/shard_map/ppermute | solution.py:70
  44.5 0.2 cut_kernel.2
  44.7 3.1 %collective-permute-start.7 = (f32[6,16,16,128]{3,2,1,0:T(8,128)S(1)}, f32[6,16,16,128]{3,2,1,0:T(8,128)S(1)}, u32[]{:S(2)}, u32[]{:S(2)}) collective-permute-start(f32[6,16,16,128]{3,2,1,0:T(8,128)S(1)} %get-tuple-element.51), channel_id=1, source_target_pairs={{32,40},{34,42},{36,44},{38,46},{39,47},{37,45},{35,43},{33,41},{4... | collective-permute-start | bytes 2359304 | tf_op jit(solution)/shard_map/ppermute | solution.py:70
  47.9 4.0 %collective-permute-start.8 = (f32[6,16,16,128]{3,2,1,0:T(8,128)S(1)}, f32[6,16,16,128]{3,2,1,0:T(8,128)S(1)}, u32[]{:S(2)}, u32[]{:S(2)}) collective-permute-start(f32[6,16,16,128]{3,2,1,0:T(8,128)S(1)} %get-tuple-element.52), channel_id=1, source_target_pairs={{32,232},{34,234},{36,236},{38,238},{39,239},{37,237},{35,235},{33... | collective-permute-start | bytes 2359304 | tf_op jit(solution)/shard_map/ppermute | solution.py:70
  51.9 3.5 %collective-permute-start.10 = (f32[8,8,16,128]{3,2,1,0:T(8,128)S(1)}, f32[8,8,16,128]{3,2,1,0:T(8,128)S(1)}, u32[]{:S(2)}, u32[]{:S(2)}) collective-permute-start(f32[8,8,16,128]{3,2,1,0:T(8,128)S(1)} %get-tuple-element.54), channel_id=1, source_target_pairs={{32,38},{34,32},{36,34},{38,36},{39,33},{37,39},{35,37},{33,35},{4... | collective-permute-start | bytes 1572872 | tf_op jit(solution)/shard_map/ppermute | solution.py:70
  55.4 0.4 collective-permute-start.9
  55.8 1.5 collective-permute-done.11.ring_ref
  57.3 12.2 %collective-permute-start.12 = (f32[33,16,128]{2,1,0:T(8,128)S(1)}, f32[33,16,128]{2,1,0:T(8,128)S(1)}, u32[]{:S(2)}, u32[]{:S(2)}) collective-permute-start(f32[33,16,128]{2,1,0:T(8,128)S(1)} %get-tuple-element.57), channel_id=1, source_target_pairs={{0,39},{1,38},{2,33},{3,32},{4,35},{5,34},{6,37},{7,36},{8,47},{9,... | collective-permute-start | bytes 811016 | tf_op jit(solution)/shard_map/ppermute | solution.py:70
  69.5 0.2 fusion.ty_ref.refs_9_
  69.7 8.6 %collective-permute-done.12.refs_1_ = f32[33,16,128]{2,1,0:T(8,128)S(1)} collective-permute-done((f32[33,16,128]{2,1,0:T(8,128)S(1)}, f32[33,16,128]{2,1,0:T(8,128)S(1)}, u32[]{:S(2)}, u32[]{:S(2)}) %collective-permute-start.12) | collective-permute-done | bytes 270368 | tf_op jit(solution)/shard_map/ppermute | solution.py:70
  78.4 5.2 %collective-permute-start.13 = (f32[2,16,16,128]{3,2,1,0:T(8,128)S(1)}, f32[2,16,16,128]{3,2,1,0:T(8,128)S(1)}, u32[]{:S(2)}, u32[]{:S(2)}) collective-permute-start(f32[2,16,16,128]{3,2,1,0:T(8,128)S(1)} %get-tuple-element.59), channel_id=1, source_target_pairs={{32,40},{34,42},{36,44},{38,46},{39,47},{37,45},{35,43},{33,41},{4... | collective-permute-start | bytes 786440 | tf_op jit(solution)/shard_map/ppermute | solution.py:70
  83.6 1.5 collective-permute-start.16
  85.1 2.1 %first_kernel.1 = (f32[4,8,128,128]{3,2,1,0:T(8,128)S(1)}, f32[128,128]{1,0:T(8,128)S(1)}, f32[8,128]{1,0:T(8,128)S(1)}) custom-call(f32[33,16,128]{2,1,0:T(8,128)S(1)} %collective-permute-done.refs_0_, f32[33,16,128]{2,1,0:T(8,128)S(1)} %collective-permute-done.12.refs_1_, f32[42,16,128]{2,1,0:T(8,128)S(1)} %collective-permute-done.1.refs_0_.refs_2_.own_0_ref, ...), custom_call_target="tpu_custom_call" | custom-call | flops 3000000000 | bytes 4194304 | tf_op jit(solution)/shard_map/first_kernel/pallas_call | solution.py:409
  87.2 0.2 collective-permute-done.15.under_a_ref
  87.4 1.2 collective-permute-done.16.over_a_ref
  88.7 1.1 collective-permute-done.14.high_a_ref
  89.7 0.8 first_edge_kernel.1
  90.5 1.9 %collective-permute-start.23 = (f32[4,16,16,128]{3,2,1,0:T(8,128)S(1)}, f32[4,16,16,128]{3,2,1,0:T(8,128)S(1)}, u32[]{:S(2)}, u32[]{:S(2)}) collective-permute-start(f32[4,16,16,128]{3,2,1,0:T(8,128)S(1)} %get-tuple-element.77), channel_id=1, source_target_pairs={{32,40},{34,42},{36,44},{38,46},{39,47},{37,45},{35,43},{33,41},{4... | collective-permute-start | bytes 1572872 | tf_op jit(solution)/shard_map/ppermute | solution.py:70
  92.4 2.3 %collective-permute-start.24 = (f32[4,16,16,128]{3,2,1,0:T(8,128)S(1)}, f32[4,16,16,128]{3,2,1,0:T(8,128)S(1)}, u32[]{:S(2)}, u32[]{:S(2)}) collective-permute-start(f32[4,16,16,128]{3,2,1,0:T(8,128)S(1)} %get-tuple-element.78), channel_id=1, source_target_pairs={{32,232},{34,234},{36,236},{38,238},{39,239},{37,237},{35,235},{33... | collective-permute-start | bytes 1572872 | tf_op jit(solution)/shard_map/ppermute | solution.py:70
  94.7 2.6 %collective-permute-start.17 = (f32[4,16,16,128]{3,2,1,0:T(8,128)S(1)}, f32[4,16,16,128]{3,2,1,0:T(8,128)S(1)}, u32[]{:S(2)}, u32[]{:S(2)}) collective-permute-start(f32[4,16,16,128]{3,2,1,0:T(8,128)S(1)} %get-tuple-element.71), channel_id=1, source_target_pairs={{32,40},{34,42},{36,44},{38,46},{39,47},{37,45},{35,43},{33,41},{4... | collective-permute-start | bytes 1572872 | tf_op jit(solution)/shard_map/ppermute | solution.py:70
  97.3 1.4 second_kernel.1.inner_ref
  98.7 5.7 %collective-permute-done.24.high_ref = f32[4,16,16,128]{3,2,1,0:T(8,128)S(1)} collective-permute-done((f32[4,16,16,128]{3,2,1,0:T(8,128)S(1)}, f32[4,16,16,128]{3,2,1,0:T(8,128)S(1)}, u32[]{:S(2)}, u32[]{:S(2)}) %collective-permute-start.24) | collective-permute-done | bytes 524320 | tf_op jit(solution)/shard_map/ppermute | solution.py:70
  104.4 0.1 second_edge_kernel.3
  104.6 5.6 %collective-permute-start.25 = (f32[4,8,16,128]{3,2,1,0:T(8,128)S(1)}, f32[4,8,16,128]{3,2,1,0:T(8,128)S(1)}, u32[]{:S(2)}, u32[]{:S(2)}) collective-permute-start(f32[4,8,16,128]{3,2,1,0:T(8,128)S(1)} %get-tuple-element.79), channel_id=1, source_target_pairs={{34,0},{35,1},{36,2},{37,3},{38,4},{39,5},{32,6},{33,7},{42,8},{43... | collective-permute-start | bytes 786440 | tf_op jit(solution)/shard_map/ppermute | solution.py:70
  110.2 0.7 collective-permute-start.26
  110.9 7.5 %collective-permute-start.27 = (f32[4,8,16,128]{3,2,1,0:T(8,128)S(1)}, f32[4,8,16,128]{3,2,1,0:T(8,128)S(1)}, u32[]{:S(2)}, u32[]{:S(2)}) collective-permute-start(f32[4,8,16,128]{3,2,1,0:T(8,128)S(1)} %get-tuple-element.81), channel_id=1, source_target_pairs={{36,0},{37,1},{38,2},{39,3},{32,4},{33,5},{34,6},{35,7},{44,8},{45... | collective-permute-start | bytes 786440 | tf_op jit(solution)/shard_map/ppermute | solution.py:70
  118.4 0.1 second_edge_kernel.2
  118.5 11.6 %collective-permute-start.19 = (f32[4,8,16,128]{3,2,1,0:T(8,128)S(1)}, f32[4,8,16,128]{3,2,1,0:T(8,128)S(1)}, u32[]{:S(2)}, u32[]{:S(2)}) collective-permute-start(f32[4,8,16,128]{3,2,1,0:T(8,128)S(1)} %get-tuple-element.73), channel_id=1, source_target_pairs={{38,0},{39,1},{32,2},{33,3},{34,4},{35,5},{36,6},{37,7},{46,8},{47... | collective-permute-start | bytes 786440 | tf_op jit(solution)/shard_map/ppermute | solution.py:70
  130.1 5.8 %collective-permute-start.20 = (f32[4,8,16,128]{3,2,1,0:T(8,128)S(1)}, f32[4,8,16,128]{3,2,1,0:T(8,128)S(1)}, u32[]{:S(2)}, u32[]{:S(2)}) collective-permute-start(f32[4,8,16,128]{3,2,1,0:T(8,128)S(1)} %get-tuple-element.74), channel_id=1, source_target_pairs={{39,0},{38,1},{33,2},{32,3},{35,4},{34,5},{37,6},{36,7},{47,8},{46... | collective-permute-start | bytes 786440 | tf_op jit(solution)/shard_map/ppermute | solution.py:70
  135.8 4.4 %collective-permute-start.21 = (f32[4,8,16,128]{3,2,1,0:T(8,128)S(1)}, f32[4,8,16,128]{3,2,1,0:T(8,128)S(1)}, u32[]{:S(2)}, u32[]{:S(2)}) collective-permute-start(f32[4,8,16,128]{3,2,1,0:T(8,128)S(1)} %get-tuple-element.75), channel_id=1, source_target_pairs={{32,0},{33,1},{34,2},{35,3},{36,4},{37,5},{38,6},{39,7},{40,8},{41... | collective-permute-start | bytes 786440 | tf_op jit(solution)/shard_map/ppermute | solution.py:70
  140.2 3.0 %collective-permute-start.22 = (f32[4,8,16,128]{3,2,1,0:T(8,128)S(1)}, f32[4,8,16,128]{3,2,1,0:T(8,128)S(1)}, u32[]{:S(2)}, u32[]{:S(2)}) collective-permute-start(f32[4,8,16,128]{3,2,1,0:T(8,128)S(1)} %get-tuple-element.76), channel_id=1, source_target_pairs={{33,0},{32,1},{35,2},{34,3},{37,4},{36,5},{39,6},{38,7},{41,8},{40... | collective-permute-start | bytes 786440 | tf_op jit(solution)/shard_map/ppermute | solution.py:70
  143.2 6.4 %local_kernel.1.local_ref = f32[4,64,16,128]{3,2,1,0:T(8,128)S(1)} custom-call(f32[4,64,16,128]{3,2,1,0:T(8,128)S(1)} %copy-done.2, f32[64,128]{1,0:T(8,128)S(1)} %fusion.ty_ref.refs_9_, f32[1,128]{1,0:T(1,128)S(1)} %multiply_bitcast_fusion.vy_ref.refs_10_), custom_call_target="tpu_custom_call" | custom-call | flops 4000000000 | bytes 4194304 | tf_op jit(solution)/shard_map/local_kernel/pallas_call | solution.py:409
  149.7 10.7 %collective-permute-done.20.refs_1_ = f32[4,8,16,128]{3,2,1,0:T(8,128)S(1)} collective-permute-done((f32[4,8,16,128]{3,2,1,0:T(8,128)S(1)}, f32[4,8,16,128]{3,2,1,0:T(8,128)S(1)}, u32[]{:S(2)}, u32[]{:S(2)}) %collective-permute-start.20) | collective-permute-done | bytes 262176 | tf_op jit(solution)/shard_map/ppermute | solution.py:70
  160.4 3.2 %collective-permute-done.22.refs_3_ = f32[4,8,16,128]{3,2,1,0:T(8,128)S(1)} collective-permute-done((f32[4,8,16,128]{3,2,1,0:T(8,128)S(1)}, f32[4,8,16,128]{3,2,1,0:T(8,128)S(1)}, u32[]{:S(2)}, u32[]{:S(2)}) %collective-permute-start.22) | collective-permute-done | bytes 262176 | tf_op jit(solution)/shard_map/ppermute | solution.py:70
  163.6 1.9 %final_kernel.1 = f32[4,64,16,128]{3,2,1,0:T(8,128)} custom-call(f32[4,64,16,128]{3,2,1,0:T(8,128)S(1)} %local_kernel.1.local_ref, f32[4,8,16,128]{3,2,1,0:T(8,128)S(1)} %collective-permute-done.19.refs_0_, f32[4,8,16,128]{3,2,1,0:T(8,128)S(1)} %collective-permute-done.20.refs_1_, f32[4,8,16,128]{3,2,1,0:T(8,128)S(1)} %collective-permute-done.21.refs_2_, ...), custom_call_target="tpu_custom_call" | custom-call | bytes 6291456 | tf_op jit(solution)/shard_map/final_kernel/pallas_call | solution.py:490
  (40 shorter events, 0.2 us)
Async XLA Ops:
  0.0 69.5 %copy-start = (f32[64,128]{1,0:T(8,128)S(1)}, f32[64,128]{1,0:T(8,128)}, u32[]{:S(2)}) copy-start(f32[64,128]{1,0:T(8,128)} %param.11) | copy-start | bytes 98308
  0.0 69.5 %copy-start.6 = (f32[128]{0:T(128)S(1)}, f32[128]{0:T(128)}, u32[]{:S(2)}) copy-start(f32[128]{0:T(128)} %param.13) | copy-start | bytes 1540
  0.0 69.5 %copy-start.7 = (s32[128]{0:T(128)S(1)}, s32[128]{0:T(128)}, u32[]{:S(2)}) copy-start(s32[128]{0:T(128)} %param.15) | copy-start | bytes 1540
  0.8 1.6 copy-start.1
  2.4 0.7 copy-start.3
  3.1 66.4 %copy-start.5 = (f32[128,128]{1,0:T(8,128)S(1)}, f32[128,128]{1,0:T(8,128)}, u32[]{:S(2)}) copy-start(f32[128,128]{1,0:T(8,128)} %constant.14.clone) | copy-start | bytes 196612
  3.1 82.0 %copy-start.4 = (f32[128,128]{1,0:T(8,128)S(1)}, f32[128,128]{1,0:T(8,128)}, u32[]{:S(2)}) copy-start(f32[128,128]{1,0:T(8,128)} %constant.15.clone.refs_8_) | copy-start | bytes 196612
  3.2 16.0 %collective-permute-start.3 = (f32[33,16,128]{2,1,0:T(8,128)S(1)}, f32[33,16,128]{2,1,0:T(8,128)S(1)}, u32[]{:S(2)}, u32[]{:S(2)}) collective-permute-start(f32[33,16,128]{2,1,0:T(8,128)S(1)} %get-tuple-element.47), channel_id=1, source_target_pairs={{0,34},{1,35},{2,36},{3,37},{4,38},{5,39},{6,32},{7,33},{8,42},{9,... | collective-permute-start | bytes 811016 | tf_op jit(solution)/shard_map/ppermute | solution.py:70
  9.9 34.7 %collective-permute-start.1 = (f32[42,16,128]{2,1,0:T(8,128)S(1)}, f32[42,16,128]{2,1,0:T(8,128)S(1)}, u32[]{:S(2)}, u32[]{:S(2)}) collective-permute-start(f32[42,16,128]{2,1,0:T(8,128)S(1)} %get-tuple-element.45), channel_id=1, source_target_pairs={{0,32},{1,33},{2,34},{3,35},{4,36},{5,37},{6,38},{7,39},{8,40},{9,... | collective-permute-start | bytes 1032200 | tf_op jit(solution)/shard_map/ppermute | solution.py:70
  9.9 34.6 %collective-permute-start.2 = (f32[41,16,128]{2,1,0:T(8,128)S(1)}, f32[41,16,128]{2,1,0:T(8,128)S(1)}, u32[]{:S(2)}, u32[]{:S(2)}) collective-permute-start(f32[41,16,128]{2,1,0:T(8,128)S(1)} %get-tuple-element.46), channel_id=1, source_target_pairs={{0,33},{1,32},{2,35},{3,34},{4,37},{5,36},{6,39},{7,38},{8,41},{9,... | collective-permute-start | bytes 1007624 | tf_op jit(solution)/shard_map/ppermute | solution.py:70
  10.6 20.2 %collective-permute-start.4 = (f32[33,16,128]{2,1,0:T(8,128)S(1)}, f32[33,16,128]{2,1,0:T(8,128)S(1)}, u32[]{:S(2)}, u32[]{:S(2)}) collective-permute-start(f32[33,16,128]{2,1,0:T(8,128)S(1)} %get-tuple-element.48), channel_id=1, source_target_pairs={{0,35},{1,34},{2,37},{3,36},{4,39},{5,38},{6,33},{7,32},{8,43},{9,... | collective-permute-start | bytes 811016 | tf_op jit(solution)/shard_map/ppermute | solution.py:70
  12.4 27.4 %collective-permute-start.5 = (f32[33,16,128]{2,1,0:T(8,128)S(1)}, f32[33,16,128]{2,1,0:T(8,128)S(1)}, u32[]{:S(2)}, u32[]{:S(2)}) collective-permute-start(f32[33,16,128]{2,1,0:T(8,128)S(1)} %get-tuple-element.49), channel_id=1, source_target_pairs={{0,36},{1,37},{2,38},{3,39},{4,32},{5,33},{6,34},{7,35},{8,44},{9,... | collective-permute-start | bytes 811016 | tf_op jit(solution)/shard_map/ppermute | solution.py:70
  19.2 25.3 %collective-permute-start.6 = (f32[33,16,128]{2,1,0:T(8,128)S(1)}, f32[33,16,128]{2,1,0:T(8,128)S(1)}, u32[]{:S(2)}, u32[]{:S(2)}) collective-permute-start(f32[33,16,128]{2,1,0:T(8,128)S(1)} %get-tuple-element.50), channel_id=1, source_target_pairs={{0,37},{1,36},{2,39},{3,38},{4,33},{5,32},{6,35},{7,34},{8,45},{9,... | collective-permute-start | bytes 811016 | tf_op jit(solution)/shard_map/ppermute | solution.py:70
  30.8 24.6 %collective-permute-start = (f32[33,16,128]{2,1,0:T(8,128)S(1)}, f32[33,16,128]{2,1,0:T(8,128)S(1)}, u32[]{:S(2)}, u32[]{:S(2)}) collective-permute-start(f32[33,16,128]{2,1,0:T(8,128)S(1)} %get-tuple-element.44), channel_id=1, source_target_pairs={{0,38},{1,39},{2,32},{3,33},{4,34},{5,35},{6,36},{7,37},{8,46},{9,... | collective-permute-start | bytes 811016 | tf_op jit(solution)/shard_map/ppermute | solution.py:70
  44.7 25.0 %collective-permute-start.7 = (f32[6,16,16,128]{3,2,1,0:T(8,128)S(1)}, f32[6,16,16,128]{3,2,1,0:T(8,128)S(1)}, u32[]{:S(2)}, u32[]{:S(2)}) collective-permute-start(f32[6,16,16,128]{3,2,1,0:T(8,128)S(1)} %get-tuple-element.51), channel_id=1, source_target_pairs={{32,40},{34,42},{36,44},{38,46},{39,47},{37,45},{35,43},{33,41},{4... | collective-permute-start | bytes 2359304 | tf_op jit(solution)/shard_map/ppermute | solution.py:70
  47.9 21.9 %collective-permute-start.8 = (f32[6,16,16,128]{3,2,1,0:T(8,128)S(1)}, f32[6,16,16,128]{3,2,1,0:T(8,128)S(1)}, u32[]{:S(2)}, u32[]{:S(2)}) collective-permute-start(f32[6,16,16,128]{3,2,1,0:T(8,128)S(1)} %get-tuple-element.52), channel_id=1, source_target_pairs={{32,232},{34,234},{36,236},{38,238},{39,239},{37,237},{35,235},{33... | collective-permute-start | bytes 2359304 | tf_op jit(solution)/shard_map/ppermute | solution.py:70
  51.9 5.4 %collective-permute-start.11 = (f32[2,8,16,128]{3,2,1,0:T(8,128)S(1)}, f32[2,8,16,128]{3,2,1,0:T(8,128)S(1)}, u32[]{:S(2)}, u32[]{:S(2)}) collective-permute-start(f32[2,8,16,128]{3,2,1,0:T(8,128)S(1)} %get-tuple-element.55), channel_id=1, source_target_pairs={{32,36},{34,38},{36,32},{38,34},{39,35},{37,33},{35,39},{33,37},{4... | collective-permute-start | bytes 393224 | tf_op jit(solution)/shard_map/ppermute | solution.py:70
  51.9 17.8 %collective-permute-start.10 = (f32[8,8,16,128]{3,2,1,0:T(8,128)S(1)}, f32[8,8,16,128]{3,2,1,0:T(8,128)S(1)}, u32[]{:S(2)}, u32[]{:S(2)}) collective-permute-start(f32[8,8,16,128]{3,2,1,0:T(8,128)S(1)} %get-tuple-element.54), channel_id=1, source_target_pairs={{32,38},{34,32},{36,34},{38,36},{39,33},{37,39},{35,37},{33,35},{4... | collective-permute-start | bytes 1572872 | tf_op jit(solution)/shard_map/ppermute | solution.py:70
  55.4 14.3 %collective-permute-start.9 = (f32[8,8,16,128]{3,2,1,0:T(8,128)S(1)}, f32[8,8,16,128]{3,2,1,0:T(8,128)S(1)}, u32[]{:S(2)}, u32[]{:S(2)}) collective-permute-start(f32[8,8,16,128]{3,2,1,0:T(8,128)S(1)} %get-tuple-element.53), channel_id=1, source_target_pairs={{32,34},{34,36},{36,38},{38,32},{39,37},{37,35},{35,33},{33,39},{4... | collective-permute-start | bytes 1572872 | tf_op jit(solution)/shard_map/ppermute | solution.py:70
  57.3 21.0 %collective-permute-start.12 = (f32[33,16,128]{2,1,0:T(8,128)S(1)}, f32[33,16,128]{2,1,0:T(8,128)S(1)}, u32[]{:S(2)}, u32[]{:S(2)}) collective-permute-start(f32[33,16,128]{2,1,0:T(8,128)S(1)} %get-tuple-element.57), channel_id=1, source_target_pairs={{0,39},{1,38},{2,33},{3,32},{4,35},{5,34},{6,37},{7,36},{8,47},{9,... | collective-permute-start | bytes 811016 | tf_op jit(solution)/shard_map/ppermute | solution.py:70
  78.4 10.3 %collective-permute-start.13 = (f32[2,16,16,128]{3,2,1,0:T(8,128)S(1)}, f32[2,16,16,128]{3,2,1,0:T(8,128)S(1)}, u32[]{:S(2)}, u32[]{:S(2)}) collective-permute-start(f32[2,16,16,128]{3,2,1,0:T(8,128)S(1)} %get-tuple-element.59), channel_id=1, source_target_pairs={{32,40},{34,42},{36,44},{38,46},{39,47},{37,45},{35,43},{33,41},{4... | collective-permute-start | bytes 786440 | tf_op jit(solution)/shard_map/ppermute | solution.py:70
  83.6 6.1 %collective-permute-start.14 = (f32[2,16,16,128]{3,2,1,0:T(8,128)S(1)}, f32[2,16,16,128]{3,2,1,0:T(8,128)S(1)}, u32[]{:S(2)}, u32[]{:S(2)}) collective-permute-start(f32[2,16,16,128]{3,2,1,0:T(8,128)S(1)} %get-tuple-element.61), channel_id=1, source_target_pairs={{32,232},{34,234},{36,236},{38,238},{39,239},{37,237},{35,235},{33... | collective-permute-start | bytes 786440 | tf_op jit(solution)/shard_map/ppermute | solution.py:70
  83.6 3.8 %collective-permute-start.15 = (f32[2,8,16,128]{3,2,1,0:T(8,128)S(1)}, f32[2,8,16,128]{3,2,1,0:T(8,128)S(1)}, u32[]{:S(2)}, u32[]{:S(2)}) collective-permute-start(f32[2,8,16,128]{3,2,1,0:T(8,128)S(1)} %get-tuple-element.63), channel_id=1, source_target_pairs={{32,34},{34,36},{36,38},{38,32},{39,37},{37,35},{35,33},{33,39},{4... | collective-permute-start | bytes 393224 | tf_op jit(solution)/shard_map/ppermute | solution.py:70
  83.6 5.0 %collective-permute-start.16 = (f32[2,8,16,128]{3,2,1,0:T(8,128)S(1)}, f32[2,8,16,128]{3,2,1,0:T(8,128)S(1)}, u32[]{:S(2)}, u32[]{:S(2)}) collective-permute-start(f32[2,8,16,128]{3,2,1,0:T(8,128)S(1)} %get-tuple-element.65), channel_id=1, source_target_pairs={{32,38},{34,32},{36,34},{38,36},{39,33},{37,39},{35,37},{33,35},{4... | collective-permute-start | bytes 393224 | tf_op jit(solution)/shard_map/ppermute | solution.py:70
  90.5 8.2 %collective-permute-start.23 = (f32[4,16,16,128]{3,2,1,0:T(8,128)S(1)}, f32[4,16,16,128]{3,2,1,0:T(8,128)S(1)}, u32[]{:S(2)}, u32[]{:S(2)}) collective-permute-start(f32[4,16,16,128]{3,2,1,0:T(8,128)S(1)} %get-tuple-element.77), channel_id=1, source_target_pairs={{32,40},{34,42},{36,44},{38,46},{39,47},{37,45},{35,43},{33,41},{4... | collective-permute-start | bytes 1572872 | tf_op jit(solution)/shard_map/ppermute | solution.py:70
  92.4 12.0 %collective-permute-start.24 = (f32[4,16,16,128]{3,2,1,0:T(8,128)S(1)}, f32[4,16,16,128]{3,2,1,0:T(8,128)S(1)}, u32[]{:S(2)}, u32[]{:S(2)}) collective-permute-start(f32[4,16,16,128]{3,2,1,0:T(8,128)S(1)} %get-tuple-element.78), channel_id=1, source_target_pairs={{32,232},{34,234},{36,236},{38,238},{39,239},{37,237},{35,235},{33... | collective-permute-start | bytes 1572872 | tf_op jit(solution)/shard_map/ppermute | solution.py:70
  94.7 23.6 %collective-permute-start.17 = (f32[4,16,16,128]{3,2,1,0:T(8,128)S(1)}, f32[4,16,16,128]{3,2,1,0:T(8,128)S(1)}, u32[]{:S(2)}, u32[]{:S(2)}) collective-permute-start(f32[4,16,16,128]{3,2,1,0:T(8,128)S(1)} %get-tuple-element.71), channel_id=1, source_target_pairs={{32,40},{34,42},{36,44},{38,46},{39,47},{37,45},{35,43},{33,41},{4... | collective-permute-start | bytes 1572872 | tf_op jit(solution)/shard_map/ppermute | solution.py:70
  97.3 21.1 %collective-permute-start.18 = (f32[4,16,16,128]{3,2,1,0:T(8,128)S(1)}, f32[4,16,16,128]{3,2,1,0:T(8,128)S(1)}, u32[]{:S(2)}, u32[]{:S(2)}) collective-permute-start(f32[4,16,16,128]{3,2,1,0:T(8,128)S(1)} %get-tuple-element.72), channel_id=1, source_target_pairs={{32,232},{34,234},{36,236},{38,238},{39,239},{37,237},{35,235},{33... | collective-permute-start | bytes 1572872 | tf_op jit(solution)/shard_map/ppermute | solution.py:70
  104.6 38.6 %copy-start.2 = (f32[4,64,16,128]{3,2,1,0:T(8,128)S(1)}, f32[4,64,16,128]{3,2,1,0:T(8,128)}, u32[]{:S(2)}) copy-start(f32[4,64,16,128]{3,2,1,0:T(8,128)} %g_ref.3) | copy-start | bytes 6291460
  104.6 25.5 %collective-permute-start.25 = (f32[4,8,16,128]{3,2,1,0:T(8,128)S(1)}, f32[4,8,16,128]{3,2,1,0:T(8,128)S(1)}, u32[]{:S(2)}, u32[]{:S(2)}) collective-permute-start(f32[4,8,16,128]{3,2,1,0:T(8,128)S(1)} %get-tuple-element.79), channel_id=1, source_target_pairs={{34,0},{35,1},{36,2},{37,3},{38,4},{39,5},{32,6},{33,7},{42,8},{43... | collective-permute-start | bytes 786440 | tf_op jit(solution)/shard_map/ppermute | solution.py:70
  110.2 25.7 %collective-permute-start.26 = (f32[4,8,16,128]{3,2,1,0:T(8,128)S(1)}, f32[4,8,16,128]{3,2,1,0:T(8,128)S(1)}, u32[]{:S(2)}, u32[]{:S(2)}) collective-permute-start(f32[4,8,16,128]{3,2,1,0:T(8,128)S(1)} %get-tuple-element.80), channel_id=1, source_target_pairs={{35,0},{34,1},{37,2},{36,3},{39,4},{38,5},{33,6},{32,7},{43,8},{42... | collective-permute-start | bytes 786440 | tf_op jit(solution)/shard_map/ppermute | solution.py:70
  110.9 29.3 %collective-permute-start.27 = (f32[4,8,16,128]{3,2,1,0:T(8,128)S(1)}, f32[4,8,16,128]{3,2,1,0:T(8,128)S(1)}, u32[]{:S(2)}, u32[]{:S(2)}) collective-permute-start(f32[4,8,16,128]{3,2,1,0:T(8,128)S(1)} %get-tuple-element.81), channel_id=1, source_target_pairs={{36,0},{37,1},{38,2},{39,3},{32,4},{33,5},{34,6},{35,7},{44,8},{45... | collective-permute-start | bytes 786440 | tf_op jit(solution)/shard_map/ppermute | solution.py:70
  118.4 31.3 %collective-permute-start.28 = (f32[4,8,16,128]{3,2,1,0:T(8,128)S(1)}, f32[4,8,16,128]{3,2,1,0:T(8,128)S(1)}, u32[]{:S(2)}, u32[]{:S(2)}) collective-permute-start(f32[4,8,16,128]{3,2,1,0:T(8,128)S(1)} %get-tuple-element.82), channel_id=1, source_target_pairs={{37,0},{36,1},{39,2},{38,3},{33,4},{32,5},{35,6},{34,7},{45,8},{44... | collective-permute-start | bytes 786440 | tf_op jit(solution)/shard_map/ppermute | solution.py:70
  118.5 31.2 %collective-permute-start.19 = (f32[4,8,16,128]{3,2,1,0:T(8,128)S(1)}, f32[4,8,16,128]{3,2,1,0:T(8,128)S(1)}, u32[]{:S(2)}, u32[]{:S(2)}) collective-permute-start(f32[4,8,16,128]{3,2,1,0:T(8,128)S(1)} %get-tuple-element.73), channel_id=1, source_target_pairs={{38,0},{39,1},{32,2},{33,3},{34,4},{35,5},{36,6},{37,7},{46,8},{47... | collective-permute-start | bytes 786440 | tf_op jit(solution)/shard_map/ppermute | solution.py:70
  130.1 30.3 %collective-permute-start.20 = (f32[4,8,16,128]{3,2,1,0:T(8,128)S(1)}, f32[4,8,16,128]{3,2,1,0:T(8,128)S(1)}, u32[]{:S(2)}, u32[]{:S(2)}) collective-permute-start(f32[4,8,16,128]{3,2,1,0:T(8,128)S(1)} %get-tuple-element.74), channel_id=1, source_target_pairs={{39,0},{38,1},{33,2},{32,3},{35,4},{34,5},{37,6},{36,7},{47,8},{46... | collective-permute-start | bytes 786440 | tf_op jit(solution)/shard_map/ppermute | solution.py:70
  135.8 24.6 %collective-permute-start.21 = (f32[4,8,16,128]{3,2,1,0:T(8,128)S(1)}, f32[4,8,16,128]{3,2,1,0:T(8,128)S(1)}, u32[]{:S(2)}, u32[]{:S(2)}) collective-permute-start(f32[4,8,16,128]{3,2,1,0:T(8,128)S(1)} %get-tuple-element.75), channel_id=1, source_target_pairs={{32,0},{33,1},{34,2},{35,3},{36,4},{37,5},{38,6},{39,7},{40,8},{41... | collective-permute-start | bytes 786440 | tf_op jit(solution)/shard_map/ppermute | solution.py:70
  140.2 23.4 %collective-permute-start.22 = (f32[4,8,16,128]{3,2,1,0:T(8,128)S(1)}, f32[4,8,16,128]{3,2,1,0:T(8,128)S(1)}, u32[]{:S(2)}, u32[]{:S(2)}) collective-permute-start(f32[4,8,16,128]{3,2,1,0:T(8,128)S(1)} %get-tuple-element.76), channel_id=1, source_target_pairs={{33,0},{32,1},{35,2},{34,3},{37,4},{36,5},{39,6},{38,7},{41,8},{40... | collective-permute-start | bytes 786440 | tf_op jit(solution)/shard_map/ppermute | solution.py:70

commit v4 on v3

--- a/solution.py
+++ b/solution.py
@@ -14,9 +14,9 @@
 BF16 = jnp.bfloat16
 K = 128
 AXES = ("gx", "ka")
-SLOTS = [(dy, ds) for dy in (3, 0, 1, 2) for ds in (0, 1)]
-GROUPS = (range(0, 2), range(2, 8))
-FIRST = SLOTS.index((0, 0))
+SLOTS = [(2, 0), (2, 1), (1, 0), (1, 1), (3, 0), (3, 1), (0, 0), (0, 1)]
+GROUPS = ((2, 3, 4, 5), (0, 1, 6, 7))
+FIRST, SECOND = SLOTS.index((0, 0)), SLOTS.index((0, 1))
 VMEM = pl.BlockSpec(memory_space=pltpu.VMEM)
 
 
@@ -211,21 +211,20 @@
     pieces[FIRST][41, 4:16] = jnp.zeros((12, K), F32)
 
 
-def cut_kernel(slots, *refs):
-    pieces, outs = refs[: len(slots)], refs[len(slots) :]
-    head_ref, tail_ref, y_low_ref, y_high_ref = outs[:4]
-    for i, slot in enumerate(slots):
+def cut_kernel(*refs):
+    pieces, (head_ref, tail_ref, y_low_ref, y_high_ref, across_ref) = refs[:8], refs[8:]
+    for i in range(8):
         head_ref[i] = pieces[i][0:16]
         tail_ref[i] = pieces[i][16:32]
         for x in range(4):
             y_low_ref[i, 2 * x : 2 * x + 2] = pieces[i][8 * x : 8 * x + 2]
             y_high_ref[i, 2 * x : 2 * x + 2] = pieces[i][8 * x + 6 : 8 * x + 8]
-        dy, ds = SLOTS[slot]
+        dy, ds = SLOTS[i]
         if dy == 0:
             rows = pieces[i][33:41]
-            y_low_ref[len(slots) + ds] = rows
-            y_high_ref[len(slots) + ds] = rows
-            outs[4][ds] = rows
+            y_low_ref[8 + ds] = rows
+            y_high_ref[8 + ds] = rows
+            across_ref[ds] = rows
 
 
 def inner_drift(center, x, layer, toward, rate):
@@ -300,8 +299,7 @@
 
 
 def first_edge_kernel(
-    inner_ref, low_a_ref, low_b_ref, high_a_ref, high_b_ref, under_a_ref, under_b_ref, over_a_ref, over_b_ref,
-    ring_ref, own_0_ref, own_1_ref, vx_ref, vy_ref, v_ref, *outs,
+    inner_ref, low_ref, high_ref, under_ref, over_ref, ring_ref, own_0_ref, own_1_ref, vx_ref, vy_ref, v_ref, *outs
 ):
     y_place, half, block = as_host()
     middle = jnp.where(y_place == 3, 1.0, 0.0)
@@ -309,20 +307,14 @@
     vy = vy_ref[...].reshape(1, 1, K)
     up_y = jnp.maximum(vy, 0.0) * 0.125
     down_y = jnp.maximum(-vy, 0.0) * 0.125
-    by_group = ((low_a_ref, high_a_ref, under_a_ref, over_a_ref), (low_b_ref, high_b_ref, under_b_ref, over_b_ref))
-
-    def beside(side, pair, rows):
-        slot = SLOTS.index(pair)
-        group = int(slot in GROUPS[1])
-        return by_group[group][side][slot - GROUPS[group].start, rows]
+
+    def beside(ref, pair, rows):
+        return ref[SLOTS.index(pair), rows]
 
     for slot in range(8):
         dy, ds = SLOTS[slot]
         at = kx_of(slot)
-        group = int(slot in GROUPS[1])
-        low_ref, high_ref = by_group[group][:2]
         up, down = rates(vx_ref, at, 0.0625)
-        i = slot - GROUPS[group].start
         for x in range(4):
             rows = slice(2 * x, 2 * x + 2)
             if dy == 0:
@@ -330,16 +322,16 @@
             elif dy == 2:
                 across = ring_ref[ds, rows]
             else:
-                across = jnp.where(half == dy // 3, under_b_ref[6 + ds, rows], over_b_ref[6 + ds, rows])
+                across = jnp.where(half == dy // 3, under_ref[8 + ds, rows], over_ref[8 + ds, rows])
             before, after = ((dy + 3) % 4, ds), ((dy + 1) % 4, ds)
-            under = jnp.where(half == 0, beside(2, before, rows), beside(2, after, rows))
-            over = jnp.where(half == 0, beside(3, after, rows), beside(3, before, rows))
+            under = jnp.where(half == 0, beside(under_ref, before, rows), beside(under_ref, after, rows))
+            over = jnp.where(half == 0, beside(over_ref, after, rows), beside(over_ref, before, rows))
             under = jnp.where(under_middle, across * middle, under)
             over = jnp.where(over_middle, across * middle, over)
             value = inner_ref[x, :, at, :] + outer_drift(
                 x,
-                lambda n: low_ref[i, 8 - 8 * n : 16 - 8 * n],
-                lambda n: high_ref[i, 8 * n : 8 * n + 8],
+                lambda n: low_ref[slot, 8 - 8 * n : 16 - 8 * n],
+                lambda n: high_ref[slot, 8 * n : 8 * n + 8],
                 up,
                 down,
             )
@@ -347,8 +339,9 @@
             top = jnp.concatenate([-down_y * over[0:1], down_y * (4.0 * over[0:1] - over[1:2])], 0)
             value = jnp.concatenate([value[0:2] + bottom, value[2:6], value[6:8] + top], 0)
             v_ref[x, :, at, :] = value
-            side = outs[2 * (slot // 4) + x // 2]
-            side[slot % 4, 8 * (x % 2) : 8 * (x % 2) + 8] = value
+            group = int(slot in GROUPS[1])
+            side = outs[2 * group + x // 2]
+            side[GROUPS[group].index(slot), 8 * (x % 2) : 8 * (x % 2) + 8] = value
 
 
 def second_kernel(v_ref, tx_ref, vx_ref, out_ref, tables):
@@ -445,25 +438,12 @@
         local_kernel, array(4, 64, 16, K), [pltpu.VMEM((2, 4, 68, 16, K), F32)], 4 * 10**9
     )(density, ty, vy)
 
-    low, high, under, over = [None] * 2, [None] * 2, [None] * 2, [None] * 2
-    for group in (1, 0):
-        slots = GROUPS[group]
-        middle = FIRST in slots
-        rows = array(len(slots) + 2 * middle, 8, 16, K)
-        head, tail, y_low, y_high, *ring = call(
-            functools.partial(cut_kernel, slots),
-            [array(len(slots), 16, 16, K)] * 2 + [rows] * 2 + [array(2, 8, 16, K)] * middle,
-            mib=2,
-        )(*pieces[slots.start : slots.stop])
-        low[group] = send(tail, x_pairs(1))
-        high[group] = send(head, x_pairs(-1))
-        under[group] = send(y_high, y_pairs(1))
-        over[group] = send(y_low, y_pairs(-1))
-        if middle:
-            across = send(ring[0], y_pairs(2))
-            pieces[0], low[1], high[1], under[1], over[1], across = lax.optimization_barrier(
-                (pieces[0], low[1], high[1], under[1], over[1], across)
-            )
+    head, tail, y_low, y_high, across = call(
+        cut_kernel, [array(8, 16, 16, K)] * 2 + [array(10, 8, 16, K)] * 2 + [array(2, 8, 16, K)]
+    )(*pieces)
+    under, over = send(y_high, y_pairs(1)), send(y_low, y_pairs(-1))
+    low, high = send(tail, x_pairs(1)), send(head, x_pairs(-1))
+    across = send(across, y_pairs(2))
     left_tables = pltpu.VMEM((4, 2 * K, 2 * K), BF16)
     inner, vx, tx = call(
         first_kernel,
@@ -472,17 +452,18 @@
         3 * 10**9,
     )(*pieces, jnp.asarray(sine_table(-1)), ty, vy)
     v, *sides = call(first_edge_kernel, [array(4, 8, K, K)] + [array(4, 16, 16, K)] * 4)(
-        inner, *low, *high, *under, *over, across, pieces[FIRST], pieces[FIRST + 1], vx, vy
+        inner, low, high, under, over, across, pieces[FIRST], pieces[SECOND], vx, vy
     )
     low = [send(sides[2 * group + 1], x_pairs(1)) for group in range(2)]
     high = [send(sides[2 * group], x_pairs(-1)) for group in range(2)]
     inner = call(second_kernel, array(4, 8, K, K), [left_tables], 2 * 10**9)(v, tx, vx)
-    pieces = []
-    for group, slots in enumerate((range(0, 4), range(4, 8))):
+    pieces = [None] * 8
+    for group, slots in enumerate(GROUPS):
         cut = call(functools.partial(second_edge_kernel, slots), [array(4, 8, 16, K)] * 4, mib=2)(
             inner, low[group], high[group], vx
         )
-        pieces += [send(piece, back(exchange_pairs(slot))) for slot, piece in zip(slots, cut)]
+        for slot, piece in zip(slots, cut):
+            pieces[slot] = send(piece, back(exchange_pairs(slot)))
 
     def by_x(*shape):
         return pl.BlockSpec((1, *shape), lambda x: (x, 0, 0, 0))

time: 166 us -> 160 us (0.964); the launches traced: 166 us -> 158 us
  starting transfers between devices: 97.2 us -> 66 us
  waiting for transfers between devices: 51.5 us -> 75.1 us
    ppermute x29 -> x25, starting transfers between devices: 97.2 us -> 66 us  [send(): return lax.ppermute(value, AXES, pairs)]
    ppermute x29 -> x25, waiting for transfers between devices: 51.5 us -> 75.1 us  [send(): return lax.ppermute(value, AXES, pairs)]
    pallas_call x9 -> x8, Pallas kernels: 11.4 us -> 11.4 us  [run(): pl.pallas_call(kernel, out_shape=outs, in_specs=[VMEM] * len(operands), o...]
  transfers between devices with their start and end apart: 29 -> 25, of which waited for: 12 -> 12; matrix products, arithmetic and copies ran while one was open for 0% -> 0% of each run, Pallas kernels for 6% -> 6%
where the time goes in v4:
time: 160 us; the launch traced here: 158 us
  waiting for transfers between devices  75.1 us (47%)
  starting transfers between devices  66 us (41%)
  Pallas kernels  13.3 us (8%)
  local copies, waits for them, and re-layouts  2.37 us (1%)
    ppermute x25, waiting for transfers between devices, send(): return lax.ppermute(value, AXES, pairs)  75.1 us
    ppermute x25, starting transfers between devices, send(): return lax.ppermute(value, AXES, pairs)  66 us
    pallas_call x8, Pallas kernels, run(): pl.pallas_call(kernel, out_shape=outs, in_specs=[VMEM] * len(operands), o...  11.4 us
  transfers between devices with their start and end apart: 25, of which 12 were waited for; matrix products, arithmetic and copies ran while one was open for 0% of the time, Pallas kernels for 6%

profile of v4, /device:TPU:39, one launch (start us, length us, event | category | flops | bytes accessed | tf_op | source)
XLA Modules:
  0.0 157.8 jit_solution(1237898668855476180)
XLA Ops:
  0.0 0.7 convert_multiply_fusion
  0.7 0.1 broadcast_in_dim.2.vel_ref
  0.8 1.6 %copy-done.1 = f32[4,64,16,128]{3,2,1,0:T(8,128)S(1)} copy-done((f32[4,64,16,128]{3,2,1,0:T(8,128)S(1)}, f32[4,64,16,128]{3,2,1,0:T(8,128)}, u32[]{:S(2)}) %copy-start.1) | copy-done | bytes 2097176
  2.4 0.7 copy-done.3
  3.0 0.2 pack_kernel.1
  3.2 8.3 %collective-permute-start = (f32[33,16,128]{2,1,0:T(8,128)S(1)}, f32[33,16,128]{2,1,0:T(8,128)S(1)}, u32[]{:S(2)}, u32[]{:S(2)}) collective-permute-start(f32[33,16,128]{2,1,0:T(8,128)S(1)} %get-tuple-element.34), channel_id=1, source_target_pairs={{0,36},{1,37},{2,38},{3,39},{4,32},{5,33},{6,34},{7,35},{8,44},{9,... | collective-permute-start | bytes 811016 | tf_op jit(solution)/shard_map/ppermute | solution.py:70
  11.5 0.5 collective-permute-start.1
  12.0 0.4 collective-permute-start.2
  12.4 5.1 %collective-permute-start.6 = (f32[42,16,128]{2,1,0:T(8,128)S(1)}, f32[42,16,128]{2,1,0:T(8,128)S(1)}, u32[]{:S(2)}, u32[]{:S(2)}) collective-permute-start(f32[42,16,128]{2,1,0:T(8,128)S(1)} %get-tuple-element.40), channel_id=1, source_target_pairs={{0,32},{1,33},{2,34},{3,35},{4,36},{5,37},{6,38},{7,39},{8,40},{9,... | collective-permute-start | bytes 1032200 | tf_op jit(solution)/shard_map/ppermute | solution.py:70
  17.5 0.7 collective-permute-start.7
  18.2 1.1 collective-permute-done.refs_0_
  19.3 1.4 collective-permute-start.3
  20.7 5.3 %collective-permute-done.1.refs_1_ = f32[33,16,128]{2,1,0:T(8,128)S(1)} collective-permute-done((f32[33,16,128]{2,1,0:T(8,128)S(1)}, f32[33,16,128]{2,1,0:T(8,128)S(1)}, u32[]{:S(2)}, u32[]{:S(2)}) %collective-permute-start.1) | collective-permute-done | bytes 270368 | tf_op jit(solution)/shard_map/ppermute | solution.py:70
  26.0 2.3 %collective-permute-start.4 = (f32[33,16,128]{2,1,0:T(8,128)S(1)}, f32[33,16,128]{2,1,0:T(8,128)S(1)}, u32[]{:S(2)}, u32[]{:S(2)}) collective-permute-start(f32[33,16,128]{2,1,0:T(8,128)S(1)} %get-tuple-element.38), channel_id=1, source_target_pairs={{0,38},{1,39},{2,32},{3,33},{4,34},{5,35},{6,36},{7,37},{8,46},{9,... | collective-permute-start | bytes 811016 | tf_op jit(solution)/shard_map/ppermute | solution.py:70
  28.3 1.1 collective-permute-done.2.refs_2_
  29.4 1.2 collective-permute-start.5
  30.6 20.7 %collective-permute-done.3.refs_3_ = f32[33,16,128]{2,1,0:T(8,128)S(1)} collective-permute-done((f32[33,16,128]{2,1,0:T(8,128)S(1)}, f32[33,16,128]{2,1,0:T(8,128)S(1)}, u32[]{:S(2)}, u32[]{:S(2)}) %collective-permute-start.3) | collective-permute-done | bytes 270368 | tf_op jit(solution)/shard_map/ppermute | solution.py:70
  51.2 5.9 %collective-permute-done.4.refs_4_ = f32[33,16,128]{2,1,0:T(8,128)S(1)} collective-permute-done((f32[33,16,128]{2,1,0:T(8,128)S(1)}, f32[33,16,128]{2,1,0:T(8,128)S(1)}, u32[]{:S(2)}, u32[]{:S(2)}) %collective-permute-start.4) | collective-permute-done | bytes 270368 | tf_op jit(solution)/shard_map/ppermute | solution.py:70
  57.2 5.6 %collective-permute-done.5.refs_5_ = f32[33,16,128]{2,1,0:T(8,128)S(1)} collective-permute-done((f32[33,16,128]{2,1,0:T(8,128)S(1)}, f32[33,16,128]{2,1,0:T(8,128)S(1)}, u32[]{:S(2)}, u32[]{:S(2)}) %collective-permute-start.5) | collective-permute-done | bytes 270368 | tf_op jit(solution)/shard_map/ppermute | solution.py:70
  62.7 0.2 cut_kernel.1
  63.0 2.7 %collective-permute-start.8 = (f32[8,16,16,128]{3,2,1,0:T(8,128)S(1)}, f32[8,16,16,128]{3,2,1,0:T(8,128)S(1)}, u32[]{:S(2)}, u32[]{:S(2)}) collective-permute-start(f32[8,16,16,128]{3,2,1,0:T(8,128)S(1)} %get-tuple-element.43), channel_id=1, source_target_pairs={{32,40},{34,42},{36,44},{38,46},{39,47},{37,45},{35,43},{33,41},{4... | collective-permute-start | bytes 3145736 | tf_op jit(solution)/shard_map/ppermute | solution.py:70
  65.7 1.2 collective-permute-start.10
  66.9 0.3 collective-permute-start.11
  67.2 0.2 fusion.ty_ref.refs_9_
  67.4 2.9 %collective-permute-start.12 = (f32[2,8,16,128]{3,2,1,0:T(8,128)S(1)}, f32[2,8,16,128]{3,2,1,0:T(8,128)S(1)}, u32[]{:S(2)}, u32[]{:S(2)}) collective-permute-start(f32[2,8,16,128]{3,2,1,0:T(8,128)S(1)} %get-tuple-element.47), channel_id=1, source_target_pairs={{32,36},{34,38},{36,32},{38,34},{39,35},{37,33},{35,39},{33,37},{4... | collective-permute-start | bytes 393224 | tf_op jit(solution)/shard_map/ppermute | solution.py:70
  70.3 2.1 %first_kernel.1 = (f32[4,8,128,128]{3,2,1,0:T(8,128)S(1)}, f32[128,128]{1,0:T(8,128)S(1)}, f32[8,128]{1,0:T(8,128)S(1)}) custom-call(f32[33,16,128]{2,1,0:T(8,128)S(1)} %collective-permute-done.refs_0_, f32[33,16,128]{2,1,0:T(8,128)S(1)} %collective-permute-done.1.refs_1_, f32[33,16,128]{2,1,0:T(8,128)S(1)} %collective-permute-done.2.refs_2_, ...), custom_call_target="tpu_custom_call" | custom-call | flops 3000000000 | bytes 4194304 | tf_op jit(solution)/shard_map/first_kernel/pallas_call | solution.py:402
  72.5 13.4 %collective-permute-done.12.ring_ref = f32[2,8,16,128]{3,2,1,0:T(8,128)S(1)} collective-permute-done((f32[2,8,16,128]{3,2,1,0:T(8,128)S(1)}, f32[2,8,16,128]{3,2,1,0:T(8,128)S(1)}, u32[]{:S(2)}, u32[]{:S(2)}) %collective-permute-start.12) | collective-permute-done | bytes 131104 | tf_op jit(solution)/shard_map/ppermute | solution.py:70
  85.9 0.8 first_edge_kernel.1
  86.6 4.7 %collective-permute-start.17 = (f32[4,16,16,128]{3,2,1,0:T(8,128)S(1)}, f32[4,16,16,128]{3,2,1,0:T(8,128)S(1)}, u32[]{:S(2)}, u32[]{:S(2)}) collective-permute-start(f32[4,16,16,128]{3,2,1,0:T(8,128)S(1)} %get-tuple-element.55), channel_id=1, source_target_pairs={{32,40},{34,42},{36,44},{38,46},{39,47},{37,45},{35,43},{33,41},{4... | collective-permute-start | bytes 1572872 | tf_op jit(solution)/shard_map/ppermute | solution.py:70
  91.4 1.7 %collective-permute-start.13 = (f32[4,16,16,128]{3,2,1,0:T(8,128)S(1)}, f32[4,16,16,128]{3,2,1,0:T(8,128)S(1)}, u32[]{:S(2)}, u32[]{:S(2)}) collective-permute-start(f32[4,16,16,128]{3,2,1,0:T(8,128)S(1)} %get-tuple-element.51), channel_id=1, source_target_pairs={{32,40},{34,42},{36,44},{38,46},{39,47},{37,45},{35,43},{33,41},{4... | collective-permute-start | bytes 1572872 | tf_op jit(solution)/shard_map/ppermute | solution.py:70
  93.1 1.4 second_kernel.1.inner_ref
  94.5 3.0 %collective-permute-done.17.low_ref = f32[4,16,16,128]{3,2,1,0:T(8,128)S(1)} collective-permute-done((f32[4,16,16,128]{3,2,1,0:T(8,128)S(1)}, f32[4,16,16,128]{3,2,1,0:T(8,128)S(1)}, u32[]{:S(2)}, u32[]{:S(2)}) %collective-permute-start.17) | collective-permute-done | bytes 524320 | tf_op jit(solution)/shard_map/ppermute | solution.py:70
  97.5 2.8 %collective-permute-done.18.high_ref = f32[4,16,16,128]{3,2,1,0:T(8,128)S(1)} collective-permute-done((f32[4,16,16,128]{3,2,1,0:T(8,128)S(1)}, f32[4,16,16,128]{3,2,1,0:T(8,128)S(1)}, u32[]{:S(2)}, u32[]{:S(2)}) %collective-permute-start.18) | collective-permute-done | bytes 524320 | tf_op jit(solution)/shard_map/ppermute | solution.py:70
  100.3 0.1 second_edge_kernel.3
  100.4 0.0 copy-start.2
  100.4 2.1 %collective-permute-start.19 = (f32[4,8,16,128]{3,2,1,0:T(8,128)S(1)}, f32[4,8,16,128]{3,2,1,0:T(8,128)S(1)}, u32[]{:S(2)}, u32[]{:S(2)}) collective-permute-start(f32[4,8,16,128]{3,2,1,0:T(8,128)S(1)} %get-tuple-element.57), channel_id=1, source_target_pairs={{34,0},{35,1},{36,2},{37,3},{38,4},{39,5},{32,6},{33,7},{42,8},{43... | collective-permute-start | bytes 786440 | tf_op jit(solution)/shard_map/ppermute | solution.py:70
  102.5 4.5 %collective-permute-start.21 = (f32[4,8,16,128]{3,2,1,0:T(8,128)S(1)}, f32[4,8,16,128]{3,2,1,0:T(8,128)S(1)}, u32[]{:S(2)}, u32[]{:S(2)}) collective-permute-start(f32[4,8,16,128]{3,2,1,0:T(8,128)S(1)} %get-tuple-element.59), channel_id=1, source_target_pairs={{38,0},{39,1},{32,2},{33,3},{34,4},{35,5},{36,6},{37,7},{46,8},{47... | collective-permute-start | bytes 786440 | tf_op jit(solution)/shard_map/ppermute | solution.py:70
  107.1 1.2 collective-permute-start.22
  108.3 0.1 second_edge_kernel.2
  108.4 2.7 %collective-permute-start.15 = (f32[4,8,16,128]{3,2,1,0:T(8,128)S(1)}, f32[4,8,16,128]{3,2,1,0:T(8,128)S(1)}, u32[]{:S(2)}, u32[]{:S(2)}) collective-permute-start(f32[4,8,16,128]{3,2,1,0:T(8,128)S(1)} %get-tuple-element.53), channel_id=1, source_target_pairs={{36,0},{37,1},{38,2},{39,3},{32,4},{33,5},{34,6},{35,7},{44,8},{45... | collective-permute-start | bytes 786440 | tf_op jit(solution)/shard_map/ppermute | solution.py:70
  111.1 4.7 %collective-permute-done.19.refs_2_ = f32[4,8,16,128]{3,2,1,0:T(8,128)S(1)} collective-permute-done((f32[4,8,16,128]{3,2,1,0:T(8,128)S(1)}, f32[4,8,16,128]{3,2,1,0:T(8,128)S(1)}, u32[]{:S(2)}, u32[]{:S(2)}) %collective-permute-start.19) | collective-permute-done | bytes 262176 | tf_op jit(solution)/shard_map/ppermute | solution.py:70
  115.8 0.9 collective-permute-start.16
  116.7 21.2 %collective-permute-start.23 = (f32[4,8,16,128]{3,2,1,0:T(8,128)S(1)}, f32[4,8,16,128]{3,2,1,0:T(8,128)S(1)}, u32[]{:S(2)}, u32[]{:S(2)}) collective-permute-start(f32[4,8,16,128]{3,2,1,0:T(8,128)S(1)} %get-tuple-element.61), channel_id=1, source_target_pairs={{32,0},{33,1},{34,2},{35,3},{36,4},{37,5},{38,6},{39,7},{40,8},{41... | collective-permute-start | bytes 786440 | tf_op jit(solution)/shard_map/ppermute | solution.py:70
  137.8 6.4 %local_kernel.1.local_ref = f32[4,64,16,128]{3,2,1,0:T(8,128)S(1)} custom-call(f32[4,64,16,128]{3,2,1,0:T(8,128)S(1)} %copy-done.2, f32[64,128]{1,0:T(8,128)S(1)} %fusion.ty_ref.refs_9_, f32[1,128]{1,0:T(1,128)S(1)} %multiply_bitcast_fusion.vy_ref.refs_10_), custom_call_target="tpu_custom_call" | custom-call | flops 4000000000 | bytes 4194304 | tf_op jit(solution)/shard_map/local_kernel/pallas_call | solution.py:402
  144.3 0.0 collective-permute-done.16.refs_1_
  144.3 0.8 collective-permute-done.23.refs_6_
  145.2 10.7 %collective-permute-done.24.refs_7_ = f32[4,8,16,128]{3,2,1,0:T(8,128)S(1)} collective-permute-done((f32[4,8,16,128]{3,2,1,0:T(8,128)S(1)}, f32[4,8,16,128]{3,2,1,0:T(8,128)S(1)}, u32[]{:S(2)}, u32[]{:S(2)}) %collective-permute-start.24) | collective-permute-done | bytes 262176 | tf_op jit(solution)/shard_map/ppermute | solution.py:70
  155.9 1.9 %final_kernel.1 = f32[4,64,16,128]{3,2,1,0:T(8,128)} custom-call(f32[4,64,16,128]{3,2,1,0:T(8,128)S(1)} %local_kernel.1.local_ref, f32[4,8,16,128]{3,2,1,0:T(8,128)S(1)} %collective-permute-done.15.refs_0_, f32[4,8,16,128]{3,2,1,0:T(8,128)S(1)} %collective-permute-done.16.refs_1_, f32[4,8,16,128]{3,2,1,0:T(8,128)S(1)} %collective-permute-done.19.refs_2_, ...), custom_call_target="tpu_custom_call" | custom-call | bytes 6291456 | tf_op jit(solution)/shard_map/final_kernel/pallas_call | solution.py:471
  (31 shorter events, 0.1 us)
Async XLA Ops:
  0.0 67.2 %copy-start = (f32[64,128]{1,0:T(8,128)S(1)}, f32[64,128]{1,0:T(8,128)}, u32[]{:S(2)}) copy-start(f32[64,128]{1,0:T(8,128)} %param.11) | copy-start | bytes 98308
  0.8 1.6 %copy-start.1 = (f32[4,64,16,128]{3,2,1,0:T(8,128)S(1)}, f32[4,64,16,128]{3,2,1,0:T(8,128)}, u32[]{:S(2)}) copy-start(f32[4,64,16,128]{3,2,1,0:T(8,128)} %g_ref.3) | copy-start | bytes 6291460
  2.4 0.7 copy-start.3
  3.0 64.2 %copy-start.6 = (f32[128]{0:T(128)S(1)}, f32[128]{0:T(128)}, u32[]{:S(2)}) copy-start(f32[128]{0:T(128)} %param.13) | copy-start | bytes 1540
  3.0 64.2 %copy-start.7 = (s32[128]{0:T(128)S(1)}, s32[128]{0:T(128)}, u32[]{:S(2)}) copy-start(s32[128]{0:T(128)} %param.15) | copy-start | bytes 1540
  3.0 64.2 %copy-start.5 = (f32[128,128]{1,0:T(8,128)S(1)}, f32[128,128]{1,0:T(8,128)}, u32[]{:S(2)}) copy-start(f32[128,128]{1,0:T(8,128)} %constant.14.clone) | copy-start | bytes 196612
  3.0 67.3 %copy-start.4 = (f32[128,128]{1,0:T(8,128)S(1)}, f32[128,128]{1,0:T(8,128)}, u32[]{:S(2)}) copy-start(f32[128,128]{1,0:T(8,128)} %constant.15.clone.refs_8_) | copy-start | bytes 196612
  3.2 16.0 %collective-permute-start = (f32[33,16,128]{2,1,0:T(8,128)S(1)}, f32[33,16,128]{2,1,0:T(8,128)S(1)}, u32[]{:S(2)}, u32[]{:S(2)}) collective-permute-start(f32[33,16,128]{2,1,0:T(8,128)S(1)} %get-tuple-element.34), channel_id=1, source_target_pairs={{0,36},{1,37},{2,38},{3,39},{4,32},{5,33},{6,34},{7,35},{8,44},{9,... | collective-permute-start | bytes 811016 | tf_op jit(solution)/shard_map/ppermute | solution.py:70
  11.5 14.5 %collective-permute-start.1 = (f32[33,16,128]{2,1,0:T(8,128)S(1)}, f32[33,16,128]{2,1,0:T(8,128)S(1)}, u32[]{:S(2)}, u32[]{:S(2)}) collective-permute-start(f32[33,16,128]{2,1,0:T(8,128)S(1)} %get-tuple-element.35), channel_id=1, source_target_pairs={{0,37},{1,36},{2,39},{3,38},{4,33},{5,32},{6,35},{7,34},{8,45},{9,... | collective-permute-start | bytes 811016 | tf_op jit(solution)/shard_map/ppermute | solution.py:70
  12.0 17.4 %collective-permute-start.2 = (f32[33,16,128]{2,1,0:T(8,128)S(1)}, f32[33,16,128]{2,1,0:T(8,128)S(1)}, u32[]{:S(2)}, u32[]{:S(2)}) collective-permute-start(f32[33,16,128]{2,1,0:T(8,128)S(1)} %get-tuple-element.36), channel_id=1, source_target_pairs={{0,34},{1,35},{2,36},{3,37},{4,38},{5,39},{6,32},{7,33},{8,42},{9,... | collective-permute-start | bytes 811016 | tf_op jit(solution)/shard_map/ppermute | solution.py:70
  12.4 50.3 %collective-permute-start.6 = (f32[42,16,128]{2,1,0:T(8,128)S(1)}, f32[42,16,128]{2,1,0:T(8,128)S(1)}, u32[]{:S(2)}, u32[]{:S(2)}) collective-permute-start(f32[42,16,128]{2,1,0:T(8,128)S(1)} %get-tuple-element.40), channel_id=1, source_target_pairs={{0,32},{1,33},{2,34},{3,35},{4,36},{5,37},{6,38},{7,39},{8,40},{9,... | collective-permute-start | bytes 1032200 | tf_op jit(solution)/shard_map/ppermute | solution.py:70
  17.5 45.3 %collective-permute-start.7 = (f32[41,16,128]{2,1,0:T(8,128)S(1)}, f32[41,16,128]{2,1,0:T(8,128)S(1)}, u32[]{:S(2)}, u32[]{:S(2)}) collective-permute-start(f32[41,16,128]{2,1,0:T(8,128)S(1)} %get-tuple-element.41), channel_id=1, source_target_pairs={{0,33},{1,32},{2,35},{3,34},{4,37},{5,36},{6,39},{7,38},{8,41},{9,... | collective-permute-start | bytes 1007624 | tf_op jit(solution)/shard_map/ppermute | solution.py:70
  19.3 32.0 %collective-permute-start.3 = (f32[33,16,128]{2,1,0:T(8,128)S(1)}, f32[33,16,128]{2,1,0:T(8,128)S(1)}, u32[]{:S(2)}, u32[]{:S(2)}) collective-permute-start(f32[33,16,128]{2,1,0:T(8,128)S(1)} %get-tuple-element.37), channel_id=1, source_target_pairs={{0,35},{1,34},{2,37},{3,36},{4,39},{5,38},{6,33},{7,32},{8,43},{9,... | collective-permute-start | bytes 811016 | tf_op jit(solution)/shard_map/ppermute | solution.py:70
  26.0 31.2 %collective-permute-start.4 = (f32[33,16,128]{2,1,0:T(8,128)S(1)}, f32[33,16,128]{2,1,0:T(8,128)S(1)}, u32[]{:S(2)}, u32[]{:S(2)}) collective-permute-start(f32[33,16,128]{2,1,0:T(8,128)S(1)} %get-tuple-element.38), channel_id=1, source_target_pairs={{0,38},{1,39},{2,32},{3,33},{4,34},{5,35},{6,36},{7,37},{8,46},{9,... | collective-permute-start | bytes 811016 | tf_op jit(solution)/shard_map/ppermute | solution.py:70
  29.4 33.4 %collective-permute-start.5 = (f32[33,16,128]{2,1,0:T(8,128)S(1)}, f32[33,16,128]{2,1,0:T(8,128)S(1)}, u32[]{:S(2)}, u32[]{:S(2)}) collective-permute-start(f32[33,16,128]{2,1,0:T(8,128)S(1)} %get-tuple-element.39), channel_id=1, source_target_pairs={{0,39},{1,38},{2,33},{3,32},{4,35},{5,34},{6,37},{7,36},{8,47},{9,... | collective-permute-start | bytes 811016 | tf_op jit(solution)/shard_map/ppermute | solution.py:70
  63.0 22.9 %collective-permute-start.8 = (f32[8,16,16,128]{3,2,1,0:T(8,128)S(1)}, f32[8,16,16,128]{3,2,1,0:T(8,128)S(1)}, u32[]{:S(2)}, u32[]{:S(2)}) collective-permute-start(f32[8,16,16,128]{3,2,1,0:T(8,128)S(1)} %get-tuple-element.43), channel_id=1, source_target_pairs={{32,40},{34,42},{36,44},{38,46},{39,47},{37,45},{35,43},{33,41},{4... | collective-permute-start | bytes 3145736 | tf_op jit(solution)/shard_map/ppermute | solution.py:70
  65.7 20.1 %collective-permute-start.9 = (f32[8,16,16,128]{3,2,1,0:T(8,128)S(1)}, f32[8,16,16,128]{3,2,1,0:T(8,128)S(1)}, u32[]{:S(2)}, u32[]{:S(2)}) collective-permute-start(f32[8,16,16,128]{3,2,1,0:T(8,128)S(1)} %get-tuple-element.44), channel_id=1, source_target_pairs={{32,232},{34,234},{36,236},{38,238},{39,239},{37,237},{35,235},{33... | collective-permute-start | bytes 3145736 | tf_op jit(solution)/shard_map/ppermute | solution.py:70
  65.7 20.1 %collective-permute-start.10 = (f32[10,8,16,128]{3,2,1,0:T(8,128)S(1)}, f32[10,8,16,128]{3,2,1,0:T(8,128)S(1)}, u32[]{:S(2)}, u32[]{:S(2)}) collective-permute-start(f32[10,8,16,128]{3,2,1,0:T(8,128)S(1)} %get-tuple-element.45), channel_id=1, source_target_pairs={{32,34},{34,36},{36,38},{38,32},{39,37},{37,35},{35,33},{33,39},{4... | collective-permute-start | bytes 1966088 | tf_op jit(solution)/shard_map/ppermute | solution.py:70
  66.9 18.9 %collective-permute-start.11 = (f32[10,8,16,128]{3,2,1,0:T(8,128)S(1)}, f32[10,8,16,128]{3,2,1,0:T(8,128)S(1)}, u32[]{:S(2)}, u32[]{:S(2)}) collective-permute-start(f32[10,8,16,128]{3,2,1,0:T(8,128)S(1)} %get-tuple-element.46), channel_id=1, source_target_pairs={{32,38},{34,32},{36,34},{38,36},{39,33},{37,39},{35,37},{33,35},{4... | collective-permute-start | bytes 1966088 | tf_op jit(solution)/shard_map/ppermute | solution.py:70
  67.4 18.4 %collective-permute-start.12 = (f32[2,8,16,128]{3,2,1,0:T(8,128)S(1)}, f32[2,8,16,128]{3,2,1,0:T(8,128)S(1)}, u32[]{:S(2)}, u32[]{:S(2)}) collective-permute-start(f32[2,8,16,128]{3,2,1,0:T(8,128)S(1)} %get-tuple-element.47), channel_id=1, source_target_pairs={{32,36},{34,38},{36,32},{38,34},{39,35},{37,33},{35,39},{33,37},{4... | collective-permute-start | bytes 393224 | tf_op jit(solution)/shard_map/ppermute | solution.py:70
  86.6 10.9 %collective-permute-start.17 = (f32[4,16,16,128]{3,2,1,0:T(8,128)S(1)}, f32[4,16,16,128]{3,2,1,0:T(8,128)S(1)}, u32[]{:S(2)}, u32[]{:S(2)}) collective-permute-start(f32[4,16,16,128]{3,2,1,0:T(8,128)S(1)} %get-tuple-element.55), channel_id=1, source_target_pairs={{32,40},{34,42},{36,44},{38,46},{39,47},{37,45},{35,43},{33,41},{4... | collective-permute-start | bytes 1572872 | tf_op jit(solution)/shard_map/ppermute | solution.py:70
  91.4 8.9 %collective-permute-start.18 = (f32[4,16,16,128]{3,2,1,0:T(8,128)S(1)}, f32[4,16,16,128]{3,2,1,0:T(8,128)S(1)}, u32[]{:S(2)}, u32[]{:S(2)}) collective-permute-start(f32[4,16,16,128]{3,2,1,0:T(8,128)S(1)} %get-tuple-element.56), channel_id=1, source_target_pairs={{32,232},{34,234},{36,236},{38,238},{39,239},{37,237},{35,235},{33... | collective-permute-start | bytes 1572872 | tf_op jit(solution)/shard_map/ppermute | solution.py:70
  91.4 15.7 %collective-permute-start.13 = (f32[4,16,16,128]{3,2,1,0:T(8,128)S(1)}, f32[4,16,16,128]{3,2,1,0:T(8,128)S(1)}, u32[]{:S(2)}, u32[]{:S(2)}) collective-permute-start(f32[4,16,16,128]{3,2,1,0:T(8,128)S(1)} %get-tuple-element.51), channel_id=1, source_target_pairs={{32,40},{34,42},{36,44},{38,46},{39,47},{37,45},{35,43},{33,41},{4... | collective-permute-start | bytes 1572872 | tf_op jit(solution)/shard_map/ppermute | solution.py:70
  93.1 15.1 %collective-permute-start.14 = (f32[4,16,16,128]{3,2,1,0:T(8,128)S(1)}, f32[4,16,16,128]{3,2,1,0:T(8,128)S(1)}, u32[]{:S(2)}, u32[]{:S(2)}) collective-permute-start(f32[4,16,16,128]{3,2,1,0:T(8,128)S(1)} %get-tuple-element.52), channel_id=1, source_target_pairs={{32,232},{34,234},{36,236},{38,238},{39,239},{37,237},{35,235},{33... | collective-permute-start | bytes 1572872 | tf_op jit(solution)/shard_map/ppermute | solution.py:70
  100.4 37.4 %copy-start.2 = (f32[4,64,16,128]{3,2,1,0:T(8,128)S(1)}, f32[4,64,16,128]{3,2,1,0:T(8,128)}, u32[]{:S(2)}) copy-start(f32[4,64,16,128]{3,2,1,0:T(8,128)} %g_ref.3) | copy-start | bytes 6291460
  100.4 15.3 %collective-permute-start.19 = (f32[4,8,16,128]{3,2,1,0:T(8,128)S(1)}, f32[4,8,16,128]{3,2,1,0:T(8,128)S(1)}, u32[]{:S(2)}, u32[]{:S(2)}) collective-permute-start(f32[4,8,16,128]{3,2,1,0:T(8,128)S(1)} %get-tuple-element.57), channel_id=1, source_target_pairs={{34,0},{35,1},{36,2},{37,3},{38,4},{39,5},{32,6},{33,7},{42,8},{43... | collective-permute-start | bytes 786440 | tf_op jit(solution)/shard_map/ppermute | solution.py:70
  102.5 14.1 %collective-permute-start.20 = (f32[4,8,16,128]{3,2,1,0:T(8,128)S(1)}, f32[4,8,16,128]{3,2,1,0:T(8,128)S(1)}, u32[]{:S(2)}, u32[]{:S(2)}) collective-permute-start(f32[4,8,16,128]{3,2,1,0:T(8,128)S(1)} %get-tuple-element.58), channel_id=1, source_target_pairs={{35,0},{34,1},{37,2},{36,3},{39,4},{38,5},{33,6},{32,7},{43,8},{42... | collective-permute-start | bytes 786440 | tf_op jit(solution)/shard_map/ppermute | solution.py:70
  102.5 35.3 %collective-permute-start.21 = (f32[4,8,16,128]{3,2,1,0:T(8,128)S(1)}, f32[4,8,16,128]{3,2,1,0:T(8,128)S(1)}, u32[]{:S(2)}, u32[]{:S(2)}) collective-permute-start(f32[4,8,16,128]{3,2,1,0:T(8,128)S(1)} %get-tuple-element.59), channel_id=1, source_target_pairs={{38,0},{39,1},{32,2},{33,3},{34,4},{35,5},{36,6},{37,7},{46,8},{47... | collective-permute-start | bytes 786440 | tf_op jit(solution)/shard_map/ppermute | solution.py:70
  107.1 37.2 %collective-permute-start.22 = (f32[4,8,16,128]{3,2,1,0:T(8,128)S(1)}, f32[4,8,16,128]{3,2,1,0:T(8,128)S(1)}, u32[]{:S(2)}, u32[]{:S(2)}) collective-permute-start(f32[4,8,16,128]{3,2,1,0:T(8,128)S(1)} %get-tuple-element.60), channel_id=1, source_target_pairs={{39,0},{38,1},{33,2},{32,3},{35,4},{34,5},{37,6},{36,7},{47,8},{46... | collective-permute-start | bytes 786440 | tf_op jit(solution)/shard_map/ppermute | solution.py:70
  108.4 35.9 %collective-permute-start.15 = (f32[4,8,16,128]{3,2,1,0:T(8,128)S(1)}, f32[4,8,16,128]{3,2,1,0:T(8,128)S(1)}, u32[]{:S(2)}, u32[]{:S(2)}) collective-permute-start(f32[4,8,16,128]{3,2,1,0:T(8,128)S(1)} %get-tuple-element.53), channel_id=1, source_target_pairs={{36,0},{37,1},{38,2},{39,3},{32,4},{33,5},{34,6},{35,7},{44,8},{45... | collective-permute-start | bytes 786440 | tf_op jit(solution)/shard_map/ppermute | solution.py:70
  115.8 28.6 %collective-permute-start.16 = (f32[4,8,16,128]{3,2,1,0:T(8,128)S(1)}, f32[4,8,16,128]{3,2,1,0:T(8,128)S(1)}, u32[]{:S(2)}, u32[]{:S(2)}) collective-permute-start(f32[4,8,16,128]{3,2,1,0:T(8,128)S(1)} %get-tuple-element.54), channel_id=1, source_target_pairs={{37,0},{36,1},{39,2},{38,3},{33,4},{32,5},{35,6},{34,7},{45,8},{44... | collective-permute-start | bytes 786440 | tf_op jit(solution)/shard_map/ppermute | solution.py:70
  116.7 28.5 %collective-permute-start.23 = (f32[4,8,16,128]{3,2,1,0:T(8,128)S(1)}, f32[4,8,16,128]{3,2,1,0:T(8,128)S(1)}, u32[]{:S(2)}, u32[]{:S(2)}) collective-permute-start(f32[4,8,16,128]{3,2,1,0:T(8,128)S(1)} %get-tuple-element.61), channel_id=1, source_target_pairs={{32,0},{33,1},{34,2},{35,3},{36,4},{37,5},{38,6},{39,7},{40,8},{41... | collective-permute-start | bytes 786440 | tf_op jit(solution)/shard_map/ppermute | solution.py:70
  137.8 18.0 %collective-permute-start.24 = (f32[4,8,16,128]{3,2,1,0:T(8,128)S(1)}, f32[4,8,16,128]{3,2,1,0:T(8,128)S(1)}, u32[]{:S(2)}, u32[]{:S(2)}) collective-permute-start(f32[4,8,16,128]{3,2,1,0:T(8,128)S(1)} %get-tuple-element.62), channel_id=1, source_target_pairs={{33,0},{32,1},{35,2},{34,3},{37,4},{36,5},{39,6},{38,7},{41,8},{40... | collective-permute-start | bytes 786440 | tf_op jit(solution)/shard_map/ppermute | solution.py:70

commit v5 on v4

--- a/solution.py
+++ b/solution.py
@@ -28,8 +28,7 @@
     x, low, core = block // 8, block // 2 % 4, block % 2
     half = part // 4
     y = part if half == 0 else 7 - part
-    z = (low + 2 if x % 2 == 0 else 5 - low) + 4 * half
-    return flat(x, y, z % 8, core)
+    return flat(x, y, (low + 2 + 4 * (half ^ x % 2)) % 8, core)
 
 
 def part_of(y, half):
@@ -66,6 +65,14 @@
     ]
 
 
+def middle_pairs(y):
+    return [
+        (place(block, part_of(y, half)), place(block, part_of(3, half)))
+        for block in range(32)
+        for half in range(2)
+    ]
+
+
 def send(value, pairs):
     return lax.ppermute(value, AXES, pairs)
 
@@ -78,8 +85,8 @@
 def as_host():
     gx, ka = lax.axis_index("gx"), lax.axis_index("ka")
     z = (ka & 1) * 4 + ((gx >> 1) & 3)
-    turn = jnp.where(((gx >> 3) & 1) == 0, z - 2, 5 - z) & 7
-    return ka >> 1, turn >> 2, (gx & 25) + (turn & 3) * 2
+    turn = (z - 2) & 7
+    return ka >> 1, (turn >> 2) ^ ((gx >> 3) & 1), (gx & 25) + (turn & 3) * 2
 
 
 def part_index(y, half):
@@ -211,20 +218,24 @@
     pieces[FIRST][41, 4:16] = jnp.zeros((12, K), F32)
 
 
+def across_kernel(first_ref, second_ref, out_ref):
+    out_ref[0] = first_ref[33:41]
+    out_ref[1] = second_ref[33:41]
+
+
 def cut_kernel(*refs):
-    pieces, (head_ref, tail_ref, y_low_ref, y_high_ref, across_ref) = refs[:8], refs[8:]
-    for i in range(8):
+    pieces, (head_ref, tail_ref) = refs[:4], refs[4:]
+    for i in range(4):
         head_ref[i] = pieces[i][0:16]
         tail_ref[i] = pieces[i][16:32]
-        for x in range(4):
-            y_low_ref[i, 2 * x : 2 * x + 2] = pieces[i][8 * x : 8 * x + 2]
-            y_high_ref[i, 2 * x : 2 * x + 2] = pieces[i][8 * x + 6 : 8 * x + 8]
-        dy, ds = SLOTS[i]
-        if dy == 0:
-            rows = pieces[i][33:41]
-            y_low_ref[8 + ds] = rows
-            y_high_ref[8 + ds] = rows
-            across_ref[ds] = rows
+
+
+def rows_kernel(*refs):
+    pieces, (bottom_ref, top_ref) = refs[:8], refs[8:]
+    for slot in range(8):
+        for x in range(4):
+            bottom_ref[slot, 2 * x : 2 * x + 2] = pieces[slot][8 * x : 8 * x + 2]
+            top_ref[slot, 2 * x : 2 * x + 2] = pieces[slot][8 * x + 6 : 8 * x + 8]
 
 
 def inner_drift(center, x, layer, toward, rate):
@@ -299,7 +310,7 @@
 
 
 def first_edge_kernel(
-    inner_ref, low_ref, high_ref, under_ref, over_ref, ring_ref, own_0_ref, own_1_ref, vx_ref, vy_ref, v_ref, *outs
+    inner_ref, low_a_ref, low_b_ref, high_a_ref, high_b_ref, under_ref, over_ref, from_0_ref, from_1_ref, from_2_ref, own_0_ref, own_1_ref, vx_ref, vy_ref, v_ref, *outs
 ):
     y_place, half, block = as_host()
     middle = jnp.where(y_place == 3, 1.0, 0.0)
@@ -315,14 +326,15 @@
         dy, ds = SLOTS[slot]
         at = kx_of(slot)
         up, down = rates(vx_ref, at, 0.0625)
+        group = int(slot in GROUPS[1])
+        i = GROUPS[group].index(slot)
+        low_ref, high_ref = ((low_a_ref, high_a_ref), (low_b_ref, high_b_ref))[group]
         for x in range(4):
             rows = slice(2 * x, 2 * x + 2)
             if dy == 0:
                 across = (own_0_ref, own_1_ref)[ds][33 + 2 * x : 35 + 2 * x]
-            elif dy == 2:
-                across = ring_ref[ds, rows]
             else:
-                across = jnp.where(half == dy // 3, under_ref[8 + ds, rows], over_ref[8 + ds, rows])
+                across = (from_2_ref, from_1_ref, from_0_ref)[dy - 1][ds, rows]
             before, after = ((dy + 3) % 4, ds), ((dy + 1) % 4, ds)
             under = jnp.where(half == 0, beside(under_ref, before, rows), beside(under_ref, after, rows))
             over = jnp.where(half == 0, beside(over_ref, after, rows), beside(over_ref, before, rows))
@@ -330,8 +342,8 @@
             over = jnp.where(over_middle, across * middle, over)
             value = inner_ref[x, :, at, :] + outer_drift(
                 x,
-                lambda n: low_ref[slot, 8 - 8 * n : 16 - 8 * n],
-                lambda n: high_ref[slot, 8 * n : 8 * n + 8],
+                lambda n: low_ref[i, 8 - 8 * n : 16 - 8 * n],
+                lambda n: high_ref[i, 8 * n : 8 * n + 8],
                 up,
                 down,
             )
@@ -339,9 +351,8 @@
             top = jnp.concatenate([-down_y * over[0:1], down_y * (4.0 * over[0:1] - over[1:2])], 0)
             value = jnp.concatenate([value[0:2] + bottom, value[2:6], value[6:8] + top], 0)
             v_ref[x, :, at, :] = value
-            group = int(slot in GROUPS[1])
             side = outs[2 * group + x // 2]
-            side[GROUPS[group].index(slot), 8 * (x % 2) : 8 * (x % 2) + 8] = value
+            side[i, 8 * (x % 2) : 8 * (x % 2) + 8] = value
 
 
 def second_kernel(v_ref, tx_ref, vx_ref, out_ref, tables):
@@ -438,12 +449,18 @@
         local_kernel, array(4, 64, 16, K), [pltpu.VMEM((2, 4, 68, 16, K), F32)], 4 * 10**9
     )(density, ty, vy)
 
-    head, tail, y_low, y_high, across = call(
-        cut_kernel, [array(8, 16, 16, K)] * 2 + [array(10, 8, 16, K)] * 2 + [array(2, 8, 16, K)]
-    )(*pieces)
+    across = call(across_kernel, array(2, 8, 16, K), mib=0)(pieces[FIRST], pieces[SECOND])
+    across = [send(across, middle_pairs(y)) for y in range(3)]
+    low, high = [None] * 2, [None] * 2
+    for group in (1, 0):
+        mine = [pieces[slot] for slot in GROUPS[group]]
+        if group == 0:
+            *mine, low[1], high[1], across[0], across[1], across[2] = lax.optimization_barrier((*mine, low[1], high[1], *across))
+        head, tail = call(cut_kernel, [array(4, 16, 16, K)] * 2, mib=2)(*mine)
+        low[group] = send(tail, x_pairs(1))
+        high[group] = send(head, x_pairs(-1))
+    y_low, y_high = call(rows_kernel, [array(8, 8, 16, K)] * 2, mib=2)(*pieces)
     under, over = send(y_high, y_pairs(1)), send(y_low, y_pairs(-1))
-    low, high = send(tail, x_pairs(1)), send(head, x_pairs(-1))
-    across = send(across, y_pairs(2))
     left_tables = pltpu.VMEM((4, 2 * K, 2 * K), BF16)
     inner, vx, tx = call(
         first_kernel,
@@ -452,7 +469,7 @@
         3 * 10**9,
     )(*pieces, jnp.asarray(sine_table(-1)), ty, vy)
     v, *sides = call(first_edge_kernel, [array(4, 8, K, K)] + [array(4, 16, 16, K)] * 4)(
-        inner, low, high, under, over, across, pieces[FIRST], pieces[SECOND], vx, vy
+        inner, *low, *high, under, over, *across, pieces[FIRST], pieces[SECOND], vx, vy
     )
     low = [send(sides[2 * group + 1], x_pairs(1)) for group in range(2)]
     high = [send(sides[2 * group], x_pairs(-1)) for group in range(2)]

time: 160 us -> 167 us (1.044); the launches traced: 158 us -> 167 us
  waiting for transfers between devices: 75.1 us -> 91 us
  starting transfers between devices: 66 us -> 58.8 us
    ppermute x25 -> x29, waiting for transfers between devices: 75.1 us -> 91 us  [send(): return lax.ppermute(value, AXES, pairs)]
    ppermute x25 -> x29, starting transfers between devices: 66 us -> 58.8 us  [send(): return lax.ppermute(value, AXES, pairs)]
    pallas_call x8 -> x11, Pallas kernels: 11.4 us -> 11.4 us  [run(): pl.pallas_call(kernel, out_shape=outs, in_specs=[VMEM] * len(operands), o...]
  transfers between devices with their start and end apart: 25 -> 29, of which waited for: 12 -> 15; matrix products, arithmetic and copies ran while one was open for 0% -> 0% of each run, Pallas kernels for 6% -> 6%
where the time goes in v5:
time: 167 us
  waiting for transfers between devices  91 us (54%)
  starting transfers between devices  58.8 us (35%)
  Pallas kernels  13.4 us (8%)
  local copies, waits for them, and re-layouts  2.37 us (1%)
    ppermute x29, waiting for transfers between devices, send(): return lax.ppermute(value, AXES, pairs)  91 us
    ppermute x29, starting transfers between devices, send(): return lax.ppermute(value, AXES, pairs)  58.8 us
    pallas_call x11, Pallas kernels, run(): pl.pallas_call(kernel, out_shape=outs, in_specs=[VMEM] * len(operands), o...  11.4 us
  transfers between devices with their start and end apart: 29, of which 15 were waited for; matrix products, arithmetic and copies ran while one was open for 0% of the time, Pallas kernels for 6%

profile of v5, /device:TPU:39, one launch (start us, length us, event | category | flops | bytes accessed | tf_op | source)
XLA Modules:
  0.0 166.6 jit_solution(4877966821473894956)
XLA Ops:
  0.0 0.7 convert_multiply_fusion
  0.8 1.6 copy-done.1
  2.4 0.7 copy-done.3
  3.0 0.1 pack_kernel.1
  3.2 5.2 %collective-permute-start.6 = (f32[42,16,128]{2,1,0:T(8,128)S(1)}, f32[42,16,128]{2,1,0:T(8,128)S(1)}, u32[]{:S(2)}, u32[]{:S(2)}) collective-permute-start(f32[42,16,128]{2,1,0:T(8,128)S(1)} %get-tuple-element.50), channel_id=1, source_target_pairs={{0,32},{1,33},{2,34},{3,35},{4,36},{5,37},{6,38},{7,39},{8,40},{9,... | collective-permute-start | bytes 1032200 | tf_op jit(solution)/shard_map/ppermute | solution.py:77
  8.4 6.2 %collective-permute-start = (f32[33,16,128]{2,1,0:T(8,128)S(1)}, f32[33,16,128]{2,1,0:T(8,128)S(1)}, u32[]{:S(2)}, u32[]{:S(2)}) collective-permute-start(f32[33,16,128]{2,1,0:T(8,128)S(1)} %get-tuple-element.44), channel_id=1, source_target_pairs={{0,36},{1,37},{2,38},{3,39},{4,32},{5,33},{6,34},{7,35},{8,44},{9,... | collective-permute-start | bytes 811016 | tf_op jit(solution)/shard_map/ppermute | solution.py:77
  14.6 4.4 %collective-permute-start.2 = (f32[33,16,128]{2,1,0:T(8,128)S(1)}, f32[33,16,128]{2,1,0:T(8,128)S(1)}, u32[]{:S(2)}, u32[]{:S(2)}) collective-permute-start(f32[33,16,128]{2,1,0:T(8,128)S(1)} %get-tuple-element.46), channel_id=1, source_target_pairs={{0,34},{1,35},{2,36},{3,37},{4,38},{5,39},{6,32},{7,33},{8,42},{9,... | collective-permute-start | bytes 811016 | tf_op jit(solution)/shard_map/ppermute | solution.py:77
  19.0 9.8 %collective-permute-done.refs_0_ = f32[33,16,128]{2,1,0:T(8,128)S(1)} collective-permute-done((f32[33,16,128]{2,1,0:T(8,128)S(1)}, f32[33,16,128]{2,1,0:T(8,128)S(1)}, u32[]{:S(2)}, u32[]{:S(2)}) %collective-permute-start) | collective-permute-done | bytes 270368 | tf_op jit(solution)/shard_map/ppermute | solution.py:77
  28.8 13.5 %collective-permute-done.1.refs_1_ = f32[33,16,128]{2,1,0:T(8,128)S(1)} collective-permute-done((f32[33,16,128]{2,1,0:T(8,128)S(1)}, f32[33,16,128]{2,1,0:T(8,128)S(1)}, u32[]{:S(2)}, u32[]{:S(2)}) %collective-permute-start.1) | collective-permute-done | bytes 270368 | tf_op jit(solution)/shard_map/ppermute | solution.py:77
  42.4 0.7 collective-permute-start.8
  43.1 0.9 collective-permute-start.9
  44.0 3.9 %collective-permute-start.3 = (f32[33,16,128]{2,1,0:T(8,128)S(1)}, f32[33,16,128]{2,1,0:T(8,128)S(1)}, u32[]{:S(2)}, u32[]{:S(2)}) collective-permute-start(f32[33,16,128]{2,1,0:T(8,128)S(1)} %get-tuple-element.47), channel_id=1, source_target_pairs={{0,35},{1,34},{2,37},{3,36},{4,39},{5,38},{6,33},{7,32},{8,43},{9,... | collective-permute-start | bytes 811016 | tf_op jit(solution)/shard_map/ppermute | solution.py:77
  47.9 1.8 %collective-permute-start.4 = (f32[33,16,128]{2,1,0:T(8,128)S(1)}, f32[33,16,128]{2,1,0:T(8,128)S(1)}, u32[]{:S(2)}, u32[]{:S(2)}) collective-permute-start(f32[33,16,128]{2,1,0:T(8,128)S(1)} %get-tuple-element.48), channel_id=1, source_target_pairs={{0,38},{1,39},{2,32},{3,33},{4,34},{5,35},{6,36},{7,37},{8,46},{9,... | collective-permute-start | bytes 811016 | tf_op jit(solution)/shard_map/ppermute | solution.py:77
  49.7 2.0 %collective-permute-start.5 = (f32[33,16,128]{2,1,0:T(8,128)S(1)}, f32[33,16,128]{2,1,0:T(8,128)S(1)}, u32[]{:S(2)}, u32[]{:S(2)}) collective-permute-start(f32[33,16,128]{2,1,0:T(8,128)S(1)} %get-tuple-element.49), channel_id=1, source_target_pairs={{0,39},{1,38},{2,33},{3,32},{4,35},{5,34},{6,37},{7,36},{8,47},{9,... | collective-permute-start | bytes 811016 | tf_op jit(solution)/shard_map/ppermute | solution.py:77
  51.7 17.8 %collective-permute-done.3.refs_3_.refs_1_ = f32[33,16,128]{2,1,0:T(8,128)S(1)} collective-permute-done((f32[33,16,128]{2,1,0:T(8,128)S(1)}, f32[33,16,128]{2,1,0:T(8,128)S(1)}, u32[]{:S(2)}, u32[]{:S(2)}) %collective-permute-start.3) | collective-permute-done | bytes 270368 | tf_op jit(solution)/shard_map/ppermute | solution.py:77
  69.4 1.3 collective-permute-start.10
  70.8 0.7 collective-permute-start.11
  71.4 4.4 %collective-permute-done.5.refs_5_.refs_3_ = f32[33,16,128]{2,1,0:T(8,128)S(1)} collective-permute-done((f32[33,16,128]{2,1,0:T(8,128)S(1)}, f32[33,16,128]{2,1,0:T(8,128)S(1)}, u32[]{:S(2)}, u32[]{:S(2)}) %collective-permute-start.5) | collective-permute-done | bytes 270368 | tf_op jit(solution)/shard_map/ppermute | solution.py:77
  75.8 0.7 collective-permute-start.12
  76.7 3.1 %collective-permute-start.16 = (f32[8,8,16,128]{3,2,1,0:T(8,128)S(1)}, f32[8,8,16,128]{3,2,1,0:T(8,128)S(1)}, u32[]{:S(2)}, u32[]{:S(2)}) collective-permute-start(f32[8,8,16,128]{3,2,1,0:T(8,128)S(1)} %get-tuple-element.64), channel_id=1, source_target_pairs={{32,38},{34,32},{36,34},{38,36},{39,33},{37,39},{35,37},{33,35},{4... | collective-permute-start | bytes 1572872 | tf_op jit(solution)/shard_map/ppermute | solution.py:77
  79.8 6.2 %collective-permute-start.13 = (f32[4,16,16,128]{3,2,1,0:T(8,128)S(1)}, f32[4,16,16,128]{3,2,1,0:T(8,128)S(1)}, u32[]{:S(2)}, u32[]{:S(2)}) collective-permute-start(f32[4,16,16,128]{3,2,1,0:T(8,128)S(1)} %get-tuple-element.59), channel_id=1, source_target_pairs={{32,40},{34,42},{36,44},{38,46},{39,47},{37,45},{35,43},{33,41},{4... | collective-permute-start | bytes 1572872 | tf_op jit(solution)/shard_map/ppermute | solution.py:77
  86.0 0.2 fusion.ty_ref.refs_9_
  86.2 2.1 %first_kernel.1 = (f32[4,8,128,128]{3,2,1,0:T(8,128)S(1)}, f32[128,128]{1,0:T(8,128)S(1)}, f32[8,128]{1,0:T(8,128)S(1)}) custom-call(f32[33,16,128]{2,1,0:T(8,128)S(1)} %collective-permute-done.refs_0_, f32[33,16,128]{2,1,0:T(8,128)S(1)} %collective-permute-done.1.refs_1_, f32[33,16,128]{2,1,0:T(8,128)S(1)} %collective-permute-done.2.refs_2_.refs_0_, ...), custom_call_target="tpu_custom_call" | custom-call | flops 3000000000 | bytes 4194304 | tf_op jit(solution)/shard_map/first_kernel/pallas_call | solution.py:413
  88.4 2.7 %collective-permute-done.15.under_ref = f32[8,8,16,128]{3,2,1,0:T(8,128)S(1)} collective-permute-done((f32[8,8,16,128]{3,2,1,0:T(8,128)S(1)}, f32[8,8,16,128]{3,2,1,0:T(8,128)S(1)}, u32[]{:S(2)}, u32[]{:S(2)}) %collective-permute-start.15) | collective-permute-done | bytes 524320 | tf_op jit(solution)/shard_map/ppermute | solution.py:77
  91.1 1.0 collective-permute-done.13.low_a_ref
  92.1 4.6 %collective-permute-done.14.high_a_ref = f32[4,16,16,128]{3,2,1,0:T(8,128)S(1)} collective-permute-done((f32[4,16,16,128]{3,2,1,0:T(8,128)S(1)}, f32[4,16,16,128]{3,2,1,0:T(8,128)S(1)}, u32[]{:S(2)}, u32[]{:S(2)}) %collective-permute-start.14) | collective-permute-done | bytes 524320 | tf_op jit(solution)/shard_map/ppermute | solution.py:77
  96.7 0.8 first_edge_kernel.1
  97.6 0.5 collective-permute-start.22
  98.1 3.4 %collective-permute-start.17 = (f32[4,16,16,128]{3,2,1,0:T(8,128)S(1)}, f32[4,16,16,128]{3,2,1,0:T(8,128)S(1)}, u32[]{:S(2)}, u32[]{:S(2)}) collective-permute-start(f32[4,16,16,128]{3,2,1,0:T(8,128)S(1)} %get-tuple-element.71), channel_id=1, source_target_pairs={{32,40},{34,42},{36,44},{38,46},{39,47},{37,45},{35,43},{33,41},{4... | collective-permute-start | bytes 1572872 | tf_op jit(solution)/shard_map/ppermute | solution.py:77
  101.5 1.4 second_kernel.1.inner_ref
  103.0 0.7 collective-permute-done.21.low_ref
  103.7 4.7 %collective-permute-done.22.high_ref = f32[4,16,16,128]{3,2,1,0:T(8,128)S(1)} collective-permute-done((f32[4,16,16,128]{3,2,1,0:T(8,128)S(1)}, f32[4,16,16,128]{3,2,1,0:T(8,128)S(1)}, u32[]{:S(2)}, u32[]{:S(2)}) %collective-permute-start.22) | collective-permute-done | bytes 524320 | tf_op jit(solution)/shard_map/ppermute | solution.py:77
  108.4 0.1 second_edge_kernel.3
  108.5 5.6 %collective-permute-start.23 = (f32[4,8,16,128]{3,2,1,0:T(8,128)S(1)}, f32[4,8,16,128]{3,2,1,0:T(8,128)S(1)}, u32[]{:S(2)}, u32[]{:S(2)}) collective-permute-start(f32[4,8,16,128]{3,2,1,0:T(8,128)S(1)} %get-tuple-element.77), channel_id=1, source_target_pairs={{34,0},{35,1},{36,2},{37,3},{38,4},{39,5},{32,6},{33,7},{42,8},{43... | collective-permute-start | bytes 786440 | tf_op jit(solution)/shard_map/ppermute | solution.py:77
  114.1 3.3 %collective-permute-start.25 = (f32[4,8,16,128]{3,2,1,0:T(8,128)S(1)}, f32[4,8,16,128]{3,2,1,0:T(8,128)S(1)}, u32[]{:S(2)}, u32[]{:S(2)}) collective-permute-start(f32[4,8,16,128]{3,2,1,0:T(8,128)S(1)} %get-tuple-element.79), channel_id=1, source_target_pairs={{38,0},{39,1},{32,2},{33,3},{34,4},{35,5},{36,6},{37,7},{46,8},{47... | collective-permute-start | bytes 786440 | tf_op jit(solution)/shard_map/ppermute | solution.py:77
  117.4 0.3 collective-permute-start.26
  117.7 16.2 %collective-permute-done.18.high_ref = f32[4,16,16,128]{3,2,1,0:T(8,128)S(1)} collective-permute-done((f32[4,16,16,128]{3,2,1,0:T(8,128)S(1)}, f32[4,16,16,128]{3,2,1,0:T(8,128)S(1)}, u32[]{:S(2)}, u32[]{:S(2)}) %collective-permute-start.18) | collective-permute-done | bytes 524320 | tf_op jit(solution)/shard_map/ppermute | solution.py:77
  133.9 0.1 second_edge_kernel.2
  134.1 0.2 collective-permute-done.23.refs_2_
  134.3 5.8 %collective-permute-start.20 = (f32[4,8,16,128]{3,2,1,0:T(8,128)S(1)}, f32[4,8,16,128]{3,2,1,0:T(8,128)S(1)}, u32[]{:S(2)}, u32[]{:S(2)}) collective-permute-start(f32[4,8,16,128]{3,2,1,0:T(8,128)S(1)} %get-tuple-element.74), channel_id=1, source_target_pairs={{37,0},{36,1},{39,2},{38,3},{33,4},{32,5},{35,6},{34,7},{45,8},{44... | collective-permute-start | bytes 786440 | tf_op jit(solution)/shard_map/ppermute | solution.py:77
  140.1 0.4 collective-permute-start.27
  140.5 2.3 %collective-permute-done.25.refs_4_ = f32[4,8,16,128]{3,2,1,0:T(8,128)S(1)} collective-permute-done((f32[4,8,16,128]{3,2,1,0:T(8,128)S(1)}, f32[4,8,16,128]{3,2,1,0:T(8,128)S(1)}, u32[]{:S(2)}, u32[]{:S(2)}) %collective-permute-start.25) | collective-permute-done | bytes 262176 | tf_op jit(solution)/shard_map/ppermute | solution.py:77
  142.8 2.4 %collective-permute-start.28 = (f32[4,8,16,128]{3,2,1,0:T(8,128)S(1)}, f32[4,8,16,128]{3,2,1,0:T(8,128)S(1)}, u32[]{:S(2)}, u32[]{:S(2)}) collective-permute-start(f32[4,8,16,128]{3,2,1,0:T(8,128)S(1)} %get-tuple-element.82), channel_id=1, source_target_pairs={{33,0},{32,1},{35,2},{34,3},{37,4},{36,5},{39,6},{38,7},{41,8},{40... | collective-permute-start | bytes 786440 | tf_op jit(solution)/shard_map/ppermute | solution.py:77
  145.2 6.4 %local_kernel.1.local_ref = f32[4,64,16,128]{3,2,1,0:T(8,128)S(1)} custom-call(f32[4,64,16,128]{3,2,1,0:T(8,128)S(1)} %copy-done.2, f32[64,128]{1,0:T(8,128)S(1)} %fusion.ty_ref.refs_9_, f32[1,128]{1,0:T(1,128)S(1)} %multiply_bitcast_fusion.vy_ref.refs_10_), custom_call_target="tpu_custom_call" | custom-call | flops 4000000000 | bytes 4194304 | tf_op jit(solution)/shard_map/local_kernel/pallas_call | solution.py:413
  151.6 3.8 %collective-permute-done.26.refs_5_ = f32[4,8,16,128]{3,2,1,0:T(8,128)S(1)} collective-permute-done((f32[4,8,16,128]{3,2,1,0:T(8,128)S(1)}, f32[4,8,16,128]{3,2,1,0:T(8,128)S(1)}, u32[]{:S(2)}, u32[]{:S(2)}) %collective-permute-start.26) | collective-permute-done | bytes 262176 | tf_op jit(solution)/shard_map/ppermute | solution.py:77
  155.4 2.1 %collective-permute-done.20.refs_1_ = f32[4,8,16,128]{3,2,1,0:T(8,128)S(1)} collective-permute-done((f32[4,8,16,128]{3,2,1,0:T(8,128)S(1)}, f32[4,8,16,128]{3,2,1,0:T(8,128)S(1)}, u32[]{:S(2)}, u32[]{:S(2)}) %collective-permute-start.20) | collective-permute-done | bytes 262176 | tf_op jit(solution)/shard_map/ppermute | solution.py:77
  157.5 7.2 %collective-permute-done.28.refs_7_ = f32[4,8,16,128]{3,2,1,0:T(8,128)S(1)} collective-permute-done((f32[4,8,16,128]{3,2,1,0:T(8,128)S(1)}, f32[4,8,16,128]{3,2,1,0:T(8,128)S(1)}, u32[]{:S(2)}, u32[]{:S(2)}) %collective-permute-start.28) | collective-permute-done | bytes 262176 | tf_op jit(solution)/shard_map/ppermute | solution.py:77
  164.7 1.9 %final_kernel.1 = f32[4,64,16,128]{3,2,1,0:T(8,128)} custom-call(f32[4,64,16,128]{3,2,1,0:T(8,128)S(1)} %local_kernel.1.local_ref, f32[4,8,16,128]{3,2,1,0:T(8,128)S(1)} %collective-permute-done.19.refs_0_, f32[4,8,16,128]{3,2,1,0:T(8,128)S(1)} %collective-permute-done.20.refs_1_, f32[4,8,16,128]{3,2,1,0:T(8,128)S(1)} %collective-permute-done.23.refs_2_, ...), custom_call_target="tpu_custom_call" | custom-call | bytes 6291456 | tf_op jit(solution)/shard_map/final_kernel/pallas_call | solution.py:488
  (42 shorter events, 0.6 us)
Async XLA Ops:
  0.0 86.0 %copy-start = (f32[64,128]{1,0:T(8,128)S(1)}, f32[64,128]{1,0:T(8,128)}, u32[]{:S(2)}) copy-start(f32[64,128]{1,0:T(8,128)} %param.11) | copy-start | bytes 98308
  0.8 1.6 copy-start.1
  2.4 0.7 copy-start.3
  3.2 39.1 %collective-permute-start.6 = (f32[42,16,128]{2,1,0:T(8,128)S(1)}, f32[42,16,128]{2,1,0:T(8,128)S(1)}, u32[]{:S(2)}, u32[]{:S(2)}) collective-permute-start(f32[42,16,128]{2,1,0:T(8,128)S(1)} %get-tuple-element.50), channel_id=1, source_target_pairs={{0,32},{1,33},{2,34},{3,35},{4,36},{5,37},{6,38},{7,39},{8,40},{9,... | collective-permute-start | bytes 1032200 | tf_op jit(solution)/shard_map/ppermute | solution.py:77
  8.4 33.9 %collective-permute-start.7 = (f32[41,16,128]{2,1,0:T(8,128)S(1)}, f32[41,16,128]{2,1,0:T(8,128)S(1)}, u32[]{:S(2)}, u32[]{:S(2)}) collective-permute-start(f32[41,16,128]{2,1,0:T(8,128)S(1)} %get-tuple-element.51), channel_id=1, source_target_pairs={{0,33},{1,32},{2,35},{3,34},{4,37},{5,36},{6,39},{7,38},{8,41},{9,... | collective-permute-start | bytes 1007624 | tf_op jit(solution)/shard_map/ppermute | solution.py:77
  8.4 20.4 %collective-permute-start = (f32[33,16,128]{2,1,0:T(8,128)S(1)}, f32[33,16,128]{2,1,0:T(8,128)S(1)}, u32[]{:S(2)}, u32[]{:S(2)}) collective-permute-start(f32[33,16,128]{2,1,0:T(8,128)S(1)} %get-tuple-element.44), channel_id=1, source_target_pairs={{0,36},{1,37},{2,38},{3,39},{4,32},{5,33},{6,34},{7,35},{8,44},{9,... | collective-permute-start | bytes 811016 | tf_op jit(solution)/shard_map/ppermute | solution.py:77
  14.6 27.7 %collective-permute-start.1 = (f32[33,16,128]{2,1,0:T(8,128)S(1)}, f32[33,16,128]{2,1,0:T(8,128)S(1)}, u32[]{:S(2)}, u32[]{:S(2)}) collective-permute-start(f32[33,16,128]{2,1,0:T(8,128)S(1)} %get-tuple-element.45), channel_id=1, source_target_pairs={{0,37},{1,36},{2,39},{3,38},{4,33},{5,32},{6,35},{7,34},{8,45},{9,... | collective-permute-start | bytes 811016 | tf_op jit(solution)/shard_map/ppermute | solution.py:77
  14.6 35.1 %collective-permute-start.2 = (f32[33,16,128]{2,1,0:T(8,128)S(1)}, f32[33,16,128]{2,1,0:T(8,128)S(1)}, u32[]{:S(2)}, u32[]{:S(2)}) collective-permute-start(f32[33,16,128]{2,1,0:T(8,128)S(1)} %get-tuple-element.46), channel_id=1, source_target_pairs={{0,34},{1,35},{2,36},{3,37},{4,38},{5,39},{6,32},{7,33},{8,42},{9,... | collective-permute-start | bytes 811016 | tf_op jit(solution)/shard_map/ppermute | solution.py:77
  42.4 37.4 %collective-permute-start.8 = (f32[4,16,16,128]{3,2,1,0:T(8,128)S(1)}, f32[4,16,16,128]{3,2,1,0:T(8,128)S(1)}, u32[]{:S(2)}, u32[]{:S(2)}) collective-permute-start(f32[4,16,16,128]{3,2,1,0:T(8,128)S(1)} %get-tuple-element.53), channel_id=1, source_target_pairs={{32,40},{34,42},{36,44},{38,46},{39,47},{37,45},{35,43},{33,41},{4... | collective-permute-start | bytes 1572872 | tf_op jit(solution)/shard_map/ppermute | solution.py:77
  43.1 36.7 %collective-permute-start.9 = (f32[4,16,16,128]{3,2,1,0:T(8,128)S(1)}, f32[4,16,16,128]{3,2,1,0:T(8,128)S(1)}, u32[]{:S(2)}, u32[]{:S(2)}) collective-permute-start(f32[4,16,16,128]{3,2,1,0:T(8,128)S(1)} %get-tuple-element.54), channel_id=1, source_target_pairs={{32,216},{34,218},{36,220},{38,222},{39,223},{37,221},{35,219},{33... | collective-permute-start | bytes 1572872 | tf_op jit(solution)/shard_map/ppermute | solution.py:77
  44.0 25.5 %collective-permute-start.3 = (f32[33,16,128]{2,1,0:T(8,128)S(1)}, f32[33,16,128]{2,1,0:T(8,128)S(1)}, u32[]{:S(2)}, u32[]{:S(2)}) collective-permute-start(f32[33,16,128]{2,1,0:T(8,128)S(1)} %get-tuple-element.47), channel_id=1, source_target_pairs={{0,35},{1,34},{2,37},{3,36},{4,39},{5,38},{6,33},{7,32},{8,43},{9,... | collective-permute-start | bytes 811016 | tf_op jit(solution)/shard_map/ppermute | solution.py:77
  47.9 22.9 %collective-permute-start.4 = (f32[33,16,128]{2,1,0:T(8,128)S(1)}, f32[33,16,128]{2,1,0:T(8,128)S(1)}, u32[]{:S(2)}, u32[]{:S(2)}) collective-permute-start(f32[33,16,128]{2,1,0:T(8,128)S(1)} %get-tuple-element.48), channel_id=1, source_target_pairs={{0,38},{1,39},{2,32},{3,33},{4,34},{5,35},{6,36},{7,37},{8,46},{9,... | collective-permute-start | bytes 811016 | tf_op jit(solution)/shard_map/ppermute | solution.py:77
  49.7 36.4 %copy-start.6 = (f32[128]{0:T(128)S(1)}, f32[128]{0:T(128)}, u32[]{:S(2)}) copy-start(f32[128]{0:T(128)} %param.13) | copy-start | bytes 1540
  49.7 36.4 %copy-start.7 = (s32[128]{0:T(128)S(1)}, s32[128]{0:T(128)}, u32[]{:S(2)}) copy-start(s32[128]{0:T(128)} %param.15) | copy-start | bytes 1540
  49.7 36.4 %copy-start.5 = (f32[128,128]{1,0:T(8,128)S(1)}, f32[128,128]{1,0:T(8,128)}, u32[]{:S(2)}) copy-start(f32[128,128]{1,0:T(8,128)} %constant.14.clone) | copy-start | bytes 196612
  49.7 36.6 %copy-start.4 = (f32[128,128]{1,0:T(8,128)S(1)}, f32[128,128]{1,0:T(8,128)}, u32[]{:S(2)}) copy-start(f32[128,128]{1,0:T(8,128)} %constant.15.clone.refs_8_) | copy-start | bytes 196612
  49.7 26.1 %collective-permute-start.5 = (f32[33,16,128]{2,1,0:T(8,128)S(1)}, f32[33,16,128]{2,1,0:T(8,128)S(1)}, u32[]{:S(2)}, u32[]{:S(2)}) collective-permute-start(f32[33,16,128]{2,1,0:T(8,128)S(1)} %get-tuple-element.49), channel_id=1, source_target_pairs={{0,39},{1,38},{2,33},{3,32},{4,35},{5,34},{6,37},{7,36},{8,47},{9,... | collective-permute-start | bytes 811016 | tf_op jit(solution)/shard_map/ppermute | solution.py:77
  69.4 7.1 %collective-permute-start.10 = (f32[2,8,16,128]{3,2,1,0:T(8,128)S(1)}, f32[2,8,16,128]{3,2,1,0:T(8,128)S(1)}, u32[]{:S(2)}, u32[]{:S(2)}) collective-permute-start(f32[2,8,16,128]{3,2,1,0:T(8,128)S(1)} %across_kernel.1), channel_id=1, source_target_pairs={{32,38},{33,39},{40,46},{41,47},{48,54},{49,55},{56,62},{57,63},{1... | collective-permute-start | bytes 393224 | tf_op jit(solution)/shard_map/ppermute | solution.py:77
  70.8 5.9 %collective-permute-start.11 = (f32[2,8,16,128]{3,2,1,0:T(8,128)S(1)}, f32[2,8,16,128]{3,2,1,0:T(8,128)S(1)}, u32[]{:S(2)}, u32[]{:S(2)}) collective-permute-start(f32[2,8,16,128]{3,2,1,0:T(8,128)S(1)} %across_kernel.1), channel_id=1, source_target_pairs={{34,38},{35,39},{42,46},{43,47},{50,54},{51,55},{58,62},{59,63},{3... | collective-permute-start | bytes 393224 | tf_op jit(solution)/shard_map/ppermute | solution.py:77
  75.8 3.9 %collective-permute-start.12 = (f32[2,8,16,128]{3,2,1,0:T(8,128)S(1)}, f32[2,8,16,128]{3,2,1,0:T(8,128)S(1)}, u32[]{:S(2)}, u32[]{:S(2)}) collective-permute-start(f32[2,8,16,128]{3,2,1,0:T(8,128)S(1)} %across_kernel.1), channel_id=1, source_target_pairs={{36,38},{37,39},{44,46},{45,47},{52,54},{53,55},{60,62},{61,63},{5... | collective-permute-start | bytes 393224 | tf_op jit(solution)/shard_map/ppermute | solution.py:77
  76.6 14.5 %collective-permute-start.15 = (f32[8,8,16,128]{3,2,1,0:T(8,128)S(1)}, f32[8,8,16,128]{3,2,1,0:T(8,128)S(1)}, u32[]{:S(2)}, u32[]{:S(2)}) collective-permute-start(f32[8,8,16,128]{3,2,1,0:T(8,128)S(1)} %get-tuple-element.63), channel_id=1, source_target_pairs={{32,34},{34,36},{36,38},{38,32},{39,37},{37,35},{35,33},{33,39},{4... | collective-permute-start | bytes 1572872 | tf_op jit(solution)/shard_map/ppermute | solution.py:77
  76.7 14.4 %collective-permute-start.16 = (f32[8,8,16,128]{3,2,1,0:T(8,128)S(1)}, f32[8,8,16,128]{3,2,1,0:T(8,128)S(1)}, u32[]{:S(2)}, u32[]{:S(2)}) collective-permute-start(f32[8,8,16,128]{3,2,1,0:T(8,128)S(1)} %get-tuple-element.64), channel_id=1, source_target_pairs={{32,38},{34,32},{36,34},{38,36},{39,33},{37,39},{35,37},{33,35},{4... | collective-permute-start | bytes 1572872 | tf_op jit(solution)/shard_map/ppermute | solution.py:77
  79.8 12.3 %collective-permute-start.13 = (f32[4,16,16,128]{3,2,1,0:T(8,128)S(1)}, f32[4,16,16,128]{3,2,1,0:T(8,128)S(1)}, u32[]{:S(2)}, u32[]{:S(2)}) collective-permute-start(f32[4,16,16,128]{3,2,1,0:T(8,128)S(1)} %get-tuple-element.59), channel_id=1, source_target_pairs={{32,40},{34,42},{36,44},{38,46},{39,47},{37,45},{35,43},{33,41},{4... | collective-permute-start | bytes 1572872 | tf_op jit(solution)/shard_map/ppermute | solution.py:77
  86.0 10.7 %collective-permute-start.14 = (f32[4,16,16,128]{3,2,1,0:T(8,128)S(1)}, f32[4,16,16,128]{3,2,1,0:T(8,128)S(1)}, u32[]{:S(2)}, u32[]{:S(2)}) collective-permute-start(f32[4,16,16,128]{3,2,1,0:T(8,128)S(1)} %get-tuple-element.61), channel_id=1, source_target_pairs={{32,216},{34,218},{36,220},{38,222},{39,223},{37,221},{35,219},{33... | collective-permute-start | bytes 1572872 | tf_op jit(solution)/shard_map/ppermute | solution.py:77
  97.5 6.2 %collective-permute-start.21 = (f32[4,16,16,128]{3,2,1,0:T(8,128)S(1)}, f32[4,16,16,128]{3,2,1,0:T(8,128)S(1)}, u32[]{:S(2)}, u32[]{:S(2)}) collective-permute-start(f32[4,16,16,128]{3,2,1,0:T(8,128)S(1)} %get-tuple-element.75), channel_id=1, source_target_pairs={{32,40},{34,42},{36,44},{38,46},{39,47},{37,45},{35,43},{33,41},{4... | collective-permute-start | bytes 1572872 | tf_op jit(solution)/shard_map/ppermute | solution.py:77
  97.6 10.8 %collective-permute-start.22 = (f32[4,16,16,128]{3,2,1,0:T(8,128)S(1)}, f32[4,16,16,128]{3,2,1,0:T(8,128)S(1)}, u32[]{:S(2)}, u32[]{:S(2)}) collective-permute-start(f32[4,16,16,128]{3,2,1,0:T(8,128)S(1)} %get-tuple-element.76), channel_id=1, source_target_pairs={{32,216},{34,218},{36,220},{38,222},{39,223},{37,221},{35,219},{33... | collective-permute-start | bytes 1572872 | tf_op jit(solution)/shard_map/ppermute | solution.py:77
  98.1 19.3 %collective-permute-start.17 = (f32[4,16,16,128]{3,2,1,0:T(8,128)S(1)}, f32[4,16,16,128]{3,2,1,0:T(8,128)S(1)}, u32[]{:S(2)}, u32[]{:S(2)}) collective-permute-start(f32[4,16,16,128]{3,2,1,0:T(8,128)S(1)} %get-tuple-element.71), channel_id=1, source_target_pairs={{32,40},{34,42},{36,44},{38,46},{39,47},{37,45},{35,43},{33,41},{4... | collective-permute-start | bytes 1572872 | tf_op jit(solution)/shard_map/ppermute | solution.py:77
  101.5 32.3 %collective-permute-start.18 = (f32[4,16,16,128]{3,2,1,0:T(8,128)S(1)}, f32[4,16,16,128]{3,2,1,0:T(8,128)S(1)}, u32[]{:S(2)}, u32[]{:S(2)}) collective-permute-start(f32[4,16,16,128]{3,2,1,0:T(8,128)S(1)} %get-tuple-element.72), channel_id=1, source_target_pairs={{32,216},{34,218},{36,220},{38,222},{39,223},{37,221},{35,219},{33... | collective-permute-start | bytes 1572872 | tf_op jit(solution)/shard_map/ppermute | solution.py:77
  108.5 36.7 %copy-start.2 = (f32[4,64,16,128]{3,2,1,0:T(8,128)S(1)}, f32[4,64,16,128]{3,2,1,0:T(8,128)}, u32[]{:S(2)}) copy-start(f32[4,64,16,128]{3,2,1,0:T(8,128)} %g_ref.3) | copy-start | bytes 6291460
  108.5 25.7 %collective-permute-start.23 = (f32[4,8,16,128]{3,2,1,0:T(8,128)S(1)}, f32[4,8,16,128]{3,2,1,0:T(8,128)S(1)}, u32[]{:S(2)}, u32[]{:S(2)}) collective-permute-start(f32[4,8,16,128]{3,2,1,0:T(8,128)S(1)} %get-tuple-element.77), channel_id=1, source_target_pairs={{34,0},{35,1},{36,2},{37,3},{38,4},{39,5},{32,6},{33,7},{42,8},{43... | collective-permute-start | bytes 786440 | tf_op jit(solution)/shard_map/ppermute | solution.py:77
  114.1 26.0 %collective-permute-start.24 = (f32[4,8,16,128]{3,2,1,0:T(8,128)S(1)}, f32[4,8,16,128]{3,2,1,0:T(8,128)S(1)}, u32[]{:S(2)}, u32[]{:S(2)}) collective-permute-start(f32[4,8,16,128]{3,2,1,0:T(8,128)S(1)} %get-tuple-element.78), channel_id=1, source_target_pairs={{35,0},{34,1},{37,2},{36,3},{39,4},{38,5},{33,6},{32,7},{43,8},{42... | collective-permute-start | bytes 786440 | tf_op jit(solution)/shard_map/ppermute | solution.py:77
  114.1 28.7 %collective-permute-start.25 = (f32[4,8,16,128]{3,2,1,0:T(8,128)S(1)}, f32[4,8,16,128]{3,2,1,0:T(8,128)S(1)}, u32[]{:S(2)}, u32[]{:S(2)}) collective-permute-start(f32[4,8,16,128]{3,2,1,0:T(8,128)S(1)} %get-tuple-element.79), channel_id=1, source_target_pairs={{38,0},{39,1},{32,2},{33,3},{34,4},{35,5},{36,6},{37,7},{46,8},{47... | collective-permute-start | bytes 786440 | tf_op jit(solution)/shard_map/ppermute | solution.py:77
  117.4 38.0 %collective-permute-start.26 = (f32[4,8,16,128]{3,2,1,0:T(8,128)S(1)}, f32[4,8,16,128]{3,2,1,0:T(8,128)S(1)}, u32[]{:S(2)}, u32[]{:S(2)}) collective-permute-start(f32[4,8,16,128]{3,2,1,0:T(8,128)S(1)} %get-tuple-element.80), channel_id=1, source_target_pairs={{39,0},{38,1},{33,2},{32,3},{35,4},{34,5},{37,6},{36,7},{47,8},{46... | collective-permute-start | bytes 786440 | tf_op jit(solution)/shard_map/ppermute | solution.py:77
  134.0 21.4 %collective-permute-start.19 = (f32[4,8,16,128]{3,2,1,0:T(8,128)S(1)}, f32[4,8,16,128]{3,2,1,0:T(8,128)S(1)}, u32[]{:S(2)}, u32[]{:S(2)}) collective-permute-start(f32[4,8,16,128]{3,2,1,0:T(8,128)S(1)} %get-tuple-element.73), channel_id=1, source_target_pairs={{36,0},{37,1},{38,2},{39,3},{32,4},{33,5},{34,6},{35,7},{44,8},{45... | collective-permute-start | bytes 786440 | tf_op jit(solution)/shard_map/ppermute | solution.py:77
  134.3 23.2 %collective-permute-start.20 = (f32[4,8,16,128]{3,2,1,0:T(8,128)S(1)}, f32[4,8,16,128]{3,2,1,0:T(8,128)S(1)}, u32[]{:S(2)}, u32[]{:S(2)}) collective-permute-start(f32[4,8,16,128]{3,2,1,0:T(8,128)S(1)} %get-tuple-element.74), channel_id=1, source_target_pairs={{37,0},{36,1},{39,2},{38,3},{33,4},{32,5},{35,6},{34,7},{45,8},{44... | collective-permute-start | bytes 786440 | tf_op jit(solution)/shard_map/ppermute | solution.py:77
  140.1 17.4 %collective-permute-start.27 = (f32[4,8,16,128]{3,2,1,0:T(8,128)S(1)}, f32[4,8,16,128]{3,2,1,0:T(8,128)S(1)}, u32[]{:S(2)}, u32[]{:S(2)}) collective-permute-start(f32[4,8,16,128]{3,2,1,0:T(8,128)S(1)} %get-tuple-element.81), channel_id=1, source_target_pairs={{32,0},{33,1},{34,2},{35,3},{36,4},{37,5},{38,6},{39,7},{40,8},{41... | collective-permute-start | bytes 786440 | tf_op jit(solution)/shard_map/ppermute | solution.py:77
  142.8 22.0 %collective-permute-start.28 = (f32[4,8,16,128]{3,2,1,0:T(8,128)S(1)}, f32[4,8,16,128]{3,2,1,0:T(8,128)S(1)}, u32[]{:S(2)}, u32[]{:S(2)}) collective-permute-start(f32[4,8,16,128]{3,2,1,0:T(8,128)S(1)} %get-tuple-element.82), channel_id=1, source_target_pairs={{33,0},{32,1},{35,2},{34,3},{37,4},{36,5},{39,6},{38,7},{41,8},{40... | collective-permute-start | bytes 786440 | tf_op jit(solution)/shard_map/ppermute | solution.py:77

commit v6 on v5

--- a/solution.py
+++ b/solution.py
@@ -103,6 +103,16 @@
     y, half, block = as_host()
     dy, ds = SLOTS[slot]
     return pl.ds(pl.multiple_of((((y - dy) & 3) * 2 + (half ^ ds)) * 16, 16), 16)
+
+
+def send_all(pieces, pairs, after):
+    came = {}
+    for slot in (0, 1, 2, 6, 7, 3, 4, 5):
+        piece = pieces[slot]
+        if slot in after:
+            piece, came[after[slot]] = lax.optimization_barrier((piece, came[after[slot]]))
+        came[slot] = send(piece, pairs(slot))
+    return [came[slot] for slot in range(8)]
 
 
 def halves(value):
@@ -224,15 +234,10 @@
 
 
 def cut_kernel(*refs):
-    pieces, (head_ref, tail_ref) = refs[:4], refs[4:]
-    for i in range(4):
-        head_ref[i] = pieces[i][0:16]
-        tail_ref[i] = pieces[i][16:32]
-
-
-def rows_kernel(*refs):
-    pieces, (bottom_ref, top_ref) = refs[:8], refs[8:]
+    pieces, (head_ref, tail_ref, bottom_ref, top_ref) = refs[:8], refs[8:]
     for slot in range(8):
+        head_ref[slot] = pieces[slot][0:16]
+        tail_ref[slot] = pieces[slot][16:32]
         for x in range(4):
             bottom_ref[slot, 2 * x : 2 * x + 2] = pieces[slot][8 * x : 8 * x + 2]
             top_ref[slot, 2 * x : 2 * x + 2] = pieces[slot][8 * x + 6 : 8 * x + 8]
@@ -310,7 +315,7 @@
 
 
 def first_edge_kernel(
-    inner_ref, low_a_ref, low_b_ref, high_a_ref, high_b_ref, under_ref, over_ref, from_0_ref, from_1_ref, from_2_ref, own_0_ref, own_1_ref, vx_ref, vy_ref, v_ref, *outs
+    inner_ref, low_ref, high_ref, under_ref, over_ref, from_0_ref, from_1_ref, from_2_ref, own_0_ref, own_1_ref, vx_ref, vy_ref, v_ref, *outs
 ):
     y_place, half, block = as_host()
     middle = jnp.where(y_place == 3, 1.0, 0.0)
@@ -328,7 +333,6 @@
         up, down = rates(vx_ref, at, 0.0625)
         group = int(slot in GROUPS[1])
         i = GROUPS[group].index(slot)
-        low_ref, high_ref = ((low_a_ref, high_a_ref), (low_b_ref, high_b_ref))[group]
         for x in range(4):
             rows = slice(2 * x, 2 * x + 2)
             if dy == 0:
@@ -342,8 +346,8 @@
             over = jnp.where(over_middle, across * middle, over)
             value = inner_ref[x, :, at, :] + outer_drift(
                 x,
-                lambda n: low_ref[i, 8 - 8 * n : 16 - 8 * n],
-                lambda n: high_ref[i, 8 * n : 8 * n + 8],
+                lambda n: low_ref[slot, 8 - 8 * n : 16 - 8 * n],
+                lambda n: high_ref[slot, 8 * n : 8 * n + 8],
                 up,
                 down,
             )
@@ -441,7 +445,7 @@
 
     sizes = [33 + 8 * (dy == 0) + (slot == FIRST) for slot, (dy, ds) in enumerate(SLOTS)]
     pieces = call(pack_kernel, [array(size, 16, K) for size in sizes])(density, vel_x, potential_x)
-    pieces = [send(piece, exchange_pairs(slot)) for slot, piece in enumerate(pieces)]
+    pieces = send_all(pieces, exchange_pairs, {3: 7, 4: 6, 5: 1})
 
     highest = lax.Precision.HIGHEST
     ty = 0.25 * jnp.dot(potential_y, jnp.asarray(sine_table(1)), precision=highest)
@@ -451,16 +455,10 @@
 
     across = call(across_kernel, array(2, 8, 16, K), mib=0)(pieces[FIRST], pieces[SECOND])
     across = [send(across, middle_pairs(y)) for y in range(3)]
-    low, high = [None] * 2, [None] * 2
-    for group in (1, 0):
-        mine = [pieces[slot] for slot in GROUPS[group]]
-        if group == 0:
-            *mine, low[1], high[1], across[0], across[1], across[2] = lax.optimization_barrier((*mine, low[1], high[1], *across))
-        head, tail = call(cut_kernel, [array(4, 16, 16, K)] * 2, mib=2)(*mine)
-        low[group] = send(tail, x_pairs(1))
-        high[group] = send(head, x_pairs(-1))
-    y_low, y_high = call(rows_kernel, [array(8, 8, 16, K)] * 2, mib=2)(*pieces)
-    under, over = send(y_high, y_pairs(1)), send(y_low, y_pairs(-1))
+    *pieces, across[0], across[1], across[2] = lax.optimization_barrier((*pieces, *across))
+    head, tail, bottom, top = call(cut_kernel, [array(8, 16, 16, K)] * 2 + [array(8, 8, 16, K)] * 2)(*pieces)
+    low, high = send(tail, x_pairs(1)), send(head, x_pairs(-1))
+    under, over = send(top, y_pairs(1)), send(bottom, y_pairs(-1))
     left_tables = pltpu.VMEM((4, 2 * K, 2 * K), BF16)
     inner, vx, tx = call(
         first_kernel,
@@ -469,7 +467,7 @@
         3 * 10**9,
     )(*pieces, jnp.asarray(sine_table(-1)), ty, vy)
     v, *sides = call(first_edge_kernel, [array(4, 8, K, K)] + [array(4, 16, 16, K)] * 4)(
-        inner, *low, *high, under, over, *across, pieces[FIRST], pieces[SECOND], vx, vy
+        inner, low, high, under, over, *across, pieces[FIRST], pieces[SECOND], vx, vy
     )
     low = [send(sides[2 * group + 1], x_pairs(1)) for group in range(2)]
     high = [send(sides[2 * group], x_pairs(-1)) for group in range(2)]
@@ -480,7 +478,8 @@
             inner, low[group], high[group], vx
         )
         for slot, piece in zip(slots, cut):
-            pieces[slot] = send(piece, back(exchange_pairs(slot)))
+            pieces[slot] = piece
+    pieces = send_all(pieces, lambda slot: back(exchange_pairs(slot)), {3: 6, 4: 7, 5: 0})
 
     def by_x(*shape):
         return pl.BlockSpec((1, *shape), lambda x: (x, 0, 0, 0))

time: 167 us -> 156 us (0.934)
  waiting for transfers between devices: 91 us -> 78.5 us
    ppermute x29 -> x27, waiting for transfers between devices: 91 us -> 78.5 us  [send(): return lax.ppermute(value, AXES, pairs)]
    ppermute x29 -> x27, starting transfers between devices: 58.8 us -> 59.3 us  [send(): return lax.ppermute(value, AXES, pairs)]
    pallas_call x11 -> x9, Pallas kernels: 11.4 us -> 11.4 us  [run(): pl.pallas_call(kernel, out_shape=outs, in_specs=[VMEM] * len(operands), o...]
  transfers between devices with their start and end apart: 29 -> 27, of which waited for: 15 -> 10; matrix products, arithmetic and copies ran while one was open for 0% -> 0% of each run, Pallas kernels for 6% -> 7%
where the time goes in v6:
time: 156 us; the launch traced here: 155 us
  waiting for transfers between devices  78.5 us (50%)
  starting transfers between devices  59.3 us (38%)
  Pallas kernels  13.3 us (9%)
  local copies, waits for them, and re-layouts  2.37 us (2%)
    ppermute x27, waiting for transfers between devices, send(): return lax.ppermute(value, AXES, pairs)  78.5 us
    ppermute x27, starting transfers between devices, send(): return lax.ppermute(value, AXES, pairs)  59.3 us
    pallas_call x9, Pallas kernels, run(): pl.pallas_call(kernel, out_shape=outs, in_specs=[VMEM] * len(operands), o...  11.4 us
  transfers between devices with their start and end apart: 27, of which 10 were waited for; matrix products, arithmetic and copies ran while one was open for 0% of the time, Pallas kernels for 7%

profile of v6, /device:TPU:39, one launch (start us, length us, event | category | flops | bytes accessed | tf_op | source)
XLA Modules:
  0.0 154.6 jit_solution(1653314950339351484)
XLA Ops:
  0.0 0.7 convert_multiply_fusion
  0.7 0.1 broadcast_in_dim.2.vel_ref
  0.8 1.6 %copy-done.1 = f32[4,64,16,128]{3,2,1,0:T(8,128)S(1)} copy-done((f32[4,64,16,128]{3,2,1,0:T(8,128)S(1)}, f32[4,64,16,128]{3,2,1,0:T(8,128)}, u32[]{:S(2)}) %copy-start.1) | copy-done | bytes 2097176
  2.4 0.7 copy-done.3
  3.0 0.2 pack_kernel.1
  3.2 0.0 copy-start.4
  3.2 5.2 %collective-permute-start.5 = (f32[42,16,128]{2,1,0:T(8,128)S(1)}, f32[42,16,128]{2,1,0:T(8,128)S(1)}, u32[]{:S(2)}, u32[]{:S(2)}) collective-permute-start(f32[42,16,128]{2,1,0:T(8,128)S(1)} %get-tuple-element.65), channel_id=1, source_target_pairs={{0,32},{1,33},{2,34},{3,35},{4,36},{5,37},{6,38},{7,39},{8,40},{9,... | collective-permute-start | bytes 1032200 | tf_op jit(solution)/shard_map/ppermute | solution.py:77
  8.4 4.1 %collective-permute-start.1 = (f32[33,16,128]{2,1,0:T(8,128)S(1)}, f32[33,16,128]{2,1,0:T(8,128)S(1)}, u32[]{:S(2)}, u32[]{:S(2)}) collective-permute-start(f32[33,16,128]{2,1,0:T(8,128)S(1)} %get-tuple-element.58), channel_id=1, source_target_pairs={{0,37},{1,36},{2,39},{3,38},{4,33},{5,32},{6,35},{7,34},{8,45},{9,... | collective-permute-start | bytes 811016 | tf_op jit(solution)/shard_map/ppermute | solution.py:77
  12.5 2.1 %collective-permute-start = (f32[33,16,128]{2,1,0:T(8,128)S(1)}, f32[33,16,128]{2,1,0:T(8,128)S(1)}, u32[]{:S(2)}, u32[]{:S(2)}) collective-permute-start(f32[33,16,128]{2,1,0:T(8,128)S(1)} %get-tuple-element.56), channel_id=1, source_target_pairs={{0,36},{1,37},{2,38},{3,39},{4,32},{5,33},{6,34},{7,35},{8,44},{9,... | collective-permute-start | bytes 811016 | tf_op jit(solution)/shard_map/ppermute | solution.py:77
  14.6 3.1 %collective-permute-start.2 = (f32[33,16,128]{2,1,0:T(8,128)S(1)}, f32[33,16,128]{2,1,0:T(8,128)S(1)}, u32[]{:S(2)}, u32[]{:S(2)}) collective-permute-start(f32[33,16,128]{2,1,0:T(8,128)S(1)} %get-tuple-element.60), channel_id=1, source_target_pairs={{0,34},{1,35},{2,36},{3,37},{4,38},{5,39},{6,32},{7,33},{8,42},{9,... | collective-permute-start | bytes 811016 | tf_op jit(solution)/shard_map/ppermute | solution.py:77
  17.8 26.3 %collective-permute-done.1.refs_1_ = f32[33,16,128]{2,1,0:T(8,128)S(1)} collective-permute-done((f32[33,16,128]{2,1,0:T(8,128)S(1)}, f32[33,16,128]{2,1,0:T(8,128)S(1)}, u32[]{:S(2)}, u32[]{:S(2)}) %collective-permute-start.1) | collective-permute-done | bytes 270368 | tf_op jit(solution)/shard_map/ppermute | solution.py:77
  44.0 3.0 %collective-permute-start.4 = (f32[33,16,128]{2,1,0:T(8,128)S(1)}, f32[33,16,128]{2,1,0:T(8,128)S(1)}, u32[]{:S(2)}, u32[]{:S(2)}) collective-permute-start(f32[33,16,128]{2,1,0:T(8,128)S(1)} %get-tuple-element.63), channel_id=1, source_target_pairs={{0,35},{1,34},{2,37},{3,36},{4,39},{5,38},{6,33},{7,32},{8,43},{9,... | collective-permute-start | bytes 811016 | tf_op jit(solution)/shard_map/ppermute | solution.py:77
  47.0 2.7 %collective-permute-start.6 = (f32[33,16,128]{2,1,0:T(8,128)S(1)}, f32[33,16,128]{2,1,0:T(8,128)S(1)}, u32[]{:S(2)}, u32[]{:S(2)}) collective-permute-start(f32[33,16,128]{2,1,0:T(8,128)S(1)} %get-tuple-element.66), channel_id=1, source_target_pairs={{0,38},{1,39},{2,32},{3,33},{4,34},{5,35},{6,36},{7,37},{8,46},{9,... | collective-permute-start | bytes 811016 | tf_op jit(solution)/shard_map/ppermute | solution.py:77
  49.8 0.7 collective-permute-start.10
  50.4 4.9 %collective-permute-start.8 = (f32[2,8,16,128]{3,2,1,0:T(8,128)S(1)}, f32[2,8,16,128]{3,2,1,0:T(8,128)S(1)}, u32[]{:S(2)}, u32[]{:S(2)}) collective-permute-start(f32[2,8,16,128]{3,2,1,0:T(8,128)S(1)} %across_kernel.1), channel_id=1, source_target_pairs={{32,38},{33,39},{40,46},{41,47},{48,54},{49,55},{56,62},{57,63},{1... | collective-permute-start | bytes 393224 | tf_op jit(solution)/shard_map/ppermute | solution.py:77
  55.4 0.7 collective-permute-start.9
  56.1 11.2 %collective-permute-done.8.from_0_ref = f32[2,8,16,128]{3,2,1,0:T(8,128)S(1)} collective-permute-done((f32[2,8,16,128]{3,2,1,0:T(8,128)S(1)}, f32[2,8,16,128]{3,2,1,0:T(8,128)S(1)}, u32[]{:S(2)}, u32[]{:S(2)}) %collective-permute-start.8) | collective-permute-done | bytes 131104 | tf_op jit(solution)/shard_map/ppermute | solution.py:77
  67.3 0.2 cut_kernel.1
  67.5 0.1 collective-permute-start.11
  67.6 0.6 collective-permute-start.12
  68.1 3.4 %collective-permute-start.14 = (f32[8,8,16,128]{3,2,1,0:T(8,128)S(1)}, f32[8,8,16,128]{3,2,1,0:T(8,128)S(1)}, u32[]{:S(2)}, u32[]{:S(2)}) collective-permute-start(f32[8,8,16,128]{3,2,1,0:T(8,128)S(1)} %get-tuple-element.82), channel_id=1, source_target_pairs={{32,38},{34,32},{36,34},{38,36},{39,33},{37,39},{35,37},{33,35},{4... | collective-permute-start | bytes 1572872 | tf_op jit(solution)/shard_map/ppermute | solution.py:77
  71.6 0.2 fusion.ty_ref.refs_9_
  71.8 2.1 %first_kernel.1 = (f32[4,8,128,128]{3,2,1,0:T(8,128)S(1)}, f32[128,128]{1,0:T(8,128)S(1)}, f32[8,128]{1,0:T(8,128)S(1)}) custom-call(f32[33,16,128]{2,1,0:T(8,128)S(1)} %collective-permute-done.refs_0_, f32[33,16,128]{2,1,0:T(8,128)S(1)} %collective-permute-done.1.refs_1_, f32[33,16,128]{2,1,0:T(8,128)S(1)} %collective-permute-done.2.refs_2_, ...), custom_call_target="tpu_custom_call" | custom-call | flops 3000000000 | bytes 4194304 | tf_op jit(solution)/shard_map/first_kernel/pallas_call | solution.py:417
  73.9 8.2 %collective-permute-done.13.under_ref = f32[8,8,16,128]{3,2,1,0:T(8,128)S(1)} collective-permute-done((f32[8,8,16,128]{3,2,1,0:T(8,128)S(1)}, f32[8,8,16,128]{3,2,1,0:T(8,128)S(1)}, u32[]{:S(2)}, u32[]{:S(2)}) %collective-permute-start.13) | collective-permute-done | bytes 524320 | tf_op jit(solution)/shard_map/ppermute | solution.py:77
  82.1 1.8 %collective-permute-done.12.high_ref = f32[8,16,16,128]{3,2,1,0:T(8,128)S(1)} collective-permute-done((f32[8,16,16,128]{3,2,1,0:T(8,128)S(1)}, f32[8,16,16,128]{3,2,1,0:T(8,128)S(1)}, u32[]{:S(2)}, u32[]{:S(2)}) %collective-permute-start.12) | collective-permute-done | bytes 1048608 | tf_op jit(solution)/shard_map/ppermute | solution.py:77
  84.0 0.7 first_edge_kernel.1
  84.7 0.1 collective-permute-start.17
  84.8 0.5 collective-permute-start.18
  85.4 3.4 %collective-permute-start.15 = (f32[4,16,16,128]{3,2,1,0:T(8,128)S(1)}, f32[4,16,16,128]{3,2,1,0:T(8,128)S(1)}, u32[]{:S(2)}, u32[]{:S(2)}) collective-permute-start(f32[4,16,16,128]{3,2,1,0:T(8,128)S(1)} %get-tuple-element.89), channel_id=1, source_target_pairs={{32,40},{34,42},{36,44},{38,46},{39,47},{37,45},{35,43},{33,41},{4... | collective-permute-start | bytes 1572872 | tf_op jit(solution)/shard_map/ppermute | solution.py:77
  88.8 1.4 second_kernel.1.inner_ref
  90.2 0.7 collective-permute-done.17.low_ref
  90.9 4.7 %collective-permute-done.18.high_ref = f32[4,16,16,128]{3,2,1,0:T(8,128)S(1)} collective-permute-done((f32[4,16,16,128]{3,2,1,0:T(8,128)S(1)}, f32[4,16,16,128]{3,2,1,0:T(8,128)S(1)}, u32[]{:S(2)}, u32[]{:S(2)}) %collective-permute-start.18) | collective-permute-done | bytes 524320 | tf_op jit(solution)/shard_map/ppermute | solution.py:77
  95.6 0.1 second_edge_kernel.3
  95.8 0.0 copy-start.2
  95.8 3.1 %collective-permute-start.24 = (f32[4,8,16,128]{3,2,1,0:T(8,128)S(1)}, f32[4,8,16,128]{3,2,1,0:T(8,128)S(1)}, u32[]{:S(2)}, u32[]{:S(2)}) collective-permute-start(f32[4,8,16,128]{3,2,1,0:T(8,128)S(1)} %get-tuple-element.102), channel_id=1, source_target_pairs={{33,0},{32,1},{35,2},{34,3},{37,4},{36,5},{39,6},{38,7},{41,8},{40... | collective-permute-start | bytes 786440 | tf_op jit(solution)/shard_map/ppermute | solution.py:77
  98.9 0.8 collective-permute-start.22
  99.7 1.7 %collective-permute-start.19 = (f32[4,8,16,128]{3,2,1,0:T(8,128)S(1)}, f32[4,8,16,128]{3,2,1,0:T(8,128)S(1)}, u32[]{:S(2)}, u32[]{:S(2)}) collective-permute-start(f32[4,8,16,128]{3,2,1,0:T(8,128)S(1)} %get-tuple-element.94), channel_id=1, source_target_pairs={{36,0},{37,1},{38,2},{39,3},{32,4},{33,5},{34,6},{35,7},{44,8},{45... | collective-permute-start | bytes 786440 | tf_op jit(solution)/shard_map/ppermute | solution.py:77
  101.4 4.3 %collective-permute-start.20 = (f32[4,8,16,128]{3,2,1,0:T(8,128)S(1)}, f32[4,8,16,128]{3,2,1,0:T(8,128)S(1)}, u32[]{:S(2)}, u32[]{:S(2)}) collective-permute-start(f32[4,8,16,128]{3,2,1,0:T(8,128)S(1)} %get-tuple-element.96), channel_id=1, source_target_pairs={{37,0},{36,1},{39,2},{38,3},{33,4},{32,5},{35,6},{34,7},{45,8},{44... | collective-permute-start | bytes 786440 | tf_op jit(solution)/shard_map/ppermute | solution.py:77
  105.7 11.9 %collective-permute-done.16.high_ref = f32[4,16,16,128]{3,2,1,0:T(8,128)S(1)} collective-permute-done((f32[4,16,16,128]{3,2,1,0:T(8,128)S(1)}, f32[4,16,16,128]{3,2,1,0:T(8,128)S(1)}, u32[]{:S(2)}, u32[]{:S(2)}) %collective-permute-start.16) | collective-permute-done | bytes 524320 | tf_op jit(solution)/shard_map/ppermute | solution.py:77
  117.6 0.1 second_edge_kernel.2
  117.7 1.3 collective-permute-start.21
  119.0 8.6 %collective-permute-start.25 = (f32[4,8,16,128]{3,2,1,0:T(8,128)S(1)}, f32[4,8,16,128]{3,2,1,0:T(8,128)S(1)}, u32[]{:S(2)}, u32[]{:S(2)}) collective-permute-start(f32[4,8,16,128]{3,2,1,0:T(8,128)S(1)} %get-tuple-element.103), channel_id=1, source_target_pairs={{38,0},{39,1},{32,2},{33,3},{34,4},{35,5},{36,6},{37,7},{46,8},{47... | collective-permute-start | bytes 786440 | tf_op jit(solution)/shard_map/ppermute | solution.py:77
  127.7 5.4 %collective-permute-done.19.refs_0_ = f32[4,8,16,128]{3,2,1,0:T(8,128)S(1)} collective-permute-done((f32[4,8,16,128]{3,2,1,0:T(8,128)S(1)}, f32[4,8,16,128]{3,2,1,0:T(8,128)S(1)}, u32[]{:S(2)}, u32[]{:S(2)}) %collective-permute-start.19) | collective-permute-done | bytes 262176 | tf_op jit(solution)/shard_map/ppermute | solution.py:77
  133.0 4.9 %collective-permute-start.26 = (f32[4,8,16,128]{3,2,1,0:T(8,128)S(1)}, f32[4,8,16,128]{3,2,1,0:T(8,128)S(1)}, u32[]{:S(2)}, u32[]{:S(2)}) collective-permute-start(f32[4,8,16,128]{3,2,1,0:T(8,128)S(1)} %get-tuple-element.104), channel_id=1, source_target_pairs={{39,0},{38,1},{33,2},{32,3},{35,4},{34,5},{37,6},{36,7},{47,8},{46... | collective-permute-start | bytes 786440 | tf_op jit(solution)/shard_map/ppermute | solution.py:77
  138.0 6.4 %local_kernel.1.local_ref = f32[4,64,16,128]{3,2,1,0:T(8,128)S(1)} custom-call(f32[4,64,16,128]{3,2,1,0:T(8,128)S(1)} %copy-done.2, f32[64,128]{1,0:T(8,128)S(1)} %fusion.ty_ref.refs_9_, f32[1,128]{1,0:T(1,128)S(1)} %multiply_bitcast_fusion.vy_ref.refs_10_), custom_call_target="tpu_custom_call" | custom-call | flops 4000000000 | bytes 4194304 | tf_op jit(solution)/shard_map/local_kernel/pallas_call | solution.py:417
  144.4 7.1 %collective-permute-done.25.refs_4_ = f32[4,8,16,128]{3,2,1,0:T(8,128)S(1)} collective-permute-done((f32[4,8,16,128]{3,2,1,0:T(8,128)S(1)}, f32[4,8,16,128]{3,2,1,0:T(8,128)S(1)}, u32[]{:S(2)}, u32[]{:S(2)}) %collective-permute-start.25) | collective-permute-done | bytes 262176 | tf_op jit(solution)/shard_map/ppermute | solution.py:77
  151.5 1.2 collective-permute-done.26.refs_5_
  152.7 1.9 %final_kernel.1 = f32[4,64,16,128]{3,2,1,0:T(8,128)} custom-call(f32[4,64,16,128]{3,2,1,0:T(8,128)S(1)} %local_kernel.1.local_ref, f32[4,8,16,128]{3,2,1,0:T(8,128)S(1)} %collective-permute-done.19.refs_0_, f32[4,8,16,128]{3,2,1,0:T(8,128)S(1)} %collective-permute-done.20.refs_1_, f32[4,8,16,128]{3,2,1,0:T(8,128)S(1)} %collective-permute-done.21.refs_2_, ...), custom_call_target="tpu_custom_call" | custom-call | bytes 6291456 | tf_op jit(solution)/shard_map/final_kernel/pallas_call | solution.py:487
  (36 shorter events, 0.1 us)
Async XLA Ops:
  0.0 71.6 %copy-start = (f32[64,128]{1,0:T(8,128)S(1)}, f32[64,128]{1,0:T(8,128)}, u32[]{:S(2)}) copy-start(f32[64,128]{1,0:T(8,128)} %param.11) | copy-start | bytes 98308
  0.8 1.6 %copy-start.1 = (f32[4,64,16,128]{3,2,1,0:T(8,128)S(1)}, f32[4,64,16,128]{3,2,1,0:T(8,128)}, u32[]{:S(2)}) copy-start(f32[4,64,16,128]{3,2,1,0:T(8,128)} %g_ref.3) | copy-start | bytes 6291460
  2.4 0.7 copy-start.3
  3.0 68.5 %copy-start.6 = (f32[128]{0:T(128)S(1)}, f32[128]{0:T(128)}, u32[]{:S(2)}) copy-start(f32[128]{0:T(128)} %param.13) | copy-start | bytes 1540
  3.0 68.5 %copy-start.7 = (s32[128]{0:T(128)S(1)}, s32[128]{0:T(128)}, u32[]{:S(2)}) copy-start(s32[128]{0:T(128)} %param.15) | copy-start | bytes 1540
  3.0 68.5 %copy-start.5 = (f32[128,128]{1,0:T(8,128)S(1)}, f32[128,128]{1,0:T(8,128)}, u32[]{:S(2)}) copy-start(f32[128,128]{1,0:T(8,128)} %constant.14.clone) | copy-start | bytes 196612
  3.2 68.6 %copy-start.4 = (f32[128,128]{1,0:T(8,128)S(1)}, f32[128,128]{1,0:T(8,128)}, u32[]{:S(2)}) copy-start(f32[128,128]{1,0:T(8,128)} %constant.15.clone.refs_8_) | copy-start | bytes 196612
  3.2 43.8 %collective-permute-start.5 = (f32[42,16,128]{2,1,0:T(8,128)S(1)}, f32[42,16,128]{2,1,0:T(8,128)S(1)}, u32[]{:S(2)}, u32[]{:S(2)}) collective-permute-start(f32[42,16,128]{2,1,0:T(8,128)S(1)} %get-tuple-element.65), channel_id=1, source_target_pairs={{0,32},{1,33},{2,34},{3,35},{4,36},{5,37},{6,38},{7,39},{8,40},{9,... | collective-permute-start | bytes 1032200 | tf_op jit(solution)/shard_map/ppermute | solution.py:77
  8.4 35.6 %collective-permute-start.3 = (f32[41,16,128]{2,1,0:T(8,128)S(1)}, f32[41,16,128]{2,1,0:T(8,128)S(1)}, u32[]{:S(2)}, u32[]{:S(2)}) collective-permute-start(f32[41,16,128]{2,1,0:T(8,128)S(1)} %get-tuple-element.62), channel_id=1, source_target_pairs={{0,33},{1,32},{2,35},{3,34},{4,37},{5,36},{6,39},{7,38},{8,41},{9,... | collective-permute-start | bytes 1007624 | tf_op jit(solution)/shard_map/ppermute | solution.py:77
  8.4 35.6 %collective-permute-start.1 = (f32[33,16,128]{2,1,0:T(8,128)S(1)}, f32[33,16,128]{2,1,0:T(8,128)S(1)}, u32[]{:S(2)}, u32[]{:S(2)}) collective-permute-start(f32[33,16,128]{2,1,0:T(8,128)S(1)} %get-tuple-element.58), channel_id=1, source_target_pairs={{0,37},{1,36},{2,39},{3,38},{4,33},{5,32},{6,35},{7,34},{8,45},{9,... | collective-permute-start | bytes 811016 | tf_op jit(solution)/shard_map/ppermute | solution.py:77
  12.5 37.3 %collective-permute-start = (f32[33,16,128]{2,1,0:T(8,128)S(1)}, f32[33,16,128]{2,1,0:T(8,128)S(1)}, u32[]{:S(2)}, u32[]{:S(2)}) collective-permute-start(f32[33,16,128]{2,1,0:T(8,128)S(1)} %get-tuple-element.56), channel_id=1, source_target_pairs={{0,36},{1,37},{2,38},{3,39},{4,32},{5,33},{6,34},{7,35},{8,44},{9,... | collective-permute-start | bytes 811016 | tf_op jit(solution)/shard_map/ppermute | solution.py:77
  14.6 35.8 %collective-permute-start.2 = (f32[33,16,128]{2,1,0:T(8,128)S(1)}, f32[33,16,128]{2,1,0:T(8,128)S(1)}, u32[]{:S(2)}, u32[]{:S(2)}) collective-permute-start(f32[33,16,128]{2,1,0:T(8,128)S(1)} %get-tuple-element.60), channel_id=1, source_target_pairs={{0,34},{1,35},{2,36},{3,37},{4,38},{5,39},{6,32},{7,33},{8,42},{9,... | collective-permute-start | bytes 811016 | tf_op jit(solution)/shard_map/ppermute | solution.py:77
  44.0 23.2 %collective-permute-start.7 = (f32[33,16,128]{2,1,0:T(8,128)S(1)}, f32[33,16,128]{2,1,0:T(8,128)S(1)}, u32[]{:S(2)}, u32[]{:S(2)}) collective-permute-start(f32[33,16,128]{2,1,0:T(8,128)S(1)} %get-tuple-element.67), channel_id=1, source_target_pairs={{0,39},{1,38},{2,33},{3,32},{4,35},{5,34},{6,37},{7,36},{8,47},{9,... | collective-permute-start | bytes 811016 | tf_op jit(solution)/shard_map/ppermute | solution.py:77
  44.0 23.2 %collective-permute-start.4 = (f32[33,16,128]{2,1,0:T(8,128)S(1)}, f32[33,16,128]{2,1,0:T(8,128)S(1)}, u32[]{:S(2)}, u32[]{:S(2)}) collective-permute-start(f32[33,16,128]{2,1,0:T(8,128)S(1)} %get-tuple-element.63), channel_id=1, source_target_pairs={{0,35},{1,34},{2,37},{3,36},{4,39},{5,38},{6,33},{7,32},{8,43},{9,... | collective-permute-start | bytes 811016 | tf_op jit(solution)/shard_map/ppermute | solution.py:77
  47.0 20.2 %collective-permute-start.6 = (f32[33,16,128]{2,1,0:T(8,128)S(1)}, f32[33,16,128]{2,1,0:T(8,128)S(1)}, u32[]{:S(2)}, u32[]{:S(2)}) collective-permute-start(f32[33,16,128]{2,1,0:T(8,128)S(1)} %get-tuple-element.66), channel_id=1, source_target_pairs={{0,38},{1,39},{2,32},{3,33},{4,34},{5,35},{6,36},{7,37},{8,46},{9,... | collective-permute-start | bytes 811016 | tf_op jit(solution)/shard_map/ppermute | solution.py:77
  49.8 5.6 %collective-permute-start.10 = (f32[2,8,16,128]{3,2,1,0:T(8,128)S(1)}, f32[2,8,16,128]{3,2,1,0:T(8,128)S(1)}, u32[]{:S(2)}, u32[]{:S(2)}) collective-permute-start(f32[2,8,16,128]{3,2,1,0:T(8,128)S(1)} %across_kernel.1), channel_id=1, source_target_pairs={{36,38},{37,39},{44,46},{45,47},{52,54},{53,55},{60,62},{61,63},{5... | collective-permute-start | bytes 393224 | tf_op jit(solution)/shard_map/ppermute | solution.py:77
  50.4 16.8 %collective-permute-start.8 = (f32[2,8,16,128]{3,2,1,0:T(8,128)S(1)}, f32[2,8,16,128]{3,2,1,0:T(8,128)S(1)}, u32[]{:S(2)}, u32[]{:S(2)}) collective-permute-start(f32[2,8,16,128]{3,2,1,0:T(8,128)S(1)} %across_kernel.1), channel_id=1, source_target_pairs={{32,38},{33,39},{40,46},{41,47},{48,54},{49,55},{56,62},{57,63},{1... | collective-permute-start | bytes 393224 | tf_op jit(solution)/shard_map/ppermute | solution.py:77
  55.4 11.8 %collective-permute-start.9 = (f32[2,8,16,128]{3,2,1,0:T(8,128)S(1)}, f32[2,8,16,128]{3,2,1,0:T(8,128)S(1)}, u32[]{:S(2)}, u32[]{:S(2)}) collective-permute-start(f32[2,8,16,128]{3,2,1,0:T(8,128)S(1)} %across_kernel.1), channel_id=1, source_target_pairs={{34,38},{35,39},{42,46},{43,47},{50,54},{51,55},{58,62},{59,63},{3... | collective-permute-start | bytes 393224 | tf_op jit(solution)/shard_map/ppermute | solution.py:77
  67.5 14.7 %collective-permute-start.11 = (f32[8,16,16,128]{3,2,1,0:T(8,128)S(1)}, f32[8,16,16,128]{3,2,1,0:T(8,128)S(1)}, u32[]{:S(2)}, u32[]{:S(2)}) collective-permute-start(f32[8,16,16,128]{3,2,1,0:T(8,128)S(1)} %get-tuple-element.79), channel_id=1, source_target_pairs={{32,40},{34,42},{36,44},{38,46},{39,47},{37,45},{35,43},{33,41},{4... | collective-permute-start | bytes 3145736 | tf_op jit(solution)/shard_map/ppermute | solution.py:77
  67.6 16.4 %collective-permute-start.12 = (f32[8,16,16,128]{3,2,1,0:T(8,128)S(1)}, f32[8,16,16,128]{3,2,1,0:T(8,128)S(1)}, u32[]{:S(2)}, u32[]{:S(2)}) collective-permute-start(f32[8,16,16,128]{3,2,1,0:T(8,128)S(1)} %get-tuple-element.80), channel_id=1, source_target_pairs={{32,216},{34,218},{36,220},{38,222},{39,223},{37,221},{35,219},{33... | collective-permute-start | bytes 3145736 | tf_op jit(solution)/shard_map/ppermute | solution.py:77
  68.1 14.0 %collective-permute-start.13 = (f32[8,8,16,128]{3,2,1,0:T(8,128)S(1)}, f32[8,8,16,128]{3,2,1,0:T(8,128)S(1)}, u32[]{:S(2)}, u32[]{:S(2)}) collective-permute-start(f32[8,8,16,128]{3,2,1,0:T(8,128)S(1)} %get-tuple-element.81), channel_id=1, source_target_pairs={{32,34},{34,36},{36,38},{38,32},{39,37},{37,35},{35,33},{33,39},{4... | collective-permute-start | bytes 1572872 | tf_op jit(solution)/shard_map/ppermute | solution.py:77
  68.1 14.0 %collective-permute-start.14 = (f32[8,8,16,128]{3,2,1,0:T(8,128)S(1)}, f32[8,8,16,128]{3,2,1,0:T(8,128)S(1)}, u32[]{:S(2)}, u32[]{:S(2)}) collective-permute-start(f32[8,8,16,128]{3,2,1,0:T(8,128)S(1)} %get-tuple-element.82), channel_id=1, source_target_pairs={{32,38},{34,32},{36,34},{38,36},{39,33},{37,39},{35,37},{33,35},{4... | collective-permute-start | bytes 1572872 | tf_op jit(solution)/shard_map/ppermute | solution.py:77
  84.7 6.2 %collective-permute-start.17 = (f32[4,16,16,128]{3,2,1,0:T(8,128)S(1)}, f32[4,16,16,128]{3,2,1,0:T(8,128)S(1)}, u32[]{:S(2)}, u32[]{:S(2)}) collective-permute-start(f32[4,16,16,128]{3,2,1,0:T(8,128)S(1)} %get-tuple-element.92), channel_id=1, source_target_pairs={{32,40},{34,42},{36,44},{38,46},{39,47},{37,45},{35,43},{33,41},{4... | collective-permute-start | bytes 1572872 | tf_op jit(solution)/shard_map/ppermute | solution.py:77
  84.8 10.8 %collective-permute-start.18 = (f32[4,16,16,128]{3,2,1,0:T(8,128)S(1)}, f32[4,16,16,128]{3,2,1,0:T(8,128)S(1)}, u32[]{:S(2)}, u32[]{:S(2)}) collective-permute-start(f32[4,16,16,128]{3,2,1,0:T(8,128)S(1)} %get-tuple-element.93), channel_id=1, source_target_pairs={{32,216},{34,218},{36,220},{38,222},{39,223},{37,221},{35,219},{33... | collective-permute-start | bytes 1572872 | tf_op jit(solution)/shard_map/ppermute | solution.py:77
  85.4 16.1 %collective-permute-start.15 = (f32[4,16,16,128]{3,2,1,0:T(8,128)S(1)}, f32[4,16,16,128]{3,2,1,0:T(8,128)S(1)}, u32[]{:S(2)}, u32[]{:S(2)}) collective-permute-start(f32[4,16,16,128]{3,2,1,0:T(8,128)S(1)} %get-tuple-element.89), channel_id=1, source_target_pairs={{32,40},{34,42},{36,44},{38,46},{39,47},{37,45},{35,43},{33,41},{4... | collective-permute-start | bytes 1572872 | tf_op jit(solution)/shard_map/ppermute | solution.py:77
  88.8 28.8 %collective-permute-start.16 = (f32[4,16,16,128]{3,2,1,0:T(8,128)S(1)}, f32[4,16,16,128]{3,2,1,0:T(8,128)S(1)}, u32[]{:S(2)}, u32[]{:S(2)}) collective-permute-start(f32[4,16,16,128]{3,2,1,0:T(8,128)S(1)} %get-tuple-element.90), channel_id=1, source_target_pairs={{32,216},{34,218},{36,220},{38,222},{39,223},{37,221},{35,219},{33... | collective-permute-start | bytes 1572872 | tf_op jit(solution)/shard_map/ppermute | solution.py:77
  95.8 42.2 %copy-start.2 = (f32[4,64,16,128]{3,2,1,0:T(8,128)S(1)}, f32[4,64,16,128]{3,2,1,0:T(8,128)}, u32[]{:S(2)}) copy-start(f32[4,64,16,128]{3,2,1,0:T(8,128)} %g_ref.3) | copy-start | bytes 6291460
  95.8 23.2 %collective-permute-start.24 = (f32[4,8,16,128]{3,2,1,0:T(8,128)S(1)}, f32[4,8,16,128]{3,2,1,0:T(8,128)S(1)}, u32[]{:S(2)}, u32[]{:S(2)}) collective-permute-start(f32[4,8,16,128]{3,2,1,0:T(8,128)S(1)} %get-tuple-element.102), channel_id=1, source_target_pairs={{33,0},{32,1},{35,2},{34,3},{37,4},{36,5},{39,6},{38,7},{41,8},{40... | collective-permute-start | bytes 786440 | tf_op jit(solution)/shard_map/ppermute | solution.py:77
  98.9 28.8 %collective-permute-start.22 = (f32[4,8,16,128]{3,2,1,0:T(8,128)S(1)}, f32[4,8,16,128]{3,2,1,0:T(8,128)S(1)}, u32[]{:S(2)}, u32[]{:S(2)}) collective-permute-start(f32[4,8,16,128]{3,2,1,0:T(8,128)S(1)} %get-tuple-element.99), channel_id=1, source_target_pairs={{32,0},{33,1},{34,2},{35,3},{36,4},{37,5},{38,6},{39,7},{40,8},{41... | collective-permute-start | bytes 786440 | tf_op jit(solution)/shard_map/ppermute | solution.py:77
  99.7 33.4 %collective-permute-start.19 = (f32[4,8,16,128]{3,2,1,0:T(8,128)S(1)}, f32[4,8,16,128]{3,2,1,0:T(8,128)S(1)}, u32[]{:S(2)}, u32[]{:S(2)}) collective-permute-start(f32[4,8,16,128]{3,2,1,0:T(8,128)S(1)} %get-tuple-element.94), channel_id=1, source_target_pairs={{36,0},{37,1},{38,2},{39,3},{32,4},{33,5},{34,6},{35,7},{44,8},{45... | collective-permute-start | bytes 786440 | tf_op jit(solution)/shard_map/ppermute | solution.py:77
  101.4 43.0 %collective-permute-start.20 = (f32[4,8,16,128]{3,2,1,0:T(8,128)S(1)}, f32[4,8,16,128]{3,2,1,0:T(8,128)S(1)}, u32[]{:S(2)}, u32[]{:S(2)}) collective-permute-start(f32[4,8,16,128]{3,2,1,0:T(8,128)S(1)} %get-tuple-element.96), channel_id=1, source_target_pairs={{37,0},{36,1},{39,2},{38,3},{33,4},{32,5},{35,6},{34,7},{45,8},{44... | collective-permute-start | bytes 786440 | tf_op jit(solution)/shard_map/ppermute | solution.py:77
  117.7 26.7 %collective-permute-start.21 = (f32[4,8,16,128]{3,2,1,0:T(8,128)S(1)}, f32[4,8,16,128]{3,2,1,0:T(8,128)S(1)}, u32[]{:S(2)}, u32[]{:S(2)}) collective-permute-start(f32[4,8,16,128]{3,2,1,0:T(8,128)S(1)} %get-tuple-element.97), channel_id=1, source_target_pairs={{34,0},{35,1},{36,2},{37,3},{38,4},{39,5},{32,6},{33,7},{42,8},{43... | collective-permute-start | bytes 786440 | tf_op jit(solution)/shard_map/ppermute | solution.py:77
  119.0 32.5 %collective-permute-start.25 = (f32[4,8,16,128]{3,2,1,0:T(8,128)S(1)}, f32[4,8,16,128]{3,2,1,0:T(8,128)S(1)}, u32[]{:S(2)}, u32[]{:S(2)}) collective-permute-start(f32[4,8,16,128]{3,2,1,0:T(8,128)S(1)} %get-tuple-element.103), channel_id=1, source_target_pairs={{38,0},{39,1},{32,2},{33,3},{34,4},{35,5},{36,6},{37,7},{46,8},{47... | collective-permute-start | bytes 786440 | tf_op jit(solution)/shard_map/ppermute | solution.py:77
  127.7 23.9 %collective-permute-start.23 = (f32[4,8,16,128]{3,2,1,0:T(8,128)S(1)}, f32[4,8,16,128]{3,2,1,0:T(8,128)S(1)}, u32[]{:S(2)}, u32[]{:S(2)}) collective-permute-start(f32[4,8,16,128]{3,2,1,0:T(8,128)S(1)} %get-tuple-element.100), channel_id=1, source_target_pairs={{35,0},{34,1},{37,2},{36,3},{39,4},{38,5},{33,6},{32,7},{43,8},{42... | collective-permute-start | bytes 786440 | tf_op jit(solution)/shard_map/ppermute | solution.py:77
  133.0 19.6 %collective-permute-start.26 = (f32[4,8,16,128]{3,2,1,0:T(8,128)S(1)}, f32[4,8,16,128]{3,2,1,0:T(8,128)S(1)}, u32[]{:S(2)}, u32[]{:S(2)}) collective-permute-start(f32[4,8,16,128]{3,2,1,0:T(8,128)S(1)} %get-tuple-element.104), channel_id=1, source_target_pairs={{39,0},{38,1},{33,2},{32,3},{35,4},{34,5},{37,6},{36,7},{47,8},{46... | collective-permute-start | bytes 786440 | tf_op jit(solution)/shard_map/ppermute | solution.py:77

commit v7 on v6

--- a/solution.py
+++ b/solution.py
@@ -315,7 +315,7 @@
 
 
 def first_edge_kernel(
-    inner_ref, low_ref, high_ref, under_ref, over_ref, from_0_ref, from_1_ref, from_2_ref, own_0_ref, own_1_ref, vx_ref, vy_ref, v_ref, *outs
+    inner_ref, under_ref, over_ref, low_ref, high_ref, from_0_ref, from_1_ref, from_2_ref, own_0_ref, own_1_ref, vx_ref, vy_ref, v_ref, *outs
 ):
     y_place, half, block = as_host()
     middle = jnp.where(y_place == 3, 1.0, 0.0)
@@ -445,7 +445,7 @@
 
     sizes = [33 + 8 * (dy == 0) + (slot == FIRST) for slot, (dy, ds) in enumerate(SLOTS)]
     pieces = call(pack_kernel, [array(size, 16, K) for size in sizes])(density, vel_x, potential_x)
-    pieces = send_all(pieces, exchange_pairs, {3: 7, 4: 6, 5: 1})
+    pieces = send_all(pieces, exchange_pairs, {3: 7, 4: 6, 5: 7})
 
     highest = lax.Precision.HIGHEST
     ty = 0.25 * jnp.dot(potential_y, jnp.asarray(sine_table(1)), precision=highest)
@@ -467,7 +467,7 @@
         3 * 10**9,
     )(*pieces, jnp.asarray(sine_table(-1)), ty, vy)
     v, *sides = call(first_edge_kernel, [array(4, 8, K, K)] + [array(4, 16, 16, K)] * 4)(
-        inner, low, high, under, over, *across, pieces[FIRST], pieces[SECOND], vx, vy
+        inner, under, over, low, high, *across, pieces[FIRST], pieces[SECOND], vx, vy
     )
     low = [send(sides[2 * group + 1], x_pairs(1)) for group in range(2)]
     high = [send(sides[2 * group], x_pairs(-1)) for group in range(2)]
@@ -479,7 +479,7 @@
         )
         for slot, piece in zip(slots, cut):
             pieces[slot] = piece
-    pieces = send_all(pieces, lambda slot: back(exchange_pairs(slot)), {3: 6, 4: 7, 5: 0})
+    pieces = send_all(pieces, lambda slot: back(exchange_pairs(slot)), {})
 
     def by_x(*shape):
         return pl.BlockSpec((1, *shape), lambda x: (x, 0, 0, 0))

time: 156 us -> 158 us (1.013)
  starting transfers between devices: 59.3 us -> 63.8 us
  waiting for transfers between devices: 78.5 us -> 75.5 us
    ppermute x27, starting transfers between devices: 59.3 us -> 63.8 us  [send(): return lax.ppermute(value, AXES, pairs)]
    ppermute x27, waiting for transfers between devices: 78.5 us -> 75.5 us  [send(): return lax.ppermute(value, AXES, pairs)]
  transfers between devices with their start and end apart: 27 -> 27, of which waited for: 10 -> 8; matrix products, arithmetic and copies ran while one was open for 0% -> 0% of each run, Pallas kernels for 7% -> 7%
where the time goes in v7:
time: 158 us; the launch traced here: 156 us
  waiting for transfers between devices  75.5 us (48%)
  starting transfers between devices  63.8 us (40%)
  Pallas kernels  13.4 us (8%)
  local copies, waits for them, and re-layouts  2.37 us (2%)
    ppermute x27, waiting for transfers between devices, send(): return lax.ppermute(value, AXES, pairs)  75.5 us
    ppermute x27, starting transfers between devices, send(): return lax.ppermute(value, AXES, pairs)  63.8 us
    pallas_call x9, Pallas kernels, run(): pl.pallas_call(kernel, out_shape=outs, in_specs=[VMEM] * len(operands), o...  11.4 us
  transfers between devices with their start and end apart: 27, of which 8 were waited for; matrix products, arithmetic and copies ran while one was open for 0% of the time, Pallas kernels for 7%

profile of v7, /device:TPU:39, one launch (start us, length us, event | category | flops | bytes accessed | tf_op | source)
XLA Modules:
  0.0 156.1 jit_solution(16236223894954567012)
XLA Ops:
  0.0 0.7 convert_multiply_fusion
  0.7 0.1 broadcast_in_dim.2.vel_ref
  0.8 1.6 %copy-done.1 = f32[4,64,16,128]{3,2,1,0:T(8,128)S(1)} copy-done((f32[4,64,16,128]{3,2,1,0:T(8,128)S(1)}, f32[4,64,16,128]{3,2,1,0:T(8,128)}, u32[]{:S(2)}) %copy-start.1) | copy-done | bytes 2097176
  2.4 0.7 copy-done.3
  3.0 0.2 pack_kernel.1
  3.2 0.0 copy-start.4
  3.2 5.2 %collective-permute-start.5 = (f32[42,16,128]{2,1,0:T(8,128)S(1)}, f32[42,16,128]{2,1,0:T(8,128)S(1)}, u32[]{:S(2)}, u32[]{:S(2)}) collective-permute-start(f32[42,16,128]{2,1,0:T(8,128)S(1)} %get-tuple-element.57), channel_id=1, source_target_pairs={{0,32},{1,33},{2,34},{3,35},{4,36},{5,37},{6,38},{7,39},{8,40},{9,... | collective-permute-start | bytes 1032200 | tf_op jit(solution)/shard_map/ppermute | solution.py:77
  8.4 6.2 %collective-permute-start = (f32[33,16,128]{2,1,0:T(8,128)S(1)}, f32[33,16,128]{2,1,0:T(8,128)S(1)}, u32[]{:S(2)}, u32[]{:S(2)}) collective-permute-start(f32[33,16,128]{2,1,0:T(8,128)S(1)} %get-tuple-element.50), channel_id=1, source_target_pairs={{0,36},{1,37},{2,38},{3,39},{4,32},{5,33},{6,34},{7,35},{8,44},{9,... | collective-permute-start | bytes 811016 | tf_op jit(solution)/shard_map/ppermute | solution.py:77
  14.6 0.0 collective-permute-start.1
  14.6 4.4 %collective-permute-start.2 = (f32[33,16,128]{2,1,0:T(8,128)S(1)}, f32[33,16,128]{2,1,0:T(8,128)S(1)}, u32[]{:S(2)}, u32[]{:S(2)}) collective-permute-start(f32[33,16,128]{2,1,0:T(8,128)S(1)} %get-tuple-element.52), channel_id=1, source_target_pairs={{0,34},{1,35},{2,36},{3,37},{4,38},{5,39},{6,32},{7,33},{8,42},{9,... | collective-permute-start | bytes 811016 | tf_op jit(solution)/shard_map/ppermute | solution.py:77
  19.0 19.6 %collective-permute-done.3.second_ref.refs_7_.own_1_ref = f32[41,16,128]{2,1,0:T(8,128)S(1)} collective-permute-done((f32[41,16,128]{2,1,0:T(8,128)S(1)}, f32[41,16,128]{2,1,0:T(8,128)S(1)}, u32[]{:S(2)}, u32[]{:S(2)}) %collective-permute-start.3) | collective-permute-done | bytes 335904 | tf_op jit(solution)/shard_map/ppermute | solution.py:77
  38.6 2.6 %collective-permute-start.7 = (f32[33,16,128]{2,1,0:T(8,128)S(1)}, f32[33,16,128]{2,1,0:T(8,128)S(1)}, u32[]{:S(2)}, u32[]{:S(2)}) collective-permute-start(f32[33,16,128]{2,1,0:T(8,128)S(1)} %get-tuple-element.61), channel_id=1, source_target_pairs={{0,39},{1,38},{2,33},{3,32},{4,35},{5,34},{6,37},{7,36},{8,47},{9,... | collective-permute-start | bytes 811016 | tf_op jit(solution)/shard_map/ppermute | solution.py:77
  41.1 0.0 collective-permute-done.5.first_ref.refs_6_.own_0_ref
  41.2 0.0 collective-permute-start.4
  41.2 5.7 %collective-permute-start.6 = (f32[33,16,128]{2,1,0:T(8,128)S(1)}, f32[33,16,128]{2,1,0:T(8,128)S(1)}, u32[]{:S(2)}, u32[]{:S(2)}) collective-permute-start(f32[33,16,128]{2,1,0:T(8,128)S(1)} %get-tuple-element.58), channel_id=1, source_target_pairs={{0,38},{1,39},{2,32},{3,33},{4,34},{5,35},{6,36},{7,37},{8,46},{9,... | collective-permute-start | bytes 811016 | tf_op jit(solution)/shard_map/ppermute | solution.py:77
  46.9 5.6 %collective-permute-done.1.refs_1_ = f32[33,16,128]{2,1,0:T(8,128)S(1)} collective-permute-done((f32[33,16,128]{2,1,0:T(8,128)S(1)}, f32[33,16,128]{2,1,0:T(8,128)S(1)}, u32[]{:S(2)}, u32[]{:S(2)}) %collective-permute-start.1) | collective-permute-done | bytes 270368 | tf_op jit(solution)/shard_map/ppermute | solution.py:77
  52.4 0.7 collective-permute-start.10
  53.1 3.7 %collective-permute-start.8 = (f32[2,8,16,128]{3,2,1,0:T(8,128)S(1)}, f32[2,8,16,128]{3,2,1,0:T(8,128)S(1)}, u32[]{:S(2)}, u32[]{:S(2)}) collective-permute-start(f32[2,8,16,128]{3,2,1,0:T(8,128)S(1)} %across_kernel.1), channel_id=1, source_target_pairs={{32,38},{33,39},{40,46},{41,47},{48,54},{49,55},{56,62},{57,63},{1... | collective-permute-start | bytes 393224 | tf_op jit(solution)/shard_map/ppermute | solution.py:77
  56.8 0.7 collective-permute-start.9
  57.5 8.8 %collective-permute-done.8.from_0_ref = f32[2,8,16,128]{3,2,1,0:T(8,128)S(1)} collective-permute-done((f32[2,8,16,128]{3,2,1,0:T(8,128)S(1)}, f32[2,8,16,128]{3,2,1,0:T(8,128)S(1)}, u32[]{:S(2)}, u32[]{:S(2)}) %collective-permute-start.8) | collective-permute-done | bytes 131104 | tf_op jit(solution)/shard_map/ppermute | solution.py:77
  66.4 0.2 cut_kernel.1
  66.6 1.4 collective-permute-start.13
  68.0 6.0 %collective-permute-start.11 = (f32[8,8,16,128]{3,2,1,0:T(8,128)S(1)}, f32[8,8,16,128]{3,2,1,0:T(8,128)S(1)}, u32[]{:S(2)}, u32[]{:S(2)}) collective-permute-start(f32[8,8,16,128]{3,2,1,0:T(8,128)S(1)} %get-tuple-element.73), channel_id=1, source_target_pairs={{32,34},{34,36},{36,38},{38,32},{39,37},{37,35},{35,33},{33,39},{4... | collective-permute-start | bytes 1572872 | tf_op jit(solution)/shard_map/ppermute | solution.py:77
  74.0 3.1 %collective-permute-start.12 = (f32[8,8,16,128]{3,2,1,0:T(8,128)S(1)}, f32[8,8,16,128]{3,2,1,0:T(8,128)S(1)}, u32[]{:S(2)}, u32[]{:S(2)}) collective-permute-start(f32[8,8,16,128]{3,2,1,0:T(8,128)S(1)} %get-tuple-element.74), channel_id=1, source_target_pairs={{32,38},{34,32},{36,34},{38,36},{39,33},{37,39},{35,37},{33,35},{4... | collective-permute-start | bytes 1572872 | tf_op jit(solution)/shard_map/ppermute | solution.py:77
  77.1 0.2 fusion.ty_ref.refs_9_
  77.3 2.1 %first_kernel.1 = (f32[4,8,128,128]{3,2,1,0:T(8,128)S(1)}, f32[128,128]{1,0:T(8,128)S(1)}, f32[8,128]{1,0:T(8,128)S(1)}) custom-call(f32[33,16,128]{2,1,0:T(8,128)S(1)} %collective-permute-done.refs_0_, f32[33,16,128]{2,1,0:T(8,128)S(1)} %collective-permute-done.1.refs_1_, f32[33,16,128]{2,1,0:T(8,128)S(1)} %collective-permute-done.2.refs_2_, ...), custom_call_target="tpu_custom_call" | custom-call | flops 3000000000 | bytes 4194304 | tf_op jit(solution)/shard_map/first_kernel/pallas_call | solution.py:417
  79.4 8.2 %collective-permute-done.11.under_ref = f32[8,8,16,128]{3,2,1,0:T(8,128)S(1)} collective-permute-done((f32[8,8,16,128]{3,2,1,0:T(8,128)S(1)}, f32[8,8,16,128]{3,2,1,0:T(8,128)S(1)}, u32[]{:S(2)}, u32[]{:S(2)}) %collective-permute-start.11) | collective-permute-done | bytes 524320 | tf_op jit(solution)/shard_map/ppermute | solution.py:77
  87.7 0.8 first_edge_kernel.1
  88.4 0.1 collective-permute-start.19
  88.5 2.4 %collective-permute-start.20 = (f32[4,16,16,128]{3,2,1,0:T(8,128)S(1)}, f32[4,16,16,128]{3,2,1,0:T(8,128)S(1)}, u32[]{:S(2)}, u32[]{:S(2)}) collective-permute-start(f32[4,16,16,128]{3,2,1,0:T(8,128)S(1)} %get-tuple-element.88), channel_id=1, source_target_pairs={{32,216},{34,218},{36,220},{38,222},{39,223},{37,221},{35,219},{33... | collective-permute-start | bytes 1572872 | tf_op jit(solution)/shard_map/ppermute | solution.py:77
  90.9 1.6 collective-permute-start.15
  92.4 0.1 collective-permute-start.16
  92.5 1.4 second_kernel.1.inner_ref
  94.0 0.7 collective-permute-done.19.low_ref
  94.6 7.9 %collective-permute-done.20.high_ref = f32[4,16,16,128]{3,2,1,0:T(8,128)S(1)} collective-permute-done((f32[4,16,16,128]{3,2,1,0:T(8,128)S(1)}, f32[4,16,16,128]{3,2,1,0:T(8,128)S(1)}, u32[]{:S(2)}, u32[]{:S(2)}) %collective-permute-start.20) | collective-permute-done | bytes 524320 | tf_op jit(solution)/shard_map/ppermute | solution.py:77
  102.5 0.2 second_edge_kernel.3
  102.7 0.0 copy-start.2
  102.7 0.1 collective-permute-start.21
  102.8 7.9 %collective-permute-start.22 = (f32[4,8,16,128]{3,2,1,0:T(8,128)S(1)}, f32[4,8,16,128]{3,2,1,0:T(8,128)S(1)}, u32[]{:S(2)}, u32[]{:S(2)}) collective-permute-start(f32[4,8,16,128]{3,2,1,0:T(8,128)S(1)} %get-tuple-element.90), channel_id=1, source_target_pairs={{35,0},{34,1},{37,2},{36,3},{39,4},{38,5},{33,6},{32,7},{43,8},{42... | collective-permute-start | bytes 786440 | tf_op jit(solution)/shard_map/ppermute | solution.py:77
  110.7 1.0 collective-permute-start.24
  111.7 22.6 %collective-permute-done.16.high_ref = f32[4,16,16,128]{3,2,1,0:T(8,128)S(1)} collective-permute-done((f32[4,16,16,128]{3,2,1,0:T(8,128)S(1)}, f32[4,16,16,128]{3,2,1,0:T(8,128)S(1)}, u32[]{:S(2)}, u32[]{:S(2)}) %collective-permute-start.16) | collective-permute-done | bytes 524320 | tf_op jit(solution)/shard_map/ppermute | solution.py:77
  134.3 0.2 second_edge_kernel.2
  134.4 0.1 collective-permute-start.17
  134.5 6.0 %collective-permute-start.18 = (f32[4,8,16,128]{3,2,1,0:T(8,128)S(1)}, f32[4,8,16,128]{3,2,1,0:T(8,128)S(1)}, u32[]{:S(2)}, u32[]{:S(2)}) collective-permute-start(f32[4,8,16,128]{3,2,1,0:T(8,128)S(1)} %get-tuple-element.86), channel_id=1, source_target_pairs={{37,0},{36,1},{39,2},{38,3},{33,4},{32,5},{35,6},{34,7},{45,8},{44... | collective-permute-start | bytes 786440 | tf_op jit(solution)/shard_map/ppermute | solution.py:77
  140.5 2.1 %collective-permute-done.23.refs_4_ = f32[4,8,16,128]{3,2,1,0:T(8,128)S(1)} collective-permute-done((f32[4,8,16,128]{3,2,1,0:T(8,128)S(1)}, f32[4,8,16,128]{3,2,1,0:T(8,128)S(1)}, u32[]{:S(2)}, u32[]{:S(2)}) %collective-permute-start.23) | collective-permute-done | bytes 262176 | tf_op jit(solution)/shard_map/ppermute | solution.py:77
  142.6 5.1 %collective-permute-start.26 = (f32[4,8,16,128]{3,2,1,0:T(8,128)S(1)}, f32[4,8,16,128]{3,2,1,0:T(8,128)S(1)}, u32[]{:S(2)}, u32[]{:S(2)}) collective-permute-start(f32[4,8,16,128]{3,2,1,0:T(8,128)S(1)} %get-tuple-element.94), channel_id=1, source_target_pairs={{33,0},{32,1},{35,2},{34,3},{37,4},{36,5},{39,6},{38,7},{41,8},{40... | collective-permute-start | bytes 786440 | tf_op jit(solution)/shard_map/ppermute | solution.py:77
  147.7 6.4 %local_kernel.1.local_ref = f32[4,64,16,128]{3,2,1,0:T(8,128)S(1)} custom-call(f32[4,64,16,128]{3,2,1,0:T(8,128)S(1)} %copy-done.2, f32[64,128]{1,0:T(8,128)S(1)} %fusion.ty_ref.refs_9_, f32[1,128]{1,0:T(1,128)S(1)} %multiply_bitcast_fusion.vy_ref.refs_10_), custom_call_target="tpu_custom_call" | custom-call | flops 4000000000 | bytes 4194304 | tf_op jit(solution)/shard_map/local_kernel/pallas_call | solution.py:417
  154.2 2.0 %final_kernel.1 = f32[4,64,16,128]{3,2,1,0:T(8,128)} custom-call(f32[4,64,16,128]{3,2,1,0:T(8,128)S(1)} %local_kernel.1.local_ref, f32[4,8,16,128]{3,2,1,0:T(8,128)S(1)} %collective-permute-done.17.refs_0_, f32[4,8,16,128]{3,2,1,0:T(8,128)S(1)} %collective-permute-done.18.refs_1_, f32[4,8,16,128]{3,2,1,0:T(8,128)S(1)} %collective-permute-done.21.refs_2_, ...), custom_call_target="tpu_custom_call" | custom-call | bytes 6291456 | tf_op jit(solution)/shard_map/final_kernel/pallas_call | solution.py:487
  (36 shorter events, 0.1 us)
Async XLA Ops:
  0.0 77.1 %copy-start = (f32[64,128]{1,0:T(8,128)S(1)}, f32[64,128]{1,0:T(8,128)}, u32[]{:S(2)}) copy-start(f32[64,128]{1,0:T(8,128)} %param.11) | copy-start | bytes 98308
  0.8 1.6 %copy-start.1 = (f32[4,64,16,128]{3,2,1,0:T(8,128)S(1)}, f32[4,64,16,128]{3,2,1,0:T(8,128)}, u32[]{:S(2)}) copy-start(f32[4,64,16,128]{3,2,1,0:T(8,128)} %g_ref.3) | copy-start | bytes 6291460
  2.4 0.7 copy-start.3
  3.0 74.0 %copy-start.6 = (f32[128]{0:T(128)S(1)}, f32[128]{0:T(128)}, u32[]{:S(2)}) copy-start(f32[128]{0:T(128)} %param.13) | copy-start | bytes 1540
  3.0 74.0 %copy-start.7 = (s32[128]{0:T(128)S(1)}, s32[128]{0:T(128)}, u32[]{:S(2)}) copy-start(s32[128]{0:T(128)} %param.15) | copy-start | bytes 1540
  3.0 74.1 %copy-start.5 = (f32[128,128]{1,0:T(8,128)S(1)}, f32[128,128]{1,0:T(8,128)}, u32[]{:S(2)}) copy-start(f32[128,128]{1,0:T(8,128)} %constant.14.clone) | copy-start | bytes 196612
  3.2 74.1 %copy-start.4 = (f32[128,128]{1,0:T(8,128)S(1)}, f32[128,128]{1,0:T(8,128)}, u32[]{:S(2)}) copy-start(f32[128,128]{1,0:T(8,128)} %constant.15.clone.refs_8_) | copy-start | bytes 196612
  3.2 37.9 %collective-permute-start.5 = (f32[42,16,128]{2,1,0:T(8,128)S(1)}, f32[42,16,128]{2,1,0:T(8,128)S(1)}, u32[]{:S(2)}, u32[]{:S(2)}) collective-permute-start(f32[42,16,128]{2,1,0:T(8,128)S(1)} %get-tuple-element.57), channel_id=1, source_target_pairs={{0,32},{1,33},{2,34},{3,35},{4,36},{5,37},{6,38},{7,39},{8,40},{9,... | collective-permute-start | bytes 1032200 | tf_op jit(solution)/shard_map/ppermute | solution.py:77
  8.4 30.2 %collective-permute-start.3 = (f32[41,16,128]{2,1,0:T(8,128)S(1)}, f32[41,16,128]{2,1,0:T(8,128)S(1)}, u32[]{:S(2)}, u32[]{:S(2)}) collective-permute-start(f32[41,16,128]{2,1,0:T(8,128)S(1)} %get-tuple-element.54), channel_id=1, source_target_pairs={{0,33},{1,32},{2,35},{3,34},{4,37},{5,36},{6,39},{7,38},{8,41},{9,... | collective-permute-start | bytes 1007624 | tf_op jit(solution)/shard_map/ppermute | solution.py:77
  8.4 32.8 %collective-permute-start = (f32[33,16,128]{2,1,0:T(8,128)S(1)}, f32[33,16,128]{2,1,0:T(8,128)S(1)}, u32[]{:S(2)}, u32[]{:S(2)}) collective-permute-start(f32[33,16,128]{2,1,0:T(8,128)S(1)} %get-tuple-element.50), channel_id=1, source_target_pairs={{0,36},{1,37},{2,38},{3,39},{4,32},{5,33},{6,34},{7,35},{8,44},{9,... | collective-permute-start | bytes 811016 | tf_op jit(solution)/shard_map/ppermute | solution.py:77
  14.6 37.8 %collective-permute-start.1 = (f32[33,16,128]{2,1,0:T(8,128)S(1)}, f32[33,16,128]{2,1,0:T(8,128)S(1)}, u32[]{:S(2)}, u32[]{:S(2)}) collective-permute-start(f32[33,16,128]{2,1,0:T(8,128)S(1)} %get-tuple-element.51), channel_id=1, source_target_pairs={{0,37},{1,36},{2,39},{3,38},{4,33},{5,32},{6,35},{7,34},{8,45},{9,... | collective-permute-start | bytes 811016 | tf_op jit(solution)/shard_map/ppermute | solution.py:77
  14.6 38.5 %collective-permute-start.2 = (f32[33,16,128]{2,1,0:T(8,128)S(1)}, f32[33,16,128]{2,1,0:T(8,128)S(1)}, u32[]{:S(2)}, u32[]{:S(2)}) collective-permute-start(f32[33,16,128]{2,1,0:T(8,128)S(1)} %get-tuple-element.52), channel_id=1, source_target_pairs={{0,34},{1,35},{2,36},{3,37},{4,38},{5,39},{6,32},{7,33},{8,42},{9,... | collective-permute-start | bytes 811016 | tf_op jit(solution)/shard_map/ppermute | solution.py:77
  38.6 27.7 %collective-permute-start.7 = (f32[33,16,128]{2,1,0:T(8,128)S(1)}, f32[33,16,128]{2,1,0:T(8,128)S(1)}, u32[]{:S(2)}, u32[]{:S(2)}) collective-permute-start(f32[33,16,128]{2,1,0:T(8,128)S(1)} %get-tuple-element.61), channel_id=1, source_target_pairs={{0,39},{1,38},{2,33},{3,32},{4,35},{5,34},{6,37},{7,36},{8,47},{9,... | collective-permute-start | bytes 811016 | tf_op jit(solution)/shard_map/ppermute | solution.py:77
  41.2 25.2 %collective-permute-start.4 = (f32[33,16,128]{2,1,0:T(8,128)S(1)}, f32[33,16,128]{2,1,0:T(8,128)S(1)}, u32[]{:S(2)}, u32[]{:S(2)}) collective-permute-start(f32[33,16,128]{2,1,0:T(8,128)S(1)} %get-tuple-element.55), channel_id=1, source_target_pairs={{0,35},{1,34},{2,37},{3,36},{4,39},{5,38},{6,33},{7,32},{8,43},{9,... | collective-permute-start | bytes 811016 | tf_op jit(solution)/shard_map/ppermute | solution.py:77
  41.2 25.2 %collective-permute-start.6 = (f32[33,16,128]{2,1,0:T(8,128)S(1)}, f32[33,16,128]{2,1,0:T(8,128)S(1)}, u32[]{:S(2)}, u32[]{:S(2)}) collective-permute-start(f32[33,16,128]{2,1,0:T(8,128)S(1)} %get-tuple-element.58), channel_id=1, source_target_pairs={{0,38},{1,39},{2,32},{3,33},{4,34},{5,35},{6,36},{7,37},{8,46},{9,... | collective-permute-start | bytes 811016 | tf_op jit(solution)/shard_map/ppermute | solution.py:77
  52.4 4.4 %collective-permute-start.10 = (f32[2,8,16,128]{3,2,1,0:T(8,128)S(1)}, f32[2,8,16,128]{3,2,1,0:T(8,128)S(1)}, u32[]{:S(2)}, u32[]{:S(2)}) collective-permute-start(f32[2,8,16,128]{3,2,1,0:T(8,128)S(1)} %across_kernel.1), channel_id=1, source_target_pairs={{36,38},{37,39},{44,46},{45,47},{52,54},{53,55},{60,62},{61,63},{5... | collective-permute-start | bytes 393224 | tf_op jit(solution)/shard_map/ppermute | solution.py:77
  53.1 13.2 %collective-permute-start.8 = (f32[2,8,16,128]{3,2,1,0:T(8,128)S(1)}, f32[2,8,16,128]{3,2,1,0:T(8,128)S(1)}, u32[]{:S(2)}, u32[]{:S(2)}) collective-permute-start(f32[2,8,16,128]{3,2,1,0:T(8,128)S(1)} %across_kernel.1), channel_id=1, source_target_pairs={{32,38},{33,39},{40,46},{41,47},{48,54},{49,55},{56,62},{57,63},{1... | collective-permute-start | bytes 393224 | tf_op jit(solution)/shard_map/ppermute | solution.py:77
  56.8 9.5 %collective-permute-start.9 = (f32[2,8,16,128]{3,2,1,0:T(8,128)S(1)}, f32[2,8,16,128]{3,2,1,0:T(8,128)S(1)}, u32[]{:S(2)}, u32[]{:S(2)}) collective-permute-start(f32[2,8,16,128]{3,2,1,0:T(8,128)S(1)} %across_kernel.1), channel_id=1, source_target_pairs={{34,38},{35,39},{42,46},{43,47},{50,54},{51,55},{58,62},{59,63},{3... | collective-permute-start | bytes 393224 | tf_op jit(solution)/shard_map/ppermute | solution.py:77
  66.6 21.1 %collective-permute-start.13 = (f32[8,16,16,128]{3,2,1,0:T(8,128)S(1)}, f32[8,16,16,128]{3,2,1,0:T(8,128)S(1)}, u32[]{:S(2)}, u32[]{:S(2)}) collective-permute-start(f32[8,16,16,128]{3,2,1,0:T(8,128)S(1)} %get-tuple-element.75), channel_id=1, source_target_pairs={{32,40},{34,42},{36,44},{38,46},{39,47},{37,45},{35,43},{33,41},{4... | collective-permute-start | bytes 3145736 | tf_op jit(solution)/shard_map/ppermute | solution.py:77
  68.0 19.6 %collective-permute-start.14 = (f32[8,16,16,128]{3,2,1,0:T(8,128)S(1)}, f32[8,16,16,128]{3,2,1,0:T(8,128)S(1)}, u32[]{:S(2)}, u32[]{:S(2)}) collective-permute-start(f32[8,16,16,128]{3,2,1,0:T(8,128)S(1)} %get-tuple-element.76), channel_id=1, source_target_pairs={{32,216},{34,218},{36,220},{38,222},{39,223},{37,221},{35,219},{33... | collective-permute-start | bytes 3145736 | tf_op jit(solution)/shard_map/ppermute | solution.py:77
  68.0 19.6 %collective-permute-start.11 = (f32[8,8,16,128]{3,2,1,0:T(8,128)S(1)}, f32[8,8,16,128]{3,2,1,0:T(8,128)S(1)}, u32[]{:S(2)}, u32[]{:S(2)}) collective-permute-start(f32[8,8,16,128]{3,2,1,0:T(8,128)S(1)} %get-tuple-element.73), channel_id=1, source_target_pairs={{32,34},{34,36},{36,38},{38,32},{39,37},{37,35},{35,33},{33,39},{4... | collective-permute-start | bytes 1572872 | tf_op jit(solution)/shard_map/ppermute | solution.py:77
  74.0 13.7 %collective-permute-start.12 = (f32[8,8,16,128]{3,2,1,0:T(8,128)S(1)}, f32[8,8,16,128]{3,2,1,0:T(8,128)S(1)}, u32[]{:S(2)}, u32[]{:S(2)}) collective-permute-start(f32[8,8,16,128]{3,2,1,0:T(8,128)S(1)} %get-tuple-element.74), channel_id=1, source_target_pairs={{32,38},{34,32},{36,34},{38,36},{39,33},{37,39},{35,37},{33,35},{4... | collective-permute-start | bytes 1572872 | tf_op jit(solution)/shard_map/ppermute | solution.py:77
  88.4 6.2 %collective-permute-start.19 = (f32[4,16,16,128]{3,2,1,0:T(8,128)S(1)}, f32[4,16,16,128]{3,2,1,0:T(8,128)S(1)}, u32[]{:S(2)}, u32[]{:S(2)}) collective-permute-start(f32[4,16,16,128]{3,2,1,0:T(8,128)S(1)} %get-tuple-element.87), channel_id=1, source_target_pairs={{32,40},{34,42},{36,44},{38,46},{39,47},{37,45},{35,43},{33,41},{4... | collective-permute-start | bytes 1572872 | tf_op jit(solution)/shard_map/ppermute | solution.py:77
  88.5 14.0 %collective-permute-start.20 = (f32[4,16,16,128]{3,2,1,0:T(8,128)S(1)}, f32[4,16,16,128]{3,2,1,0:T(8,128)S(1)}, u32[]{:S(2)}, u32[]{:S(2)}) collective-permute-start(f32[4,16,16,128]{3,2,1,0:T(8,128)S(1)} %get-tuple-element.88), channel_id=1, source_target_pairs={{32,216},{34,218},{36,220},{38,222},{39,223},{37,221},{35,219},{33... | collective-permute-start | bytes 1572872 | tf_op jit(solution)/shard_map/ppermute | solution.py:77
  90.9 19.8 %collective-permute-start.15 = (f32[4,16,16,128]{3,2,1,0:T(8,128)S(1)}, f32[4,16,16,128]{3,2,1,0:T(8,128)S(1)}, u32[]{:S(2)}, u32[]{:S(2)}) collective-permute-start(f32[4,16,16,128]{3,2,1,0:T(8,128)S(1)} %get-tuple-element.83), channel_id=1, source_target_pairs={{32,40},{34,42},{36,44},{38,46},{39,47},{37,45},{35,43},{33,41},{4... | collective-permute-start | bytes 1572872 | tf_op jit(solution)/shard_map/ppermute | solution.py:77
  92.4 41.8 %collective-permute-start.16 = (f32[4,16,16,128]{3,2,1,0:T(8,128)S(1)}, f32[4,16,16,128]{3,2,1,0:T(8,128)S(1)}, u32[]{:S(2)}, u32[]{:S(2)}) collective-permute-start(f32[4,16,16,128]{3,2,1,0:T(8,128)S(1)} %get-tuple-element.84), channel_id=1, source_target_pairs={{32,216},{34,218},{36,220},{38,222},{39,223},{37,221},{35,219},{33... | collective-permute-start | bytes 1572872 | tf_op jit(solution)/shard_map/ppermute | solution.py:77
  102.7 45.0 %copy-start.2 = (f32[4,64,16,128]{3,2,1,0:T(8,128)S(1)}, f32[4,64,16,128]{3,2,1,0:T(8,128)}, u32[]{:S(2)}) copy-start(f32[4,64,16,128]{3,2,1,0:T(8,128)} %g_ref.3) | copy-start | bytes 6291460
  102.7 31.8 %collective-permute-start.21 = (f32[4,8,16,128]{3,2,1,0:T(8,128)S(1)}, f32[4,8,16,128]{3,2,1,0:T(8,128)S(1)}, u32[]{:S(2)}, u32[]{:S(2)}) collective-permute-start(f32[4,8,16,128]{3,2,1,0:T(8,128)S(1)} %get-tuple-element.89), channel_id=1, source_target_pairs={{34,0},{35,1},{36,2},{37,3},{38,4},{39,5},{32,6},{33,7},{42,8},{43... | collective-permute-start | bytes 786440 | tf_op jit(solution)/shard_map/ppermute | solution.py:77
  102.8 37.7 %collective-permute-start.22 = (f32[4,8,16,128]{3,2,1,0:T(8,128)S(1)}, f32[4,8,16,128]{3,2,1,0:T(8,128)S(1)}, u32[]{:S(2)}, u32[]{:S(2)}) collective-permute-start(f32[4,8,16,128]{3,2,1,0:T(8,128)S(1)} %get-tuple-element.90), channel_id=1, source_target_pairs={{35,0},{34,1},{37,2},{36,3},{39,4},{38,5},{33,6},{32,7},{43,8},{42... | collective-permute-start | bytes 786440 | tf_op jit(solution)/shard_map/ppermute | solution.py:77
  110.7 32.0 %collective-permute-start.23 = (f32[4,8,16,128]{3,2,1,0:T(8,128)S(1)}, f32[4,8,16,128]{3,2,1,0:T(8,128)S(1)}, u32[]{:S(2)}, u32[]{:S(2)}) collective-permute-start(f32[4,8,16,128]{3,2,1,0:T(8,128)S(1)} %get-tuple-element.91), channel_id=1, source_target_pairs={{38,0},{39,1},{32,2},{33,3},{34,4},{35,5},{36,6},{37,7},{46,8},{47... | collective-permute-start | bytes 786440 | tf_op jit(solution)/shard_map/ppermute | solution.py:77
  110.7 43.5 %collective-permute-start.24 = (f32[4,8,16,128]{3,2,1,0:T(8,128)S(1)}, f32[4,8,16,128]{3,2,1,0:T(8,128)S(1)}, u32[]{:S(2)}, u32[]{:S(2)}) collective-permute-start(f32[4,8,16,128]{3,2,1,0:T(8,128)S(1)} %get-tuple-element.92), channel_id=1, source_target_pairs={{39,0},{38,1},{33,2},{32,3},{35,4},{34,5},{37,6},{36,7},{47,8},{46... | collective-permute-start | bytes 786440 | tf_op jit(solution)/shard_map/ppermute | solution.py:77
  134.4 19.7 %collective-permute-start.17 = (f32[4,8,16,128]{3,2,1,0:T(8,128)S(1)}, f32[4,8,16,128]{3,2,1,0:T(8,128)S(1)}, u32[]{:S(2)}, u32[]{:S(2)}) collective-permute-start(f32[4,8,16,128]{3,2,1,0:T(8,128)S(1)} %get-tuple-element.85), channel_id=1, source_target_pairs={{36,0},{37,1},{38,2},{39,3},{32,4},{33,5},{34,6},{35,7},{44,8},{45... | collective-permute-start | bytes 786440 | tf_op jit(solution)/shard_map/ppermute | solution.py:77
  134.5 19.6 %collective-permute-start.18 = (f32[4,8,16,128]{3,2,1,0:T(8,128)S(1)}, f32[4,8,16,128]{3,2,1,0:T(8,128)S(1)}, u32[]{:S(2)}, u32[]{:S(2)}) collective-permute-start(f32[4,8,16,128]{3,2,1,0:T(8,128)S(1)} %get-tuple-element.86), channel_id=1, source_target_pairs={{37,0},{36,1},{39,2},{38,3},{33,4},{32,5},{35,6},{34,7},{45,8},{44... | collective-permute-start | bytes 786440 | tf_op jit(solution)/shard_map/ppermute | solution.py:77
  140.5 13.7 %collective-permute-start.25 = (f32[4,8,16,128]{3,2,1,0:T(8,128)S(1)}, f32[4,8,16,128]{3,2,1,0:T(8,128)S(1)}, u32[]{:S(2)}, u32[]{:S(2)}) collective-permute-start(f32[4,8,16,128]{3,2,1,0:T(8,128)S(1)} %get-tuple-element.93), channel_id=1, source_target_pairs={{32,0},{33,1},{34,2},{35,3},{36,4},{37,5},{38,6},{39,7},{40,8},{41... | collective-permute-start | bytes 786440 | tf_op jit(solution)/shard_map/ppermute | solution.py:77
  142.6 11.5 %collective-permute-start.26 = (f32[4,8,16,128]{3,2,1,0:T(8,128)S(1)}, f32[4,8,16,128]{3,2,1,0:T(8,128)S(1)}, u32[]{:S(2)}, u32[]{:S(2)}) collective-permute-start(f32[4,8,16,128]{3,2,1,0:T(8,128)S(1)} %get-tuple-element.94), channel_id=1, source_target_pairs={{33,0},{32,1},{35,2},{34,3},{37,4},{36,5},{39,6},{38,7},{41,8},{40... | collective-permute-start | bytes 786440 | tf_op jit(solution)/shard_map/ppermute | solution.py:77

commit v8 on v6

--- a/solution.py
+++ b/solution.py
@@ -18,6 +18,7 @@
 GROUPS = ((2, 3, 4, 5), (0, 1, 6, 7))
 FIRST, SECOND = SLOTS.index((0, 0)), SLOTS.index((0, 1))
 VMEM = pl.BlockSpec(memory_space=pltpu.VMEM)
+HBM = pl.BlockSpec(memory_space=pltpu.HBM)
 
 
 def flat(x, y, z, core):
@@ -48,9 +49,9 @@
     ]
 
 
-def x_pairs(step):
+def x_pairs(odd):
     return [
-        (place(block, part), place((block + step) % 32, part))
+        (place(block, part), place((block + (1 if block % 2 == odd else -1)) % 32, part))
         for block in range(32)
         for part in range(8)
     ]
@@ -234,10 +235,11 @@
 
 
 def cut_kernel(*refs):
-    pieces, (head_ref, tail_ref, bottom_ref, top_ref) = refs[:8], refs[8:]
+    pieces, (away_ref, near_ref, bottom_ref, top_ref) = refs[:8], refs[8:]
+    core = lax.axis_index("gx") & 1
     for slot in range(8):
-        head_ref[slot] = pieces[slot][0:16]
-        tail_ref[slot] = pieces[slot][16:32]
+        away_ref[slot] = pieces[slot][pl.ds(core * 16, 16)]
+        near_ref[slot] = pieces[slot][pl.ds(16 - core * 16, 16)]
         for x in range(4):
             bottom_ref[slot, 2 * x : 2 * x + 2] = pieces[slot][8 * x : 8 * x + 2]
             top_ref[slot, 2 * x : 2 * x + 2] = pieces[slot][8 * x + 6 : 8 * x + 8]
@@ -276,6 +278,20 @@
     return up[None], down[None]
 
 
+def outer_layers(away_ref, near_ref, i):
+    even = (lax.axis_index("gx") & 1) == 0
+
+    def low(n):
+        at = slice(8 - 8 * n, 16 - 8 * n)
+        return jnp.where(even, away_ref[i, at], near_ref[i, at])
+
+    def high(n):
+        at = slice(8 * n, 8 * n + 8)
+        return jnp.where(even, near_ref[i, at], away_ref[i, at])
+
+    return low, high
+
+
 def first_kernel(*refs):
     pieces, (sine_ref, ty_ref, vy_ref), (v_ref, vx_ref, tx_ref), (field, tables) = refs[:8], refs[8:11], refs[11:14], refs[14:]
     for slot in range(8):
@@ -315,7 +331,7 @@
 
 
 def first_edge_kernel(
-    inner_ref, low_ref, high_ref, under_ref, over_ref, from_0_ref, from_1_ref, from_2_ref, own_0_ref, own_1_ref, vx_ref, vy_ref, v_ref, *outs
+    inner_ref, away_ref, near_ref, under_ref, over_ref, from_0_ref, from_1_ref, from_2_ref, own_0_ref, own_1_ref, vx_ref, vy_ref, v_ref, *outs
 ):
     y_place, half, block = as_host()
     middle = jnp.where(y_place == 3, 1.0, 0.0)
@@ -333,6 +349,9 @@
         up, down = rates(vx_ref, at, 0.0625)
         group = int(slot in GROUPS[1])
         i = GROUPS[group].index(slot)
+        low, high = outer_layers(away_ref, near_ref, slot)
+        even = (lax.axis_index("gx") & 1) == 0
+        layers = []
         for x in range(4):
             rows = slice(2 * x, 2 * x + 2)
             if dy == 0:
@@ -344,19 +363,17 @@
             over = jnp.where(half == 0, beside(over_ref, after, rows), beside(over_ref, before, rows))
             under = jnp.where(under_middle, across * middle, under)
             over = jnp.where(over_middle, across * middle, over)
-            value = inner_ref[x, :, at, :] + outer_drift(
-                x,
-                lambda n: low_ref[slot, 8 - 8 * n : 16 - 8 * n],
-                lambda n: high_ref[slot, 8 * n : 8 * n + 8],
-                up,
-                down,
-            )
+            value = inner_ref[x, :, at, :] + outer_drift(x, low, high, up, down)
             bottom = jnp.concatenate([up_y * (4.0 * under[1:2] - under[0:1]), -up_y * under[1:2]], 0)
             top = jnp.concatenate([-down_y * over[0:1], down_y * (4.0 * over[0:1] - over[1:2])], 0)
             value = jnp.concatenate([value[0:2] + bottom, value[2:6], value[6:8] + top], 0)
             v_ref[x, :, at, :] = value
-            side = outs[2 * group + x // 2]
-            side[i, 8 * (x % 2) : 8 * (x % 2) + 8] = value
+            layers.append(value)
+        near_out, away_out = outs[2 * group : 2 * group + 2]
+        for x in range(2):
+            at = slice(8 * x, 8 * x + 8)
+            away_out[i, at] = jnp.where(even, layers[x], layers[x + 2])
+            near_out[i, at] = jnp.where(even, layers[x + 2], layers[x])
 
 
 def second_kernel(v_ref, tx_ref, vx_ref, out_ref, tables):
@@ -376,25 +393,26 @@
                 out_ref[x, y] = wigner[i] + inner_drift(mine[i], x, lambda at: v_ref[at, y], toward, rate)
 
 
-def second_edge_kernel(slots, inner_ref, low_ref, high_ref, vx_ref, *pieces):
+def second_edge_kernel(slots, inner_ref, away_ref, near_ref, vx_ref, *pieces):
     for i, slot in enumerate(slots):
         at = kx_of(slot)
         up, down = rates(vx_ref, at, 0.125)
-        for x in range(4):
-            pieces[i][x] = inner_ref[x, :, at, :] + outer_drift(
-                x,
-                lambda n: low_ref[i, 8 - 8 * n : 16 - 8 * n],
-                lambda n: high_ref[i, 8 * n : 8 * n + 8],
-                up,
-                down,
-            )
+        low, high = outer_layers(away_ref, near_ref, i)
+        for x in range(4):
+            pieces[i][x] = inner_ref[x, :, at, :] + outer_drift(x, low, high, up, down)
 
 
 def final_kernel(local_ref, *refs):
-    pieces, out_ref = refs[:8], refs[8]
-    for slot in range(8):
-        at = rows_to(slot)
-        out_ref[:, at] = local_ref[:, at] + pieces[slot][...]
+    pieces, (out_ref, total, sems) = refs[:8], refs[8:]
+    copies = []
+    for x in range(4):
+        for slot in range(8):
+            at = rows_to(slot)
+            total[x, at] = local_ref[x, at] + pieces[slot][x]
+        copies.append(pltpu.make_async_copy(total.at[x], out_ref.at[x], sems.at[x]))
+        copies[-1].start()
+    for copy in copies:
+        copy.wait()
 
 
 MIB = 1 << 20
@@ -412,17 +430,17 @@
     return pl.CostEstimate(flops=flops, bytes_accessed=mib * MIB, transcendentals=0)
 
 
-def call(kernel, outs, scratch=(), flops=0, mib=4):
+def call(kernel, outs, scratch=(), flops=0, mib=4, ins=None, out_specs=None):
     def run(*operands):
         return pl.pallas_call(
             kernel,
             out_shape=outs,
-            in_specs=[VMEM] * len(operands),
-            out_specs=[VMEM] * len(outs) if isinstance(outs, list) else VMEM,
+            in_specs=ins or [VMEM] * len(operands),
+            out_specs=out_specs or ([VMEM] * len(outs) if isinstance(outs, list) else VMEM),
             scratch_shapes=list(scratch),
             compiler_params=params(),
             cost_estimate=cost(flops, mib),
-            name=(kernel.func if isinstance(kernel, functools.partial) else kernel).__name__,
+            name=kernel.func.__name__ if isinstance(kernel, functools.partial) else kernel.__name__,
         )(*operands)
 
     return run
@@ -456,8 +474,8 @@
     across = call(across_kernel, array(2, 8, 16, K), mib=0)(pieces[FIRST], pieces[SECOND])
     across = [send(across, middle_pairs(y)) for y in range(3)]
     *pieces, across[0], across[1], across[2] = lax.optimization_barrier((*pieces, *across))
-    head, tail, bottom, top = call(cut_kernel, [array(8, 16, 16, K)] * 2 + [array(8, 8, 16, K)] * 2)(*pieces)
-    low, high = send(tail, x_pairs(1)), send(head, x_pairs(-1))
+    away, near, bottom, top = call(cut_kernel, [array(8, 16, 16, K)] * 2 + [array(8, 8, 16, K)] * 2)(*pieces)
+    near, away = send(near, x_pairs(0)), send(away, x_pairs(1))
     under, over = send(top, y_pairs(1)), send(bottom, y_pairs(-1))
     left_tables = pltpu.VMEM((4, 2 * K, 2 * K), BF16)
     inner, vx, tx = call(
@@ -467,32 +485,25 @@
         3 * 10**9,
     )(*pieces, jnp.asarray(sine_table(-1)), ty, vy)
     v, *sides = call(first_edge_kernel, [array(4, 8, K, K)] + [array(4, 16, 16, K)] * 4)(
-        inner, low, high, under, over, *across, pieces[FIRST], pieces[SECOND], vx, vy
+        inner, away, near, under, over, *across, pieces[FIRST], pieces[SECOND], vx, vy
     )
-    low = [send(sides[2 * group + 1], x_pairs(1)) for group in range(2)]
-    high = [send(sides[2 * group], x_pairs(-1)) for group in range(2)]
+    away = [send(sides[2 * group + 1], x_pairs(1)) for group in range(2)]
+    near = [send(sides[2 * group], x_pairs(0)) for group in range(2)]
     inner = call(second_kernel, array(4, 8, K, K), [left_tables], 2 * 10**9)(v, tx, vx)
     pieces = [None] * 8
     for group, slots in enumerate(GROUPS):
         cut = call(functools.partial(second_edge_kernel, slots), [array(4, 8, 16, K)] * 4, mib=2)(
-            inner, low[group], high[group], vx
+            inner, away[group], near[group], vx
         )
         for slot, piece in zip(slots, cut):
             pieces[slot] = piece
     pieces = send_all(pieces, lambda slot: back(exchange_pairs(slot)), {3: 6, 4: 7, 5: 0})
 
-    def by_x(*shape):
-        return pl.BlockSpec((1, *shape), lambda x: (x, 0, 0, 0))
-
-    return pl.pallas_call(
+    return call(
         final_kernel,
-        grid=(4,),
-        out_shape=array(4, 64, 16, K),
-        in_specs=[by_x(64, 16, K)] + [by_x(8, 16, K)] * 8,
-        out_specs=by_x(64, 16, K),
-        compiler_params=params(),
-        cost_estimate=cost(0, 6),
-        name="final_kernel",
+        array(4, 64, 16, K),
+        [pltpu.VMEM((4, 64, 16, K), F32), pltpu.SemaphoreType.DMA((4,))],
+        out_specs=HBM,
     )(local, *pieces)
 
 

time: 156 us -> 158 us (1.013)
  starting transfers between devices: 59.3 us -> 61.1 us
    ppermute x27, starting transfers between devices: 59.3 us -> 61.1 us  [send(): return lax.ppermute(value, AXES, pairs)]
  transfers between devices with their start and end apart: 27 -> 27, of which waited for: 10 -> 8; matrix products, arithmetic and copies ran while one was open for 0% -> 0% of each run, Pallas kernels for 7% -> 7%
where the time goes in v8:
time: 158 us
  waiting for transfers between devices  79.7 us (50%)
  starting transfers between devices  61.1 us (39%)
  Pallas kernels  13.1 us (8%)
  local copies, waits for them, and re-layouts  2.37 us (2%)
    ppermute x27, waiting for transfers between devices, send(): return lax.ppermute(value, AXES, pairs)  79.7 us
    ppermute x27, starting transfers between devices, send(): return lax.ppermute(value, AXES, pairs)  61.1 us
    pallas_call x10, Pallas kernels, run(): pl.pallas_call(kernel, out_shape=outs, in_specs=ins or [VMEM] * len(opera...  13.1 us
  transfers between devices with their start and end apart: 27, of which 8 were waited for; matrix products, arithmetic and copies ran while one was open for 0% of the time, Pallas kernels for 7%

profile of v8, /device:TPU:39, one launch (start us, length us, event | category | flops | bytes accessed | tf_op | source)
XLA Modules:
  0.0 157.5 jit_solution(14517323494533416422)
XLA Ops:
  0.0 0.7 convert_multiply_fusion
  0.7 0.1 broadcast_in_dim.2.vel_ref
  0.8 1.6 %copy-done.1 = f32[4,64,16,128]{3,2,1,0:T(8,128)S(1)} copy-done((f32[4,64,16,128]{3,2,1,0:T(8,128)S(1)}, f32[4,64,16,128]{3,2,1,0:T(8,128)}, u32[]{:S(2)}) %copy-start.1) | copy-done | bytes 2097176
  2.4 0.7 copy-done.3
  3.0 0.2 pack_kernel.1
  3.2 0.0 copy-start.4
  3.2 5.2 %collective-permute-start.5 = (f32[42,16,128]{2,1,0:T(8,128)S(1)}, f32[42,16,128]{2,1,0:T(8,128)S(1)}, u32[]{:S(2)}, u32[]{:S(2)}) collective-permute-start(f32[42,16,128]{2,1,0:T(8,128)S(1)} %get-tuple-element.65), channel_id=1, source_target_pairs={{0,32},{1,33},{2,34},{3,35},{4,36},{5,37},{6,38},{7,39},{8,40},{9,... | collective-permute-start | bytes 1032200 | tf_op jit(solution)/shard_map/ppermute | solution.py:78
  8.4 0.0 collective-permute-start.3
  8.4 4.1 %collective-permute-start.1 = (f32[33,16,128]{2,1,0:T(8,128)S(1)}, f32[33,16,128]{2,1,0:T(8,128)S(1)}, u32[]{:S(2)}, u32[]{:S(2)}) collective-permute-start(f32[33,16,128]{2,1,0:T(8,128)S(1)} %get-tuple-element.58), channel_id=1, source_target_pairs={{0,37},{1,36},{2,39},{3,38},{4,33},{5,32},{6,35},{7,34},{8,45},{9,... | collective-permute-start | bytes 811016 | tf_op jit(solution)/shard_map/ppermute | solution.py:78
  12.5 2.1 %collective-permute-start = (f32[33,16,128]{2,1,0:T(8,128)S(1)}, f32[33,16,128]{2,1,0:T(8,128)S(1)}, u32[]{:S(2)}, u32[]{:S(2)}) collective-permute-start(f32[33,16,128]{2,1,0:T(8,128)S(1)} %get-tuple-element.56), channel_id=1, source_target_pairs={{0,36},{1,37},{2,38},{3,39},{4,32},{5,33},{6,34},{7,35},{8,44},{9,... | collective-permute-start | bytes 811016 | tf_op jit(solution)/shard_map/ppermute | solution.py:78
  14.6 3.1 %collective-permute-start.2 = (f32[33,16,128]{2,1,0:T(8,128)S(1)}, f32[33,16,128]{2,1,0:T(8,128)S(1)}, u32[]{:S(2)}, u32[]{:S(2)}) collective-permute-start(f32[33,16,128]{2,1,0:T(8,128)S(1)} %get-tuple-element.60), channel_id=1, source_target_pairs={{0,34},{1,35},{2,36},{3,37},{4,38},{5,39},{6,32},{7,33},{8,42},{9,... | collective-permute-start | bytes 811016 | tf_op jit(solution)/shard_map/ppermute | solution.py:78
  17.8 26.3 %collective-permute-done.1.refs_1_ = f32[33,16,128]{2,1,0:T(8,128)S(1)} collective-permute-done((f32[33,16,128]{2,1,0:T(8,128)S(1)}, f32[33,16,128]{2,1,0:T(8,128)S(1)}, u32[]{:S(2)}, u32[]{:S(2)}) %collective-permute-start.1) | collective-permute-done | bytes 270368 | tf_op jit(solution)/shard_map/ppermute | solution.py:78
  44.0 0.0 collective-permute-start.7
  44.0 3.0 %collective-permute-start.4 = (f32[33,16,128]{2,1,0:T(8,128)S(1)}, f32[33,16,128]{2,1,0:T(8,128)S(1)}, u32[]{:S(2)}, u32[]{:S(2)}) collective-permute-start(f32[33,16,128]{2,1,0:T(8,128)S(1)} %get-tuple-element.63), channel_id=1, source_target_pairs={{0,35},{1,34},{2,37},{3,36},{4,39},{5,38},{6,33},{7,32},{8,43},{9,... | collective-permute-start | bytes 811016 | tf_op jit(solution)/shard_map/ppermute | solution.py:78
  47.0 2.7 %collective-permute-start.6 = (f32[33,16,128]{2,1,0:T(8,128)S(1)}, f32[33,16,128]{2,1,0:T(8,128)S(1)}, u32[]{:S(2)}, u32[]{:S(2)}) collective-permute-start(f32[33,16,128]{2,1,0:T(8,128)S(1)} %get-tuple-element.66), channel_id=1, source_target_pairs={{0,38},{1,39},{2,32},{3,33},{4,34},{5,35},{6,36},{7,37},{8,46},{9,... | collective-permute-start | bytes 811016 | tf_op jit(solution)/shard_map/ppermute | solution.py:78
  49.8 0.7 collective-permute-start.10
  50.4 4.9 %collective-permute-start.8 = (f32[2,8,16,128]{3,2,1,0:T(8,128)S(1)}, f32[2,8,16,128]{3,2,1,0:T(8,128)S(1)}, u32[]{:S(2)}, u32[]{:S(2)}) collective-permute-start(f32[2,8,16,128]{3,2,1,0:T(8,128)S(1)} %across_kernel.1), channel_id=1, source_target_pairs={{32,38},{33,39},{40,46},{41,47},{48,54},{49,55},{56,62},{57,63},{1... | collective-permute-start | bytes 393224 | tf_op jit(solution)/shard_map/ppermute | solution.py:78
  55.4 0.7 collective-permute-start.9
  56.1 11.2 %collective-permute-done.8.from_0_ref = f32[2,8,16,128]{3,2,1,0:T(8,128)S(1)} collective-permute-done((f32[2,8,16,128]{3,2,1,0:T(8,128)S(1)}, f32[2,8,16,128]{3,2,1,0:T(8,128)S(1)}, u32[]{:S(2)}, u32[]{:S(2)}) %collective-permute-start.8) | collective-permute-done | bytes 131104 | tf_op jit(solution)/shard_map/ppermute | solution.py:78
  67.3 0.2 cut_kernel.1
  67.5 0.1 collective-permute-start.11
  67.6 0.6 collective-permute-start.12
  68.2 3.4 %collective-permute-start.14 = (f32[8,8,16,128]{3,2,1,0:T(8,128)S(1)}, f32[8,8,16,128]{3,2,1,0:T(8,128)S(1)}, u32[]{:S(2)}, u32[]{:S(2)}) collective-permute-start(f32[8,8,16,128]{3,2,1,0:T(8,128)S(1)} %get-tuple-element.82), channel_id=1, source_target_pairs={{32,38},{34,32},{36,34},{38,36},{39,33},{37,39},{35,37},{33,35},{4... | collective-permute-start | bytes 1572872 | tf_op jit(solution)/shard_map/ppermute | solution.py:78
  71.6 0.2 fusion.ty_ref.refs_9_
  71.8 2.1 %first_kernel.1 = (f32[4,8,128,128]{3,2,1,0:T(8,128)S(1)}, f32[128,128]{1,0:T(8,128)S(1)}, f32[8,128]{1,0:T(8,128)S(1)}) custom-call(f32[33,16,128]{2,1,0:T(8,128)S(1)} %collective-permute-done.refs_0_, f32[33,16,128]{2,1,0:T(8,128)S(1)} %collective-permute-done.1.refs_1_, f32[33,16,128]{2,1,0:T(8,128)S(1)} %collective-permute-done.2.refs_2_, ...), custom_call_target="tpu_custom_call" | custom-call | flops 3000000000 | bytes 4194304 | tf_op jit(solution)/shard_map/first_kernel/pallas_call | solution.py:435
  73.9 9.8 %collective-permute-done.13.under_ref = f32[8,8,16,128]{3,2,1,0:T(8,128)S(1)} collective-permute-done((f32[8,8,16,128]{3,2,1,0:T(8,128)S(1)}, f32[8,8,16,128]{3,2,1,0:T(8,128)S(1)}, u32[]{:S(2)}, u32[]{:S(2)}) %collective-permute-start.13) | collective-permute-done | bytes 524320 | tf_op jit(solution)/shard_map/ppermute | solution.py:78
  83.8 0.1 collective-permute-done.11.away_ref
  83.9 1.0 first_edge_kernel.1
  84.9 3.9 %collective-permute-start.17 = (f32[4,16,16,128]{3,2,1,0:T(8,128)S(1)}, f32[4,16,16,128]{3,2,1,0:T(8,128)S(1)}, u32[]{:S(2)}, u32[]{:S(2)}) collective-permute-start(f32[4,16,16,128]{3,2,1,0:T(8,128)S(1)} %get-tuple-element.92), channel_id=1, source_target_pairs={{32,216},{34,218},{36,220},{38,222},{39,223},{37,221},{35,219},{33... | collective-permute-start | bytes 1572872 | tf_op jit(solution)/shard_map/ppermute | solution.py:78
  88.8 0.2 collective-permute-start.15
  89.0 0.3 collective-permute-start.16
  89.3 1.4 second_kernel.1.inner_ref
  90.7 4.9 %collective-permute-done.17.away_ref = f32[4,16,16,128]{3,2,1,0:T(8,128)S(1)} collective-permute-done((f32[4,16,16,128]{3,2,1,0:T(8,128)S(1)}, f32[4,16,16,128]{3,2,1,0:T(8,128)S(1)}, u32[]{:S(2)}, u32[]{:S(2)}) %collective-permute-start.17) | collective-permute-done | bytes 524320 | tf_op jit(solution)/shard_map/ppermute | solution.py:78
  95.7 0.2 second_edge_kernel.3
  95.9 0.0 copy-start.2
  95.9 0.6 collective-permute-start.24
  96.5 1.9 %collective-permute-start.22 = (f32[4,8,16,128]{3,2,1,0:T(8,128)S(1)}, f32[4,8,16,128]{3,2,1,0:T(8,128)S(1)}, u32[]{:S(2)}, u32[]{:S(2)}) collective-permute-start(f32[4,8,16,128]{3,2,1,0:T(8,128)S(1)} %get-tuple-element.99), channel_id=1, source_target_pairs={{32,0},{33,1},{34,2},{35,3},{36,4},{37,5},{38,6},{39,7},{40,8},{41... | collective-permute-start | bytes 786440 | tf_op jit(solution)/shard_map/ppermute | solution.py:78
  98.3 2.4 %collective-permute-start.19 = (f32[4,8,16,128]{3,2,1,0:T(8,128)S(1)}, f32[4,8,16,128]{3,2,1,0:T(8,128)S(1)}, u32[]{:S(2)}, u32[]{:S(2)}) collective-permute-start(f32[4,8,16,128]{3,2,1,0:T(8,128)S(1)} %get-tuple-element.94), channel_id=1, source_target_pairs={{36,0},{37,1},{38,2},{39,3},{32,4},{33,5},{34,6},{35,7},{44,8},{45... | collective-permute-start | bytes 786440 | tf_op jit(solution)/shard_map/ppermute | solution.py:78
  100.7 18.7 %collective-permute-done.15.away_ref = f32[4,16,16,128]{3,2,1,0:T(8,128)S(1)} collective-permute-done((f32[4,16,16,128]{3,2,1,0:T(8,128)S(1)}, f32[4,16,16,128]{3,2,1,0:T(8,128)S(1)}, u32[]{:S(2)}, u32[]{:S(2)}) %collective-permute-start.15) | collective-permute-done | bytes 524320 | tf_op jit(solution)/shard_map/ppermute | solution.py:78
  119.4 0.2 second_edge_kernel.2
  119.6 5.5 %collective-permute-start.21 = (f32[4,8,16,128]{3,2,1,0:T(8,128)S(1)}, f32[4,8,16,128]{3,2,1,0:T(8,128)S(1)}, u32[]{:S(2)}, u32[]{:S(2)}) collective-permute-start(f32[4,8,16,128]{3,2,1,0:T(8,128)S(1)} %get-tuple-element.97), channel_id=1, source_target_pairs={{34,0},{35,1},{36,2},{37,3},{38,4},{39,5},{32,6},{33,7},{42,8},{43... | collective-permute-start | bytes 786440 | tf_op jit(solution)/shard_map/ppermute | solution.py:78
  125.1 0.1 collective-permute-start.25
  125.2 5.6 %collective-permute-start.23 = (f32[4,8,16,128]{3,2,1,0:T(8,128)S(1)}, f32[4,8,16,128]{3,2,1,0:T(8,128)S(1)}, u32[]{:S(2)}, u32[]{:S(2)}) collective-permute-start(f32[4,8,16,128]{3,2,1,0:T(8,128)S(1)} %get-tuple-element.100), channel_id=1, source_target_pairs={{35,0},{34,1},{37,2},{36,3},{39,4},{38,5},{33,6},{32,7},{43,8},{42... | collective-permute-start | bytes 786440 | tf_op jit(solution)/shard_map/ppermute | solution.py:78
  130.8 2.0 %collective-permute-done.19.refs_0_ = f32[4,8,16,128]{3,2,1,0:T(8,128)S(1)} collective-permute-done((f32[4,8,16,128]{3,2,1,0:T(8,128)S(1)}, f32[4,8,16,128]{3,2,1,0:T(8,128)S(1)}, u32[]{:S(2)}, u32[]{:S(2)}) %collective-permute-start.19) | collective-permute-done | bytes 262176 | tf_op jit(solution)/shard_map/ppermute | solution.py:78
  132.8 10.1 %collective-permute-start.26 = (f32[4,8,16,128]{3,2,1,0:T(8,128)S(1)}, f32[4,8,16,128]{3,2,1,0:T(8,128)S(1)}, u32[]{:S(2)}, u32[]{:S(2)}) collective-permute-start(f32[4,8,16,128]{3,2,1,0:T(8,128)S(1)} %get-tuple-element.104), channel_id=1, source_target_pairs={{39,0},{38,1},{33,2},{32,3},{35,4},{34,5},{37,6},{36,7},{47,8},{46... | collective-permute-start | bytes 786440 | tf_op jit(solution)/shard_map/ppermute | solution.py:78
  142.9 6.4 %local_kernel.1.local_ref = f32[4,64,16,128]{3,2,1,0:T(8,128)S(1)} custom-call(f32[4,64,16,128]{3,2,1,0:T(8,128)S(1)} %copy-done.2, f32[64,128]{1,0:T(8,128)S(1)} %fusion.ty_ref.refs_9_, f32[1,128]{1,0:T(1,128)S(1)} %multiply_bitcast_fusion.vy_ref.refs_10_), custom_call_target="tpu_custom_call" | custom-call | flops 4000000000 | bytes 4194304 | tf_op jit(solution)/shard_map/local_kernel/pallas_call | solution.py:435
  149.4 6.6 %collective-permute-done.25.refs_4_ = f32[4,8,16,128]{3,2,1,0:T(8,128)S(1)} collective-permute-done((f32[4,8,16,128]{3,2,1,0:T(8,128)S(1)}, f32[4,8,16,128]{3,2,1,0:T(8,128)S(1)}, u32[]{:S(2)}, u32[]{:S(2)}) %collective-permute-start.25) | collective-permute-done | bytes 262176 | tf_op jit(solution)/shard_map/ppermute | solution.py:78
  156.0 1.4 final_kernel.1
  (36 shorter events, 0.1 us)
Async XLA Ops:
  0.0 71.6 %copy-start = (f32[64,128]{1,0:T(8,128)S(1)}, f32[64,128]{1,0:T(8,128)}, u32[]{:S(2)}) copy-start(f32[64,128]{1,0:T(8,128)} %param.11) | copy-start | bytes 98308
  0.8 1.6 %copy-start.1 = (f32[4,64,16,128]{3,2,1,0:T(8,128)S(1)}, f32[4,64,16,128]{3,2,1,0:T(8,128)}, u32[]{:S(2)}) copy-start(f32[4,64,16,128]{3,2,1,0:T(8,128)} %g_ref.3) | copy-start | bytes 6291460
  2.4 0.7 copy-start.3
  3.0 68.5 %copy-start.6 = (f32[128]{0:T(128)S(1)}, f32[128]{0:T(128)}, u32[]{:S(2)}) copy-start(f32[128]{0:T(128)} %param.13) | copy-start | bytes 1540
  3.0 68.5 %copy-start.7 = (s32[128]{0:T(128)S(1)}, s32[128]{0:T(128)}, u32[]{:S(2)}) copy-start(s32[128]{0:T(128)} %param.15) | copy-start | bytes 1540
  3.0 68.6 %copy-start.5 = (f32[128,128]{1,0:T(8,128)S(1)}, f32[128,128]{1,0:T(8,128)}, u32[]{:S(2)}) copy-start(f32[128,128]{1,0:T(8,128)} %constant.14.clone) | copy-start | bytes 196612
  3.2 68.6 %copy-start.4 = (f32[128,128]{1,0:T(8,128)S(1)}, f32[128,128]{1,0:T(8,128)}, u32[]{:S(2)}) copy-start(f32[128,128]{1,0:T(8,128)} %constant.15.clone.refs_8_) | copy-start | bytes 196612
  3.2 43.8 %collective-permute-start.5 = (f32[42,16,128]{2,1,0:T(8,128)S(1)}, f32[42,16,128]{2,1,0:T(8,128)S(1)}, u32[]{:S(2)}, u32[]{:S(2)}) collective-permute-start(f32[42,16,128]{2,1,0:T(8,128)S(1)} %get-tuple-element.65), channel_id=1, source_target_pairs={{0,32},{1,33},{2,34},{3,35},{4,36},{5,37},{6,38},{7,39},{8,40},{9,... | collective-permute-start | bytes 1032200 | tf_op jit(solution)/shard_map/ppermute | solution.py:78
  8.4 35.6 %collective-permute-start.3 = (f32[41,16,128]{2,1,0:T(8,128)S(1)}, f32[41,16,128]{2,1,0:T(8,128)S(1)}, u32[]{:S(2)}, u32[]{:S(2)}) collective-permute-start(f32[41,16,128]{2,1,0:T(8,128)S(1)} %get-tuple-element.62), channel_id=1, source_target_pairs={{0,33},{1,32},{2,35},{3,34},{4,37},{5,36},{6,39},{7,38},{8,41},{9,... | collective-permute-start | bytes 1007624 | tf_op jit(solution)/shard_map/ppermute | solution.py:78
  8.4 35.6 %collective-permute-start.1 = (f32[33,16,128]{2,1,0:T(8,128)S(1)}, f32[33,16,128]{2,1,0:T(8,128)S(1)}, u32[]{:S(2)}, u32[]{:S(2)}) collective-permute-start(f32[33,16,128]{2,1,0:T(8,128)S(1)} %get-tuple-element.58), channel_id=1, source_target_pairs={{0,37},{1,36},{2,39},{3,38},{4,33},{5,32},{6,35},{7,34},{8,45},{9,... | collective-permute-start | bytes 811016 | tf_op jit(solution)/shard_map/ppermute | solution.py:78
  12.5 37.3 %collective-permute-start = (f32[33,16,128]{2,1,0:T(8,128)S(1)}, f32[33,16,128]{2,1,0:T(8,128)S(1)}, u32[]{:S(2)}, u32[]{:S(2)}) collective-permute-start(f32[33,16,128]{2,1,0:T(8,128)S(1)} %get-tuple-element.56), channel_id=1, source_target_pairs={{0,36},{1,37},{2,38},{3,39},{4,32},{5,33},{6,34},{7,35},{8,44},{9,... | collective-permute-start | bytes 811016 | tf_op jit(solution)/shard_map/ppermute | solution.py:78
  14.6 35.8 %collective-permute-start.2 = (f32[33,16,128]{2,1,0:T(8,128)S(1)}, f32[33,16,128]{2,1,0:T(8,128)S(1)}, u32[]{:S(2)}, u32[]{:S(2)}) collective-permute-start(f32[33,16,128]{2,1,0:T(8,128)S(1)} %get-tuple-element.60), channel_id=1, source_target_pairs={{0,34},{1,35},{2,36},{3,37},{4,38},{5,39},{6,32},{7,33},{8,42},{9,... | collective-permute-start | bytes 811016 | tf_op jit(solution)/shard_map/ppermute | solution.py:78
  44.0 23.2 %collective-permute-start.7 = (f32[33,16,128]{2,1,0:T(8,128)S(1)}, f32[33,16,128]{2,1,0:T(8,128)S(1)}, u32[]{:S(2)}, u32[]{:S(2)}) collective-permute-start(f32[33,16,128]{2,1,0:T(8,128)S(1)} %get-tuple-element.67), channel_id=1, source_target_pairs={{0,39},{1,38},{2,33},{3,32},{4,35},{5,34},{6,37},{7,36},{8,47},{9,... | collective-permute-start | bytes 811016 | tf_op jit(solution)/shard_map/ppermute | solution.py:78
  44.0 23.2 %collective-permute-start.4 = (f32[33,16,128]{2,1,0:T(8,128)S(1)}, f32[33,16,128]{2,1,0:T(8,128)S(1)}, u32[]{:S(2)}, u32[]{:S(2)}) collective-permute-start(f32[33,16,128]{2,1,0:T(8,128)S(1)} %get-tuple-element.63), channel_id=1, source_target_pairs={{0,35},{1,34},{2,37},{3,36},{4,39},{5,38},{6,33},{7,32},{8,43},{9,... | collective-permute-start | bytes 811016 | tf_op jit(solution)/shard_map/ppermute | solution.py:78
  47.0 20.2 %collective-permute-start.6 = (f32[33,16,128]{2,1,0:T(8,128)S(1)}, f32[33,16,128]{2,1,0:T(8,128)S(1)}, u32[]{:S(2)}, u32[]{:S(2)}) collective-permute-start(f32[33,16,128]{2,1,0:T(8,128)S(1)} %get-tuple-element.66), channel_id=1, source_target_pairs={{0,38},{1,39},{2,32},{3,33},{4,34},{5,35},{6,36},{7,37},{8,46},{9,... | collective-permute-start | bytes 811016 | tf_op jit(solution)/shard_map/ppermute | solution.py:78
  49.8 5.6 %collective-permute-start.10 = (f32[2,8,16,128]{3,2,1,0:T(8,128)S(1)}, f32[2,8,16,128]{3,2,1,0:T(8,128)S(1)}, u32[]{:S(2)}, u32[]{:S(2)}) collective-permute-start(f32[2,8,16,128]{3,2,1,0:T(8,128)S(1)} %across_kernel.1), channel_id=1, source_target_pairs={{36,38},{37,39},{44,46},{45,47},{52,54},{53,55},{60,62},{61,63},{5... | collective-permute-start | bytes 393224 | tf_op jit(solution)/shard_map/ppermute | solution.py:78
  50.4 16.8 %collective-permute-start.8 = (f32[2,8,16,128]{3,2,1,0:T(8,128)S(1)}, f32[2,8,16,128]{3,2,1,0:T(8,128)S(1)}, u32[]{:S(2)}, u32[]{:S(2)}) collective-permute-start(f32[2,8,16,128]{3,2,1,0:T(8,128)S(1)} %across_kernel.1), channel_id=1, source_target_pairs={{32,38},{33,39},{40,46},{41,47},{48,54},{49,55},{56,62},{57,63},{1... | collective-permute-start | bytes 393224 | tf_op jit(solution)/shard_map/ppermute | solution.py:78
  55.4 11.8 %collective-permute-start.9 = (f32[2,8,16,128]{3,2,1,0:T(8,128)S(1)}, f32[2,8,16,128]{3,2,1,0:T(8,128)S(1)}, u32[]{:S(2)}, u32[]{:S(2)}) collective-permute-start(f32[2,8,16,128]{3,2,1,0:T(8,128)S(1)} %across_kernel.1), channel_id=1, source_target_pairs={{34,38},{35,39},{42,46},{43,47},{50,54},{51,55},{58,62},{59,63},{3... | collective-permute-start | bytes 393224 | tf_op jit(solution)/shard_map/ppermute | solution.py:78
  67.5 16.4 %collective-permute-start.11 = (f32[8,16,16,128]{3,2,1,0:T(8,128)S(1)}, f32[8,16,16,128]{3,2,1,0:T(8,128)S(1)}, u32[]{:S(2)}, u32[]{:S(2)}) collective-permute-start(f32[8,16,16,128]{3,2,1,0:T(8,128)S(1)} %get-tuple-element.79), channel_id=1, source_target_pairs={{32,216},{34,218},{36,220},{38,222},{39,223},{37,221},{35,219},{33... | collective-permute-start | bytes 3145736 | tf_op jit(solution)/shard_map/ppermute | solution.py:78
  67.6 16.3 %collective-permute-start.12 = (f32[8,16,16,128]{3,2,1,0:T(8,128)S(1)}, f32[8,16,16,128]{3,2,1,0:T(8,128)S(1)}, u32[]{:S(2)}, u32[]{:S(2)}) collective-permute-start(f32[8,16,16,128]{3,2,1,0:T(8,128)S(1)} %get-tuple-element.80), channel_id=1, source_target_pairs={{32,40},{34,42},{36,44},{38,46},{39,47},{37,45},{35,43},{33,41},{4... | collective-permute-start | bytes 3145736 | tf_op jit(solution)/shard_map/ppermute | solution.py:78
  68.2 15.6 %collective-permute-start.13 = (f32[8,8,16,128]{3,2,1,0:T(8,128)S(1)}, f32[8,8,16,128]{3,2,1,0:T(8,128)S(1)}, u32[]{:S(2)}, u32[]{:S(2)}) collective-permute-start(f32[8,8,16,128]{3,2,1,0:T(8,128)S(1)} %get-tuple-element.81), channel_id=1, source_target_pairs={{32,34},{34,36},{36,38},{38,32},{39,37},{37,35},{35,33},{33,39},{4... | collective-permute-start | bytes 1572872 | tf_op jit(solution)/shard_map/ppermute | solution.py:78
  68.2 15.6 %collective-permute-start.14 = (f32[8,8,16,128]{3,2,1,0:T(8,128)S(1)}, f32[8,8,16,128]{3,2,1,0:T(8,128)S(1)}, u32[]{:S(2)}, u32[]{:S(2)}) collective-permute-start(f32[8,8,16,128]{3,2,1,0:T(8,128)S(1)} %get-tuple-element.82), channel_id=1, source_target_pairs={{32,38},{34,32},{36,34},{38,36},{39,33},{37,39},{35,37},{33,35},{4... | collective-permute-start | bytes 1572872 | tf_op jit(solution)/shard_map/ppermute | solution.py:78
  84.9 10.8 %collective-permute-start.17 = (f32[4,16,16,128]{3,2,1,0:T(8,128)S(1)}, f32[4,16,16,128]{3,2,1,0:T(8,128)S(1)}, u32[]{:S(2)}, u32[]{:S(2)}) collective-permute-start(f32[4,16,16,128]{3,2,1,0:T(8,128)S(1)} %get-tuple-element.92), channel_id=1, source_target_pairs={{32,216},{34,218},{36,220},{38,222},{39,223},{37,221},{35,219},{33... | collective-permute-start | bytes 1572872 | tf_op jit(solution)/shard_map/ppermute | solution.py:78
  88.8 6.9 %collective-permute-start.18 = (f32[4,16,16,128]{3,2,1,0:T(8,128)S(1)}, f32[4,16,16,128]{3,2,1,0:T(8,128)S(1)}, u32[]{:S(2)}, u32[]{:S(2)}) collective-permute-start(f32[4,16,16,128]{3,2,1,0:T(8,128)S(1)} %get-tuple-element.93), channel_id=1, source_target_pairs={{32,40},{34,42},{36,44},{38,46},{39,47},{37,45},{35,43},{33,41},{4... | collective-permute-start | bytes 1572872 | tf_op jit(solution)/shard_map/ppermute | solution.py:78
  88.8 30.6 %collective-permute-start.15 = (f32[4,16,16,128]{3,2,1,0:T(8,128)S(1)}, f32[4,16,16,128]{3,2,1,0:T(8,128)S(1)}, u32[]{:S(2)}, u32[]{:S(2)}) collective-permute-start(f32[4,16,16,128]{3,2,1,0:T(8,128)S(1)} %get-tuple-element.89), channel_id=1, source_target_pairs={{32,216},{34,218},{36,220},{38,222},{39,223},{37,221},{35,219},{33... | collective-permute-start | bytes 1572872 | tf_op jit(solution)/shard_map/ppermute | solution.py:78
  89.0 30.4 %collective-permute-start.16 = (f32[4,16,16,128]{3,2,1,0:T(8,128)S(1)}, f32[4,16,16,128]{3,2,1,0:T(8,128)S(1)}, u32[]{:S(2)}, u32[]{:S(2)}) collective-permute-start(f32[4,16,16,128]{3,2,1,0:T(8,128)S(1)} %get-tuple-element.90), channel_id=1, source_target_pairs={{32,40},{34,42},{36,44},{38,46},{39,47},{37,45},{35,43},{33,41},{4... | collective-permute-start | bytes 1572872 | tf_op jit(solution)/shard_map/ppermute | solution.py:78
  95.9 47.1 %copy-start.2 = (f32[4,64,16,128]{3,2,1,0:T(8,128)S(1)}, f32[4,64,16,128]{3,2,1,0:T(8,128)}, u32[]{:S(2)}) copy-start(f32[4,64,16,128]{3,2,1,0:T(8,128)} %g_ref.3) | copy-start | bytes 6291460
  95.9 29.2 %collective-permute-start.24 = (f32[4,8,16,128]{3,2,1,0:T(8,128)S(1)}, f32[4,8,16,128]{3,2,1,0:T(8,128)S(1)}, u32[]{:S(2)}, u32[]{:S(2)}) collective-permute-start(f32[4,8,16,128]{3,2,1,0:T(8,128)S(1)} %get-tuple-element.102), channel_id=1, source_target_pairs={{33,0},{32,1},{35,2},{34,3},{37,4},{36,5},{39,6},{38,7},{41,8},{40... | collective-permute-start | bytes 786440 | tf_op jit(solution)/shard_map/ppermute | solution.py:78
  96.5 28.8 %collective-permute-start.22 = (f32[4,8,16,128]{3,2,1,0:T(8,128)S(1)}, f32[4,8,16,128]{3,2,1,0:T(8,128)S(1)}, u32[]{:S(2)}, u32[]{:S(2)}) collective-permute-start(f32[4,8,16,128]{3,2,1,0:T(8,128)S(1)} %get-tuple-element.99), channel_id=1, source_target_pairs={{32,0},{33,1},{34,2},{35,3},{36,4},{37,5},{38,6},{39,7},{40,8},{41... | collective-permute-start | bytes 786440 | tf_op jit(solution)/shard_map/ppermute | solution.py:78
  98.3 34.5 %collective-permute-start.19 = (f32[4,8,16,128]{3,2,1,0:T(8,128)S(1)}, f32[4,8,16,128]{3,2,1,0:T(8,128)S(1)}, u32[]{:S(2)}, u32[]{:S(2)}) collective-permute-start(f32[4,8,16,128]{3,2,1,0:T(8,128)S(1)} %get-tuple-element.94), channel_id=1, source_target_pairs={{36,0},{37,1},{38,2},{39,3},{32,4},{33,5},{34,6},{35,7},{44,8},{45... | collective-permute-start | bytes 786440 | tf_op jit(solution)/shard_map/ppermute | solution.py:78
  119.4 30.0 %collective-permute-start.20 = (f32[4,8,16,128]{3,2,1,0:T(8,128)S(1)}, f32[4,8,16,128]{3,2,1,0:T(8,128)S(1)}, u32[]{:S(2)}, u32[]{:S(2)}) collective-permute-start(f32[4,8,16,128]{3,2,1,0:T(8,128)S(1)} %get-tuple-element.96), channel_id=1, source_target_pairs={{37,0},{36,1},{39,2},{38,3},{33,4},{32,5},{35,6},{34,7},{45,8},{44... | collective-permute-start | bytes 786440 | tf_op jit(solution)/shard_map/ppermute | solution.py:78
  119.6 29.8 %collective-permute-start.21 = (f32[4,8,16,128]{3,2,1,0:T(8,128)S(1)}, f32[4,8,16,128]{3,2,1,0:T(8,128)S(1)}, u32[]{:S(2)}, u32[]{:S(2)}) collective-permute-start(f32[4,8,16,128]{3,2,1,0:T(8,128)S(1)} %get-tuple-element.97), channel_id=1, source_target_pairs={{34,0},{35,1},{36,2},{37,3},{38,4},{39,5},{32,6},{33,7},{42,8},{43... | collective-permute-start | bytes 786440 | tf_op jit(solution)/shard_map/ppermute | solution.py:78
  125.1 30.8 %collective-permute-start.25 = (f32[4,8,16,128]{3,2,1,0:T(8,128)S(1)}, f32[4,8,16,128]{3,2,1,0:T(8,128)S(1)}, u32[]{:S(2)}, u32[]{:S(2)}) collective-permute-start(f32[4,8,16,128]{3,2,1,0:T(8,128)S(1)} %get-tuple-element.103), channel_id=1, source_target_pairs={{38,0},{39,1},{32,2},{33,3},{34,4},{35,5},{36,6},{37,7},{46,8},{47... | collective-permute-start | bytes 786440 | tf_op jit(solution)/shard_map/ppermute | solution.py:78
  125.2 30.7 %collective-permute-start.23 = (f32[4,8,16,128]{3,2,1,0:T(8,128)S(1)}, f32[4,8,16,128]{3,2,1,0:T(8,128)S(1)}, u32[]{:S(2)}, u32[]{:S(2)}) collective-permute-start(f32[4,8,16,128]{3,2,1,0:T(8,128)S(1)} %get-tuple-element.100), channel_id=1, source_target_pairs={{35,0},{34,1},{37,2},{36,3},{39,4},{38,5},{33,6},{32,7},{43,8},{42... | collective-permute-start | bytes 786440 | tf_op jit(solution)/shard_map/ppermute | solution.py:78
  132.8 23.1 %collective-permute-start.26 = (f32[4,8,16,128]{3,2,1,0:T(8,128)S(1)}, f32[4,8,16,128]{3,2,1,0:T(8,128)S(1)}, u32[]{:S(2)}, u32[]{:S(2)}) collective-permute-start(f32[4,8,16,128]{3,2,1,0:T(8,128)S(1)} %get-tuple-element.104), channel_id=1, source_target_pairs={{39,0},{38,1},{33,2},{32,3},{35,4},{34,5},{37,6},{36,7},{47,8},{46... | collective-permute-start | bytes 786440 | tf_op jit(solution)/shard_map/ppermute | solution.py:78

commit v9 on v8

--- a/solution.py
+++ b/solution.py
@@ -393,7 +393,8 @@
                 out_ref[x, y] = wigner[i] + inner_drift(mine[i], x, lambda at: v_ref[at, y], toward, rate)
 
 
-def second_edge_kernel(slots, inner_ref, away_ref, near_ref, vx_ref, *pieces):
+def second_edge_kernel(slots, inner_ref, one_ref, other_ref, vx_ref, *pieces):
+    away_ref, near_ref = (other_ref, one_ref) if slots == GROUPS[0] else (one_ref, other_ref)
     for i, slot in enumerate(slots):
         at = kx_of(slot)
         up, down = rates(vx_ref, at, 0.125)
@@ -493,7 +494,7 @@
     pieces = [None] * 8
     for group, slots in enumerate(GROUPS):
         cut = call(functools.partial(second_edge_kernel, slots), [array(4, 8, 16, K)] * 4, mib=2)(
-            inner, away[group], near[group], vx
+            inner, *((near[0], away[0]) if group == 0 else (away[1], near[1])), vx
         )
         for slot, piece in zip(slots, cut):
             pieces[slot] = piece

time: 158 us -> 156 us (0.987)
  starting transfers between devices: 61.1 us -> 57.5 us
    ppermute x27, starting transfers between devices: 61.1 us -> 57.5 us  [send(): return lax.ppermute(value, AXES, pairs)]
  transfers between devices with their start and end apart: 27 -> 27, of which waited for: 8 -> 10; matrix products, arithmetic and copies ran while one was open for 0% -> 0% of each run, Pallas kernels for 7% -> 7%
where the time goes in v9:
time: 156 us; the launch traced here: 155 us
  waiting for transfers between devices  80.6 us (52%)
  starting transfers between devices  57.5 us (37%)
  Pallas kernels  13.1 us (8%)
  local copies, waits for them, and re-layouts  2.37 us (2%)
    ppermute x27, waiting for transfers between devices, send(): return lax.ppermute(value, AXES, pairs)  80.6 us
    ppermute x27, starting transfers between devices, send(): return lax.ppermute(value, AXES, pairs)  57.5 us
    pallas_call x10, Pallas kernels, run(): pl.pallas_call(kernel, out_shape=outs, in_specs=ins or [VMEM] * len(opera...  13.1 us
  transfers between devices with their start and end apart: 27, of which 10 were waited for; matrix products, arithmetic and copies ran while one was open for 0% of the time, Pallas kernels for 7%

profile of v9, /device:TPU:39, one launch (start us, length us, event | category | flops | bytes accessed | tf_op | source)
XLA Modules:
  0.0 154.9 jit_solution(14730430563704617506)
XLA Ops:
  0.0 0.7 convert_multiply_fusion
  0.7 0.1 broadcast_in_dim.2.vel_ref
  0.8 1.6 %copy-done.1 = f32[4,64,16,128]{3,2,1,0:T(8,128)S(1)} copy-done((f32[4,64,16,128]{3,2,1,0:T(8,128)S(1)}, f32[4,64,16,128]{3,2,1,0:T(8,128)}, u32[]{:S(2)}) %copy-start.1) | copy-done | bytes 2097176
  2.4 0.7 copy-done.3
  3.0 0.2 pack_kernel.1
  3.2 0.0 copy-start.4
  3.2 5.2 %collective-permute-start.5 = (f32[42,16,128]{2,1,0:T(8,128)S(1)}, f32[42,16,128]{2,1,0:T(8,128)S(1)}, u32[]{:S(2)}, u32[]{:S(2)}) collective-permute-start(f32[42,16,128]{2,1,0:T(8,128)S(1)} %get-tuple-element.65), channel_id=1, source_target_pairs={{0,32},{1,33},{2,34},{3,35},{4,36},{5,37},{6,38},{7,39},{8,40},{9,... | collective-permute-start | bytes 1032200 | tf_op jit(solution)/shard_map/ppermute | solution.py:78
  8.4 4.1 %collective-permute-start.1 = (f32[33,16,128]{2,1,0:T(8,128)S(1)}, f32[33,16,128]{2,1,0:T(8,128)S(1)}, u32[]{:S(2)}, u32[]{:S(2)}) collective-permute-start(f32[33,16,128]{2,1,0:T(8,128)S(1)} %get-tuple-element.58), channel_id=1, source_target_pairs={{0,37},{1,36},{2,39},{3,38},{4,33},{5,32},{6,35},{7,34},{8,45},{9,... | collective-permute-start | bytes 811016 | tf_op jit(solution)/shard_map/ppermute | solution.py:78
  12.5 2.1 %collective-permute-start = (f32[33,16,128]{2,1,0:T(8,128)S(1)}, f32[33,16,128]{2,1,0:T(8,128)S(1)}, u32[]{:S(2)}, u32[]{:S(2)}) collective-permute-start(f32[33,16,128]{2,1,0:T(8,128)S(1)} %get-tuple-element.56), channel_id=1, source_target_pairs={{0,36},{1,37},{2,38},{3,39},{4,32},{5,33},{6,34},{7,35},{8,44},{9,... | collective-permute-start | bytes 811016 | tf_op jit(solution)/shard_map/ppermute | solution.py:78
  14.6 3.1 %collective-permute-start.2 = (f32[33,16,128]{2,1,0:T(8,128)S(1)}, f32[33,16,128]{2,1,0:T(8,128)S(1)}, u32[]{:S(2)}, u32[]{:S(2)}) collective-permute-start(f32[33,16,128]{2,1,0:T(8,128)S(1)} %get-tuple-element.60), channel_id=1, source_target_pairs={{0,34},{1,35},{2,36},{3,37},{4,38},{5,39},{6,32},{7,33},{8,42},{9,... | collective-permute-start | bytes 811016 | tf_op jit(solution)/shard_map/ppermute | solution.py:78
  17.8 26.3 %collective-permute-done.1.refs_1_ = f32[33,16,128]{2,1,0:T(8,128)S(1)} collective-permute-done((f32[33,16,128]{2,1,0:T(8,128)S(1)}, f32[33,16,128]{2,1,0:T(8,128)S(1)}, u32[]{:S(2)}, u32[]{:S(2)}) %collective-permute-start.1) | collective-permute-done | bytes 270368 | tf_op jit(solution)/shard_map/ppermute | solution.py:78
  44.0 3.0 %collective-permute-start.4 = (f32[33,16,128]{2,1,0:T(8,128)S(1)}, f32[33,16,128]{2,1,0:T(8,128)S(1)}, u32[]{:S(2)}, u32[]{:S(2)}) collective-permute-start(f32[33,16,128]{2,1,0:T(8,128)S(1)} %get-tuple-element.63), channel_id=1, source_target_pairs={{0,35},{1,34},{2,37},{3,36},{4,39},{5,38},{6,33},{7,32},{8,43},{9,... | collective-permute-start | bytes 811016 | tf_op jit(solution)/shard_map/ppermute | solution.py:78
  47.0 2.7 %collective-permute-start.6 = (f32[33,16,128]{2,1,0:T(8,128)S(1)}, f32[33,16,128]{2,1,0:T(8,128)S(1)}, u32[]{:S(2)}, u32[]{:S(2)}) collective-permute-start(f32[33,16,128]{2,1,0:T(8,128)S(1)} %get-tuple-element.66), channel_id=1, source_target_pairs={{0,38},{1,39},{2,32},{3,33},{4,34},{5,35},{6,36},{7,37},{8,46},{9,... | collective-permute-start | bytes 811016 | tf_op jit(solution)/shard_map/ppermute | solution.py:78
  49.8 0.7 collective-permute-start.10
  50.4 4.9 %collective-permute-start.8 = (f32[2,8,16,128]{3,2,1,0:T(8,128)S(1)}, f32[2,8,16,128]{3,2,1,0:T(8,128)S(1)}, u32[]{:S(2)}, u32[]{:S(2)}) collective-permute-start(f32[2,8,16,128]{3,2,1,0:T(8,128)S(1)} %across_kernel.1), channel_id=1, source_target_pairs={{32,38},{33,39},{40,46},{41,47},{48,54},{49,55},{56,62},{57,63},{1... | collective-permute-start | bytes 393224 | tf_op jit(solution)/shard_map/ppermute | solution.py:78
  55.4 0.7 collective-permute-start.9
  56.1 11.2 %collective-permute-done.8.from_0_ref = f32[2,8,16,128]{3,2,1,0:T(8,128)S(1)} collective-permute-done((f32[2,8,16,128]{3,2,1,0:T(8,128)S(1)}, f32[2,8,16,128]{3,2,1,0:T(8,128)S(1)}, u32[]{:S(2)}, u32[]{:S(2)}) %collective-permute-start.8) | collective-permute-done | bytes 131104 | tf_op jit(solution)/shard_map/ppermute | solution.py:78
  67.3 0.2 cut_kernel.1
  67.5 0.1 collective-permute-start.11
  67.6 0.6 collective-permute-start.12
  68.2 3.4 %collective-permute-start.14 = (f32[8,8,16,128]{3,2,1,0:T(8,128)S(1)}, f32[8,8,16,128]{3,2,1,0:T(8,128)S(1)}, u32[]{:S(2)}, u32[]{:S(2)}) collective-permute-start(f32[8,8,16,128]{3,2,1,0:T(8,128)S(1)} %get-tuple-element.82), channel_id=1, source_target_pairs={{32,38},{34,32},{36,34},{38,36},{39,33},{37,39},{35,37},{33,35},{4... | collective-permute-start | bytes 1572872 | tf_op jit(solution)/shard_map/ppermute | solution.py:78
  71.6 0.2 fusion.ty_ref.refs_9_
  71.8 2.1 %first_kernel.1 = (f32[4,8,128,128]{3,2,1,0:T(8,128)S(1)}, f32[128,128]{1,0:T(8,128)S(1)}, f32[8,128]{1,0:T(8,128)S(1)}) custom-call(f32[33,16,128]{2,1,0:T(8,128)S(1)} %collective-permute-done.refs_0_, f32[33,16,128]{2,1,0:T(8,128)S(1)} %collective-permute-done.1.refs_1_, f32[33,16,128]{2,1,0:T(8,128)S(1)} %collective-permute-done.2.refs_2_, ...), custom_call_target="tpu_custom_call" | custom-call | flops 3000000000 | bytes 4194304 | tf_op jit(solution)/shard_map/first_kernel/pallas_call | solution.py:436
  73.9 9.8 %collective-permute-done.13.under_ref = f32[8,8,16,128]{3,2,1,0:T(8,128)S(1)} collective-permute-done((f32[8,8,16,128]{3,2,1,0:T(8,128)S(1)}, f32[8,8,16,128]{3,2,1,0:T(8,128)S(1)}, u32[]{:S(2)}, u32[]{:S(2)}) %collective-permute-start.13) | collective-permute-done | bytes 524320 | tf_op jit(solution)/shard_map/ppermute | solution.py:78
  83.8 0.1 collective-permute-done.11.away_ref
  83.9 1.0 first_edge_kernel.1
  84.9 3.9 %collective-permute-start.17 = (f32[4,16,16,128]{3,2,1,0:T(8,128)S(1)}, f32[4,16,16,128]{3,2,1,0:T(8,128)S(1)}, u32[]{:S(2)}, u32[]{:S(2)}) collective-permute-start(f32[4,16,16,128]{3,2,1,0:T(8,128)S(1)} %get-tuple-element.92), channel_id=1, source_target_pairs={{32,216},{34,218},{36,220},{38,222},{39,223},{37,221},{35,219},{33... | collective-permute-start | bytes 1572872 | tf_op jit(solution)/shard_map/ppermute | solution.py:78
  88.8 0.5 collective-permute-start.15
  89.3 0.1 collective-permute-start.16
  89.4 1.4 second_kernel.1.inner_ref
  90.8 4.8 %collective-permute-done.17.one_ref = f32[4,16,16,128]{3,2,1,0:T(8,128)S(1)} collective-permute-done((f32[4,16,16,128]{3,2,1,0:T(8,128)S(1)}, f32[4,16,16,128]{3,2,1,0:T(8,128)S(1)}, u32[]{:S(2)}, u32[]{:S(2)}) %collective-permute-start.17) | collective-permute-done | bytes 524320 | tf_op jit(solution)/shard_map/ppermute | solution.py:78
  95.7 0.2 second_edge_kernel.3
  95.9 0.6 collective-permute-start.24
  96.5 1.9 %collective-permute-start.22 = (f32[4,8,16,128]{3,2,1,0:T(8,128)S(1)}, f32[4,8,16,128]{3,2,1,0:T(8,128)S(1)}, u32[]{:S(2)}, u32[]{:S(2)}) collective-permute-start(f32[4,8,16,128]{3,2,1,0:T(8,128)S(1)} %get-tuple-element.99), channel_id=1, source_target_pairs={{32,0},{33,1},{34,2},{35,3},{36,4},{37,5},{38,6},{39,7},{40,8},{41... | collective-permute-start | bytes 786440 | tf_op jit(solution)/shard_map/ppermute | solution.py:78
  98.3 2.4 %collective-permute-start.19 = (f32[4,8,16,128]{3,2,1,0:T(8,128)S(1)}, f32[4,8,16,128]{3,2,1,0:T(8,128)S(1)}, u32[]{:S(2)}, u32[]{:S(2)}) collective-permute-start(f32[4,8,16,128]{3,2,1,0:T(8,128)S(1)} %get-tuple-element.94), channel_id=1, source_target_pairs={{36,0},{37,1},{38,2},{39,3},{32,4},{33,5},{34,6},{35,7},{44,8},{45... | collective-permute-start | bytes 786440 | tf_op jit(solution)/shard_map/ppermute | solution.py:78
  100.7 3.6 %collective-permute-start.20 = (f32[4,8,16,128]{3,2,1,0:T(8,128)S(1)}, f32[4,8,16,128]{3,2,1,0:T(8,128)S(1)}, u32[]{:S(2)}, u32[]{:S(2)}) collective-permute-start(f32[4,8,16,128]{3,2,1,0:T(8,128)S(1)} %get-tuple-element.96), channel_id=1, source_target_pairs={{37,0},{36,1},{39,2},{38,3},{33,4},{32,5},{35,6},{34,7},{45,8},{44... | collective-permute-start | bytes 786440 | tf_op jit(solution)/shard_map/ppermute | solution.py:78
  104.3 13.8 %collective-permute-done.16.other_ref = f32[4,16,16,128]{3,2,1,0:T(8,128)S(1)} collective-permute-done((f32[4,16,16,128]{3,2,1,0:T(8,128)S(1)}, f32[4,16,16,128]{3,2,1,0:T(8,128)S(1)}, u32[]{:S(2)}, u32[]{:S(2)}) %collective-permute-start.16) | collective-permute-done | bytes 524320 | tf_op jit(solution)/shard_map/ppermute | solution.py:78
  118.2 0.2 second_edge_kernel.2
  118.3 1.4 collective-permute-start.21
  119.8 3.3 %collective-permute-start.25 = (f32[4,8,16,128]{3,2,1,0:T(8,128)S(1)}, f32[4,8,16,128]{3,2,1,0:T(8,128)S(1)}, u32[]{:S(2)}, u32[]{:S(2)}) collective-permute-start(f32[4,8,16,128]{3,2,1,0:T(8,128)S(1)} %get-tuple-element.103), channel_id=1, source_target_pairs={{38,0},{39,1},{32,2},{33,3},{34,4},{35,5},{36,6},{37,7},{46,8},{47... | collective-permute-start | bytes 786440 | tf_op jit(solution)/shard_map/ppermute | solution.py:78
  123.1 1.9 %collective-permute-done.22.refs_6_ = f32[4,8,16,128]{3,2,1,0:T(8,128)S(1)} collective-permute-done((f32[4,8,16,128]{3,2,1,0:T(8,128)S(1)}, f32[4,8,16,128]{3,2,1,0:T(8,128)S(1)}, u32[]{:S(2)}, u32[]{:S(2)}) %collective-permute-start.22) | collective-permute-done | bytes 262176 | tf_op jit(solution)/shard_map/ppermute | solution.py:78
  125.0 5.2 %collective-permute-start.23 = (f32[4,8,16,128]{3,2,1,0:T(8,128)S(1)}, f32[4,8,16,128]{3,2,1,0:T(8,128)S(1)}, u32[]{:S(2)}, u32[]{:S(2)}) collective-permute-start(f32[4,8,16,128]{3,2,1,0:T(8,128)S(1)} %get-tuple-element.100), channel_id=1, source_target_pairs={{35,0},{34,1},{37,2},{36,3},{39,4},{38,5},{33,6},{32,7},{43,8},{42... | collective-permute-start | bytes 786440 | tf_op jit(solution)/shard_map/ppermute | solution.py:78
  130.3 4.2 %collective-permute-done.19.refs_0_ = f32[4,8,16,128]{3,2,1,0:T(8,128)S(1)} collective-permute-done((f32[4,8,16,128]{3,2,1,0:T(8,128)S(1)}, f32[4,8,16,128]{3,2,1,0:T(8,128)S(1)}, u32[]{:S(2)}, u32[]{:S(2)}) %collective-permute-start.19) | collective-permute-done | bytes 262176 | tf_op jit(solution)/shard_map/ppermute | solution.py:78
  134.4 4.0 %collective-permute-start.26 = (f32[4,8,16,128]{3,2,1,0:T(8,128)S(1)}, f32[4,8,16,128]{3,2,1,0:T(8,128)S(1)}, u32[]{:S(2)}, u32[]{:S(2)}) collective-permute-start(f32[4,8,16,128]{3,2,1,0:T(8,128)S(1)} %get-tuple-element.104), channel_id=1, source_target_pairs={{39,0},{38,1},{33,2},{32,3},{35,4},{34,5},{37,6},{36,7},{47,8},{46... | collective-permute-start | bytes 786440 | tf_op jit(solution)/shard_map/ppermute | solution.py:78
  138.4 6.4 %local_kernel.1.local_ref = f32[4,64,16,128]{3,2,1,0:T(8,128)S(1)} custom-call(f32[4,64,16,128]{3,2,1,0:T(8,128)S(1)} %copy-done.2, f32[64,128]{1,0:T(8,128)S(1)} %fusion.ty_ref.refs_9_, f32[1,128]{1,0:T(1,128)S(1)} %multiply_bitcast_fusion.vy_ref.refs_10_), custom_call_target="tpu_custom_call" | custom-call | flops 4000000000 | bytes 4194304 | tf_op jit(solution)/shard_map/local_kernel/pallas_call | solution.py:436
  144.9 6.5 %collective-permute-done.25.refs_4_ = f32[4,8,16,128]{3,2,1,0:T(8,128)S(1)} collective-permute-done((f32[4,8,16,128]{3,2,1,0:T(8,128)S(1)}, f32[4,8,16,128]{3,2,1,0:T(8,128)S(1)}, u32[]{:S(2)}, u32[]{:S(2)}) %collective-permute-start.25) | collective-permute-done | bytes 262176 | tf_op jit(solution)/shard_map/ppermute | solution.py:78
  151.4 1.9 %collective-permute-done.26.refs_5_ = f32[4,8,16,128]{3,2,1,0:T(8,128)S(1)} collective-permute-done((f32[4,8,16,128]{3,2,1,0:T(8,128)S(1)}, f32[4,8,16,128]{3,2,1,0:T(8,128)S(1)}, u32[]{:S(2)}, u32[]{:S(2)}) %collective-permute-start.26) | collective-permute-done | bytes 262176 | tf_op jit(solution)/shard_map/ppermute | solution.py:78
  153.3 1.4 final_kernel.1
  (36 shorter events, 0.1 us)
Async XLA Ops:
  0.0 71.6 %copy-start = (f32[64,128]{1,0:T(8,128)S(1)}, f32[64,128]{1,0:T(8,128)}, u32[]{:S(2)}) copy-start(f32[64,128]{1,0:T(8,128)} %param.11) | copy-start | bytes 98308
  0.8 1.6 %copy-start.1 = (f32[4,64,16,128]{3,2,1,0:T(8,128)S(1)}, f32[4,64,16,128]{3,2,1,0:T(8,128)}, u32[]{:S(2)}) copy-start(f32[4,64,16,128]{3,2,1,0:T(8,128)} %g_ref.3) | copy-start | bytes 6291460
  2.4 0.7 copy-start.3
  3.0 68.5 %copy-start.6 = (f32[128]{0:T(128)S(1)}, f32[128]{0:T(128)}, u32[]{:S(2)}) copy-start(f32[128]{0:T(128)} %param.13) | copy-start | bytes 1540
  3.0 68.5 %copy-start.7 = (s32[128]{0:T(128)S(1)}, s32[128]{0:T(128)}, u32[]{:S(2)}) copy-start(s32[128]{0:T(128)} %param.15) | copy-start | bytes 1540
  3.0 68.6 %copy-start.5 = (f32[128,128]{1,0:T(8,128)S(1)}, f32[128,128]{1,0:T(8,128)}, u32[]{:S(2)}) copy-start(f32[128,128]{1,0:T(8,128)} %constant.14.clone) | copy-start | bytes 196612
  3.2 68.6 %copy-start.4 = (f32[128,128]{1,0:T(8,128)S(1)}, f32[128,128]{1,0:T(8,128)}, u32[]{:S(2)}) copy-start(f32[128,128]{1,0:T(8,128)} %constant.15.clone.refs_8_) | copy-start | bytes 196612
  3.2 43.8 %collective-permute-start.5 = (f32[42,16,128]{2,1,0:T(8,128)S(1)}, f32[42,16,128]{2,1,0:T(8,128)S(1)}, u32[]{:S(2)}, u32[]{:S(2)}) collective-permute-start(f32[42,16,128]{2,1,0:T(8,128)S(1)} %get-tuple-element.65), channel_id=1, source_target_pairs={{0,32},{1,33},{2,34},{3,35},{4,36},{5,37},{6,38},{7,39},{8,40},{9,... | collective-permute-start | bytes 1032200 | tf_op jit(solution)/shard_map/ppermute | solution.py:78
  8.4 35.6 %collective-permute-start.3 = (f32[41,16,128]{2,1,0:T(8,128)S(1)}, f32[41,16,128]{2,1,0:T(8,128)S(1)}, u32[]{:S(2)}, u32[]{:S(2)}) collective-permute-start(f32[41,16,128]{2,1,0:T(8,128)S(1)} %get-tuple-element.62), channel_id=1, source_target_pairs={{0,33},{1,32},{2,35},{3,34},{4,37},{5,36},{6,39},{7,38},{8,41},{9,... | collective-permute-start | bytes 1007624 | tf_op jit(solution)/shard_map/ppermute | solution.py:78
  8.4 35.6 %collective-permute-start.1 = (f32[33,16,128]{2,1,0:T(8,128)S(1)}, f32[33,16,128]{2,1,0:T(8,128)S(1)}, u32[]{:S(2)}, u32[]{:S(2)}) collective-permute-start(f32[33,16,128]{2,1,0:T(8,128)S(1)} %get-tuple-element.58), channel_id=1, source_target_pairs={{0,37},{1,36},{2,39},{3,38},{4,33},{5,32},{6,35},{7,34},{8,45},{9,... | collective-permute-start | bytes 811016 | tf_op jit(solution)/shard_map/ppermute | solution.py:78
  12.5 37.3 %collective-permute-start = (f32[33,16,128]{2,1,0:T(8,128)S(1)}, f32[33,16,128]{2,1,0:T(8,128)S(1)}, u32[]{:S(2)}, u32[]{:S(2)}) collective-permute-start(f32[33,16,128]{2,1,0:T(8,128)S(1)} %get-tuple-element.56), channel_id=1, source_target_pairs={{0,36},{1,37},{2,38},{3,39},{4,32},{5,33},{6,34},{7,35},{8,44},{9,... | collective-permute-start | bytes 811016 | tf_op jit(solution)/shard_map/ppermute | solution.py:78
  14.6 35.8 %collective-permute-start.2 = (f32[33,16,128]{2,1,0:T(8,128)S(1)}, f32[33,16,128]{2,1,0:T(8,128)S(1)}, u32[]{:S(2)}, u32[]{:S(2)}) collective-permute-start(f32[33,16,128]{2,1,0:T(8,128)S(1)} %get-tuple-element.60), channel_id=1, source_target_pairs={{0,34},{1,35},{2,36},{3,37},{4,38},{5,39},{6,32},{7,33},{8,42},{9,... | collective-permute-start | bytes 811016 | tf_op jit(solution)/shard_map/ppermute | solution.py:78
  44.0 23.2 %collective-permute-start.7 = (f32[33,16,128]{2,1,0:T(8,128)S(1)}, f32[33,16,128]{2,1,0:T(8,128)S(1)}, u32[]{:S(2)}, u32[]{:S(2)}) collective-permute-start(f32[33,16,128]{2,1,0:T(8,128)S(1)} %get-tuple-element.67), channel_id=1, source_target_pairs={{0,39},{1,38},{2,33},{3,32},{4,35},{5,34},{6,37},{7,36},{8,47},{9,... | collective-permute-start | bytes 811016 | tf_op jit(solution)/shard_map/ppermute | solution.py:78
  44.0 23.2 %collective-permute-start.4 = (f32[33,16,128]{2,1,0:T(8,128)S(1)}, f32[33,16,128]{2,1,0:T(8,128)S(1)}, u32[]{:S(2)}, u32[]{:S(2)}) collective-permute-start(f32[33,16,128]{2,1,0:T(8,128)S(1)} %get-tuple-element.63), channel_id=1, source_target_pairs={{0,35},{1,34},{2,37},{3,36},{4,39},{5,38},{6,33},{7,32},{8,43},{9,... | collective-permute-start | bytes 811016 | tf_op jit(solution)/shard_map/ppermute | solution.py:78
  47.0 20.2 %collective-permute-start.6 = (f32[33,16,128]{2,1,0:T(8,128)S(1)}, f32[33,16,128]{2,1,0:T(8,128)S(1)}, u32[]{:S(2)}, u32[]{:S(2)}) collective-permute-start(f32[33,16,128]{2,1,0:T(8,128)S(1)} %get-tuple-element.66), channel_id=1, source_target_pairs={{0,38},{1,39},{2,32},{3,33},{4,34},{5,35},{6,36},{7,37},{8,46},{9,... | collective-permute-start | bytes 811016 | tf_op jit(solution)/shard_map/ppermute | solution.py:78
  49.8 5.6 %collective-permute-start.10 = (f32[2,8,16,128]{3,2,1,0:T(8,128)S(1)}, f32[2,8,16,128]{3,2,1,0:T(8,128)S(1)}, u32[]{:S(2)}, u32[]{:S(2)}) collective-permute-start(f32[2,8,16,128]{3,2,1,0:T(8,128)S(1)} %across_kernel.1), channel_id=1, source_target_pairs={{36,38},{37,39},{44,46},{45,47},{52,54},{53,55},{60,62},{61,63},{5... | collective-permute-start | bytes 393224 | tf_op jit(solution)/shard_map/ppermute | solution.py:78
  50.4 16.8 %collective-permute-start.8 = (f32[2,8,16,128]{3,2,1,0:T(8,128)S(1)}, f32[2,8,16,128]{3,2,1,0:T(8,128)S(1)}, u32[]{:S(2)}, u32[]{:S(2)}) collective-permute-start(f32[2,8,16,128]{3,2,1,0:T(8,128)S(1)} %across_kernel.1), channel_id=1, source_target_pairs={{32,38},{33,39},{40,46},{41,47},{48,54},{49,55},{56,62},{57,63},{1... | collective-permute-start | bytes 393224 | tf_op jit(solution)/shard_map/ppermute | solution.py:78
  55.4 11.8 %collective-permute-start.9 = (f32[2,8,16,128]{3,2,1,0:T(8,128)S(1)}, f32[2,8,16,128]{3,2,1,0:T(8,128)S(1)}, u32[]{:S(2)}, u32[]{:S(2)}) collective-permute-start(f32[2,8,16,128]{3,2,1,0:T(8,128)S(1)} %across_kernel.1), channel_id=1, source_target_pairs={{34,38},{35,39},{42,46},{43,47},{50,54},{51,55},{58,62},{59,63},{3... | collective-permute-start | bytes 393224 | tf_op jit(solution)/shard_map/ppermute | solution.py:78
  67.5 16.4 %collective-permute-start.11 = (f32[8,16,16,128]{3,2,1,0:T(8,128)S(1)}, f32[8,16,16,128]{3,2,1,0:T(8,128)S(1)}, u32[]{:S(2)}, u32[]{:S(2)}) collective-permute-start(f32[8,16,16,128]{3,2,1,0:T(8,128)S(1)} %get-tuple-element.79), channel_id=1, source_target_pairs={{32,216},{34,218},{36,220},{38,222},{39,223},{37,221},{35,219},{33... | collective-permute-start | bytes 3145736 | tf_op jit(solution)/shard_map/ppermute | solution.py:78
  67.6 16.3 %collective-permute-start.12 = (f32[8,16,16,128]{3,2,1,0:T(8,128)S(1)}, f32[8,16,16,128]{3,2,1,0:T(8,128)S(1)}, u32[]{:S(2)}, u32[]{:S(2)}) collective-permute-start(f32[8,16,16,128]{3,2,1,0:T(8,128)S(1)} %get-tuple-element.80), channel_id=1, source_target_pairs={{32,40},{34,42},{36,44},{38,46},{39,47},{37,45},{35,43},{33,41},{4... | collective-permute-start | bytes 3145736 | tf_op jit(solution)/shard_map/ppermute | solution.py:78
  68.2 15.6 %collective-permute-start.13 = (f32[8,8,16,128]{3,2,1,0:T(8,128)S(1)}, f32[8,8,16,128]{3,2,1,0:T(8,128)S(1)}, u32[]{:S(2)}, u32[]{:S(2)}) collective-permute-start(f32[8,8,16,128]{3,2,1,0:T(8,128)S(1)} %get-tuple-element.81), channel_id=1, source_target_pairs={{32,34},{34,36},{36,38},{38,32},{39,37},{37,35},{35,33},{33,39},{4... | collective-permute-start | bytes 1572872 | tf_op jit(solution)/shard_map/ppermute | solution.py:78
  68.2 15.6 %collective-permute-start.14 = (f32[8,8,16,128]{3,2,1,0:T(8,128)S(1)}, f32[8,8,16,128]{3,2,1,0:T(8,128)S(1)}, u32[]{:S(2)}, u32[]{:S(2)}) collective-permute-start(f32[8,8,16,128]{3,2,1,0:T(8,128)S(1)} %get-tuple-element.82), channel_id=1, source_target_pairs={{32,38},{34,32},{36,34},{38,36},{39,33},{37,39},{35,37},{33,35},{4... | collective-permute-start | bytes 1572872 | tf_op jit(solution)/shard_map/ppermute | solution.py:78
  84.9 10.8 %collective-permute-start.17 = (f32[4,16,16,128]{3,2,1,0:T(8,128)S(1)}, f32[4,16,16,128]{3,2,1,0:T(8,128)S(1)}, u32[]{:S(2)}, u32[]{:S(2)}) collective-permute-start(f32[4,16,16,128]{3,2,1,0:T(8,128)S(1)} %get-tuple-element.92), channel_id=1, source_target_pairs={{32,216},{34,218},{36,220},{38,222},{39,223},{37,221},{35,219},{33... | collective-permute-start | bytes 1572872 | tf_op jit(solution)/shard_map/ppermute | solution.py:78
  88.8 6.9 %collective-permute-start.18 = (f32[4,16,16,128]{3,2,1,0:T(8,128)S(1)}, f32[4,16,16,128]{3,2,1,0:T(8,128)S(1)}, u32[]{:S(2)}, u32[]{:S(2)}) collective-permute-start(f32[4,16,16,128]{3,2,1,0:T(8,128)S(1)} %get-tuple-element.93), channel_id=1, source_target_pairs={{32,40},{34,42},{36,44},{38,46},{39,47},{37,45},{35,43},{33,41},{4... | collective-permute-start | bytes 1572872 | tf_op jit(solution)/shard_map/ppermute | solution.py:78
  88.8 11.9 %collective-permute-start.15 = (f32[4,16,16,128]{3,2,1,0:T(8,128)S(1)}, f32[4,16,16,128]{3,2,1,0:T(8,128)S(1)}, u32[]{:S(2)}, u32[]{:S(2)}) collective-permute-start(f32[4,16,16,128]{3,2,1,0:T(8,128)S(1)} %get-tuple-element.89), channel_id=1, source_target_pairs={{32,40},{34,42},{36,44},{38,46},{39,47},{37,45},{35,43},{33,41},{4... | collective-permute-start | bytes 1572872 | tf_op jit(solution)/shard_map/ppermute | solution.py:78
  89.3 28.9 %collective-permute-start.16 = (f32[4,16,16,128]{3,2,1,0:T(8,128)S(1)}, f32[4,16,16,128]{3,2,1,0:T(8,128)S(1)}, u32[]{:S(2)}, u32[]{:S(2)}) collective-permute-start(f32[4,16,16,128]{3,2,1,0:T(8,128)S(1)} %get-tuple-element.90), channel_id=1, source_target_pairs={{32,216},{34,218},{36,220},{38,222},{39,223},{37,221},{35,219},{33... | collective-permute-start | bytes 1572872 | tf_op jit(solution)/shard_map/ppermute | solution.py:78
  95.9 42.6 %copy-start.2 = (f32[4,64,16,128]{3,2,1,0:T(8,128)S(1)}, f32[4,64,16,128]{3,2,1,0:T(8,128)}, u32[]{:S(2)}) copy-start(f32[4,64,16,128]{3,2,1,0:T(8,128)} %g_ref.3) | copy-start | bytes 6291460
  95.9 23.9 %collective-permute-start.24 = (f32[4,8,16,128]{3,2,1,0:T(8,128)S(1)}, f32[4,8,16,128]{3,2,1,0:T(8,128)S(1)}, u32[]{:S(2)}, u32[]{:S(2)}) collective-permute-start(f32[4,8,16,128]{3,2,1,0:T(8,128)S(1)} %get-tuple-element.102), channel_id=1, source_target_pairs={{33,0},{32,1},{35,2},{34,3},{37,4},{36,5},{39,6},{38,7},{41,8},{40... | collective-permute-start | bytes 786440 | tf_op jit(solution)/shard_map/ppermute | solution.py:78
  96.5 28.6 %collective-permute-start.22 = (f32[4,8,16,128]{3,2,1,0:T(8,128)S(1)}, f32[4,8,16,128]{3,2,1,0:T(8,128)S(1)}, u32[]{:S(2)}, u32[]{:S(2)}) collective-permute-start(f32[4,8,16,128]{3,2,1,0:T(8,128)S(1)} %get-tuple-element.99), channel_id=1, source_target_pairs={{32,0},{33,1},{34,2},{35,3},{36,4},{37,5},{38,6},{39,7},{40,8},{41... | collective-permute-start | bytes 786440 | tf_op jit(solution)/shard_map/ppermute | solution.py:78
  98.3 36.1 %collective-permute-start.19 = (f32[4,8,16,128]{3,2,1,0:T(8,128)S(1)}, f32[4,8,16,128]{3,2,1,0:T(8,128)S(1)}, u32[]{:S(2)}, u32[]{:S(2)}) collective-permute-start(f32[4,8,16,128]{3,2,1,0:T(8,128)S(1)} %get-tuple-element.94), channel_id=1, source_target_pairs={{36,0},{37,1},{38,2},{39,3},{32,4},{33,5},{34,6},{35,7},{44,8},{45... | collective-permute-start | bytes 786440 | tf_op jit(solution)/shard_map/ppermute | solution.py:78
  100.7 44.2 %collective-permute-start.20 = (f32[4,8,16,128]{3,2,1,0:T(8,128)S(1)}, f32[4,8,16,128]{3,2,1,0:T(8,128)S(1)}, u32[]{:S(2)}, u32[]{:S(2)}) collective-permute-start(f32[4,8,16,128]{3,2,1,0:T(8,128)S(1)} %get-tuple-element.96), channel_id=1, source_target_pairs={{37,0},{36,1},{39,2},{38,3},{33,4},{32,5},{35,6},{34,7},{45,8},{44... | collective-permute-start | bytes 786440 | tf_op jit(solution)/shard_map/ppermute | solution.py:78
  118.3 26.5 %collective-permute-start.21 = (f32[4,8,16,128]{3,2,1,0:T(8,128)S(1)}, f32[4,8,16,128]{3,2,1,0:T(8,128)S(1)}, u32[]{:S(2)}, u32[]{:S(2)}) collective-permute-start(f32[4,8,16,128]{3,2,1,0:T(8,128)S(1)} %get-tuple-element.97), channel_id=1, source_target_pairs={{34,0},{35,1},{36,2},{37,3},{38,4},{39,5},{32,6},{33,7},{42,8},{43... | collective-permute-start | bytes 786440 | tf_op jit(solution)/shard_map/ppermute | solution.py:78
  119.8 31.6 %collective-permute-start.25 = (f32[4,8,16,128]{3,2,1,0:T(8,128)S(1)}, f32[4,8,16,128]{3,2,1,0:T(8,128)S(1)}, u32[]{:S(2)}, u32[]{:S(2)}) collective-permute-start(f32[4,8,16,128]{3,2,1,0:T(8,128)S(1)} %get-tuple-element.103), channel_id=1, source_target_pairs={{38,0},{39,1},{32,2},{33,3},{34,4},{35,5},{36,6},{37,7},{46,8},{47... | collective-permute-start | bytes 786440 | tf_op jit(solution)/shard_map/ppermute | solution.py:78
  125.0 26.4 %collective-permute-start.23 = (f32[4,8,16,128]{3,2,1,0:T(8,128)S(1)}, f32[4,8,16,128]{3,2,1,0:T(8,128)S(1)}, u32[]{:S(2)}, u32[]{:S(2)}) collective-permute-start(f32[4,8,16,128]{3,2,1,0:T(8,128)S(1)} %get-tuple-element.100), channel_id=1, source_target_pairs={{35,0},{34,1},{37,2},{36,3},{39,4},{38,5},{33,6},{32,7},{43,8},{42... | collective-permute-start | bytes 786440 | tf_op jit(solution)/shard_map/ppermute | solution.py:78
  134.4 18.9 %collective-permute-start.26 = (f32[4,8,16,128]{3,2,1,0:T(8,128)S(1)}, f32[4,8,16,128]{3,2,1,0:T(8,128)S(1)}, u32[]{:S(2)}, u32[]{:S(2)}) collective-permute-start(f32[4,8,16,128]{3,2,1,0:T(8,128)S(1)} %get-tuple-element.104), channel_id=1, source_target_pairs={{39,0},{38,1},{33,2},{32,3},{35,4},{34,5},{37,6},{36,7},{47,8},{46... | collective-permute-start | bytes 786440 | tf_op jit(solution)/shard_map/ppermute | solution.py:78
